TPU v7x, 32 devices: a whole 2x2x4 slice. The times are simulated.
32 devices in a mesh: grp: 1, row: 16 (over z, y, core), col: 2 (over x), ch: 1.
Axes of the slice: x: 2, y: 2, z: 4, core: 2. Of those that a mesh axis runs over, the one named last changes fastest.
Arguments:
- pair: bfloat16 [256, 256, 128], P(('grp', 'row'), 'col'), may hold values from -6 to 6
- cotangent: bfloat16 [256, 256, 128], P(('grp', 'row'), 'col'), may hold values from -6 to 6
- lengths: int32 [1], P('grp'), may hold values from 128 to 256
- norm_gain: float32 [2, 128], replicated, may hold values from 0.25 to 1.75
- norm_bias: float32 [2, 128], replicated, may hold values from -1.5 to 1.5
- proj_weight: bfloat16 [2, 2, 128, 128], P(None, None, None, 'ch'), may hold values from -0.5 to 0.5
- gate_weight: bfloat16 [2, 2, 128, 128], P(None, None, None, 'ch'), may hold values from -0.5 to 0.5
- mid_gain: float32 [2, 128], P(None, 'ch'), may hold values from 0.25 to 1.75
- mid_bias: float32 [2, 128], P(None, 'ch'), may hold values from -1.5 to 1.5
- out_weight: bfloat16 [2, 128, 128], replicated, may hold values from -0.5 to 0.5
- outgate_weight: bfloat16 [2, 128, 128], replicated, may hold values from -0.5 to 0.5
Outputs:
- new_pair: bfloat16 [256, 256, 128], P(('grp', 'row'), 'col')
- grad_pair: bfloat16 [256, 256, 128], P(('grp', 'row'), 'col')
- grad_norm_gain: float32 [2, 128], P('grp')
- grad_norm_bias: float32 [2, 128], P('grp')
- grad_proj_weight: float32 [2, 2, 128, 128], P('grp', None, None, 'ch')
- grad_gate_weight: float32 [2, 2, 128, 128], P('grp', None, None, 'ch')
- grad_mid_gain: float32 [2, 128], P('grp', 'ch')
- grad_mid_bias: float32 [2, 128], P('grp', 'ch')
- grad_out_weight: float32 [2, 128, 128], P('grp')
- grad_outgate_weight: float32 [2, 128, 128], P('grp')
Inputs may be any that keep to these rules, and one draw needn't show every extreme that they name: Residues from lengths on are padding of the complex.
All inputs are finite; a program needn't handle non-finite values.
Results may differ from a plain program's by a relative error of at most 0.02.
Values may be sent and summed in bfloat16 or wider, within the bound.
No kernel may reach another device: no remote copies, remote signals or barrier semaphores. Data moves between devices by JAX's collectives and lax.ppermute only.
A program may use at most 64 MiB of HBM per device.

v0:
```python
import jax
import jax.numpy as jnp
from jax import lax
from jax.sharding import PartitionSpec as P

H = 128


EPS = 1e-05


def product(spec, left, right):
    return jnp.einsum(spec, left, right, preferred_element_type=jnp.float32)


def norm_channels(values):
    average = jnp.mean(values, -1, keepdims=True)
    centred = values - average
    variance = jnp.mean(centred * centred, -1, keepdims=True)
    inverse = lax.rsqrt(variance + EPS)
    return (centred * inverse, inverse)


def forward_module(pair_in, pair_mask, weights, incoming):
    gain_in, bias_in, proj_w, gate_w, gain_mid, bias_mid, out_w, outgate_w = weights
    scaled_in, inverse_in = norm_channels(pair_in.astype(jnp.float32))
    normed = (scaled_in * gain_in + bias_in).astype(jnp.bfloat16)
    projected = product("ijc,sch->shij", normed, proj_w)
    gating = jax.nn.sigmoid(product("ijc,sch->shij", normed, gate_w))
    hidden = (projected * gating * pair_mask).astype(jnp.bfloat16)
    left_side, right_side = (
        lax.all_to_all(hidden[0], "row", split_axis=0, concat_axis=1, tiled=True),
        lax.all_to_all(hidden[1], "row", split_axis=0, concat_axis=1, tiled=True),
    )
    if incoming:
        left_side = jnp.swapaxes(left_side, 1, 2)
        right_side = jnp.swapaxes(right_side, 1, 2)
    else:
        left_side, right_side = (
            lax.all_to_all(left_side, "col", split_axis=1, concat_axis=2, tiled=True),
            lax.all_to_all(right_side, "col", split_axis=1, concat_axis=2, tiled=True),
        )
    triangle = product(
        "cik,cjk->cij", left_side, lax.all_gather(right_side, "col", axis=1, tiled=True)
    ).astype(jnp.bfloat16)
    triangle = lax.all_to_all(
        lax.all_to_all(triangle, "col", split_axis=2, concat_axis=1, tiled=True),
        "row",
        split_axis=1,
        concat_axis=0,
        tiled=True,
    )
    tri_values = triangle.astype(jnp.float32)
    total, squares = lax.psum((jnp.sum(tri_values, 0), jnp.sum(tri_values * tri_values, 0)), "ch")
    average = total / H
    inverse_mid = lax.rsqrt(squares / H - average * average + EPS)
    scaled_mid = (tri_values - average) * inverse_mid
    unit = (scaled_mid * gain_mid[:, None, None] + bias_mid[:, None, None]).astype(jnp.bfloat16)
    unit_full = lax.all_gather(unit, "ch", axis=0, tiled=True)
    outer = product("hij,hc->ijc", unit_full, out_w)
    outgate = jax.nn.sigmoid(product("ijc,cd->ijd", normed, outgate_w))
    result = (pair_in.astype(jnp.float32) + outer * outgate).astype(jnp.bfloat16)
    saved = (
        scaled_in,
        inverse_in,
        normed,
        projected,
        gating,
        left_side,
        right_side,
        scaled_mid,
        inverse_mid,
        unit_full,
        outer,
        outgate,
    )
    return (result, saved)


def backward_module(grad_out, pair_mask, weights, saved, incoming):
    gain_in, bias_in, proj_w, gate_w, gain_mid, bias_mid, out_w, outgate_w = weights
    (
        scaled_in,
        inverse_in,
        normed,
        projected,
        gating,
        left_side,
        right_side,
        scaled_mid,
        inverse_mid,
        unit_full,
        outer,
        outgate,
    ) = saved
    d_outer = (grad_out * outgate).astype(jnp.bfloat16)
    d_gatepre = (grad_out * outer * outgate * (1.0 - outgate)).astype(jnp.bfloat16)
    grad_out_w = product("hij,ijc->hc", unit_full, d_outer)
    grad_outgate_w = product("ijc,ijd->cd", normed, d_gatepre)
    width = gain_mid.shape[0]
    own_rows = lax.dynamic_slice_in_dim(out_w, lax.axis_index("ch") * width, width, 0)
    d_unit = product("ijc,hc->hij", d_outer, own_rows)
    d_normed = product("ijd,cd->ijc", d_gatepre, outgate_w)
    weighted = d_unit * gain_mid[:, None, None]
    grad_gain_mid = jnp.sum(d_unit * scaled_mid, (1, 2))
    grad_bias_mid = jnp.sum(d_unit, (1, 2))
    first_sum, second_sum = lax.psum(
        (jnp.sum(weighted, 0), jnp.sum(weighted * scaled_mid, 0)), "ch"
    )
    d_tri = (inverse_mid * (weighted - first_sum / H - scaled_mid * (second_sum / H))).astype(
        jnp.bfloat16
    )
    grad_rows = lax.all_to_all(d_tri, "row", split_axis=0, concat_axis=1, tiled=True)
    grad_cols = lax.all_to_all(grad_rows, "col", split_axis=1, concat_axis=2, tiled=True)
    d_left = product(
        "cij,cjk->cik", grad_cols, lax.all_gather(right_side, "col", axis=1, tiled=True)
    )
    partial_terms = product("cij,cik->cjk", grad_cols, left_side)
    d_right = lax.psum_scatter(
        partial_terms.astype(jnp.bfloat16), "col", scatter_dimension=1, tiled=True
    ).astype(jnp.float32)
    d_left = d_left.astype(jnp.bfloat16)
    d_right = d_right.astype(jnp.bfloat16)
    if incoming:
        d_left = jnp.swapaxes(d_left, 1, 2)
        d_right = jnp.swapaxes(d_right, 1, 2)
    else:
        d_left, d_right = (
            lax.all_to_all(d_left, "col", split_axis=2, concat_axis=1, tiled=True),
            lax.all_to_all(d_right, "col", split_axis=2, concat_axis=1, tiled=True),
        )
    d_left, d_right = (
        lax.all_to_all(d_left, "row", split_axis=1, concat_axis=0, tiled=True),
        lax.all_to_all(d_right, "row", split_axis=1, concat_axis=0, tiled=True),
    )
    d_hidden = jnp.stack([d_left, d_right]).astype(jnp.float32)
    d_proj = (d_hidden * gating * pair_mask).astype(jnp.bfloat16)
    d_gate = (d_hidden * projected * gating * (1.0 - gating) * pair_mask).astype(jnp.bfloat16)
    grad_proj_w = product("ijc,shij->sch", normed, d_proj)
    grad_gate_w = product("ijc,shij->sch", normed, d_gate)
    partial_input = product("shij,sch->ijc", d_proj, proj_w) + product(
        "shij,sch->ijc", d_gate, gate_w
    )
    d_normed = d_normed + lax.psum(partial_input.astype(jnp.bfloat16), "ch").astype(jnp.float32)
    weighted_in = d_normed * gain_in
    grad_gain_in = jnp.sum(d_normed * scaled_in, (0, 1))
    grad_bias_in = jnp.sum(d_normed, (0, 1))
    d_pair = inverse_in * (
        weighted_in
        - jnp.mean(weighted_in, -1, keepdims=True)
        - scaled_in * jnp.mean(weighted_in * scaled_in, -1, keepdims=True)
    )
    grads = (
        grad_gain_in,
        grad_bias_in,
        grad_proj_w,
        grad_gate_w,
        grad_gain_mid,
        grad_bias_mid,
        grad_out_w,
        grad_outgate_w,
    )
    return (grad_out + d_pair, grads)


def per_device(
    pair,
    cotangent,
    lengths,
    norm_gain,
    norm_bias,
    proj_weight,
    gate_weight,
    mid_gain,
    mid_bias,
    out_weight,
    outgate_weight,
):
    rows_here = pair.shape[0]
    cols_here = pair.shape[1]
    row_ids = lax.axis_index("row") * rows_here + lax.iota(jnp.int32, rows_here)
    col_ids = lax.axis_index("col") * cols_here + lax.iota(jnp.int32, cols_here)
    limit = lengths[0]
    pair_mask = ((row_ids[:, None] < limit) & (col_ids[None, :] < limit)).astype(jnp.float32)
    state = pair
    stash = []
    for layer in range(2):
        weights = (
            norm_gain[layer],
            norm_bias[layer],
            proj_weight[layer],
            gate_weight[layer],
            mid_gain[layer],
            mid_bias[layer],
            out_weight[layer],
            outgate_weight[layer],
        )
        state, saved = forward_module(state, pair_mask, weights, layer == 1)
        stash.append(saved)
    grad_state = cotangent.astype(jnp.float32)
    per_layer = [None, None]
    for layer in (1, 0):
        weights = (
            norm_gain[layer],
            norm_bias[layer],
            proj_weight[layer],
            gate_weight[layer],
            mid_gain[layer],
            mid_bias[layer],
            out_weight[layer],
            outgate_weight[layer],
        )
        grad_state, grads = backward_module(
            grad_state, pair_mask, weights, stash[layer], layer == 1
        )
        per_layer[layer] = grads
    lower = per_layer[0]
    upper = per_layer[1]
    summed = lax.psum(
        (
            lower[0],
            lower[1],
            lower[2],
            lower[3],
            lower[4],
            lower[5],
            lower[6],
            lower[7],
            upper[0],
            upper[1],
            upper[2],
            upper[3],
            upper[4],
            upper[5],
            upper[6],
            upper[7],
        ),
        ("row", "col"),
    )
    per_layer = [summed[0:8], summed[8:16]]
    stacked = [jnp.stack([per_layer[0][index], per_layer[1][index]]) for index in range(8)]
    return (
        state,
        grad_state.astype(jnp.bfloat16),
        stacked[0],
        stacked[1],
        stacked[2],
        stacked[3],
        stacked[4],
        stacked[5],
        stacked[6],
        stacked[7],
    )


def solution(mesh):
    in_specs = (
        P(("grp", "row"), "col", None),
        P(("grp", "row"), "col", None),
        P("grp"),
        P(),
        P(),
        P(None, None, None, "ch"),
        P(None, None, None, "ch"),
        P(None, "ch"),
        P(None, "ch"),
        P(),
        P(),
    )
    out_specs = (
        P(("grp", "row"), "col", None),
        P(("grp", "row"), "col", None),
        P("grp", None),
        P("grp", None),
        P("grp", None, None, "ch"),
        P("grp", None, None, "ch"),
        P("grp", "ch"),
        P("grp", "ch"),
        P("grp", None, None),
        P("grp", None, None),
    )
    return jax.shard_map(
        per_device, mesh=mesh, in_specs=in_specs, out_specs=out_specs, check_vma=False
    )
```

profile of v0, /device:TPU:0, one launch (start us, length us, event | category | flops | bytes accessed | tf_op | source)
XLA Modules:
  0.0 617.7 jit_solution(17248424253775647969)
XLA Ops:
  10.3 2.3 fusion.15
  13.1 21.7 %all_to_all.330 = bf16[128,16,128]{2,1,0:T(8,128)(2,1)S(1)} all-to-all(bf16[128,16,128]{2,1,0:T(8,128)(2,1)S(1)} %copy.363), channel_id=1, replica_groups=mesh['grp'=1,'row'=16,'col'=2,'ch'=1] {'row'}, dimensions={0} | all-to-all | bytes 1048576 | tf_op jit(solution)/shard_map/all_to_all | solution.py:33
  36.0 3.5 all-to-all-start.3
  40.6 7.2 %all-to-all-done.3 = bf16[8,256,128]{2,0,1:T(8,128)(2,1)S(1)} async-done(((bf16[8,256,128]{2,0,1:T(8,128)(2,1)}), bf16[8,256,128]{2,0,1:T(8,128)(2,1)S(1)}, u32[]{:S(2)}, u32[]{:S(2)}) %all-to-all-start.3) | async-done | bytes 524320 | tf_op jit(solution)/shard_map/all_to_all | solution.py:41
  47.9 4.4 all-to-all-start
  54.0 12.7 %all-to-all-done = bf16[128,16,128]{2,1,0:T(8,128)(2,1)S(1)} async-done(((bf16[128,16,128]{2,1,0:T(8,128)(2,1)}), bf16[128,16,128]{2,1,0:T(8,128)(2,1)S(1)}, u32[]{:S(2)}, u32[]{:S(2)}) %all-to-all-start) | async-done | bytes 524320 | tf_op jit(solution)/shard_map/all_to_all | solution.py:32
  67.1 15.2 %all_to_all.331 = bf16[8,256,128]{2,0,1:T(8,128)(2,1)S(1)} all-to-all(bf16[8,256,128]{2,0,1:T(8,128)(2,1)S(1)} %copy.360), channel_id=1, replica_groups=mesh['grp'=1,'row'=16,'col'=2,'ch'=1] {'col'}, dimensions={1} | all-to-all | bytes 1048576 | tf_op jit(solution)/shard_map/all_to_all | solution.py:40
  83.2 1.9 convolution_convert_fusion.5
  85.5 10.6 %all_to_all.332 = bf16[8,128,256]{1,0,2:T(8,128)(2,1)S(1)} all-to-all(bf16[8,128,256]{1,0,2:T(8,128)(2,1)S(1)} %copy.368), channel_id=1, replica_groups=mesh['grp'=1,'row'=16,'col'=2,'ch'=1] {'col'}, dimensions={2} | all-to-all | bytes 1048576 | tf_op jit(solution)/shard_map/all_to_all | solution.py:47
  97.3 5.7 all-to-all-start.5
  104.5 13.0 %all-to-all-done.5 = bf16[8,256,128]{2,0,1:T(8,128)(2,1)S(1)} async-done(((bf16[8,256,128]{2,0,1:T(8,128)(2,1)}), bf16[8,256,128]{2,0,1:T(8,128)(2,1)S(1)}, u32[]{:S(2)}, u32[]{:S(2)}) %all-to-all-start.5) | async-done | bytes 524320 | tf_op jit(solution)/shard_map/all_to_all | solution.py:46
  121.4 2.3 fusion.13
  124.2 18.4 %all_to_all.333 = bf16[128,16,128]{2,1,0:T(8,128)(2,1)S(1)} all-to-all(bf16[128,16,128]{2,1,0:T(8,128)(2,1)S(1)} %copy.384), channel_id=1, replica_groups=mesh['grp'=1,'row'=16,'col'=2,'ch'=1] {'row'}, dimensions={0} | all-to-all | bytes 1048576 | tf_op jit(solution)/shard_map/all_to_all | solution.py:33
  144.1 18.4 %all_to_all.334 = bf16[128,16,128]{2,1,0:T(8,128)(2,1)S(1)} all-to-all(bf16[128,16,128]{2,1,0:T(8,128)(2,1)S(1)} %copy.382), channel_id=1, replica_groups=mesh['grp'=1,'row'=16,'col'=2,'ch'=1] {'row'}, dimensions={0} | all-to-all | bytes 1048576 | tf_op jit(solution)/shard_map/all_to_all | solution.py:32
  163.6 1.7 convolution_convert_fusion.4
  165.7 10.7 %all_to_all.335 = bf16[8,128,256]{1,0,2:T(8,128)(2,1)S(1)} all-to-all(bf16[8,128,256]{1,0,2:T(8,128)(2,1)S(1)} %copy.388), channel_id=1, replica_groups=mesh['grp'=1,'row'=16,'col'=2,'ch'=1] {'col'}, dimensions={2} | all-to-all | bytes 1048576 | tf_op jit(solution)/shard_map/all_to_all | solution.py:47
  177.6 5.6 all-to-all-start.9
  184.9 12.8 %all-to-all-done.9 = bf16[8,256,128]{2,0,1:T(8,128)(2,1)S(1)} async-done(((bf16[8,256,128]{2,0,1:T(8,128)(2,1)}), bf16[8,256,128]{2,0,1:T(8,128)(2,1)S(1)}, u32[]{:S(2)}, u32[]{:S(2)}) %all-to-all-start.9) | async-done | bytes 524320 | tf_op jit(solution)/shard_map/all_to_all | solution.py:46
  199.8 1.6 copy.405
  203.4 1.8 fusion.60
  208.8 1.9 multiply_convert_fusion.3
  212.2 18.4 %all_to_all.336 = bf16[128,16,128]{2,1,0:T(8,128)(2,1)S(1)} all-to-all(bf16[128,16,128]{2,1,0:T(8,128)(2,1)S(1)} %copy.406), channel_id=1, replica_groups=mesh['grp'=1,'row'=16,'col'=2,'ch'=1] {'row'}, dimensions={0} | all-to-all | bytes 1048576 | tf_op jit(solution)/shard_map/all_to_all | solution.py:113
  231.0 10.8 %all_to_all.337 = bf16[8,256,128]{2,0,1:T(8,128)(2,1)S(1)} all-to-all(bf16[8,256,128]{2,0,1:T(8,128)(2,1)S(1)} %copy.408), channel_id=1, replica_groups=mesh['grp'=1,'row'=16,'col'=2,'ch'=1] {'col'}, dimensions={1} | all-to-all | bytes 1048576 | tf_op jit(solution)/shard_map/all_to_all | solution.py:114
  243.1 2.2 all_to_all.281
  245.3 2.5 convolution_convert_fusion.1
  247.8 1.9 convolution_convert_fusion.3
  250.9 4.4 all-to-all-start.12
  255.3 11.8 %reduce-scatter.3.cloned.1.call-done = bf16[8,128,256]{2,1,0:T(8,128)(2,1)} async-done(((bf16[8,256,256]{2,1,0:T(8,128)(2,1)}), bf16[8,128,256]{2,1,0:T(8,128)(2,1)}) %reduce-scatter.3.cloned.1.call-update) | async-done | bytes 524304 | tf_op jit(solution)/shard_map/reduce_scatter | solution.py:119
  267.1 2.1 copy.416
  269.7 5.2 all-to-all-start.13
  275.2 2.3 copy.428
  277.5 2.6 copy.429
  282.5 7.0 %all-to-all-done.13 = bf16[8,256,128]{2,0,1:T(8,128)(2,1)} async-done(((bf16[8,256,128]{2,0,1:T(8,128)(2,1)}), bf16[8,256,128]{2,0,1:T(8,128)(2,1)}, u32[]{:S(2)}, u32[]{:S(2)}) %all-to-all-start.13) | async-done | bytes 524320 | tf_op jit(solution)/shard_map/all_to_all | solution.py:134
  289.4 1.9 copy.418
  291.4 2.3 copy.420
  293.6 3.2 fusion.1
  304.0 1.9 multiply_convert_fusion
  307.4 18.4 %all_to_all.338 = bf16[128,16,128]{2,1,0:T(8,128)(2,1)S(1)} all-to-all(bf16[128,16,128]{2,1,0:T(8,128)(2,1)S(1)} %copy.430), channel_id=1, replica_groups=mesh['grp'=1,'row'=16,'col'=2,'ch'=1] {'row'}, dimensions={0} | all-to-all | bytes 1048576 | tf_op jit(solution)/shard_map/all_to_all | solution.py:113
  326.1 10.8 %all_to_all.339 = bf16[8,256,128]{2,0,1:T(8,128)(2,1)S(1)} all-to-all(bf16[8,256,128]{2,0,1:T(8,128)(2,1)S(1)} %copy.432), channel_id=1, replica_groups=mesh['grp'=1,'row'=16,'col'=2,'ch'=1] {'col'}, dimensions={1} | all-to-all | bytes 1048576 | tf_op jit(solution)/shard_map/all_to_all | solution.py:114
  338.3 2.2 all_to_all.295
  340.5 2.5 convolution_convert_fusion
  343.0 1.7 convolution_convert_fusion.2
  345.8 3.5 all-to-all-start.16
  349.3 18.5 %reduce-scatter.5.cloned.1.call-done = bf16[8,128,256]{2,1,0:T(8,128)(2,1)} async-done(((bf16[8,256,256]{2,1,0:T(8,128)(2,1)}), bf16[8,128,256]{2,1,0:T(8,128)(2,1)}) %reduce-scatter.5.cloned.1.call-update) | async-done | bytes 524304 | tf_op jit(solution)/shard_map/reduce_scatter | solution.py:119
  367.9 2.1 copy.442
  370.8 3.5 all-to-all-start.18
  374.3 2.2 copy.532
  376.6 6.0 all-to-all-done.18
  383.4 5.9 all-to-all-start.17
  389.3 2.1 copy.467
  391.4 2.0 reduce_sum.239
  393.4 2.1 convolution_bitcast_fusion.8
  395.5 1.6 convolution_bitcast_fusion.10
  397.0 2.0 reduce_sum.238
  399.1 2.3 copy.535
  401.4 2.3 all-to-all-done.17
  403.7 4.2 all-to-all-start.19
  408.1 2.1 convolution_bitcast_fusion.9
  410.2 2.7 convolution_bitcast_fusion.11
  415.8 6.6 %all-to-all-done.19 = bf16[8,256,128]{2,0,1:T(8,128)(2,1)} async-done(((bf16[8,256,128]{2,0,1:T(8,128)(2,1)}), bf16[8,256,128]{2,0,1:T(8,128)(2,1)}, u32[]{:S(2)}, u32[]{:S(2)}) %all-to-all-start.19) | async-done | bytes 524320 | tf_op jit(solution)/shard_map/all_to_all | solution.py:134
  424.1 3.1 fusion.7
  430.0 1.8 fusion.25
  435.1 39.2 %all-reduce = (f32[1,128]{1,0:T(1,128)S(1)}, f32[1,128]{1,0:T(1,128)S(1)}, f32[1,128]{1,0:T(1,128)S(1)}, f32[1,128]{1,0:T(1,128)S(1)}, f32[1,128]{1,0:T(1,128)S(...) all-reduce(f32[1,128]{1,0:T(1,128)S(1)} %bitcast.413, ...), channel_id=1, replica_groups=mesh['grp'=1,'row'=16,'col'=2,'ch'=1] {'row','col'}, use_global_device_ids=true, to_apply=%region_21.0 | all-reduce | flops 1024 | bytes 8192 | tf_op jit(solution)/shard_map/psum | solution.py:219
  476.6 129.1 %all-reduce.4.cloned.1.call-done = (f32[1,2,128,128]{2,3,1,0:T(8,128)}, f32[1,2,128,128]{2,3,1,0:T(8,128)}, f32[1,2,128,128]{2,3,1,0:T(8,128)}, f32[1,2,128,128]...) async-done(((f32[1,2,128,128]{2,3,1,0:T(8,128)}, f32[1,2,128,128]{2,3,1,0:T(8,128)}, ...) | async-done | bytes 786448 | tf_op jit(solution)/shard_map/psum | solution.py:219
  (259 shorter events, 67.4 us)
Async XLA Ops:
  7.2 2.4 copy-start.64
  7.2 2.4 copy-start.65
  7.2 2.5 copy-start.27
  9.6 94.4 %copy-start.47 = (f32[128]{0:T(128)}, f32[128]{0:T(128)S(1)}, u32[]{:S(2)}) copy-start(f32[128]{0:T(128)S(1)} %get-tuple-element.142) | copy-start | bytes 1540
  9.6 94.4 %copy-start.55 = (f32[128]{0:T(128)}, f32[128]{0:T(128)S(1)}, u32[]{:S(2)}) copy-start(f32[128]{0:T(128)S(1)} %get-tuple-element.131) | copy-start | bytes 1540
  9.6 111.8 %copy-start.40 = (f32[128]{0:T(128)}, f32[128]{0:T(128)S(1)}, u32[]{:S(2)}) copy-start(f32[128]{0:T(128)S(1)} %get-tuple-element.143) | copy-start | bytes 1540
  9.6 111.8 %copy-start.57 = (f32[128]{0:T(128)}, f32[128]{0:T(128)S(1)}, u32[]{:S(2)}) copy-start(f32[128]{0:T(128)S(1)} %get-tuple-element.130) | copy-start | bytes 1540
  9.7 283.9 %copy-start.30 = (f32[16,128]{1,0:T(8,128)}, f32[16,128]{1,0:T(8,128)S(1)}, u32[]{:S(2)}) copy-start(f32[16,128]{1,0:T(8,128)S(1)} %and_convert_fusion) | copy-start | bytes 24580
  10.3 2.3 copy-start.6
  36.0 11.9 %all-to-all-start.3 = ((bf16[8,256,128]{2,0,1:T(8,128)(2,1)}), bf16[8,256,128]{2,0,1:T(8,128)(2,1)S(1)}, u32[]{:S(2)}, u32[]{:S(2)}) async-start(bf16[8,256,128]{2,0,1:T(8,128)(2,1)} %copy.365), calls=%async_computation.3 | async-start | bytes 1048576 | tf_op jit(solution)/shard_map/all_to_all | solution.py:41
  47.9 18.9 %all-to-all-start = ((bf16[128,16,128]{2,1,0:T(8,128)(2,1)}), bf16[128,16,128]{2,1,0:T(8,128)(2,1)S(1)}, u32[]{:S(2)}, u32[]{:S(2)}) async-start(bf16[128,16,128]{2,1,0:T(8,128)(2,1)} %copy.358), calls=%async_computation | async-start | bytes 1048576 | tf_op jit(solution)/shard_map/all_to_all | solution.py:32
  52.3 31.0 %all-gather.3.cloned.1.call-start = ((), (), s32[]{:S(2)}) async-start(), calls=%async_computation.22 | async-start | bytes 1572864 | tf_op jit(solution)/shard_map/all_gather | solution.py:44
  83.2 12.9 %copy-start.8 = (bf16[8,128,256]{2,1,0:T(8,128)(2,1)}, bf16[8,128,256]{2,1,0:T(8,128)(2,1)S(1)}, u32[]{:S(2)}) copy-start(bf16[8,128,256]{2,1,0:T(8,128)(2,1)S(1)} %all_to_all.247) | copy-start | bytes 1572868
  85.1 18.0 %copy-start.66 = (f32[2,128]{1,0:T(2,128)S(1)}, f32[2,128]{1,0:T(2,128)}, u32[]{:S(2)}) copy-start(f32[2,128]{1,0:T(2,128)} %param.19) | copy-start | bytes 3076
  85.1 18.0 %copy-start.67 = (f32[2,128]{1,0:T(2,128)S(1)}, f32[2,128]{1,0:T(2,128)}, u32[]{:S(2)}) copy-start(f32[2,128]{1,0:T(2,128)} %param.18) | copy-start | bytes 3076
  85.1 18.8 %copy-start.32 = (bf16[2,128,128]{2,1,0:T(8,128)(2,1)S(1)}, bf16[2,128,128]{2,1,0:T(8,128)(2,1)}, u32[]{:S(2)}) copy-start(bf16[2,128,128]{2,1,0:T(8,128)(2,1)} %param.21) | copy-start | bytes 196612
  97.3 20.2 %all-to-all-start.5 = ((bf16[8,256,128]{2,0,1:T(8,128)(2,1)}), bf16[8,256,128]{2,0,1:T(8,128)(2,1)S(1)}, u32[]{:S(2)}, u32[]{:S(2)}) async-start(bf16[8,256,128]{2,0,1:T(8,128)(2,1)} %bitcast.29), calls=%async_computation.5 | async-start | bytes 1048576 | tf_op jit(solution)/shard_map/all_to_all | solution.py:46
  103.0 60.6 %all-gather.5.cloned.1.call-start = ((), (), s32[]{:S(2)}) async-start(), calls=%async_computation.23 | async-start | bytes 1572864 | tf_op jit(solution)/shard_map/all_gather | solution.py:44
  104.5 14.8 %copy-start.12 = (f32[16,128,128]{1,2,0:T(8,128)}, f32[16,128,128]{1,2,0:T(8,128)S(1)}, u32[]{:S(2)}) copy-start(f32[16,128,128]{1,2,0:T(8,128)S(1)} %fusion.21) | copy-start | bytes 3145732
  104.5 14.8 %copy-start.28 = (bf16[2,128,128]{2,1,0:T(8,128)(2,1)S(1)}, bf16[2,128,128]{2,1,0:T(8,128)(2,1)}, u32[]{:S(2)}) copy-start(bf16[2,128,128]{2,1,0:T(8,128)(2,1)} %param.20) | copy-start | bytes 196612
  121.4 2.3 copy-start.7
  162.5 13.8 %copy-start.10 = (bf16[8,16,16,128]{3,2,1,0:T(8,128)(2,1)}, bf16[8,16,16,128]{3,2,1,0:T(8,128)(2,1)S(1)}, u32[]{:S(2)}) copy-start(bf16[8,16,16,128]{3,2,1,0:T(8,128)(2,1)S(1)} %copy.383) | copy-start | bytes 1572868
  177.6 20.1 %all-to-all-start.9 = ((bf16[8,256,128]{2,0,1:T(8,128)(2,1)}), bf16[8,256,128]{2,0,1:T(8,128)(2,1)S(1)}, u32[]{:S(2)}, u32[]{:S(2)}) async-start(bf16[8,256,128]{2,0,1:T(8,128)(2,1)} %bitcast.61), calls=%async_computation.9 | async-start | bytes 1048576 | tf_op jit(solution)/shard_map/all_to_all | solution.py:46
  183.2 83.9 %reduce-scatter.3.cloned.1.call-start = ((), (), s32[]{:S(2)}) async-start(), calls=%async_computation.24 | async-start | bytes 1572864 | tf_op jit(solution)/shard_map/reduce_scatter | solution.py:119
  201.3 2.0 copy-start.33
  201.3 2.0 copy-start.41
  201.4 2.0 copy-start.58
  203.4 2.8 copy-start.45
  230.6 14.7 %copy-start.11 = (bf16[8,16,16,128]{3,2,1,0:T(8,128)(2,1)S(1)}, bf16[8,16,16,128]{3,2,1,0:T(8,128)(2,1)}, u32[]{:S(2)}) copy-start(bf16[8,16,16,128]{3,2,1,0:T(8,128)(2,1)} %copy-done.10) | copy-start | bytes 1572868
  250.9 18.9 %all-to-all-start.12 = ((bf16[8,256,128]{2,0,1:T(8,128)(2,1)}), bf16[8,256,128]{2,0,1:T(8,128)(2,1)S(1)}, u32[]{:S(2)}, u32[]{:S(2)}) async-start(bf16[8,256,128]{2,0,1:T(8,128)(2,1)} %copy.412), calls=%async_computation.12 | async-start | bytes 1048576 | tf_op jit(solution)/shard_map/all_to_all | solution.py:133
  269.7 19.7 %all-to-all-start.13 = ((bf16[8,256,128]{2,0,1:T(8,128)(2,1)}), bf16[8,256,128]{2,0,1:T(8,128)(2,1)}, u32[]{:S(2)}, u32[]{:S(2)}) async-start(bf16[8,256,128]{2,0,1:T(8,128)(2,1)} %copy.416), calls=%async_computation.14 | async-start | bytes 1048576 | tf_op jit(solution)/shard_map/all_to_all | solution.py:134
  274.9 93.0 %reduce-scatter.5.cloned.1.call-start = ((), (), s32[]{:S(2)}) async-start(), calls=%async_computation.25 | async-start | bytes 1572864 | tf_op jit(solution)/shard_map/reduce_scatter | solution.py:119
  325.8 14.7 %copy-start.9 = (bf16[8,128,256]{2,1,0:T(8,128)(2,1)S(1)}, bf16[8,128,256]{2,1,0:T(8,128)(2,1)}, u32[]{:S(2)}) copy-start(bf16[8,128,256]{2,1,0:T(8,128)(2,1)} %copy-done.8) | copy-start | bytes 1572868
  345.8 24.2 %all-to-all-start.16 = ((bf16[8,128,256]{1,0,2:T(8,128)(2,1)}), bf16[8,128,256]{1,0,2:T(8,128)(2,1)S(1)}, u32[]{:S(2)}, u32[]{:S(2)}) async-start(bf16[8,128,256]{1,0,2:T(8,128)(2,1)} %copy.435), calls=%async_computation.17 | async-start | bytes 1048576 | tf_op jit(solution)/shard_map/all_to_all | solution.py:129
  370.8 11.8 %all-to-all-start.18 = ((bf16[8,128,256]{1,0,2:T(8,128)(2,1)}), bf16[8,128,256]{1,0,2:T(8,128)(2,1)S(1)}, u32[]{:S(2)}, u32[]{:S(2)}) async-start(bf16[8,128,256]{1,0,2:T(8,128)(2,1)} %copy.442), calls=%async_computation.20 | async-start | bytes 1048576 | tf_op jit(solution)/shard_map/all_to_all | solution.py:130
  374.3 19.0 %copy-start.43 = (f32[128]{0:T(128)S(1)}, f32[128]{0:T(128)}, u32[]{:S(2)}) copy-start(f32[128]{0:T(128)} %copy-done.40) | copy-start | bytes 1540
  374.3 19.0 %copy-start.59 = (f32[128]{0:T(128)S(1)}, f32[128]{0:T(128)}, u32[]{:S(2)}) copy-start(f32[128]{0:T(128)} %copy-done.57) | copy-start | bytes 1540
  383.4 20.3 %all-to-all-start.17 = ((bf16[8,256,128]{2,0,1:T(8,128)(2,1)}), bf16[8,256,128]{2,0,1:T(8,128)(2,1)S(1)}, u32[]{:S(2)}, u32[]{:S(2)}) async-start(bf16[8,256,128]{2,0,1:T(8,128)(2,1)} %bitcast.382), calls=%async_computation.18 | async-start | bytes 1048576 | tf_op jit(solution)/shard_map/all_to_all | solution.py:133
  389.3 6.2 %copy-start.46 = (f32[128]{0:T(128)S(1)}, f32[128]{0:T(128)}, u32[]{:S(2)}) copy-start(f32[128]{0:T(128)} %get-tuple-element.146) | copy-start | bytes 1540
  389.3 6.2 copy-start.54
  393.3 2.1 copy-start.16
  397.0 11.0 %copy-start.48 = (f32[128]{0:T(128)S(1)}, f32[128]{0:T(128)}, u32[]{:S(2)}) copy-start(f32[128]{0:T(128)} %copy-done.47) | copy-start | bytes 1540
  397.0 11.0 %copy-start.56 = (f32[128]{0:T(128)S(1)}, f32[128]{0:T(128)}, u32[]{:S(2)}) copy-start(f32[128]{0:T(128)} %copy-done.55) | copy-start | bytes 1540
  399.1 11.1 %copy-start.1 = (f32[128,16,128]{0,2,1:T(8,128)S(1)}, f32[128,16,128]{0,2,1:T(8,128)}, u32[]{:S(2)}) copy-start(f32[128,16,128]{0,2,1:T(8,128)} %copy.429) | copy-start | bytes 3145732
  399.1 11.1 %copy-start.51 = (f32[128]{0:T(128)S(1)}, f32[128]{0:T(128)}, u32[]{:S(2)}) copy-start(f32[128]{0:T(128)} %get-tuple-element.147) | copy-start | bytes 1540
  399.1 11.1 %copy-start.68 = (f32[128]{0:T(128)S(1)}, f32[128]{0:T(128)}, u32[]{:S(2)}) copy-start(f32[128]{0:T(128)} %get-tuple-element.120) | copy-start | bytes 1540
  403.7 18.7 %all-to-all-start.19 = ((bf16[8,256,128]{2,0,1:T(8,128)(2,1)}), bf16[8,256,128]{2,0,1:T(8,128)(2,1)}, u32[]{:S(2)}, u32[]{:S(2)}) async-start(bf16[8,256,128]{2,0,1:T(8,128)(2,1)} %bitcast.381), calls=%async_computation.21 | async-start | bytes 1048576 | tf_op jit(solution)/shard_map/all_to_all | solution.py:134
  408.0 197.7 %all-reduce.4.cloned.1.call-start = ((), (), s32[]{:S(2)}) async-start(), calls=%async_computation.26 | async-start | bytes 1572864 | tf_op jit(solution)/shard_map/psum | solution.py:219
  408.0 4.8 copy-start.18
  410.2 3.9 copy-start.21
  415.2 8.9 %copy-start.31 = (f32[16,128]{1,0:T(8,128)S(1)}, f32[16,128]{1,0:T(8,128)}, u32[]{:S(2)}) copy-start(f32[16,128]{1,0:T(8,128)} %copy-done.30) | copy-start | bytes 24580
  430.0 1.8 copy-start.24
  430.0 1.8 copy-start.35
  430.0 1.8 copy-start.49
  433.0 2.0 copy-start.52
  433.0 2.0 copy-start.53
  433.0 2.0 copy-start.60
  433.0 2.0 copy-start.61
  433.0 2.0 copy-start.62
  433.1 2.0 copy-start.63
  605.7 3.7 copy-start.38
  605.7 3.7 copy-start.39
  605.7 4.4 copy-start.36
  605.7 4.4 copy-start.37
  (20 other events, 25.6 us)
Sparse Core Ops, SparseCore 0:
  55.2 25.9 all-gather.2
  143.8 19.7 all-gather.4
  248.0 19.0 reduce-scatter.2
  343.2 24.6 reduce-scatter.4
  474.4 131.2 all-reduce.3
where the time goes:
time: 629 us; the launch traced here: 618 us
  waiting for transfers between devices  229 us (36%)
  blocking collectives  193 us (31%)
  local copies, waits for them, and re-layouts  64 us (10%)
  starting transfers between devices  46.2 us (7%)
  matrix products  43.1 us (7%)
  other arithmetic  27 us (4%)
  between operations  16 us (3%)
    psum x1, waiting for transfers between devices, per_device(): lax.psum((lower[0], lower[1], lower[2], lower[3], lower[4], lower[5], low...  129 us
    dot_general x30, matrix products, product(): return jnp.einsum(spec, left, right, preferred_element_type=jnp.float32)  43.1 us
    all_to_all x2, blocking collectives, forward_module(): lax.all_to_all(hidden[1], 'row', split_axis=0, concat_axis=1, tiled=True)  40 us
    psum x1, blocking collectives, per_device(): lax.psum((lower[0], lower[1], lower[2], lower[3], lower[4], lower[5], low...  39.2 us
    all_to_all x2, blocking collectives, backward_module(): lax.all_to_all(d_tri, 'row', split_axis=0, concat_axis=1, tiled=True)  36.7 us
    reduce_scatter x2, waiting for transfers between devices, backward_module(): lax.psum_scatter(partial_terms.astype(jnp.bfloat16), 'col', scatter_dimen...  30.3 us
    all_to_all x2, waiting for transfers between devices, forward_module(): lax.all_to_all(lax.all_to_all(triangle, 'col', split_axis=2, concat_axis=...  25.7 us
    all_to_all x2, blocking collectives, backward_module(): lax.all_to_all(grad_rows, 'col', split_axis=1, concat_axis=2, tiled=True)  21.7 us
  transfers between devices with their start and end apart: 15, of which 13 were waited for; matrix products, arithmetic and copies ran while one was open for 8% of the time, Pallas kernels for 0%

commit v1 on v0

--- a/solution.py
+++ b/solution.py
@@ -1,6 +1,10 @@
+import functools
+
 import jax
 import jax.numpy as jnp
 from jax import lax
+from jax.experimental import pallas as pl
+from jax.experimental.pallas import tpu as pltpu
 from jax.sharding import PartitionSpec as P
 
 H = 128
@@ -11,6 +15,483 @@
 
 def product(spec, left, right):
     return jnp.einsum(spec, left, right, preferred_element_type=jnp.float32)
+
+
+F32 = jnp.float32
+BF16 = jnp.bfloat16
+
+
+def dot(left, right):
+    return lax.dot_general(left, right, (((1,), (0,)), ((), ())), preferred_element_type=F32)
+
+
+def dot_rt(left, right):
+    return lax.dot_general(left, right, (((1,), (1,)), ((), ())), preferred_element_type=F32)
+
+
+def dot_lt(left, right):
+    return lax.dot_general(left, right, (((0,), (0,)), ((), ())), preferred_element_type=F32)
+
+
+def sigmoid(values):
+    return 1.0 / (1.0 + jnp.exp(-values))
+
+
+def norm_rows(values):
+    scale = 1.0 / values.shape[0]
+    average = jnp.sum(values, 0, keepdims=True) * scale
+    centred = values - average
+    variance = jnp.sum(centred * centred, 0, keepdims=True) * scale
+    inverse = lax.rsqrt(variance + EPS)
+    return centred * inverse, inverse
+
+
+def turned(weight):
+    return jnp.transpose(weight.astype(F32)).astype(BF16)
+
+
+def column(ref, module, lanes):
+    row = ref[module : module + 1, :]
+    return jnp.transpose(jnp.broadcast_to(row, (lanes, row.shape[1])))
+
+
+def as_row(total):
+    return jnp.sum(jnp.transpose(total), 0, keepdims=True)
+
+
+def row_mask(lengths_ref, step, rows, lanes):
+    limit = lengths_ref[0]
+    row_id = lax.axis_index("row") * rows + step
+    col_id = lax.axis_index("col") * lanes + lax.broadcasted_iota(jnp.int32, (1, lanes), 1)
+    return jnp.where((row_id < limit) & (col_id < limit), 1.0, 0.0).astype(F32)
+
+
+def load_in_weights(proj_ref, gate_ref, module, scratch):
+    width = proj_ref.shape[-1]
+    for side in range(2):
+        scratch[side * width : (side + 1) * width, :] = turned(proj_ref[module, side])
+        scratch[(2 + side) * width : (3 + side) * width, :] = turned(gate_ref[module, side])
+
+
+def edges(normed, in_weights, mask):
+    pre = dot(in_weights, normed)
+    half = pre.shape[0] // 2
+    return pre[:half] * sigmoid(pre[half:]) * mask
+
+
+def put_rows(scratch, values, step, rows):
+    scratch[pl.ds(step, values.shape[0], stride=rows), :] = values
+
+
+def get_rows(scratch, step, channels, rows):
+    return scratch[pl.ds(step, channels, stride=rows), :]
+
+
+def spread_edges(scratch, out_ref):
+    shards, sides, group, rows, lanes = out_ref.shape
+    block = shards * group * rows
+    for side in range(sides):
+        part = scratch[side * block : (side + 1) * block, :]
+        out_ref[:, side] = part.reshape(shards, group, rows, lanes).astype(BF16)
+
+
+def collect_edges(in_ref, scratch):
+    shards, sides, group, rows, lanes = in_ref.shape
+    block = shards * group * rows
+    for side in range(sides):
+        scratch[side * block : (side + 1) * block, :] = (
+            in_ref[:, side].astype(F32).reshape(block, lanes)
+        )
+
+
+def start_kernel(lengths, pair, ngain, nbias, proj_w, gate_w, edge_out, normed_out, wts, scr):
+    rows, lanes, channels = pair.shape
+    load_in_weights(proj_w, gate_w, 0, wts)
+    gain, bias = column(ngain, 0, lanes), column(nbias, 0, lanes)
+
+    def body(step, carry):
+        scaled, _ = norm_rows(jnp.transpose(pair[step].astype(F32)))
+        normed = (scaled * gain + bias).astype(BF16)
+        normed_out[step] = normed
+        put_rows(scr, edges(normed, wts[...], row_mask(lengths, step, rows, lanes)), step, rows)
+        return carry
+
+    lax.fori_loop(0, rows, body, 0)
+    spread_edges(scr, edge_out)
+
+
+def mid_norm(tri):
+    scale = 1.0 / tri.shape[0]
+    average = jnp.sum(tri, 0, keepdims=True) * scale
+    squares = jnp.sum(tri * tri, 0, keepdims=True) * scale
+    inverse = lax.rsqrt(squares - average * average + EPS)
+    return (tri - average) * inverse, inverse
+
+
+def between_kernel(
+    lengths, tri, pair, normed0, ngain, nbias, mgain, mbias, out_w, outgate_w, proj_w, gate_w,
+    edge_out, mid_out, normed_out, wts, scr,
+):
+    rows, lanes, channels = pair.shape
+    load_in_weights(proj_w, gate_w, 1, wts)
+    out_t, outgate_t = turned(out_w[0]), turned(outgate_w[0])
+    gain, bias = column(ngain, 1, lanes), column(nbias, 1, lanes)
+    gain_mid, bias_mid = column(mgain, 0, lanes), column(mbias, 0, lanes)
+    scr[0 : channels * rows, :] = tri[...].astype(F32).reshape(channels * rows, lanes)
+
+    def body(step, carry):
+        scaled_mid, _ = mid_norm(get_rows(scr, step, channels, rows))
+        unit = (scaled_mid * gain_mid + bias_mid).astype(BF16)
+        outer = dot(out_t, unit)
+        outgate = sigmoid(dot(outgate_t, normed0[step]))
+        mid = (jnp.transpose(pair[step].astype(F32)) + outer * outgate).astype(BF16)
+        mid_out[step] = mid
+        scaled, _ = norm_rows(mid.astype(F32))
+        normed = (scaled * gain + bias).astype(BF16)
+        normed_out[step] = normed
+        here = edges(normed, wts[...], row_mask(lengths, step, rows, lanes))
+        put_rows(scr, here, step, rows)
+        return carry
+
+    lax.fori_loop(0, rows, body, 0)
+    spread_edges(scr, edge_out)
+
+
+def triangle_kernel(incoming, edge, tri_out):
+    many, few, _, group, rows, lanes = edge.shape
+
+    def whole(side, channel):
+        parts = [edge[:, c, side, channel].reshape(many * rows, lanes) for c in range(few)]
+        return jnp.concatenate(parts, axis=1)
+
+    for channel in range(group):
+        left, right = whole(0, channel), whole(1, channel)
+        tri = (dot_lt if incoming else dot_rt)(left, right).astype(BF16)
+        for c in range(few):
+            part = tri[:, c * lanes : (c + 1) * lanes]
+            tri_out[:, c, channel] = part.reshape(many, rows, lanes)
+
+
+def edge_grad_kernel(incoming, edge, d_tri, grad_out):
+    many, few, _, group, rows, lanes = edge.shape
+
+    def whole(ref, *index):
+        parts = [ref[(slice(None), c) + index].reshape(many * rows, lanes) for c in range(few)]
+        return jnp.concatenate(parts, axis=1)
+
+    for channel in range(group):
+        left, right = whole(edge, 0, channel), whole(edge, 1, channel)
+        grad = whole(d_tri, channel)
+        if incoming:
+            d_left, d_right = dot_rt(right, grad), dot(left, grad)
+        else:
+            d_left, d_right = dot(grad, right), dot_lt(grad, left)
+        for side, value in ((0, d_left), (1, d_right)):
+            value = value.astype(BF16)
+            for c in range(few):
+                part = value[:, c * lanes : (c + 1) * lanes]
+                grad_out[:, c, side, channel] = part.reshape(many, rows, lanes)
+
+
+def mid_backward(
+    step, grad, tri, normed, gain_mid, bias_mid, out_t, outgate_t, out_w,
+    unit_out, d_outer_out, d_gatepre_out, sum_gain, sum_bias,
+):
+    scaled_mid, inverse_mid = mid_norm(tri)
+    unit = (scaled_mid * gain_mid + bias_mid).astype(BF16)
+    outer = dot(out_t, unit)
+    outgate = sigmoid(dot(outgate_t, normed))
+    gated = grad * outgate
+    d_outer = gated.astype(BF16)
+    d_gatepre = (gated * outer * (1.0 - outgate)).astype(BF16)
+    unit_out[step] = unit
+    d_outer_out[step] = d_outer
+    d_gatepre_out[step] = d_gatepre
+    d_unit = dot(out_w, d_outer)
+    sum_gain[...] += d_unit * scaled_mid
+    sum_bias[...] += d_unit
+    weighted = d_unit * gain_mid
+    scale = 1.0 / weighted.shape[0]
+    first = jnp.sum(weighted, 0, keepdims=True) * scale
+    second = jnp.sum(weighted * scaled_mid, 0, keepdims=True) * scale
+    d_tri = inverse_mid * (weighted - first - scaled_mid * second)
+    return d_tri, outer * outgate
+
+
+def turn_kernel(
+    tri, mid, normed1, cot, mgain, mbias, out_w, outgate_w,
+    d_tri_out, new_out, unit_out, d_outer_out, d_gatepre_out, small_out, scr, sum_gain, sum_bias,
+):
+    rows, channels, lanes = mid.shape
+    out_t, outgate_t = turned(out_w[1]), turned(outgate_w[1])
+    gain_mid, bias_mid = column(mgain, 1, lanes), column(mbias, 1, lanes)
+    scr[...] = tri[...].astype(F32).reshape(channels * rows, lanes)
+    sum_gain[...] = jnp.zeros_like(sum_gain)
+    sum_bias[...] = jnp.zeros_like(sum_bias)
+
+    def body(step, carry):
+        grad = jnp.transpose(cot[step].astype(F32))
+        d_tri, update = mid_backward(
+            step, grad, get_rows(scr, step, channels, rows), normed1[step], gain_mid, bias_mid,
+            out_t, outgate_t, out_w[1], unit_out, d_outer_out, d_gatepre_out, sum_gain, sum_bias,
+        )
+        new_out[step] = jnp.transpose(mid[step].astype(F32) + update).astype(BF16)
+        put_rows(scr, d_tri, step, rows)
+        return carry
+
+    lax.fori_loop(0, rows, body, 0)
+    d_tri_out[...] = scr[...].reshape(d_tri_out.shape).astype(BF16)
+    small_out[0:1, :] = as_row(sum_gain[...])
+    small_out[1:2, :] = as_row(sum_bias[...])
+
+
+def in_backward(
+    step, grad, base, d_edges, normed, d_gatepre, mask, gain, wts, proj_w, gate_w, outgate_w,
+    d_in_out, sum_gain, sum_bias,
+):
+    pre = dot(wts[...], normed)
+    half = pre.shape[0] // 2
+    gating = sigmoid(pre[half:])
+    through = d_edges * gating * mask
+    d_proj = through.astype(BF16)
+    d_gate = (through * pre[:half] * (1.0 - gating)).astype(BF16)
+    d_in_out[step, 0:half] = d_proj
+    d_in_out[step, half:] = d_gate
+    width = half // 2
+    d_normed = dot(outgate_w, d_gatepre)
+    for side in range(2):
+        d_normed += dot(proj_w[side], d_proj[side * width : (side + 1) * width])
+        d_normed += dot(gate_w[side], d_gate[side * width : (side + 1) * width])
+    scaled, inverse = norm_rows(base)
+    sum_gain[...] += d_normed * scaled
+    sum_bias[...] += d_normed
+    weighted = d_normed * gain
+    scale = 1.0 / weighted.shape[0]
+    first = jnp.sum(weighted, 0, keepdims=True) * scale
+    second = jnp.sum(weighted * scaled, 0, keepdims=True) * scale
+    return grad + inverse * (weighted - first - scaled * second)
+
+
+def middle_kernel(
+    lengths, d_edge, mid, normed1, d_gatepre1, cot, tri0, normed0,
+    ngain, mgain, mbias, proj_w, gate_w, out_w, outgate_w,
+    d_tri_out, grad_out, d_in_out, unit_out, d_outer_out, d_gatepre_out, small_out,
+    wts, scr, scr_tri, sums,
+):
+    rows, channels, lanes = mid.shape
+    load_in_weights(proj_w, gate_w, 1, wts)
+    out_t, outgate_t = turned(out_w[0]), turned(outgate_w[0])
+    gain = column(ngain, 1, lanes)
+    gain_mid, bias_mid = column(mgain, 0, lanes), column(mbias, 0, lanes)
+    collect_edges(d_edge, scr)
+    scr_tri[...] = tri0[...].astype(F32).reshape(channels * rows, lanes)
+    sums[...] = jnp.zeros_like(sums)
+
+    def body(step, carry):
+        grad = in_backward(
+            step, jnp.transpose(cot[step].astype(F32)), mid[step].astype(F32),
+            get_rows(scr, step, scr.shape[0] // rows, rows), normed1[step], d_gatepre1[step],
+            row_mask(lengths, step, rows, lanes), gain, wts, proj_w[1], gate_w[1], outgate_w[1],
+            d_in_out, sums.at[0], sums.at[1],
+        )
+        grad_out[step] = grad
+        d_tri, _ = mid_backward(
+            step, grad, get_rows(scr_tri, step, channels, rows), normed0[step], gain_mid, bias_mid,
+            out_t, outgate_t, out_w[0], unit_out, d_outer_out, d_gatepre_out,
+            sums.at[2], sums.at[3],
+        )
+        put_rows(scr_tri, d_tri, step, rows)
+        return carry
+
+    lax.fori_loop(0, rows, body, 0)
+    d_tri_out[...] = scr_tri[...].reshape(d_tri_out.shape).astype(BF16)
+    for index in range(4):
+        small_out[index : index + 1, :] = as_row(sums[index])
+
+
+def finish_kernel(
+    lengths, d_edge, pair, normed0, d_gatepre0, grad, ngain, proj_w, gate_w, outgate_w,
+    grad_out, d_in_out, small_out, wts, scr, sums,
+):
+    rows, lanes, channels = pair.shape
+    load_in_weights(proj_w, gate_w, 0, wts)
+    gain = column(ngain, 0, lanes)
+    collect_edges(d_edge, scr)
+    sums[...] = jnp.zeros_like(sums)
+
+    def body(step, carry):
+        total = in_backward(
+            step, grad[step], jnp.transpose(pair[step].astype(F32)),
+            get_rows(scr, step, scr.shape[0] // rows, rows), normed0[step], d_gatepre0[step],
+            row_mask(lengths, step, rows, lanes), gain, wts, proj_w[0], gate_w[0], outgate_w[0],
+            d_in_out, sums.at[0], sums.at[1],
+        )
+        grad_out[step] = jnp.transpose(total).astype(BF16)
+        return carry
+
+    lax.fori_loop(0, rows, body, 0)
+    for index in range(2):
+        small_out[index : index + 1, :] = as_row(sums[index])
+
+
+def in_weight_kernel(normed, d_in, out_ref):
+    rows = normed.shape[0]
+    width = normed.shape[1]
+    flat = jnp.concatenate([normed[step] for step in range(rows)], axis=1)
+    for part in range(d_in.shape[1] // width):
+        block = slice(part * width, (part + 1) * width)
+        other = jnp.concatenate([d_in[step, block] for step in range(rows)], axis=1)
+        out_ref[block, :] = dot_rt(flat, other).astype(out_ref.dtype)
+
+
+def out_weight_kernel(unit, d_outer, normed, d_gatepre, out_ref):
+    rows = normed.shape[0]
+    width = normed.shape[1]
+    for part, (left, right) in enumerate(((unit, d_outer), (normed, d_gatepre))):
+        first = jnp.concatenate([left[step] for step in range(rows)], axis=1)
+        second = jnp.concatenate([right[step] for step in range(rows)], axis=1)
+        block = slice(part * width, (part + 1) * width)
+        out_ref[block, :] = dot_rt(first, second).astype(out_ref.dtype)
+
+
+SCALARS = pl.BlockSpec(memory_space=pltpu.SMEM)
+VECTORS = pl.BlockSpec(memory_space=pltpu.VMEM)
+
+
+def call(kernel, name, outs, args, scratch=(), flops=0, scalars=0):
+    shapes = [jax.ShapeDtypeStruct(shape, dtype) for shape, dtype in outs]
+    moved = sum(a.size * a.dtype.itemsize for a in list(args) + shapes)
+    result = pl.pallas_call(
+        kernel,
+        name=name,
+        out_shape=shapes,
+        in_specs=[SCALARS] * scalars + [VECTORS] * (len(args) - scalars),
+        out_specs=[VECTORS] * len(shapes),
+        scratch_shapes=[pltpu.VMEM(shape, dtype) for shape, dtype in scratch],
+        compiler_params=pltpu.CompilerParams(vmem_limit_bytes=32 * 1024 * 1024),
+        cost_estimate=pl.CostEstimate(flops=flops, bytes_accessed=moved, transcendentals=0),
+    )(*args)
+    return result
+
+
+def exchange(values):
+    return lax.all_to_all(values, ("row", "col"), split_axis=0, concat_axis=0, tiled=True)
+
+
+def grouped_device(
+    pair, cotangent, lengths, ngain, nbias, proj_w, gate_w, mgain, mbias, out_w, outgate_w,
+    *, many, few,
+):
+    rows, lanes, channels = pair.shape
+    shards = many * few
+    group = H // shards
+    edge_shape = (shards, 2, group, rows, lanes)
+    grid_shape = (many, few, 2, group, rows, lanes)
+    tri_shape = (shards, group, rows, lanes)
+    tile = (rows, channels, lanes)
+    wts = ((4 * H, channels), BF16)
+    big = ((2 * H * rows, lanes), F32)
+    mid = ((H * rows, lanes), F32)
+    positions = rows * lanes
+    triangle = 2 * group * (many * rows) ** 2 * (few * lanes)
+    dense = 2 * positions * channels * H
+
+    edge, normed0 = call(
+        start_kernel, "start", [(edge_shape, BF16), (tile, BF16)],
+        [lengths, pair, ngain, nbias, proj_w, gate_w], [wts, big], 4 * dense, 1,
+    )
+    edge0 = exchange(edge).reshape(grid_shape)
+    (tri,) = call(
+        functools.partial(triangle_kernel, False), "outgoing",
+        [((many, few, group, rows, lanes), BF16)], [edge0], (), triangle,
+    )
+    tri0 = exchange(tri.reshape(tri_shape))
+    edge, mid_t, normed1 = call(
+        between_kernel, "between", [(edge_shape, BF16), (tile, BF16), (tile, BF16)],
+        [lengths, tri0, pair, normed0, ngain, nbias, mgain, mbias, out_w, outgate_w, proj_w, gate_w],
+        [wts, big], 6 * dense, 1,
+    )
+    edge1 = exchange(edge).reshape(grid_shape)
+    (tri,) = call(
+        functools.partial(triangle_kernel, True), "incoming",
+        [((many, few, group, rows, lanes), BF16)], [edge1], (), triangle,
+    )
+    tri1 = exchange(tri.reshape(tri_shape))
+    d_tri, new_pair, unit1, d_outer1, d_gatepre1, small_mid1 = call(
+        turn_kernel, "turn",
+        [(tri_shape, BF16), (pair.shape, BF16), (tile, BF16), (tile, BF16), (tile, BF16),
+         ((2, H), F32)],
+        [tri1, mid_t, normed1, cotangent, mgain, mbias, out_w, outgate_w],
+        [mid, ((H, lanes), F32), ((H, lanes), F32)], 3 * dense,
+    )
+    d_tri = exchange(d_tri).reshape(many, few, group, rows, lanes)
+    (d_edge,) = call(
+        functools.partial(edge_grad_kernel, True), "incoming_grad",
+        [(grid_shape, BF16)], [edge1, d_tri], (), 2 * triangle,
+    )
+    d_edge = exchange(d_edge.reshape(edge_shape))
+    (out_grads1,) = call(
+        out_weight_kernel, "out_weights_upper", [((2 * H, channels), BF16)],
+        [unit1, d_outer1, normed1, d_gatepre1], (), 2 * dense,
+    )
+    d_tri, grad, d_in1, unit0, d_outer0, d_gatepre0, small_mid = call(
+        middle_kernel, "middle",
+        [(tri_shape, BF16), (tile, F32), ((rows, 4 * H, lanes), BF16), (tile, BF16), (tile, BF16),
+         (tile, BF16), ((4, H), F32)],
+        [lengths, d_edge, mid_t, normed1, d_gatepre1, cotangent, tri0, normed0,
+         ngain, mgain, mbias, proj_w, gate_w, out_w, outgate_w],
+        [wts, big, mid, ((4, H, lanes), F32)], 12 * dense, 1,
+    )
+    d_tri = exchange(d_tri).reshape(many, few, group, rows, lanes)
+    (in_grads1,) = call(
+        in_weight_kernel, "in_weights_upper", [((4 * H, H), BF16)], [normed1, d_in1], (), 4 * dense,
+    )
+    (out_grads0,) = call(
+        out_weight_kernel, "out_weights_lower", [((2 * H, channels), BF16)],
+        [unit0, d_outer0, normed0, d_gatepre0], (), 2 * dense,
+    )
+    (d_edge,) = call(
+        functools.partial(edge_grad_kernel, False), "outgoing_grad",
+        [(grid_shape, BF16)], [edge0, d_tri], (), 2 * triangle,
+    )
+    d_edge = exchange(d_edge.reshape(edge_shape))
+    grad_pair, d_in0, small0 = call(
+        finish_kernel, "finish",
+        [(pair.shape, BF16), ((rows, 4 * H, lanes), BF16), ((2, H), F32)],
+        [lengths, d_edge, pair, normed0, d_gatepre0, grad, ngain, proj_w, gate_w, outgate_w],
+        [wts, big, ((2, H, lanes), F32)], 9 * dense, 1,
+    )
+    (in_grads0,) = call(
+        in_weight_kernel, "in_weights_lower", [((4 * H, H), BF16)], [normed0, d_in0], (), 4 * dense,
+    )
+    small = jnp.concatenate([small0, small_mid[2:4], small_mid[0:2], small_mid1], axis=0)
+    high = small.astype(BF16)
+    low = (small - high.astype(F32)).astype(BF16)
+    every = jnp.concatenate([high, low], axis=0)
+    weights = jnp.concatenate([in_grads0, out_grads0, in_grads1, out_grads1], axis=0)
+    share = weights.shape[0] // shards
+    packed = jnp.concatenate(
+        [weights.reshape(shards, share, H), jnp.broadcast_to(every[None], (shards,) + every.shape)],
+        axis=1,
+    )
+    summed = jnp.sum(exchange(packed).astype(F32), axis=0)
+    small = summed[share : share + 8] + summed[share + 8 :]
+    own = summed[:share].astype(BF16)
+    weights = exchange(jnp.broadcast_to(own[None], (shards,) + own.shape))
+    weights = weights.reshape(2, 6, H, H).astype(F32)
+    small = small.reshape(2, 4, H)
+    return (
+        new_pair,
+        grad_pair,
+        small[:, 0],
+        small[:, 1],
+        weights[:, 0:2],
+        weights[:, 2:4],
+        small[:, 2],
+        small[:, 3],
+        weights[:, 4],
+        weights[:, 5],
+    )
 
 
 def norm_channels(values):
@@ -279,6 +760,11 @@
         P("grp", None, None),
         P("grp", None, None),
     )
+    many, few = mesh.shape["row"], mesh.shape["col"]
+    if mesh.shape["ch"] == 1 and H % (many * few) == 0:
+        body = functools.partial(grouped_device, many=many, few=few)
+    else:
+        body = per_device
     return jax.shard_map(
-        per_device, mesh=mesh, in_specs=in_specs, out_specs=out_specs, check_vma=False
-    )
+        body, mesh=mesh, in_specs=in_specs, out_specs=out_specs, check_vma=False
+    )

time: 629 us -> 288 us (0.46); the launches traced: 618 us -> 287 us
  waiting for transfers between devices: 229 us -> 31.8 us
  local copies, waits for them, and re-layouts: 64 us -> 14.4 us
  Pallas kernels: 0 us -> 46.8 us
  matrix products: 43.1 us -> 0 us
  starting transfers between devices: 46.2 us -> 7.24 us
  other arithmetic: 27 us -> 0.26 us
  between operations: 16 us -> 1.63 us
  blocking collectives: 193 us -> 185 us
    psum x1 -> x0, waiting for transfers between devices: 129 us -> none  [per_device(): lax.psum((lower[0], lower[1], lower[2], lower[3], lower[4], lower[5], low...]
    pallas_call x0 -> x13, Pallas kernels: none -> 46.8 us  [call(): pl.pallas_call(kernel, name=name, out_shape=shapes, in_specs=[SCALARS] *...]
    dot_general x30 -> x0, matrix products: 43.1 us -> none  [product(): return jnp.einsum(spec, left, right, preferred_element_type=jnp.float32)]
    psum x1 -> x0, blocking collectives: 39.2 us -> none  [per_device(): lax.psum((lower[0], lower[1], lower[2], lower[3], lower[4], lower[5], low...]
    all_to_all x10 -> x2, starting transfers between devices: 45.8 us -> 7.24 us  [exchange(): lax.all_to_all(values, ('row', 'col'), split_axis=0, concat_axis=0, tiled...]
    all_to_all x10 -> x2, waiting for transfers between devices: 68.1 us -> 31.8 us  [exchange(): lax.all_to_all(values, ('row', 'col'), split_axis=0, concat_axis=0, tiled...]
    all_to_all x10 -> x8, blocking collectives: 153 us -> 185 us  [exchange(): lax.all_to_all(values, ('row', 'col'), split_axis=0, concat_axis=0, tiled...]
    reduce_scatter x2 -> x0, waiting for transfers between devices: 30.3 us -> none  [backward_module(): lax.psum_scatter(partial_terms.astype(jnp.bfloat16), 'col', scatter_dimen...]
  transfers between devices with their start and end apart: 15 -> 2, of which waited for: 13 -> 2; matrix products, arithmetic and copies ran while one was open for 8% -> 0% of each run, Pallas kernels for 0% -> 1%
where the time goes in v1:
time: 288 us; the launch traced here: 287 us
  blocking collectives  185 us (64%)
  Pallas kernels  46.8 us (16%)
  waiting for transfers between devices  31.8 us (11%)
  local copies, waits for them, and re-layouts  14.4 us (5%)
  starting transfers between devices  7.24 us (3%)
    all_to_all x8, blocking collectives, exchange(): lax.all_to_all(values, ('row', 'col'), split_axis=0, concat_axis=0, tiled...  185 us
    pallas_call x13, Pallas kernels, call(): pl.pallas_call(kernel, name=name, out_shape=shapes, in_specs=[SCALARS] *...  46.8 us
    all_to_all x2, waiting for transfers between devices, exchange(): lax.all_to_all(values, ('row', 'col'), split_axis=0, concat_axis=0, tiled...  31.8 us
    unnamed x62, local copies, waits for them, and re-layouts  11.4 us
    all_to_all x2, starting transfers between devices, exchange(): lax.all_to_all(values, ('row', 'col'), split_axis=0, concat_axis=0, tiled...  7.24 us
  transfers between devices with their start and end apart: 2, of which 2 were waited for; matrix products, arithmetic and copies ran while one was open for 0% of the time, Pallas kernels for 1%

profile of v1, /device:TPU:0, one launch (start us, length us, event | category | flops | bytes accessed | tf_op | source)
XLA Modules:
  0.0 286.9 jit_solution(17116784877523195594)
XLA Ops:
  1.3 0.0 copy-start.1
  1.3 1.0 copy-done.1
  2.3 0.9 copy-done.5
  3.2 0.9 copy-done.7
  4.1 0.7 copy-done.27
  4.8 0.7 copy-done.29
  5.5 6.2 %start.1 = (bf16[32,2,4,16,128]{4,3,2,1,0:T(8,128)(2,1)S(1)}, bf16[16,128,128]{2,1,0:T(8,128)(2,1)S(1)}) custom-call(s32[1]{0:T(128)S(6)} %copy.23.lengths, bf16[16,128,128]{2,1,0:T(8,128)(2,1)S(1)} %copy-done.1, f32[2,128]{1,0:T(2,128)S(1)} %copy-done.27, f32[2,128]{1,0:T(2,128)S(1)} %copy-done.29, bf16[2,2,128,128]{3,2,1,0:T(8,128)(2,1)S(1)} %copy-done.5, ...), custom_call_target="tpu_custom_call" | custom-call | flops 268435456 | bytes 2361348 | tf_op jit(solution)/shard_map/start/pallas_call | solution.py:364
  11.7 0.0 copy-start.6
  11.7 0.0 copy-start.8
  11.7 0.0 copy-start.9
  11.7 0.0 copy-start.12
  11.7 0.0 copy-start.25
  11.8 0.0 copy-start.26
  11.8 0.0 copy-start.28
  11.8 0.0 copy-start.30
  11.8 33.3 %all_to_all.50 = bf16[32,2,4,16,128]{4,3,2,1,0:T(8,128)(2,1)S(1)} all-to-all(bf16[32,2,4,16,128]{4,3,2,1,0:T(8,128)(2,1)S(1)} %get-tuple-element.31), channel_id=1, replica_groups=mesh['grp'=1,'row'=16,'col'=2,'ch'=1] {'row','col'}, dimensions={0} | all-to-all | bytes 2097152 | tf_op jit(solution)/shard_map/all_to_all | solution.py:378
  45.1 0.3 outgoing.1
  45.5 18.4 %all_to_all.51.tri.tri0 = bf16[32,4,16,128]{3,2,1,0:T(8,128)(2,1)S(1)} all-to-all(bf16[32,4,16,128]{3,2,1,0:T(8,128)(2,1)S(1)} %bitcast.27), channel_id=1, replica_groups=mesh['grp'=1,'row'=16,'col'=2,'ch'=1] {'row','col'}, dimensions={0} | all-to-all | bytes 1048576 | tf_op jit(solution)/shard_map/all_to_all | solution.py:378
  63.9 0.0 copy-done.6
  63.9 0.0 copy-done.8
  63.9 0.0 copy-done.9
  63.9 0.0 copy-done.12
  64.0 8.1 %between.1 = (bf16[32,2,4,16,128]{4,3,2,1,0:T(8,128)(2,1)S(1)}, bf16[16,128,128]{2,1,0:T(8,128)(2,1)S(1)}, bf16[16,128,128]{2,1,0:T(8,128)(2,1)S(1)}) custom-call(s32[1]{0:T(128)S(6)} %copy.23.lengths, bf16[32,4,16,128]{3,2,1,0:T(8,128)(2,1)S(1)} %all_to_all.51.tri.tri0, bf16[16,128,128]{2,1,0:T(8,128)(2,1)S(1)} %copy-done.1, ...), custom_call_target="tpu_custom_call" | custom-call | flops 402653184 | bytes 4067332 | tf_op jit(solution)/shard_map/between/pallas_call | solution.py:364
  72.1 0.0 copy-start
  72.1 29.7 %all_to_all.52 = bf16[32,2,4,16,128]{4,3,2,1,0:T(8,128)(2,1)S(1)} all-to-all(bf16[32,2,4,16,128]{4,3,2,1,0:T(8,128)(2,1)S(1)} %get-tuple-element.33), channel_id=1, replica_groups=mesh['grp'=1,'row'=16,'col'=2,'ch'=1] {'row','col'}, dimensions={0} | all-to-all | bytes 2097152 | tf_op jit(solution)/shard_map/all_to_all | solution.py:378
  101.8 0.3 incoming.1
  102.2 18.4 %all_to_all.53.tri = bf16[32,4,16,128]{3,2,1,0:T(8,128)(2,1)S(1)} all-to-all(bf16[32,4,16,128]{3,2,1,0:T(8,128)(2,1)S(1)} %bitcast.28), channel_id=1, replica_groups=mesh['grp'=1,'row'=16,'col'=2,'ch'=1] {'row','col'}, dimensions={0} | all-to-all | bytes 1048576 | tf_op jit(solution)/shard_map/all_to_all | solution.py:378
  120.6 6.9 %turn.1 = (bf16[32,4,16,128]{3,2,1,0:T(8,128)(2,1)S(1)}, bf16[16,128,128]{2,1,0:T(8,128)(2,1)}, bf16[16,128,128]{2,1,0:T(8,128)(2,1)S(1)}, bf16[16,128,128]{2,1,...) custom-call(bf16[32,4,16,128]{3,2,1,0:T(8,128)(2,1)S(1)} %all_to_all.53.tri, ...), custom_call_target="tpu_custom_call" | custom-call | flops 201326592 | bytes 4852736 | tf_op jit(solution)/shard_map/turn/pallas_call | solution.py:364
  127.5 18.4 %all_to_all.54 = bf16[32,4,16,128]{3,2,1,0:T(8,128)(2,1)S(1)} all-to-all(bf16[32,4,16,128]{3,2,1,0:T(8,128)(2,1)S(1)} %get-tuple-element.37), channel_id=1, replica_groups=mesh['grp'=1,'row'=16,'col'=2,'ch'=1] {'row','col'}, dimensions={0} | all-to-all | bytes 1048576 | tf_op jit(solution)/shard_map/all_to_all | solution.py:378
  145.9 0.4 incoming_grad.1
  146.4 29.7 %all_to_all.55.d_edge = bf16[32,2,4,16,128]{4,3,2,1,0:T(8,128)(2,1)S(1)} all-to-all(bf16[32,2,4,16,128]{4,3,2,1,0:T(8,128)(2,1)S(1)} %bitcast.24), channel_id=1, replica_groups=mesh['grp'=1,'row'=16,'col'=2,'ch'=1] {'row','col'}, dimensions={0} | all-to-all | bytes 2097152 | tf_op jit(solution)/shard_map/all_to_all | solution.py:378
  176.0 11.3 %middle.1 = (bf16[32,4,16,128]{3,2,1,0:T(8,128)(2,1)S(1)}, f32[16,128,128]{2,1,0:T(8,128)S(1)}, bf16[16,512,128]{2,1,0:T(8,128)(2,1)S(1)}, bf16[16,128,128]{2,1,...) custom-call(s32[1]{0:T(128)S(6)} %copy.23.lengths, ...), custom_call_target="tpu_custom_call" | custom-call | flops 805306368 | bytes 9835524 | tf_op jit(solution)/shard_map/middle/pallas_call | solution.py:364
  187.3 0.0 copy-start.19
  187.3 0.8 copy-done.19
  188.1 18.4 %all_to_all.56 = bf16[32,4,16,128]{3,2,1,0:T(8,128)(2,1)S(1)} all-to-all(bf16[32,4,16,128]{3,2,1,0:T(8,128)(2,1)S(1)} %get-tuple-element.39), channel_id=1, replica_groups=mesh['grp'=1,'row'=16,'col'=2,'ch'=1] {'row','col'}, dimensions={0} | all-to-all | bytes 1048576 | tf_op jit(solution)/shard_map/all_to_all | solution.py:378
  206.5 1.5 outgoing_grad.1
  208.0 3.6 %all-to-all-start.7 = ((bf16[32,2,4,16,128]{4,3,2,1,0:T(8,128)(2,1)}), bf16[32,2,4,16,128]{4,3,2,1,0:T(8,128)(2,1)S(1)}, u32[]{:S(2)}, u32[]{:S(2)}) async-start(bf16[32,2,4,16,128]{4,3,2,1,0:T(8,128)(2,1)} %bitcast.7), calls=%async_computation.7 | async-start | bytes 2097152 | tf_op jit(solution)/shard_map/all_to_all | solution.py:378
  211.7 0.0 copy-start.14
  211.7 1.0 copy-done.14
  212.7 1.0 copy-done.16
  213.7 0.4 out_weights_upper.1
  214.2 0.0 copy-start.18
  214.2 1.2 copy-done.18
  215.4 1.0 copy-done.20
  216.5 0.4 out_weights_lower.1
  216.9 0.0 copy-start.23
  216.9 0.7 in_weights_upper.1
  217.6 0.0 copy-start.21
  217.6 0.6 copy-done.21
  218.3 19.6 %all-to-all-done.7.d_edge = bf16[32,2,4,16,128]{4,3,2,1,0:T(8,128)(2,1)S(1)} async-done(((bf16[32,2,4,16,128]{4,3,2,1,0:T(8,128)(2,1)}), bf16[32,2,4,16,128]{4,3,2,1,0:T(8,128)(2,1)S(1)}, u32[]{:S(2)}, u32[]{:S(2)}) %all-to-all-start.7) | async-done | bytes 1048608 | tf_op jit(solution)/shard_map/all_to_all | solution.py:378
  237.9 1.2 copy-done.11
  239.1 9.4 %finish.1 = (bf16[16,128,128]{2,1,0:T(8,128)(2,1)}, bf16[16,512,128]{2,1,0:T(8,128)(2,1)S(1)}, f32[2,128]{1,0:T(2,128)S(1)}) custom-call(s32[1]{0:T(128)S(6)} %copy.23.lengths, bf16[32,2,4,16,128]{4,3,2,1,0:T(8,128)(2,1)S(1)} %all-to-all-done.7.d_edge, bf16[16,128,128]{2,1,0:T(8,128)(2,1)S(1)} %copy-done.2, ...), custom_call_target="tpu_custom_call" | custom-call | flops 603979776 | bytes 6621188 | tf_op jit(solution)/shard_map/finish/pallas_call | solution.py:364
  248.5 0.7 in_weights_lower.1
  249.3 0.1 copy-done.22
  249.5 0.1 pad_maximum_fusion
  249.5 18.4 %all_to_all.57 = bf16[32,64,128]{2,1,0:T(8,128)(2,1)S(1)} all-to-all(bf16[32,64,128]{2,1,0:T(8,128)(2,1)S(1)} %pad_maximum_fusion), channel_id=1, replica_groups=mesh['grp'=1,'row'=16,'col'=2,'ch'=1] {'row','col'}, dimensions={0} | all-to-all | bytes 1048576 | tf_op jit(solution)/shard_map/all_to_all | solution.py:378
  268.0 0.1 convert_reduce_fusion
  268.1 0.8 broadcast_in_dim.5
  268.9 3.6 %all-to-all-start.9 = ((bf16[32,48,128]{2,1,0:T(8,128)(2,1)}), bf16[32,48,128]{2,1,0:T(8,128)(2,1)S(1)}, u32[]{:S(2)}, u32[]{:S(2)}) async-start(bf16[32,48,128]{2,1,0:T(8,128)(2,1)} %broadcast_in_dim.5), calls=%async_computation.9 | async-start | bytes 786432 | tf_op jit(solution)/shard_map/all_to_all | solution.py:378
  272.5 0.6 fusion.2
  273.1 12.2 %all-to-all-done.9 = bf16[32,48,128]{2,1,0:T(8,128)(2,1)S(1)} async-done(((bf16[32,48,128]{2,1,0:T(8,128)(2,1)}), bf16[32,48,128]{2,1,0:T(8,128)(2,1)S(1)}, u32[]{:S(2)}, u32[]{:S(2)}) %all-to-all-start.9) | async-done | bytes 393248 | tf_op jit(solution)/shard_map/all_to_all | solution.py:378
  285.2 0.8 fusion.1
  286.1 0.1 convert.5
  286.1 0.7 slice_bitcast_fusion
  (38 shorter events, 0.1 us)
Async XLA Ops:
  1.3 1.0 copy-start.1
  2.3 0.9 copy-start.5
  3.2 0.9 copy-start.7
  4.1 0.7 copy-start.27
  4.8 0.7 copy-start.29
  11.7 52.2 %copy-start.6 = (bf16[2,2,128,128]{3,2,1,0:T(8,128)(2,1)S(1)}, bf16[2,2,128,128]{3,2,1,0:T(8,128)(2,1)}, u32[]{:S(2)}) copy-start(bf16[2,2,128,128]{3,2,1,0:T(8,128)(2,1)} %proj_w.7) | copy-start | bytes 393220
  11.7 52.2 %copy-start.8 = (bf16[2,2,128,128]{3,2,1,0:T(8,128)(2,1)S(1)}, bf16[2,2,128,128]{3,2,1,0:T(8,128)(2,1)}, u32[]{:S(2)}) copy-start(bf16[2,2,128,128]{3,2,1,0:T(8,128)(2,1)} %gate_w.7) | copy-start | bytes 393220
  11.7 52.2 %copy-start.9 = (bf16[2,128,128]{2,1,0:T(8,128)(2,1)S(1)}, bf16[2,128,128]{2,1,0:T(8,128)(2,1)}, u32[]{:S(2)}) copy-start(bf16[2,128,128]{2,1,0:T(8,128)(2,1)} %outgate_w.7) | copy-start | bytes 196612
  11.7 52.2 %copy-start.12 = (bf16[2,128,128]{2,1,0:T(8,128)(2,1)S(1)}, bf16[2,128,128]{2,1,0:T(8,128)(2,1)}, u32[]{:S(2)}) copy-start(bf16[2,128,128]{2,1,0:T(8,128)(2,1)} %out_w.5) | copy-start | bytes 196612
  11.7 52.2 %copy-start.25 = (f32[2,128]{1,0:T(2,128)S(1)}, f32[2,128]{1,0:T(2,128)}, u32[]{:S(2)}) copy-start(f32[2,128]{1,0:T(2,128)} %mgain.5) | copy-start | bytes 3076
  11.8 52.2 %copy-start.26 = (f32[2,128]{1,0:T(2,128)S(1)}, f32[2,128]{1,0:T(2,128)}, u32[]{:S(2)}) copy-start(f32[2,128]{1,0:T(2,128)} %mbias.5) | copy-start | bytes 3076
  11.8 52.2 %copy-start.28 = (f32[2,128]{1,0:T(2,128)S(1)}, f32[2,128]{1,0:T(2,128)}, u32[]{:S(2)}) copy-start(f32[2,128]{1,0:T(2,128)} %ngain.7) | copy-start | bytes 3076
  11.8 52.2 %copy-start.30 = (f32[2,128]{1,0:T(2,128)S(1)}, f32[2,128]{1,0:T(2,128)}, u32[]{:S(2)}) copy-start(f32[2,128]{1,0:T(2,128)} %nbias.3) | copy-start | bytes 3076
  72.1 48.5 %copy-start = (bf16[16,128,128]{2,1,0:T(8,128)(2,1)S(1)}, bf16[16,128,128]{2,1,0:T(8,128)(2,1)}, u32[]{:S(2)}) copy-start(bf16[16,128,128]{2,1,0:T(8,128)(2,1)} %cot.3) | copy-start | bytes 1572868
  127.5 48.5 %copy-start.13 = (bf16[16,128,128]{2,1,0:T(8,128)(2,1)}, bf16[16,128,128]{2,1,0:T(8,128)(2,1)S(1)}, u32[]{:S(2)}) copy-start(bf16[16,128,128]{2,1,0:T(8,128)(2,1)S(1)} %get-tuple-element.47.unit) | copy-start | bytes 1572868
  127.5 48.5 %copy-start.15 = (bf16[16,128,128]{2,1,0:T(8,128)(2,1)}, bf16[16,128,128]{2,1,0:T(8,128)(2,1)S(1)}, u32[]{:S(2)}) copy-start(bf16[16,128,128]{2,1,0:T(8,128)(2,1)S(1)} %get-tuple-element.48.d_outer) | copy-start | bytes 1572868
  187.3 0.8 copy-start.19
  188.1 19.9 %copy-start.3 = (bf16[16,512,128]{2,1,0:T(8,128)(2,1)}, bf16[16,512,128]{2,1,0:T(8,128)(2,1)S(1)}, u32[]{:S(2)}) copy-start(bf16[16,512,128]{2,1,0:T(8,128)(2,1)S(1)} %get-tuple-element.46.d_in) | copy-start | bytes 6291460
  188.1 19.9 %copy-start.10 = (f32[16,128,128]{2,1,0:T(8,128)}, f32[16,128,128]{2,1,0:T(8,128)S(1)}, u32[]{:S(2)}) copy-start(f32[16,128,128]{2,1,0:T(8,128)S(1)} %get-tuple-element.41.grad) | copy-start | bytes 3145732
  188.1 19.9 %copy-start.17 = (bf16[16,128,128]{2,1,0:T(8,128)(2,1)}, bf16[16,128,128]{2,1,0:T(8,128)(2,1)S(1)}, u32[]{:S(2)}) copy-start(bf16[16,128,128]{2,1,0:T(8,128)(2,1)S(1)} %get-tuple-element.44.unit) | copy-start | bytes 1572868
  208.0 29.9 %all-to-all-start.7 = ((bf16[32,2,4,16,128]{4,3,2,1,0:T(8,128)(2,1)}), bf16[32,2,4,16,128]{4,3,2,1,0:T(8,128)(2,1)S(1)}, u32[]{:S(2)}, u32[]{:S(2)}) async-start(bf16[32,2,4,16,128]{4,3,2,1,0:T(8,128)(2,1)} %bitcast.7), calls=%async_computation.7 | async-start | bytes 2097152 | tf_op jit(solution)/shard_map/all_to_all | solution.py:378
  211.7 1.0 copy-start.14
  212.7 1.0 copy-start.16
  213.7 3.2 %copy-start.4 = (bf16[16,512,128]{2,1,0:T(8,128)(2,1)S(1)}, bf16[16,512,128]{2,1,0:T(8,128)(2,1)}, u32[]{:S(2)}) copy-start(bf16[16,512,128]{2,1,0:T(8,128)(2,1)} %copy-done.3) | copy-start | bytes 6291460
  214.2 1.2 copy-start.18
  215.4 1.0 copy-start.20
  216.5 21.4 %copy-start.2 = (bf16[16,128,128]{2,1,0:T(8,128)(2,1)S(1)}, bf16[16,128,128]{2,1,0:T(8,128)(2,1)}, u32[]{:S(2)}) copy-start(bf16[16,128,128]{2,1,0:T(8,128)(2,1)} %pair.5) | copy-start | bytes 1572868
  216.9 1.4 copy-start.23
  217.6 0.7 copy-start.21
  237.9 1.2 copy-start.11
  248.5 0.9 copy-start.22
  248.5 0.9 copy-start.24
  268.9 16.4 %all-to-all-start.9 = ((bf16[32,48,128]{2,1,0:T(8,128)(2,1)}), bf16[32,48,128]{2,1,0:T(8,128)(2,1)S(1)}, u32[]{:S(2)}, u32[]{:S(2)}) async-start(bf16[32,48,128]{2,1,0:T(8,128)(2,1)} %broadcast_in_dim.5), calls=%async_computation.9 | async-start | bytes 786432 | tf_op jit(solution)/shard_map/all_to_all | solution.py:378

commit v2 on v1

--- a/solution.py
+++ b/solution.py
@@ -87,24 +87,39 @@
     return scratch[pl.ds(step, channels, stride=rows), :]
 
 
-def spread_edges(scratch, out_ref):
-    shards, sides, group, rows, lanes = out_ref.shape
-    block = shards * group * rows
-    for side in range(sides):
-        part = scratch[side * block : (side + 1) * block, :]
-        out_ref[:, side] = part.reshape(shards, group, rows, lanes).astype(BF16)
-
-
-def collect_edges(in_ref, scratch):
-    shards, sides, group, rows, lanes = in_ref.shape
-    block = shards * group * rows
-    for side in range(sides):
-        scratch[side * block : (side + 1) * block, :] = (
-            in_ref[:, side].astype(F32).reshape(block, lanes)
-        )
-
-
-def start_kernel(lengths, pair, ngain, nbias, proj_w, gate_w, edge_out, normed_out, wts, scr):
+def spread_edges(scratch, out_refs):
+    shards, sides, group, rows, lanes = out_refs[0].shape
+    view = scratch.reshape(sides, shards, len(out_refs), group, rows, lanes)
+    for chunk, out_ref in enumerate(out_refs):
+        for side in range(sides):
+            out_ref[:, side] = view[side, :, chunk].astype(BF16)
+
+
+def collect_edges(in_refs, scratch):
+    shards, sides, group, rows, lanes = in_refs[0].shape
+    view = scratch.reshape(sides, shards, len(in_refs), group, rows, lanes)
+    for chunk, in_ref in enumerate(in_refs):
+        for side in range(sides):
+            view[side, :, chunk] = in_ref[:, side].astype(F32)
+
+
+def spread_triangle(scratch, out_refs):
+    shards, group, rows, lanes = out_refs[0].shape
+    view = scratch.reshape(shards, len(out_refs), group, rows, lanes)
+    for chunk, out_ref in enumerate(out_refs):
+        out_ref[...] = view[:, chunk].astype(BF16)
+
+
+def collect_triangle(in_refs, scratch, channels):
+    shards, group, rows, lanes = in_refs[0].shape
+    view = scratch.at[0 : channels * rows].reshape(shards, len(in_refs), group, rows, lanes)
+    for chunk, in_ref in enumerate(in_refs):
+        view[:, chunk] = in_ref[...].astype(F32)
+
+
+def start_kernel(
+    lengths, pair, ngain, nbias, proj_w, gate_w, edge_a, edge_b, normed_out, wts, scr
+):
     rows, lanes, channels = pair.shape
     load_in_weights(proj_w, gate_w, 0, wts)
     gain, bias = column(ngain, 0, lanes), column(nbias, 0, lanes)
@@ -116,8 +131,8 @@
         put_rows(scr, edges(normed, wts[...], row_mask(lengths, step, rows, lanes)), step, rows)
         return carry
 
-    lax.fori_loop(0, rows, body, 0)
-    spread_edges(scr, edge_out)
+    lax.fori_loop(0, rows, body, 0, unroll=2)
+    spread_edges(scr, (edge_a, edge_b))
 
 
 def mid_norm(tri):
@@ -129,15 +144,15 @@
 
 
 def between_kernel(
-    lengths, tri, pair, normed0, ngain, nbias, mgain, mbias, out_w, outgate_w, proj_w, gate_w,
-    edge_out, mid_out, normed_out, wts, scr,
+    lengths, tri_a, tri_b, pair, normed0, ngain, nbias, mgain, mbias, out_w, outgate_w, proj_w,
+    gate_w, edge_a, edge_b, mid_out, normed_out, wts, scr,
 ):
     rows, lanes, channels = pair.shape
     load_in_weights(proj_w, gate_w, 1, wts)
     out_t, outgate_t = turned(out_w[0]), turned(outgate_w[0])
     gain, bias = column(ngain, 1, lanes), column(nbias, 1, lanes)
     gain_mid, bias_mid = column(mgain, 0, lanes), column(mbias, 0, lanes)
-    scr[0 : channels * rows, :] = tri[...].astype(F32).reshape(channels * rows, lanes)
+    collect_triangle((tri_a, tri_b), scr, channels)
 
     def body(step, carry):
         scaled_mid, _ = mid_norm(get_rows(scr, step, channels, rows))
@@ -153,8 +168,8 @@
         put_rows(scr, here, step, rows)
         return carry
 
-    lax.fori_loop(0, rows, body, 0)
-    spread_edges(scr, edge_out)
+    lax.fori_loop(0, rows, body, 0, unroll=2)
+    spread_edges(scr, (edge_a, edge_b))
 
 
 def triangle_kernel(incoming, edge, tri_out):
@@ -219,13 +234,13 @@
 
 
 def turn_kernel(
-    tri, mid, normed1, cot, mgain, mbias, out_w, outgate_w,
-    d_tri_out, new_out, unit_out, d_outer_out, d_gatepre_out, small_out, scr, sum_gain, sum_bias,
+    tri_a, tri_b, mid, normed1, cot, mgain, mbias, out_w, outgate_w,
+    d_tri_a, d_tri_b, new_out, unit_out, d_outer_out, d_gatepre_out, small_out, scr, sum_gain, sum_bias,
 ):
     rows, channels, lanes = mid.shape
     out_t, outgate_t = turned(out_w[1]), turned(outgate_w[1])
     gain_mid, bias_mid = column(mgain, 1, lanes), column(mbias, 1, lanes)
-    scr[...] = tri[...].astype(F32).reshape(channels * rows, lanes)
+    collect_triangle((tri_a, tri_b), scr, channels)
     sum_gain[...] = jnp.zeros_like(sum_gain)
     sum_bias[...] = jnp.zeros_like(sum_bias)
 
@@ -239,8 +254,8 @@
         put_rows(scr, d_tri, step, rows)
         return carry
 
-    lax.fori_loop(0, rows, body, 0)
-    d_tri_out[...] = scr[...].reshape(d_tri_out.shape).astype(BF16)
+    lax.fori_loop(0, rows, body, 0, unroll=2)
+    spread_triangle(scr, (d_tri_a, d_tri_b))
     small_out[0:1, :] = as_row(sum_gain[...])
     small_out[1:2, :] = as_row(sum_bias[...])
 
@@ -273,9 +288,9 @@
 
 
 def middle_kernel(
-    lengths, d_edge, mid, normed1, d_gatepre1, cot, tri0, normed0,
+    lengths, d_edge_a, d_edge_b, mid, normed1, d_gatepre1, cot, tri_a, tri_b, normed0,
     ngain, mgain, mbias, proj_w, gate_w, out_w, outgate_w,
-    d_tri_out, grad_out, d_in_out, unit_out, d_outer_out, d_gatepre_out, small_out,
+    d_tri_a, d_tri_b, grad_out, d_in_out, unit_out, d_outer_out, d_gatepre_out, small_out,
     wts, scr, scr_tri, sums,
 ):
     rows, channels, lanes = mid.shape
@@ -283,8 +298,8 @@
     out_t, outgate_t = turned(out_w[0]), turned(outgate_w[0])
     gain = column(ngain, 1, lanes)
     gain_mid, bias_mid = column(mgain, 0, lanes), column(mbias, 0, lanes)
-    collect_edges(d_edge, scr)
-    scr_tri[...] = tri0[...].astype(F32).reshape(channels * rows, lanes)
+    collect_edges((d_edge_a, d_edge_b), scr)
+    collect_triangle((tri_a, tri_b), scr_tri, channels)
     sums[...] = jnp.zeros_like(sums)
 
     def body(step, carry):
@@ -303,20 +318,20 @@
         put_rows(scr_tri, d_tri, step, rows)
         return carry
 
-    lax.fori_loop(0, rows, body, 0)
-    d_tri_out[...] = scr_tri[...].reshape(d_tri_out.shape).astype(BF16)
+    lax.fori_loop(0, rows, body, 0, unroll=2)
+    spread_triangle(scr_tri, (d_tri_a, d_tri_b))
     for index in range(4):
         small_out[index : index + 1, :] = as_row(sums[index])
 
 
 def finish_kernel(
-    lengths, d_edge, pair, normed0, d_gatepre0, grad, ngain, proj_w, gate_w, outgate_w,
+    lengths, d_edge_a, d_edge_b, pair, normed0, d_gatepre0, grad, ngain, proj_w, gate_w, outgate_w,
     grad_out, d_in_out, small_out, wts, scr, sums,
 ):
     rows, lanes, channels = pair.shape
     load_in_weights(proj_w, gate_w, 0, wts)
     gain = column(ngain, 0, lanes)
-    collect_edges(d_edge, scr)
+    collect_edges((d_edge_a, d_edge_b), scr)
     sums[...] = jnp.zeros_like(sums)
 
     def body(step, carry):
@@ -329,7 +344,7 @@
         grad_out[step] = jnp.transpose(total).astype(BF16)
         return carry
 
-    lax.fori_loop(0, rows, body, 0)
+    lax.fori_loop(0, rows, body, 0, unroll=2)
     for index in range(2):
         small_out[index : index + 1, :] = as_row(sums[index])
 
@@ -384,10 +399,12 @@
 ):
     rows, lanes, channels = pair.shape
     shards = many * few
-    group = H // shards
+    chunks = 2
+    group = H // (shards * chunks)
     edge_shape = (shards, 2, group, rows, lanes)
     grid_shape = (many, few, 2, group, rows, lanes)
     tri_shape = (shards, group, rows, lanes)
+    tri_grid = (many, few, group, rows, lanes)
     tile = (rows, channels, lanes)
     wts = ((4 * H, channels), BF16)
     big = ((2 * H * rows, lanes), F32)
@@ -396,53 +413,62 @@
     triangle = 2 * group * (many * rows) ** 2 * (few * lanes)
     dense = 2 * positions * channels * H
 
-    edge, normed0 = call(
-        start_kernel, "start", [(edge_shape, BF16), (tile, BF16)],
+    def triangles(name, incoming, edges_in):
+        out = []
+        for edge in edges_in:
+            (tri,) = call(
+                functools.partial(triangle_kernel, incoming), name, [(tri_grid, BF16)], [edge],
+                (), triangle,
+            )
+            out.append(exchange(tri.reshape(tri_shape)))
+        return out
+
+    def edge_grads(name, incoming, edges_in, d_tris):
+        out = []
+        for edge, d_tri in zip(edges_in, d_tris):
+            (d_edge,) = call(
+                functools.partial(edge_grad_kernel, incoming), name, [(grid_shape, BF16)],
+                [edge, exchange(d_tri).reshape(tri_grid)], (), 2 * triangle,
+            )
+            out.append(exchange(d_edge.reshape(edge_shape)))
+        return out
+
+    *edge, normed0 = call(
+        start_kernel, "start", [(edge_shape, BF16)] * chunks + [(tile, BF16)],
         [lengths, pair, ngain, nbias, proj_w, gate_w], [wts, big], 4 * dense, 1,
     )
-    edge0 = exchange(edge).reshape(grid_shape)
-    (tri,) = call(
-        functools.partial(triangle_kernel, False), "outgoing",
-        [((many, few, group, rows, lanes), BF16)], [edge0], (), triangle,
-    )
-    tri0 = exchange(tri.reshape(tri_shape))
-    edge, mid_t, normed1 = call(
-        between_kernel, "between", [(edge_shape, BF16), (tile, BF16), (tile, BF16)],
-        [lengths, tri0, pair, normed0, ngain, nbias, mgain, mbias, out_w, outgate_w, proj_w, gate_w],
+    edge0 = [exchange(part).reshape(grid_shape) for part in edge]
+    tri0 = triangles("outgoing", False, edge0)
+    *edge, mid_t, normed1 = call(
+        between_kernel, "between", [(edge_shape, BF16)] * chunks + [(tile, BF16), (tile, BF16)],
+        [lengths, *tri0, pair, normed0, ngain, nbias, mgain, mbias, out_w, outgate_w, proj_w,
+         gate_w],
         [wts, big], 6 * dense, 1,
     )
-    edge1 = exchange(edge).reshape(grid_shape)
-    (tri,) = call(
-        functools.partial(triangle_kernel, True), "incoming",
-        [((many, few, group, rows, lanes), BF16)], [edge1], (), triangle,
-    )
-    tri1 = exchange(tri.reshape(tri_shape))
-    d_tri, new_pair, unit1, d_outer1, d_gatepre1, small_mid1 = call(
+    edge1 = [exchange(part).reshape(grid_shape) for part in edge]
+    tri1 = triangles("incoming", True, edge1)
+    *d_tri, new_pair, unit1, d_outer1, d_gatepre1, small_mid1 = call(
         turn_kernel, "turn",
-        [(tri_shape, BF16), (pair.shape, BF16), (tile, BF16), (tile, BF16), (tile, BF16),
-         ((2, H), F32)],
-        [tri1, mid_t, normed1, cotangent, mgain, mbias, out_w, outgate_w],
+        [(tri_shape, BF16)] * chunks
+        + [(pair.shape, BF16), (tile, BF16), (tile, BF16), (tile, BF16), ((2, H), F32)],
+        [*tri1, mid_t, normed1, cotangent, mgain, mbias, out_w, outgate_w],
         [mid, ((H, lanes), F32), ((H, lanes), F32)], 3 * dense,
     )
-    d_tri = exchange(d_tri).reshape(many, few, group, rows, lanes)
-    (d_edge,) = call(
-        functools.partial(edge_grad_kernel, True), "incoming_grad",
-        [(grid_shape, BF16)], [edge1, d_tri], (), 2 * triangle,
-    )
-    d_edge = exchange(d_edge.reshape(edge_shape))
+    d_edge = edge_grads("incoming_grad", True, edge1, d_tri)
     (out_grads1,) = call(
         out_weight_kernel, "out_weights_upper", [((2 * H, channels), BF16)],
         [unit1, d_outer1, normed1, d_gatepre1], (), 2 * dense,
     )
-    d_tri, grad, d_in1, unit0, d_outer0, d_gatepre0, small_mid = call(
+    *d_tri, grad, d_in1, unit0, d_outer0, d_gatepre0, small_mid = call(
         middle_kernel, "middle",
-        [(tri_shape, BF16), (tile, F32), ((rows, 4 * H, lanes), BF16), (tile, BF16), (tile, BF16),
-         (tile, BF16), ((4, H), F32)],
-        [lengths, d_edge, mid_t, normed1, d_gatepre1, cotangent, tri0, normed0,
+        [(tri_shape, BF16)] * chunks
+        + [(tile, F32), ((rows, 4 * H, lanes), BF16), (tile, BF16), (tile, BF16),
+           (tile, BF16), ((4, H), F32)],
+        [lengths, *d_edge, mid_t, normed1, d_gatepre1, cotangent, *tri0, normed0,
          ngain, mgain, mbias, proj_w, gate_w, out_w, outgate_w],
         [wts, big, mid, ((4, H, lanes), F32)], 12 * dense, 1,
     )
-    d_tri = exchange(d_tri).reshape(many, few, group, rows, lanes)
+    d_edge = edge_grads("outgoing_grad", False, edge0, d_tri)
     (in_grads1,) = call(
         in_weight_kernel, "in_weights_upper", [((4 * H, H), BF16)], [normed1, d_in1], (), 4 * dense,
     )
@@ -450,15 +476,12 @@
         out_weight_kernel, "out_weights_lower", [((2 * H, channels), BF16)],
         [unit0, d_outer0, normed0, d_gatepre0], (), 2 * dense,
     )
-    (d_edge,) = call(
-        functools.partial(edge_grad_kernel, False), "outgoing_grad",
-        [(grid_shape, BF16)], [edge0, d_tri], (), 2 * triangle,
-    )
-    d_edge = exchange(d_edge.reshape(edge_shape))
+    early = jnp.concatenate([in_grads1, out_grads1, out_grads0], axis=0)
+    early = jnp.sum(exchange(early.reshape(shards, -1, H)).astype(F32), axis=0).astype(BF16)
     grad_pair, d_in0, small0 = call(
         finish_kernel, "finish",
         [(pair.shape, BF16), ((rows, 4 * H, lanes), BF16), ((2, H), F32)],
-        [lengths, d_edge, pair, normed0, d_gatepre0, grad, ngain, proj_w, gate_w, outgate_w],
+        [lengths, *d_edge, pair, normed0, d_gatepre0, grad, ngain, proj_w, gate_w, outgate_w],
         [wts, big, ((2, H, lanes), F32)], 9 * dense, 1,
     )
     (in_grads0,) = call(
@@ -467,30 +490,31 @@
     small = jnp.concatenate([small0, small_mid[2:4], small_mid[0:2], small_mid1], axis=0)
     high = small.astype(BF16)
     low = (small - high.astype(F32)).astype(BF16)
-    every = jnp.concatenate([high, low], axis=0)
-    weights = jnp.concatenate([in_grads0, out_grads0, in_grads1, out_grads1], axis=0)
-    share = weights.shape[0] // shards
+    every = jnp.concatenate([high, low, early], axis=0)
+    share = 4 * H // shards
     packed = jnp.concatenate(
-        [weights.reshape(shards, share, H), jnp.broadcast_to(every[None], (shards,) + every.shape)],
+        [in_grads0.reshape(shards, share, H), jnp.broadcast_to(every[None], (shards,) + every.shape)],
         axis=1,
     )
-    summed = jnp.sum(exchange(packed).astype(F32), axis=0)
+    packed = exchange(packed)
+    summed = jnp.sum(packed[:, : share + 16].astype(F32), axis=0)
     small = summed[share : share + 8] + summed[share + 8 :]
+    early = packed[:, share + 16 :].reshape(8, H, H).astype(F32)
     own = summed[:share].astype(BF16)
-    weights = exchange(jnp.broadcast_to(own[None], (shards,) + own.shape))
-    weights = weights.reshape(2, 6, H, H).astype(F32)
+    late = exchange(jnp.broadcast_to(own[None], (shards,) + own.shape))
+    late = late.reshape(4, H, H).astype(F32)
     small = small.reshape(2, 4, H)
     return (
         new_pair,
         grad_pair,
         small[:, 0],
         small[:, 1],
-        weights[:, 0:2],
-        weights[:, 2:4],
+        jnp.stack([late[0:2], early[0:2]]),
+        jnp.stack([late[2:4], early[2:4]]),
         small[:, 2],
         small[:, 3],
-        weights[:, 4],
-        weights[:, 5],
+        jnp.stack([early[6], early[4]]),
+        jnp.stack([early[7], early[5]]),
     )
 
 

time: 288 us -> 363 us (1.26)
  waiting for transfers between devices: 31.8 us -> 118 us
  blocking collectives: 185 us -> 129 us
  starting transfers between devices: 7.24 us -> 36.9 us
  local copies, waits for them, and re-layouts: 14.4 us -> 31 us
  Pallas kernels: 46.8 us -> 40.9 us
    all_to_all x2 -> x11, waiting for transfers between devices: 31.8 us -> 118 us  [exchange(): lax.all_to_all(values, ('row', 'col'), split_axis=0, concat_axis=0, tiled...]
    all_to_all x8, blocking collectives: 185 us -> 129 us  [exchange(): lax.all_to_all(values, ('row', 'col'), split_axis=0, concat_axis=0, tiled...]
    all_to_all x2 -> x11, starting transfers between devices: 7.24 us -> 36.9 us  [exchange(): lax.all_to_all(values, ('row', 'col'), split_axis=0, concat_axis=0, tiled...]
    unnamed x62 -> x108, local copies, waits for them, and re-layouts: 11.4 us -> 29.6 us
    pallas_call x13 -> x17, Pallas kernels: 46.8 us -> 40.9 us  [call(): pl.pallas_call(kernel, name=name, out_shape=shapes, in_specs=[SCALARS] *...]
  transfers between devices with their start and end apart: 2 -> 11, of which waited for: 2 -> 11; matrix products, arithmetic and copies ran while one was open for 0% -> 1% of each run, Pallas kernels for 1% -> 2%
where the time goes in v2:
time: 363 us; the launch traced here: 361 us
  blocking collectives  129 us (36%)
  waiting for transfers between devices  118 us (33%)
  Pallas kernels  40.9 us (11%)
  starting transfers between devices  36.9 us (10%)
  local copies, waits for them, and re-layouts  31 us (9%)
    all_to_all x8, blocking collectives, exchange(): lax.all_to_all(values, ('row', 'col'), split_axis=0, concat_axis=0, tiled...  129 us
    all_to_all x11, waiting for transfers between devices, exchange(): lax.all_to_all(values, ('row', 'col'), split_axis=0, concat_axis=0, tiled...  118 us
    pallas_call x17, Pallas kernels, call(): pl.pallas_call(kernel, name=name, out_shape=shapes, in_specs=[SCALARS] *...  40.9 us
    all_to_all x11, starting transfers between devices, exchange(): lax.all_to_all(values, ('row', 'col'), split_axis=0, concat_axis=0, tiled...  36.9 us
    unnamed x108, local copies, waits for them, and re-layouts  29.6 us
  transfers between devices with their start and end apart: 11, of which 11 were waited for; matrix products, arithmetic and copies ran while one was open for 1% of the time, Pallas kernels for 2%

profile of v2, /device:TPU:0, one launch (start us, length us, event | category | flops | bytes accessed | tf_op | source)
XLA Modules:
  0.0 361.3 jit_solution(4847443753259232717)
XLA Ops:
  1.3 1.0 copy-done.4
  2.3 0.9 copy-done.19
  3.2 0.9 copy-done.21
  5.5 4.6 %start.1 = (bf16[32,2,2,16,128]{4,3,2,1,0:T(8,128)(2,1)}, bf16[32,2,2,16,128]{4,3,2,1,0:T(8,128)(2,1)S(1)}, bf16[16,128,128]{2,1,0:T(8,128)(2,1)S(1)}) custom-call(s32[1]{0:T(128)S(6)} %copy.21.lengths, bf16[16,128,128]{2,1,0:T(8,128)(2,1)S(1)} %copy-done.4, f32[2,128]{1,0:T(2,128)S(1)} %copy-done.48, f32[2,128]{1,0:T(2,128)S(1)} %copy-done.52, ...), custom_call_target="tpu_custom_call" | custom-call | flops 268435456 | bytes 2361348 | tf_op jit(solution)/shard_map/start/pallas_call | solution.py:379
  10.1 22.1 %all_to_all.95 = bf16[32,2,2,16,128]{4,3,2,1,0:T(8,128)(2,1)S(1)} all-to-all(bf16[32,2,2,16,128]{4,3,2,1,0:T(8,128)(2,1)S(1)} %get-tuple-element.36), channel_id=1, replica_groups=mesh['grp'=1,'row'=16,'col'=2,'ch'=1] {'row','col'}, dimensions={0} | all-to-all | bytes 1048576 | tf_op jit(solution)/shard_map/all_to_all | solution.py:393
  32.3 3.6 %all-to-all-start = ((bf16[32,2,2,16,128]{4,3,2,1,0:T(8,128)(2,1)}), bf16[32,2,2,16,128]{4,3,2,1,0:T(8,128)(2,1)S(1)}, u32[]{:S(2)}, u32[]{:S(2)}) async-start(bf16[32,2,2,16,128]{4,3,2,1,0:T(8,128)(2,1)} %get-tuple-element.35), calls=%async_computation | async-start | bytes 1048576 | tf_op jit(solution)/shard_map/all_to_all | solution.py:393
  35.9 1.0 outgoing.3
  36.9 14.0 %all-to-all-done = bf16[32,2,2,16,128]{4,3,2,1,0:T(8,128)(2,1)S(1)} async-done(((bf16[32,2,2,16,128]{4,3,2,1,0:T(8,128)(2,1)}), bf16[32,2,2,16,128]{4,3,2,1,0:T(8,128)(2,1)S(1)}, u32[]{:S(2)}, u32[]{:S(2)}) %all-to-all-start) | async-done | bytes 524320 | tf_op jit(solution)/shard_map/all_to_all | solution.py:393
  50.9 3.6 %all-to-all-start.3 = ((bf16[32,2,16,128]{3,2,1,0:T(8,128)(2,1)}), bf16[32,2,16,128]{3,2,1,0:T(8,128)(2,1)S(1)}, u32[]{:S(2)}, u32[]{:S(2)}) async-start(bf16[32,2,16,128]{3,2,1,0:T(8,128)(2,1)} %bitcast.3), calls=%async_computation.3 | async-start | bytes 524288 | tf_op jit(solution)/shard_map/all_to_all | solution.py:393
  54.8 10.4 %all-to-all-done.3.tri_b = bf16[32,2,16,128]{3,2,1,0:T(8,128)(2,1)S(1)} async-done(((bf16[32,2,16,128]{3,2,1,0:T(8,128)(2,1)}), bf16[32,2,16,128]{3,2,1,0:T(8,128)(2,1)S(1)}, u32[]{:S(2)}, u32[]{:S(2)}) %all-to-all-start.3) | async-done | bytes 262176 | tf_op jit(solution)/shard_map/all_to_all | solution.py:393
  65.2 12.8 %all_to_all.96.tri_a = bf16[32,2,16,128]{3,2,1,0:T(8,128)(2,1)S(1)} all-to-all(bf16[32,2,16,128]{3,2,1,0:T(8,128)(2,1)S(1)} %bitcast.45), channel_id=1, replica_groups=mesh['grp'=1,'row'=16,'col'=2,'ch'=1] {'row','col'}, dimensions={0} | all-to-all | bytes 524288 | tf_op jit(solution)/shard_map/all_to_all | solution.py:393
  78.1 5.3 %between.1 = (bf16[32,2,2,16,128]{4,3,2,1,0:T(8,128)(2,1)S(1)}, bf16[32,2,2,16,128]{4,3,2,1,0:T(8,128)(2,1)S(1)}, bf16[16,128,128]{2,1,0:T(8,128)(2,1)S(1)}, bf16[16,128,128]{2,1,0:T(8,128)(2,1)S(1)}) custom-call(s32[1]{0:T(128)S(6)} %copy.21.lengths, bf16[32,2,16,128]{3,2,1,0:T(8,128)(2,1)S(1)} %all_to_all.96.tri_a, ...), custom_call_target="tpu_custom_call" | custom-call | flops 402653184 | bytes 4067332 | tf_op jit(solution)/shard_map/between/pallas_call | solution.py:379
  83.4 0.8 copy-done.7
  84.3 17.1 %all_to_all.97 = bf16[32,2,2,16,128]{4,3,2,1,0:T(8,128)(2,1)S(1)} all-to-all(bf16[32,2,2,16,128]{4,3,2,1,0:T(8,128)(2,1)S(1)} %get-tuple-element.39), channel_id=1, replica_groups=mesh['grp'=1,'row'=16,'col'=2,'ch'=1] {'row','col'}, dimensions={0} | all-to-all | bytes 1048576 | tf_op jit(solution)/shard_map/all_to_all | solution.py:393
  101.4 3.6 %all-to-all-start.4 = ((bf16[32,2,2,16,128]{4,3,2,1,0:T(8,128)(2,1)}), bf16[32,2,2,16,128]{4,3,2,1,0:T(8,128)(2,1)S(1)}, u32[]{:S(2)}, u32[]{:S(2)}) async-start(bf16[32,2,2,16,128]{4,3,2,1,0:T(8,128)(2,1)} %copy-done.35), calls=%async_computation.4 | async-start | bytes 1048576 | tf_op jit(solution)/shard_map/all_to_all | solution.py:393
  106.0 14.0 %all-to-all-done.4 = bf16[32,2,2,16,128]{4,3,2,1,0:T(8,128)(2,1)S(1)} async-done(((bf16[32,2,2,16,128]{4,3,2,1,0:T(8,128)(2,1)}), bf16[32,2,2,16,128]{4,3,2,1,0:T(8,128)(2,1)S(1)}, u32[]{:S(2)}, u32[]{:S(2)}) %all-to-all-start.4) | async-done | bytes 524320 | tf_op jit(solution)/shard_map/all_to_all | solution.py:393
  120.0 3.7 %all-to-all-start.7 = ((bf16[32,2,16,128]{3,2,1,0:T(8,128)(2,1)}), bf16[32,2,16,128]{3,2,1,0:T(8,128)(2,1)}, u32[]{:S(2)}, u32[]{:S(2)}) async-start(bf16[32,2,16,128]{3,2,1,0:T(8,128)(2,1)} %bitcast.43), calls=%async_computation.7 | async-start | bytes 524288 | tf_op jit(solution)/shard_map/all_to_all | solution.py:393
  124.7 9.7 %all-to-all-done.7.tri_b = bf16[32,2,16,128]{3,2,1,0:T(8,128)(2,1)} async-done(((bf16[32,2,16,128]{3,2,1,0:T(8,128)(2,1)}), bf16[32,2,16,128]{3,2,1,0:T(8,128)(2,1)}, u32[]{:S(2)}, u32[]{:S(2)}) %all-to-all-start.7) | async-done | bytes 262176 | tf_op jit(solution)/shard_map/all_to_all | solution.py:393
  134.4 13.3 %all_to_all.98.tri_a = bf16[32,2,16,128]{3,2,1,0:T(8,128)(2,1)S(1)} all-to-all(bf16[32,2,16,128]{3,2,1,0:T(8,128)(2,1)} %bitcast.46), channel_id=1, replica_groups=mesh['grp'=1,'row'=16,'col'=2,'ch'=1] {'row','col'}, dimensions={0} | all-to-all | bytes 524288 | tf_op jit(solution)/shard_map/all_to_all | solution.py:393
  147.7 1.0 copy-done.2
  148.7 1.0 copy-done.8
  149.8 0.8 copy-done.25
  150.6 0.8 copy-done.33
  151.5 6.5 %turn.1 = (bf16[32,2,16,128]{3,2,1,0:T(8,128)(2,1)S(1)}, bf16[32,2,16,128]{3,2,1,0:T(8,128)(2,1)S(1)}, bf16[16,128,128]{2,1,0:T(8,128)(2,1)}, bf16[16,128,128]{2...) custom-call(bf16[32,2,16,128]{3,2,1,0:T(8,128)(2,1)S(1)} %all_to_all, ...), custom_call_target="tpu_custom_call" | custom-call | flops 201326592 | bytes 4852736 | tf_op jit(solution)/shard_map/turn/pallas_call | solution.py:379
  158.7 0.8 copy-done.36
  159.6 0.8 copy-done.38
  160.4 13.1 %all_to_all.99 = bf16[32,2,16,128]{3,2,1,0:T(8,128)(2,1)} all-to-all(bf16[32,2,16,128]{3,2,1,0:T(8,128)(2,1)S(1)} %get-tuple-element.43), channel_id=1, replica_groups=mesh['grp'=1,'row'=16,'col'=2,'ch'=1] {'row','col'}, dimensions={0} | all-to-all | bytes 524288 | tf_op jit(solution)/shard_map/all_to_all | solution.py:393
  173.5 3.3 all-to-all-start.10
  176.8 0.9 copy-done.30
  178.8 8.6 %all-to-all-done.10 = bf16[32,2,16,128]{3,2,1,0:T(8,128)(2,1)} async-done(((bf16[32,2,16,128]{3,2,1,0:T(8,128)(2,1)}), bf16[32,2,16,128]{3,2,1,0:T(8,128)(2,1)}, u32[]{:S(2)}, u32[]{:S(2)}) %all-to-all-start.10) | async-done | bytes 262176 | tf_op jit(solution)/shard_map/all_to_all | solution.py:393
  187.4 3.3 all-to-all-start.9
  190.8 1.3 incoming_grad.3
  192.8 12.9 %all-to-all-done.9.d_edge_a = bf16[32,2,2,16,128]{4,3,2,1,0:T(8,128)(2,1)} async-done(((bf16[32,2,2,16,128]{4,3,2,1,0:T(8,128)(2,1)}), bf16[32,2,2,16,128]{4,3,2,1,0:T(8,128)(2,1)}, u32[]{:S(2)}, u32[]{:S(2)}) %all-to-all-start.9) | async-done | bytes 524320 | tf_op jit(solution)/shard_map/all_to_all | solution.py:393
  205.7 18.6 %all_to_all.100.d_edge_b = bf16[32,2,2,16,128]{4,3,2,1,0:T(8,128)(2,1)S(1)} all-to-all(bf16[32,2,2,16,128]{4,3,2,1,0:T(8,128)(2,1)} %bitcast.40), channel_id=1, replica_groups=mesh['grp'=1,'row'=16,'col'=2,'ch'=1] {'row','col'}, dimensions={0} | all-to-all | bytes 1048576 | tf_op jit(solution)/shard_map/all_to_all | solution.py:393
  224.3 1.0 copy-done.3
  225.3 1.0 copy-done.9
  226.4 1.0 copy-done.15
  227.4 9.3 %middle.1 = (bf16[32,2,16,128]{3,2,1,0:T(8,128)(2,1)S(1)}, bf16[32,2,16,128]{3,2,1,0:T(8,128)(2,1)S(1)}, f32[16,128,128]{2,1,0:T(8,128)S(1)}, bf16[16,512,128]{2...) custom-call(s32[1]{0:T(128)S(6)} %copy.21.lengths, ...), custom_call_target="tpu_custom_call" | custom-call | flops 805306368 | bytes 9835524 | tf_op jit(solution)/shard_map/middle/pallas_call | solution.py:379
  236.8 1.3 copy-done.10
  238.9 1.0 copy-done.27
  239.9 0.8 copy-done.40
  241.5 14.1 %all_to_all.101 = bf16[32,2,16,128]{3,2,1,0:T(8,128)(2,1)S(1)} all-to-all(bf16[32,2,16,128]{3,2,1,0:T(8,128)(2,1)S(1)} %get-tuple-element.46), channel_id=1, replica_groups=mesh['grp'=1,'row'=16,'col'=2,'ch'=1] {'row','col'}, dimensions={0} | all-to-all | bytes 524288 | tf_op jit(solution)/shard_map/all_to_all | solution.py:393
  255.6 2.6 all-to-all-start.14
  258.2 1.0 copy-done.16
  259.2 1.0 copy-done.37
  260.3 1.0 copy-done.39
  261.8 1.2 copy-done.41
  263.0 1.0 copy-done.43
  265.9 3.0 all-to-all-done.14
  268.9 3.3 all-to-all-start.16
  272.2 1.1 outgoing_grad.2
  273.3 9.5 %all-to-all-done.16 = bf16[32,32,128]{2,1,0:T(8,128)(2,1)} async-done(((bf16[32,32,128]{2,1,0:T(8,128)(2,1)}), bf16[32,32,128]{2,1,0:T(8,128)(2,1)}, u32[]{:S(2)}, u32[]{:S(2)}) %all-to-all-start.16) | async-done | bytes 262176 | tf_op jit(solution)/shard_map/all_to_all | solution.py:393
  282.8 2.6 all-to-all-start.13
  285.5 1.1 outgoing_grad.3
  286.6 13.8 %all-to-all-done.13.d_edge_a = bf16[32,2,2,16,128]{4,3,2,1,0:T(8,128)(2,1)S(1)} async-done(((bf16[32,2,2,16,128]{4,3,2,1,0:T(8,128)(2,1)}), bf16[32,2,2,16,128]{4,3,2,1,0:T(8,128)(2,1)S(1)}, u32[]{:S(2)}, u32[]{:S(2)}) %all-to-all-start.13) | async-done | bytes 524320 | tf_op jit(solution)/shard_map/all_to_all | solution.py:393
  300.4 3.5 all-to-all-start.15
  304.0 1.0 reduce_sum.21
  305.0 14.0 %all-to-all-done.15.d_edge_b = bf16[32,2,2,16,128]{4,3,2,1,0:T(8,128)(2,1)S(1)} async-done(((bf16[32,2,2,16,128]{4,3,2,1,0:T(8,128)(2,1)}), bf16[32,2,2,16,128]{4,3,2,1,0:T(8,128)(2,1)S(1)}, u32[]{:S(2)}, u32[]{:S(2)}) %all-to-all-start.15) | async-done | bytes 524320 | tf_op jit(solution)/shard_map/all_to_all | solution.py:393
  319.0 1.2 copy-done.28
  320.2 7.3 %finish.1 = (bf16[16,128,128]{2,1,0:T(8,128)(2,1)}, bf16[16,512,128]{2,1,0:T(8,128)(2,1)S(1)}, f32[2,128]{1,0:T(2,128)S(1)}) custom-call(s32[1]{0:T(128)S(6)} %copy.21.lengths, bf16[32,2,2,16,128]{4,3,2,1,0:T(8,128)(2,1)S(1)} %all-to-all-done.13.d_edge_a, bf16[32,2,2,16,128]{4,3,2,1,0:T(8,128)(2,1)S(1)} %all-to-all-done.15.d_edge_b, ...), custom_call_target="tpu_custom_call" | custom-call | flops 603979776 | bytes 6621188 | tf_op jit(solution)/shard_map/finish/pallas_call | solution.py:379
  328.4 18.4 %all_to_all.102 = bf16[32,64,128]{2,1,0:T(8,128)(2,1)S(1)} all-to-all(bf16[32,64,128]{2,1,0:T(8,128)(2,1)S(1)} %pad_maximum_fusion), channel_id=1, replica_groups=mesh['grp'=1,'row'=16,'col'=2,'ch'=1] {'row','col'}, dimensions={0} | all-to-all | bytes 1048576 | tf_op jit(solution)/shard_map/all_to_all | solution.py:393
  348.2 3.6 %all-to-all-start.18 = ((bf16[32,16,128]{2,1,0:T(8,128)(2,1)}), bf16[32,16,128]{2,1,0:T(8,128)(2,1)S(1)}, u32[]{:S(2)}, u32[]{:S(2)}) async-start(bf16[32,16,128]{2,1,0:T(8,128)(2,1)} %broadcast_in_dim.5), calls=%async_computation.18 | async-start | bytes 262144 | tf_op jit(solution)/shard_map/all_to_all | solution.py:393
  352.6 7.8 %all-to-all-done.18 = bf16[32,16,128]{2,1,0:T(8,128)(2,1)S(1)} async-done(((bf16[32,16,128]{2,1,0:T(8,128)(2,1)}), bf16[32,16,128]{2,1,0:T(8,128)(2,1)S(1)}, u32[]{:S(2)}, u32[]{:S(2)}) %all-to-all-start.18) | async-done | bytes 131104 | tf_op jit(solution)/shard_map/all_to_all | solution.py:393
  360.4 0.8 pad_maximum_fusion.2
  (110 shorter events, 13.2 us)
Async XLA Ops:
  1.3 1.0 copy-start.4
  2.3 0.9 copy-start.19
  3.2 0.9 copy-start.21
  4.1 0.7 copy-start.48
  32.2 45.8 %copy-start.5 = (bf16[16,128,128]{2,1,0:T(8,128)(2,1)S(1)}, bf16[16,128,128]{2,1,0:T(8,128)(2,1)}, u32[]{:S(2)}) copy-start(bf16[16,128,128]{2,1,0:T(8,128)(2,1)} %pair.5) | copy-start | bytes 1572868
  32.2 45.8 %copy-start.20 = (bf16[2,2,128,128]{3,2,1,0:T(8,128)(2,1)S(1)}, bf16[2,2,128,128]{3,2,1,0:T(8,128)(2,1)}, u32[]{:S(2)}) copy-start(bf16[2,2,128,128]{3,2,1,0:T(8,128)(2,1)} %proj_w.7) | copy-start | bytes 393220
  32.2 45.8 %copy-start.22 = (bf16[2,2,128,128]{3,2,1,0:T(8,128)(2,1)S(1)}, bf16[2,2,128,128]{3,2,1,0:T(8,128)(2,1)}, u32[]{:S(2)}) copy-start(bf16[2,2,128,128]{3,2,1,0:T(8,128)(2,1)} %gate_w.7) | copy-start | bytes 393220
  32.2 45.8 %copy-start.24 = (bf16[2,128,128]{2,1,0:T(8,128)(2,1)S(1)}, bf16[2,128,128]{2,1,0:T(8,128)(2,1)}, u32[]{:S(2)}) copy-start(bf16[2,128,128]{2,1,0:T(8,128)(2,1)} %outgate_w.7) | copy-start | bytes 196612
  32.2 45.8 %copy-start.32 = (bf16[2,128,128]{2,1,0:T(8,128)(2,1)S(1)}, bf16[2,128,128]{2,1,0:T(8,128)(2,1)}, u32[]{:S(2)}) copy-start(bf16[2,128,128]{2,1,0:T(8,128)(2,1)} %out_w.5) | copy-start | bytes 196612
  32.2 45.8 %copy-start.46 = (f32[2,128]{1,0:T(2,128)S(1)}, f32[2,128]{1,0:T(2,128)}, u32[]{:S(2)}) copy-start(f32[2,128]{1,0:T(2,128)} %mgain.5) | copy-start | bytes 3076
  32.2 45.8 %copy-start.47 = (f32[2,128]{1,0:T(2,128)S(1)}, f32[2,128]{1,0:T(2,128)}, u32[]{:S(2)}) copy-start(f32[2,128]{1,0:T(2,128)} %mbias.5) | copy-start | bytes 3076
  32.2 45.8 %copy-start.49 = (f32[2,128]{1,0:T(2,128)S(1)}, f32[2,128]{1,0:T(2,128)}, u32[]{:S(2)}) copy-start(f32[2,128]{1,0:T(2,128)} %ngain.7) | copy-start | bytes 3076
  32.3 45.8 %copy-start.53 = (f32[2,128]{1,0:T(2,128)S(1)}, f32[2,128]{1,0:T(2,128)}, u32[]{:S(2)}) copy-start(f32[2,128]{1,0:T(2,128)} %nbias.3) | copy-start | bytes 3076
  32.3 18.6 %all-to-all-start = ((bf16[32,2,2,16,128]{4,3,2,1,0:T(8,128)(2,1)}), bf16[32,2,2,16,128]{4,3,2,1,0:T(8,128)(2,1)S(1)}, u32[]{:S(2)}, u32[]{:S(2)}) async-start(bf16[32,2,2,16,128]{4,3,2,1,0:T(8,128)(2,1)} %get-tuple-element.35), calls=%async_computation | async-start | bytes 1048576 | tf_op jit(solution)/shard_map/all_to_all | solution.py:393
  50.9 14.3 %all-to-all-start.3 = ((bf16[32,2,16,128]{3,2,1,0:T(8,128)(2,1)}), bf16[32,2,16,128]{3,2,1,0:T(8,128)(2,1)S(1)}, u32[]{:S(2)}, u32[]{:S(2)}) async-start(bf16[32,2,16,128]{3,2,1,0:T(8,128)(2,1)} %bitcast.3), calls=%async_computation.3 | async-start | bytes 524288 | tf_op jit(solution)/shard_map/all_to_all | solution.py:393
  78.0 5.4 %copy-start = (bf16[32,2,16,128]{3,2,1,0:T(8,128)(2,1)}, bf16[32,2,16,128]{3,2,1,0:T(8,128)(2,1)S(1)}, u32[]{:S(2)}) copy-start(bf16[32,2,16,128]{3,2,1,0:T(8,128)(2,1)S(1)} %all_to_all.96.tri_a) | copy-start | bytes 786436
  83.4 0.8 copy-start.7
  84.3 17.1 %copy-start.35 = (bf16[32,2,2,16,128]{4,3,2,1,0:T(8,128)(2,1)}, bf16[32,2,2,16,128]{4,3,2,1,0:T(8,128)(2,1)S(1)}, u32[]{:S(2)}) copy-start(bf16[32,2,2,16,128]{4,3,2,1,0:T(8,128)(2,1)S(1)} %get-tuple-element.38) | copy-start | bytes 1572868
  101.4 18.6 %all-to-all-start.4 = ((bf16[32,2,2,16,128]{4,3,2,1,0:T(8,128)(2,1)}), bf16[32,2,2,16,128]{4,3,2,1,0:T(8,128)(2,1)S(1)}, u32[]{:S(2)}, u32[]{:S(2)}) async-start(bf16[32,2,2,16,128]{4,3,2,1,0:T(8,128)(2,1)} %copy-done.35), calls=%async_computation.4 | async-start | bytes 1048576 | tf_op jit(solution)/shard_map/all_to_all | solution.py:393
  105.3 0.7 copy-start.29
  120.0 14.4 %all-to-all-start.7 = ((bf16[32,2,16,128]{3,2,1,0:T(8,128)(2,1)}), bf16[32,2,16,128]{3,2,1,0:T(8,128)(2,1)}, u32[]{:S(2)}, u32[]{:S(2)}) async-start(bf16[32,2,16,128]{3,2,1,0:T(8,128)(2,1)} %bitcast.43), calls=%async_computation.7 | async-start | bytes 524288 | tf_op jit(solution)/shard_map/all_to_all | solution.py:393
  124.0 0.7 copy-start.31
  147.7 1.0 copy-start.2
  148.7 1.0 copy-start.8
  149.8 0.8 copy-start.25
  150.6 0.8 copy-start.33
  157.9 0.8 copy-start.14
  158.7 0.8 copy-start.36
  159.6 0.8 copy-start.38
  160.4 13.1 %copy-start.45 = (bf16[32,2,16,128]{3,2,1,0:T(8,128)(2,1)}, bf16[32,2,16,128]{3,2,1,0:T(8,128)(2,1)S(1)}, u32[]{:S(2)}) copy-start(bf16[32,2,16,128]{3,2,1,0:T(8,128)(2,1)S(1)} %get-tuple-element.44) | copy-start | bytes 786436
  173.5 14.0 %all-to-all-start.10 = ((bf16[32,2,16,128]{3,2,1,0:T(8,128)(2,1)}), bf16[32,2,16,128]{3,2,1,0:T(8,128)(2,1)}, u32[]{:S(2)}, u32[]{:S(2)}) async-start(bf16[32,2,16,128]{3,2,1,0:T(8,128)(2,1)} %copy-done.45), calls=%async_computation.10 | async-start | bytes 524288 | tf_op jit(solution)/shard_map/all_to_all | solution.py:393
  176.8 1.0 copy-start.30
  178.0 0.8 copy-start.17
  178.8 45.5 %copy-start.1 = (bf16[32,2,16,128]{3,2,1,0:T(8,128)(2,1)S(1)}, bf16[32,2,16,128]{3,2,1,0:T(8,128)(2,1)}, u32[]{:S(2)}) copy-start(bf16[32,2,16,128]{3,2,1,0:T(8,128)(2,1)} %copy-done) | copy-start | bytes 786436
  178.8 45.5 %copy-start.23 = (bf16[2,2,128,128]{3,2,1,0:T(8,128)(2,1)S(1)}, bf16[2,2,128,128]{3,2,1,0:T(8,128)(2,1)}, u32[]{:S(2)}) copy-start(bf16[2,2,128,128]{3,2,1,0:T(8,128)(2,1)} %gate_w.7) | copy-start | bytes 393220
  178.8 45.5 %copy-start.26 = (bf16[2,128,128]{2,1,0:T(8,128)(2,1)S(1)}, bf16[2,128,128]{2,1,0:T(8,128)(2,1)}, u32[]{:S(2)}) copy-start(bf16[2,128,128]{2,1,0:T(8,128)(2,1)} %outgate_w.7) | copy-start | bytes 196612
  178.8 45.5 %copy-start.34 = (bf16[2,128,128]{2,1,0:T(8,128)(2,1)S(1)}, bf16[2,128,128]{2,1,0:T(8,128)(2,1)}, u32[]{:S(2)}) copy-start(bf16[2,128,128]{2,1,0:T(8,128)(2,1)} %out_w.5) | copy-start | bytes 196612
  187.4 18.3 %all-to-all-start.9 = ((bf16[32,2,2,16,128]{4,3,2,1,0:T(8,128)(2,1)}), bf16[32,2,2,16,128]{4,3,2,1,0:T(8,128)(2,1)}, u32[]{:S(2)}, u32[]{:S(2)}) async-start(bf16[32,2,2,16,128]{4,3,2,1,0:T(8,128)(2,1)} %bitcast.39), calls=%async_computation.9 | async-start | bytes 1048576 | tf_op jit(solution)/shard_map/all_to_all | solution.py:393
  192.0 0.8 copy-start.18
  224.3 1.0 copy-start.3
  225.3 1.0 copy-start.9
  226.4 1.0 copy-start.15
  236.7 1.3 copy-start.10
  238.1 0.8 copy-start.12
  238.9 1.0 copy-start.27
  239.9 0.8 copy-start.40
  240.7 0.8 copy-start.42
  241.5 14.1 %copy-start.44 = (bf16[32,2,16,128]{3,2,1,0:T(8,128)(2,1)}, bf16[32,2,16,128]{3,2,1,0:T(8,128)(2,1)S(1)}, u32[]{:S(2)}) copy-start(bf16[32,2,16,128]{3,2,1,0:T(8,128)(2,1)S(1)} %get-tuple-element.47) | copy-start | bytes 786436
  241.5 14.1 %copy-start.50 = (f32[4,128]{1,0:T(4,128)}, f32[4,128]{1,0:T(4,128)S(1)}, u32[]{:S(2)}) copy-start(f32[4,128]{1,0:T(4,128)S(1)} %get-tuple-element.53) | copy-start | bytes 6148
  241.5 20.3 %copy-start.13 = (bf16[16,128,128]{2,1,0:T(8,128)(2,1)S(1)}, bf16[16,128,128]{2,1,0:T(8,128)(2,1)}, u32[]{:S(2)}) copy-start(bf16[16,128,128]{2,1,0:T(8,128)(2,1)} %copy-done.12) | copy-start | bytes 1572868
  255.6 13.3 %all-to-all-start.14 = ((bf16[32,2,16,128]{3,2,1,0:T(8,128)(2,1)}), bf16[32,2,16,128]{3,2,1,0:T(8,128)(2,1)S(1)}, u32[]{:S(2)}, u32[]{:S(2)}) async-start(bf16[32,2,16,128]{3,2,1,0:T(8,128)(2,1)} %copy-done.44), calls=%async_computation.14 | async-start | bytes 524288 | tf_op jit(solution)/shard_map/all_to_all | solution.py:393
  258.2 1.0 copy-start.16
  259.2 1.0 copy-start.37
  260.3 1.0 copy-start.39
  261.3 3.2 copy-start.11
  261.7 1.2 copy-start.41
  263.0 1.0 copy-start.43
  268.9 14.0 %all-to-all-start.16 = ((bf16[32,32,128]{2,1,0:T(8,128)(2,1)}), bf16[32,32,128]{2,1,0:T(8,128)(2,1)}, u32[]{:S(2)}, u32[]{:S(2)}) async-start(bf16[32,32,128]{2,1,0:T(8,128)(2,1)} %bitcast.17), calls=%async_computation.16 | async-start | bytes 524288 | tf_op jit(solution)/shard_map/all_to_all | solution.py:393
  272.2 31.8 %copy-start.51 = (f32[4,128]{1,0:T(4,128)S(1)}, f32[4,128]{1,0:T(4,128)}, u32[]{:S(2)}) copy-start(f32[4,128]{1,0:T(4,128)} %copy-done.50) | copy-start | bytes 6148
  273.3 45.7 %copy-start.6 = (bf16[16,128,128]{2,1,0:T(8,128)(2,1)S(1)}, bf16[16,128,128]{2,1,0:T(8,128)(2,1)}, u32[]{:S(2)}) copy-start(bf16[16,128,128]{2,1,0:T(8,128)(2,1)} %pair.5) | copy-start | bytes 1572868
  282.8 17.6 %all-to-all-start.13 = ((bf16[32,2,2,16,128]{4,3,2,1,0:T(8,128)(2,1)}), bf16[32,2,2,16,128]{4,3,2,1,0:T(8,128)(2,1)S(1)}, u32[]{:S(2)}, u32[]{:S(2)}) async-start(bf16[32,2,2,16,128]{4,3,2,1,0:T(8,128)(2,1)} %bitcast.13), calls=%async_computation.13 | async-start | bytes 1048576 | tf_op jit(solution)/shard_map/all_to_all | solution.py:393
  300.4 18.6 %all-to-all-start.15 = ((bf16[32,2,2,16,128]{4,3,2,1,0:T(8,128)(2,1)}), bf16[32,2,2,16,128]{4,3,2,1,0:T(8,128)(2,1)S(1)}, u32[]{:S(2)}, u32[]{:S(2)}) async-start(bf16[32,2,2,16,128]{4,3,2,1,0:T(8,128)(2,1)} %bitcast.15), calls=%async_computation.15 | async-start | bytes 1048576 | tf_op jit(solution)/shard_map/all_to_all | solution.py:393
  319.0 1.2 copy-start.28
  348.2 12.3 %all-to-all-start.18 = ((bf16[32,16,128]{2,1,0:T(8,128)(2,1)}), bf16[32,16,128]{2,1,0:T(8,128)(2,1)S(1)}, u32[]{:S(2)}, u32[]{:S(2)}) async-start(bf16[32,16,128]{2,1,0:T(8,128)(2,1)} %broadcast_in_dim.5), calls=%async_computation.18 | async-start | bytes 262144 | tf_op jit(solution)/shard_map/all_to_all | solution.py:393
  (1 other events, 0.7 us)

commit v3 on v0

--- a/solution.py
+++ b/solution.py
@@ -1,6 +1,10 @@
+import functools
+
 import jax
 import jax.numpy as jnp
 from jax import lax
+from jax.experimental import pallas as pl
+from jax.experimental.pallas import tpu as pltpu
 from jax.sharding import PartitionSpec as P
 
 H = 128
@@ -11,6 +15,645 @@
 
 def product(spec, left, right):
     return jnp.einsum(spec, left, right, preferred_element_type=jnp.float32)
+
+
+F32 = jnp.float32
+BF16 = jnp.bfloat16
+
+
+def dot(left, right):
+    return lax.dot_general(left, right, (((1,), (0,)), ((), ())), preferred_element_type=F32)
+
+
+def dot_rt(left, right):
+    return lax.dot_general(left, right, (((1,), (1,)), ((), ())), preferred_element_type=F32)
+
+
+def dot_lt(left, right):
+    return lax.dot_general(left, right, (((0,), (0,)), ((), ())), preferred_element_type=F32)
+
+
+def sigmoid(values):
+    return 1.0 / (1.0 + jnp.exp(-values))
+
+
+def norm_rows(values):
+    scale = 1.0 / values.shape[0]
+    average = jnp.sum(values, 0, keepdims=True) * scale
+    centred = values - average
+    variance = jnp.sum(centred * centred, 0, keepdims=True) * scale
+    inverse = lax.rsqrt(variance + EPS)
+    return centred * inverse, inverse
+
+
+def turned(weight):
+    return jnp.transpose(weight.astype(F32)).astype(BF16)
+
+
+def column(ref, module, lanes):
+    row = ref[module : module + 1, :]
+    return jnp.transpose(jnp.broadcast_to(row, (lanes, row.shape[1])))
+
+
+def as_row(total):
+    return jnp.sum(jnp.transpose(total), 0, keepdims=True)
+
+
+def row_mask(lengths_ref, step, rows, lanes):
+    limit = lengths_ref[0]
+    row_id = lax.axis_index("row") * rows + step
+    col_id = lax.axis_index("col") * lanes + lax.broadcasted_iota(jnp.int32, (1, lanes), 1)
+    return jnp.where((row_id < limit) & (col_id < limit), 1.0, 0.0).astype(F32)
+
+
+def load_in_weights(proj_ref, gate_ref, module, scratch):
+    width = proj_ref.shape[-1]
+    for side in range(2):
+        scratch[side * width : (side + 1) * width, :] = turned(proj_ref[module, side])
+        scratch[(2 + side) * width : (3 + side) * width, :] = turned(gate_ref[module, side])
+
+
+def put_rows(scratch, values, step, rows):
+    scratch[pl.ds(step, values.shape[0], stride=rows), :] = values
+
+
+def get_rows(scratch, step, channels, rows):
+    return scratch[pl.ds(step, channels, stride=rows), :]
+
+
+def spread_edges(scratch, out_ref):
+    shards, sides, group, rows, lanes = out_ref.shape
+    block = shards * group * rows
+    for side in range(sides):
+        part = scratch[side * block : (side + 1) * block, :]
+        out_ref[:, side] = part.reshape(shards, group, rows, lanes).astype(BF16)
+
+
+def collect_edges(in_ref, scratch):
+    shards, sides, group, rows, lanes = in_ref.shape
+    block = shards * group * rows
+    for side in range(sides):
+        scratch[side * block : (side + 1) * block, :] = (
+            in_ref[:, side].astype(F32).reshape(block, lanes)
+        )
+
+
+def collect_triangle(in_ref, scratch):
+    block = in_ref.size // in_ref.shape[-1]
+    scratch[0:block, :] = in_ref[...].astype(F32).reshape(block, in_ref.shape[-1])
+
+
+def each_row(rows, unroll, body):
+    def step_body(step, carry):
+        body(step)
+        return carry
+
+    lax.fori_loop(0, rows, step_body, 0, unroll=unroll)
+
+
+def mid_norm(tri):
+    scale = 1.0 / tri.shape[0]
+    average = jnp.sum(tri, 0, keepdims=True) * scale
+    squares = jnp.sum(tri * tri, 0, keepdims=True) * scale
+    inverse = lax.rsqrt(squares - average * average + EPS)
+    return (tri - average) * inverse, inverse
+
+
+def norm_backward(weighted, scaled, inverse):
+    scale = 1.0 / weighted.shape[0]
+    first = jnp.sum(weighted, 0, keepdims=True) * scale
+    second = jnp.sum(weighted * scaled, 0, keepdims=True) * scale
+    return inverse * (weighted - first - scaled * second)
+
+
+def edges(normed, in_weights, mask):
+    pre = dot(in_weights, normed)
+    half = pre.shape[0] // 2
+    return pre[:half] * sigmoid(pre[half:]) * mask
+
+
+def start_kernel(
+    lengths, pair_far, ngain_far, nbias_far, proj_far, gate_far,
+    edge_out, normed_out, pair, ngain, nbias, proj_w, gate_w, sems, wts, scr,
+):
+    far = (proj_far.at[0], gate_far.at[0], ngain_far, nbias_far, pair_far)
+    near = (proj_w.at[0], gate_w.at[0], ngain, nbias, pair)
+    copies = [
+        pltpu.make_async_copy(source, target, sems.at[index])
+        for index, (source, target) in enumerate(zip(far, near))
+    ]
+    for copy in copies:
+        copy.start()
+    for copy in copies:
+        copy.wait()
+    rows, lanes, channels = pair.shape
+    load_in_weights(proj_w, gate_w, 0, wts)
+    gain, bias = column(ngain, 0, lanes), column(nbias, 0, lanes)
+
+    def body(step):
+        scaled, _ = norm_rows(jnp.transpose(pair[step].astype(F32)))
+        normed = (scaled * gain + bias).astype(BF16)
+        normed_out[step] = normed
+        put_rows(scr, edges(normed, wts[...], row_mask(lengths, step, rows, lanes)), step, rows)
+
+    each_row(rows, 4, body)
+    spread_edges(scr, edge_out)
+
+
+def out_gate_kernel(pair, normed, outgate_w, pair_out, gate_out):
+    outgate_t = turned(outgate_w[0])
+
+    def body(step):
+        pair_out[step] = jnp.transpose(pair[step].astype(F32)).astype(BF16)
+        gate_out[step] = sigmoid(dot(outgate_t, normed[step]))
+
+    each_row(pair.shape[0], 2, body)
+
+
+def between_kernel(
+    lengths, tri, pair_t, outgate, ngain, nbias, mgain, mbias, out_w, proj_w, gate_w,
+    edge_out, mid_out, normed_out, scaled_mid_out, inverse_mid_out, wts, scr,
+):
+    rows, channels, lanes = pair_t.shape
+    load_in_weights(proj_w, gate_w, 1, wts)
+    out_t = turned(out_w[0])
+    gain, bias = column(ngain, 1, lanes), column(nbias, 1, lanes)
+    gain_mid, bias_mid = column(mgain, 0, lanes), column(mbias, 0, lanes)
+    collect_triangle(tri, scr)
+
+    def body(step):
+        scaled_mid, inverse_mid = mid_norm(get_rows(scr, step, channels, rows))
+        scaled_mid_out[step] = scaled_mid
+        inverse_mid_out[pl.ds(step, 1), :] = inverse_mid
+        unit = (scaled_mid * gain_mid + bias_mid).astype(BF16)
+        outer = dot(out_t, unit)
+        mid = (pair_t[step].astype(F32) + outer * outgate[step]).astype(BF16)
+        mid_out[step] = mid
+        scaled, _ = norm_rows(mid.astype(F32))
+        normed = (scaled * gain + bias).astype(BF16)
+        normed_out[step] = normed
+        here = edges(normed, wts[...], row_mask(lengths, step, rows, lanes))
+        put_rows(scr, here, step, rows)
+
+    each_row(rows, 4, body)
+    spread_edges(scr, edge_out)
+
+
+def upstream_kernel(cot, normed, out_w, outgate_w, cot_out, gate_out, d_outer_out, d_unit_out):
+    outgate_t = turned(outgate_w[1])
+
+    def body(step):
+        grad = jnp.transpose(cot[step].astype(F32))
+        outgate = sigmoid(dot(outgate_t, normed[step]))
+        d_outer = (grad * outgate).astype(BF16)
+        cot_out[step] = grad
+        gate_out[step] = outgate
+        d_outer_out[step] = d_outer
+        d_unit_out[step] = dot(out_w[1], d_outer)
+
+    each_row(cot.shape[0], 2, body)
+
+
+def turn_kernel(tri, d_unit, mgain, d_tri_out, scr):
+    rows, channels, lanes = d_unit.shape
+    gain_mid = column(mgain, 1, lanes)
+    collect_triangle(tri, scr)
+
+    def body(step):
+        scaled_mid, inverse_mid = mid_norm(get_rows(scr, step, channels, rows))
+        put_rows(scr, norm_backward(d_unit[step] * gain_mid, scaled_mid, inverse_mid), step, rows)
+
+    each_row(rows, 4, body)
+    d_tri_out[...] = scr[...].reshape(d_tri_out.shape).astype(BF16)
+
+
+def out_weight_grads(unit, d_outer, normed, d_gatepre, out_ref):
+    width = unit.shape[0]
+    out_ref[0:width, :] = dot_rt(unit[...], d_outer[...]).astype(out_ref.dtype)
+    out_ref[width:, :] = dot_rt(normed[...], d_gatepre[...]).astype(out_ref.dtype)
+
+
+def lane_block(step, lanes):
+    return pl.ds(pl.multiple_of(step * lanes, lanes), lanes)
+
+
+def behind_turn_kernel(
+    tri, mid, normed, outgate, grad, d_outer, d_unit, mgain, mbias, out_w, outgate_w,
+    new_out, d_normed_out, weights_out, small_out, scr, unit_all, outer_all, normed_all, gate_all,
+    sums,
+):
+    rows, channels, lanes = mid.shape
+    out_t = turned(out_w[1])
+    gain_mid, bias_mid = column(mgain, 1, lanes), column(mbias, 1, lanes)
+    collect_triangle(tri, scr)
+    sums[...] = jnp.zeros_like(sums)
+
+    def body(step):
+        here = lane_block(step, lanes)
+        scaled_mid, _ = mid_norm(get_rows(scr, step, channels, rows))
+        unit = (scaled_mid * gain_mid + bias_mid).astype(BF16)
+        outer = dot(out_t, unit)
+        gate = outgate[step]
+        update = outer * gate
+        new_out[step] = jnp.transpose(mid[step].astype(F32) + update).astype(BF16)
+        d_gatepre = (grad[step] * update * (1.0 - gate)).astype(BF16)
+        d_normed_out[step] = dot(outgate_w[1], d_gatepre)
+        unit_all[:, here] = unit
+        outer_all[:, here] = d_outer[step]
+        normed_all[:, here] = normed[step]
+        gate_all[:, here] = d_gatepre
+        sums[0] += d_unit[step] * scaled_mid
+        sums[1] += d_unit[step]
+
+    each_row(rows, 2, body)
+    out_weight_grads(unit_all, outer_all, normed_all, gate_all, weights_out)
+    for index in range(2):
+        small_out[index : index + 1, :] = as_row(sums[index])
+
+
+def edge_factor_kernel(
+    module, lengths, base, normed, proj_w, gate_w,
+    proj_out, gate_out, scaled_out, inverse_out, wts,
+):
+    rows, channels, lanes = base.shape
+    load_in_weights(proj_w, gate_w, module, wts)
+
+    def body(step):
+        pre = dot(wts[...], normed[step])
+        half = pre.shape[0] // 2
+        gating = sigmoid(pre[half:])
+        factor = gating * row_mask(lengths, step, rows, lanes)
+        proj_out[step] = factor
+        gate_out[step] = factor * pre[:half] * (1.0 - gating)
+        scaled, inverse = norm_rows(base[step].astype(F32))
+        scaled_out[step] = scaled
+        inverse_out[pl.ds(step, 1), :] = inverse
+
+    each_row(rows, 2, body)
+
+
+def in_normed(d_in, all_w, proj_w, gate_w):
+    width = proj_w.shape[-1]
+    total = all_w
+    for side in range(2):
+        total = total + dot(proj_w[side], d_in[side * width : (side + 1) * width])
+        total = total + dot(gate_w[side], d_in[(2 + side) * width : (3 + side) * width])
+    return total
+
+
+def middle_kernel(
+    d_edge, proj_factor, gate_factor, d_normed_gate, scaled_in, inverse_in, cot, outgate,
+    scaled_mid, inverse_mid, ngain, mgain, proj_w, gate_w, out_w,
+    d_tri_out, grad_out, d_in_out, d_normed_out, d_unit_out, scr, scr_tri,
+):
+    rows, channels, lanes = cot.shape
+    gain, gain_mid = column(ngain, 1, lanes), column(mgain, 0, lanes)
+    collect_edges(d_edge, scr)
+    half = proj_factor.shape[1]
+
+    def body(step):
+        here = get_rows(scr, step, half, rows)
+        d_proj = (here * proj_factor[step]).astype(BF16)
+        d_gate = (here * gate_factor[step]).astype(BF16)
+        d_in = jnp.concatenate([d_proj, d_gate], axis=0)
+        d_in_out[step] = d_in
+        d_normed = in_normed(d_in, d_normed_gate[step], proj_w[1], gate_w[1])
+        d_normed_out[step] = d_normed
+        grad = cot[step] + norm_backward(
+            d_normed * gain, scaled_in[step], inverse_in[pl.ds(step, 1), :]
+        )
+        grad_out[step] = grad
+        d_unit = dot(out_w[0], (grad * outgate[step]).astype(BF16))
+        d_unit_out[step] = d_unit
+        d_tri = norm_backward(d_unit * gain_mid, scaled_mid[step], inverse_mid[pl.ds(step, 1), :])
+        put_rows(scr_tri, d_tri, step, rows)
+
+    each_row(rows, 4, body)
+    d_tri_out[...] = scr_tri[...].reshape(d_tri_out.shape).astype(BF16)
+
+
+def behind_middle_kernel(
+    grad, outgate, scaled_mid, d_unit, normed0, d_in1, normed1, d_normed1, scaled1,
+    mgain, mbias, out_w, outgate_w,
+    d_normed_out, out_weights, in_weights, small_out,
+    unit_all, outer_all, normed_all, gate_all, upper_all, d_in_all, sums,
+):
+    rows, channels, lanes = grad.shape
+    out_t = turned(out_w[0])
+    gain_mid, bias_mid = column(mgain, 0, lanes), column(mbias, 0, lanes)
+    sums[...] = jnp.zeros_like(sums)
+
+    def body(step):
+        here = lane_block(step, lanes)
+        scaled = scaled_mid[step]
+        unit = (scaled * gain_mid + bias_mid).astype(BF16)
+        outer = dot(out_t, unit)
+        gate = outgate[step]
+        gated = grad[step] * gate
+        d_gatepre = (gated * outer * (1.0 - gate)).astype(BF16)
+        d_normed_out[step] = dot(outgate_w[0], d_gatepre)
+        unit_all[:, here] = unit
+        outer_all[:, here] = gated.astype(BF16)
+        normed_all[:, here] = normed0[step]
+        gate_all[:, here] = d_gatepre
+        upper_all[:, here] = normed1[step]
+        d_in_all[:, here] = d_in1[step]
+        sums[0] += d_unit[step] * scaled
+        sums[1] += d_unit[step]
+        sums[2] += d_normed1[step] * scaled1[step]
+        sums[3] += d_normed1[step]
+
+    each_row(rows, 2, body)
+    out_weight_grads(unit_all, outer_all, normed_all, gate_all, out_weights)
+    in_weight_grads(upper_all, d_in_all, in_weights)
+    for index in range(4):
+        small_out[index : index + 1, :] = as_row(sums[index])
+
+
+def in_weight_grads(normed_all, d_in_all, out_ref):
+    width = normed_all.shape[0]
+    for part in range(d_in_all.shape[0] // width):
+        block = slice(part * width, (part + 1) * width)
+        out_ref[block, :] = dot_rt(normed_all[...], d_in_all[block, :]).astype(out_ref.dtype)
+
+
+def finish_kernel(
+    d_edge, proj_factor, gate_factor, normed, out0, in1, out1,
+    packed_out, d_in_out, scr, normed_all, d_in_all,
+):
+    rows, half, lanes = proj_factor.shape
+    collect_edges(d_edge, scr)
+
+    def body(step):
+        place = lane_block(step, lanes)
+        here = get_rows(scr, step, half, rows)
+        d_proj = (here * proj_factor[step]).astype(BF16)
+        d_gate = (here * gate_factor[step]).astype(BF16)
+        d_in_out[step, 0:half] = d_proj
+        d_in_out[step, half:] = d_gate
+        d_in_all[0:half, place] = d_proj
+        d_in_all[half:, place] = d_gate
+        normed_all[:, place] = normed[step]
+
+    each_row(rows, 4, body)
+    first, second, third = d_in_all.shape[0], out0.shape[0], in1.shape[0]
+    in_weight_grads(normed_all, d_in_all, packed_out.at[0:first])
+    packed_out[first : first + second, :] = out0[...]
+    packed_out[first + second : first + second + third, :] = in1[...]
+    packed_out[first + second + third :, :] = out1[...]
+
+
+def behind_finish_kernel(
+    d_in, d_normed_gate, grad, scaled_in, inverse_in, ngain, proj_w, gate_w,
+    grad_out, small_out, sums,
+):
+    rows, channels, lanes = grad.shape
+    gain = column(ngain, 0, lanes)
+    sums[...] = jnp.zeros_like(sums)
+
+    def body(step):
+        d_normed = in_normed(d_in[step], d_normed_gate[step], proj_w[0], gate_w[0])
+        scaled = scaled_in[step]
+        sums[0] += d_normed * scaled
+        sums[1] += d_normed
+        total = grad[step] + norm_backward(d_normed * gain, scaled, inverse_in[pl.ds(step, 1), :])
+        grad_out[step] = jnp.transpose(total).astype(BF16)
+
+    each_row(rows, 2, body)
+    for index in range(2):
+        small_out[index : index + 1, :] = as_row(sums[index])
+
+
+def sum_kernel(parts, small0, small_middle, small1, shared_out):
+    shards, share, width = parts.shape
+    own = jnp.sum(parts[...].astype(F32), axis=0).astype(BF16)
+    small = jnp.concatenate(
+        [small0[...], small_middle[0:2], small_middle[2:4], small1[...]], axis=0
+    )
+    high = small.astype(BF16).astype(F32)
+    extra = jnp.concatenate([high, small - high], axis=0).astype(BF16)
+    for shard in range(shards):
+        shared_out[shard, 0:share] = own
+        shared_out[shard, share:] = extra
+
+
+def unpack_kernel(share, shared, proj_out, gate_out, out_out, outgate_out, small_out):
+    shards, _, width = shared.shape
+    total = jnp.sum(shared[:, share:, :].astype(F32), axis=0)
+    small_out[...] = total[0:8] + total[8:16]
+    weights = shared[:, 0:share, :].reshape(shards * share, width).astype(F32)
+    for module in range(2):
+        blocks = [
+            weights[(6 * module + part) * width : (6 * module + part + 1) * width]
+            for part in range(6)
+        ]
+        for side in range(2):
+            proj_out[module, side] = blocks[side]
+            gate_out[module, side] = blocks[2 + side]
+        out_out[module] = blocks[4]
+        outgate_out[module] = blocks[5]
+
+
+def triangle_kernel(incoming, edge, tri_out):
+    many, few, _, group, rows, lanes = edge.shape
+
+    def whole(side, channel):
+        parts = [edge[:, c, side, channel].reshape(many * rows, lanes) for c in range(few)]
+        return jnp.concatenate(parts, axis=1)
+
+    for channel in range(group):
+        left, right = whole(0, channel), whole(1, channel)
+        tri = (dot_lt if incoming else dot_rt)(left, right).astype(BF16)
+        for c in range(few):
+            part = tri[:, c * lanes : (c + 1) * lanes]
+            tri_out[:, c, channel] = part.reshape(many, rows, lanes)
+
+
+def edge_grad_kernel(incoming, edge, d_tri, grad_out):
+    many, few, _, group, rows, lanes = edge.shape
+
+    def whole(ref, *index):
+        parts = [ref[(slice(None), c) + index].reshape(many * rows, lanes) for c in range(few)]
+        return jnp.concatenate(parts, axis=1)
+
+    for channel in range(group):
+        left, right = whole(edge, 0, channel), whole(edge, 1, channel)
+        grad = whole(d_tri, channel)
+        if incoming:
+            d_left, d_right = dot_rt(right, grad), dot(left, grad)
+        else:
+            d_left, d_right = dot(grad, right), dot_lt(grad, left)
+        for side, value in ((0, d_left), (1, d_right)):
+            value = value.astype(BF16)
+            for c in range(few):
+                part = value[:, c * lanes : (c + 1) * lanes]
+                grad_out[:, c, side, channel] = part.reshape(many, rows, lanes)
+
+
+SCALARS = pl.BlockSpec(memory_space=pltpu.SMEM)
+VECTORS = pl.BlockSpec(memory_space=pltpu.VMEM)
+FAR = pl.BlockSpec(memory_space=pltpu.HBM)
+
+
+def call(kernel, name, outs, args, scratch=(), flops=0, scalars=0, grant=16, far=False):
+    shapes = [jax.ShapeDtypeStruct(shape, dtype) for shape, dtype in outs]
+    moved = sum(a.size * a.dtype.itemsize for a in list(args) + shapes)
+    rest = FAR if far else VECTORS
+    return pl.pallas_call(
+        kernel,
+        name=name,
+        out_shape=shapes,
+        in_specs=[SCALARS] * scalars + [rest] * (len(args) - scalars),
+        out_specs=[VECTORS] * len(shapes),
+        scratch_shapes=[
+            pltpu.VMEM(*item) if isinstance(item, tuple) else item for item in scratch
+        ],
+        compiler_params=pltpu.CompilerParams(vmem_limit_bytes=grant * 1024 * 1024),
+        cost_estimate=pl.CostEstimate(flops=flops, bytes_accessed=moved, transcendentals=0),
+    )(*args)
+
+
+def exchange(values):
+    return lax.all_to_all(values, ("row", "col"), split_axis=0, concat_axis=0, tiled=True)
+
+
+def grouped_device(
+    pair, cotangent, lengths, ngain, nbias, proj_w, gate_w, mgain, mbias, out_w, outgate_w,
+    *, many, few,
+):
+    rows, lanes, channels = pair.shape
+    shards = many * few
+    group = H // shards
+    edge = ((shards, 2, group, rows, lanes), BF16)
+    grid = ((many, few, 2, group, rows, lanes), BF16)
+    tri = ((shards, group, rows, lanes), BF16)
+    tri_grid = ((many, few, group, rows, lanes), BF16)
+    tile = ((rows, channels, lanes), BF16)
+    wide = ((rows, channels, lanes), F32)
+    row = ((rows, lanes), F32)
+    factor = ((rows, 2 * H, lanes), F32)
+    d_in = ((rows, 4 * H, lanes), BF16)
+    wts = ((4 * H, channels), BF16)
+    big = ((2 * H * rows, lanes), F32)
+    mid = ((H * rows, lanes), F32)
+    positions = rows * lanes
+    flat = ((H, positions), BF16)
+    flat_in = ((4 * H, positions), BF16)
+    out_rows = ((2 * H, channels), BF16)
+    in_rows = ((4 * H, H), BF16)
+    triangle = 2 * group * (many * rows) ** 2 * (few * lanes)
+    dense = 2 * positions * channels * H
+
+    def sums(count):
+        return ((count, H, lanes), F32)
+
+    def small(count):
+        return ((count, H), F32)
+
+    sent, normed0 = call(
+        start_kernel, "start", [edge, tile], [lengths, pair, ngain, nbias, proj_w, gate_w],
+        [(pair.shape, BF16), (ngain.shape, F32), (nbias.shape, F32), (proj_w.shape, BF16),
+         (gate_w.shape, BF16), pltpu.SemaphoreType.DMA((5,)), wts, big],
+        4 * dense, 1, far=True,
+    )
+    edge0 = exchange(sent).reshape(grid[0])
+    pair_t, outgate0 = call(
+        out_gate_kernel, "out_gate", [tile, wide], [pair, normed0, outgate_w], (), dense,
+    )
+    (here,) = call(
+        functools.partial(triangle_kernel, False), "outgoing", [tri_grid], [edge0], (), triangle,
+    )
+    tri0 = exchange(here.reshape(tri[0]))
+    sent, mid_t, normed1, scaled_mid0, inverse_mid0 = call(
+        between_kernel, "between", [edge, tile, tile, wide, row],
+        [lengths, tri0, pair_t, outgate0, ngain, nbias, mgain, mbias, out_w, proj_w, gate_w],
+        [wts, big], 5 * dense, 1,
+    )
+    edge1 = exchange(sent).reshape(grid[0])
+    cot_t, outgate1, d_outer1, d_unit1 = call(
+        upstream_kernel, "upstream", [wide, wide, tile, wide],
+        [cotangent, normed1, out_w, outgate_w], (), 2 * dense,
+    )
+    (here,) = call(
+        functools.partial(triangle_kernel, True), "incoming", [tri_grid], [edge1], (), triangle,
+    )
+    tri1 = exchange(here.reshape(tri[0]))
+    (sent,) = call(turn_kernel, "turn", [tri], [tri1, d_unit1, mgain], [mid], dense)
+    d_tri1 = exchange(sent).reshape(tri_grid[0])
+    new_pair, d_normed_gate1, out_grads1, small1 = call(
+        behind_turn_kernel, "behind_turn", [(pair.shape, BF16), wide, out_rows, small(2)],
+        [tri1, mid_t, normed1, outgate1, cot_t, d_outer1, d_unit1, mgain, mbias, out_w, outgate_w],
+        [mid, flat, flat, flat, flat, sums(2)], 4 * dense,
+    )
+    (sent,) = call(
+        functools.partial(edge_grad_kernel, True), "incoming_grad", [grid], [edge1, d_tri1],
+        (), 2 * triangle,
+    )
+    d_edge1 = exchange(sent.reshape(edge[0]))
+    proj_factor1, gate_factor1, scaled1, inverse1 = call(
+        functools.partial(edge_factor_kernel, 1), "edge_factors_upper",
+        [factor, factor, wide, row], [lengths, mid_t, normed1, proj_w, gate_w], [wts],
+        4 * dense, 1,
+    )
+    sent, grad, d_in1, d_normed1, d_unit0 = call(
+        middle_kernel, "middle", [tri, wide, d_in, wide, wide],
+        [d_edge1, proj_factor1, gate_factor1, d_normed_gate1, scaled1, inverse1, cot_t, outgate0,
+         scaled_mid0, inverse_mid0, ngain, mgain, proj_w, gate_w, out_w],
+        [big, mid], 5 * dense, grant=24,
+    )
+    d_tri0 = exchange(sent).reshape(tri_grid[0])
+    d_normed_gate0, out_grads0, in_grads1, small_middle = call(
+        behind_middle_kernel, "behind_middle", [wide, out_rows, in_rows, small(4)],
+        [grad, outgate0, scaled_mid0, d_unit0, normed0, d_in1, normed1, d_normed1, scaled1,
+         mgain, mbias, out_w, outgate_w],
+        [flat, flat, flat, flat, flat, flat_in, sums(4)], 8 * dense, grant=24,
+    )
+    (sent,) = call(
+        functools.partial(edge_grad_kernel, False), "outgoing_grad", [grid], [edge0, d_tri0],
+        (), 2 * triangle,
+    )
+    d_edge0 = exchange(sent.reshape(edge[0]))
+    proj_factor0, gate_factor0, scaled0, inverse0 = call(
+        functools.partial(edge_factor_kernel, 0), "edge_factors_lower",
+        [factor, factor, wide, row], [lengths, pair_t, normed0, proj_w, gate_w], [wts],
+        4 * dense, 1,
+    )
+    share = 12 * H // shards
+    packed, d_in0 = call(
+        finish_kernel, "finish", [((12 * H, H), BF16), d_in],
+        [d_edge0, proj_factor0, gate_factor0, normed0, out_grads0, in_grads1, out_grads1],
+        [big, flat, flat_in], 4 * dense,
+    )
+    parts = exchange(packed.reshape(shards, share, H))
+    grad_pair, small0 = call(
+        behind_finish_kernel, "behind_finish", [(pair.shape, BF16), small(2)],
+        [d_in0, d_normed_gate0, grad, scaled0, inverse0, ngain, proj_w, gate_w], [sums(2)],
+        4 * dense,
+    )
+    (shared,) = call(
+        sum_kernel, "sum_weights", [((shards, share + 16, H), BF16)],
+        [parts, small0, small_middle, small1],
+    )
+    shared = exchange(shared)
+    grad_proj, grad_gate, grad_out, grad_outgate, small_all = call(
+        functools.partial(unpack_kernel, share), "unpack",
+        [(proj_w.shape, F32), (gate_w.shape, F32), (out_w.shape, F32), (outgate_w.shape, F32),
+         small(8)],
+        [shared],
+    )
+    small_all = small_all.reshape(2, 4, H)
+    return (
+        new_pair,
+        grad_pair,
+        small_all[:, 0],
+        small_all[:, 1],
+        grad_proj,
+        grad_gate,
+        small_all[:, 2],
+        small_all[:, 3],
+        grad_out,
+        grad_outgate,
+    )
 
 
 def norm_channels(values):
@@ -279,6 +922,11 @@
         P("grp", None, None),
         P("grp", None, None),
     )
+    many, few = mesh.shape["row"], mesh.shape["col"]
+    if mesh.shape["ch"] == 1 and H % (many * few) == 0:
+        body = functools.partial(grouped_device, many=many, few=few)
+    else:
+        body = per_device
     return jax.shard_map(
-        per_device, mesh=mesh, in_specs=in_specs, out_specs=out_specs, check_vma=False
-    )
+        body, mesh=mesh, in_specs=in_specs, out_specs=out_specs, check_vma=False
+    )

time: 629 us -> 291 us (0.46); the launches traced: 618 us -> 288 us
  waiting for transfers between devices: 229 us -> 35.2 us
  blocking collectives: 193 us -> 118 us
  Pallas kernels: 0 us -> 47.6 us
  matrix products: 43.1 us -> 0 us
  starting transfers between devices: 46.2 us -> 18.6 us
  other arithmetic: 27 us -> 0 us
  between operations: 16 us -> 1.79 us
    psum x1 -> x0, waiting for transfers between devices: 129 us -> none  [per_device(): lax.psum((lower[0], lower[1], lower[2], lower[3], lower[4], lower[5], low...]
    unnamed x144 -> x164, local copies, waits for them, and re-layouts: 13.7 us -> 66.9 us
    pallas_call x0 -> x18, Pallas kernels: none -> 47.6 us  [call(): pl.pallas_call(kernel, name=name, out_shape=shapes, in_specs=[SCALARS] *...]
    dot_general x30 -> x0, matrix products: 43.1 us -> none  [product(): return jnp.einsum(spec, left, right, preferred_element_type=jnp.float32)]
    psum x1 -> x0, blocking collectives: 39.2 us -> none  [per_device(): lax.psum((lower[0], lower[1], lower[2], lower[3], lower[4], lower[5], low...]
    all_to_all x10 -> x5, blocking collectives: 153 us -> 118 us  [exchange(): lax.all_to_all(values, ('row', 'col'), split_axis=0, concat_axis=0, tiled...]
    all_to_all x10 -> x5, waiting for transfers between devices: 68.1 us -> 35.2 us  [exchange(): lax.all_to_all(values, ('row', 'col'), split_axis=0, concat_axis=0, tiled...]
    reduce_scatter x2 -> x0, waiting for transfers between devices: 30.3 us -> none  [backward_module(): lax.psum_scatter(partial_terms.astype(jnp.bfloat16), 'col', scatter_dimen...]
  transfers between devices with their start and end apart: 15 -> 5, of which waited for: 13 -> 5; matrix products, arithmetic and copies ran while one was open for 8% -> 0% of each run, Pallas kernels for 0% -> 8%
where the time goes in v3:
time: 291 us; the launch traced here: 288 us
  blocking collectives  118 us (41%)
  local copies, waits for them, and re-layouts  67.4 us (23%)
  Pallas kernels  47.6 us (16%)
  waiting for transfers between devices  35.2 us (12%)
  starting transfers between devices  18.6 us (6%)
    all_to_all x5, blocking collectives, exchange(): lax.all_to_all(values, ('row', 'col'), split_axis=0, concat_axis=0, tiled...  118 us
    unnamed x164, local copies, waits for them, and re-layouts  66.9 us
    pallas_call x18, Pallas kernels, call(): pl.pallas_call(kernel, name=name, out_shape=shapes, in_specs=[SCALARS] *...  47.6 us
    all_to_all x5, waiting for transfers between devices, exchange(): lax.all_to_all(values, ('row', 'col'), split_axis=0, concat_axis=0, tiled...  35.2 us
    all_to_all x5, starting transfers between devices, exchange(): lax.all_to_all(values, ('row', 'col'), split_axis=0, concat_axis=0, tiled...  18.6 us
  transfers between devices with their start and end apart: 5, of which 5 were waited for; matrix products, arithmetic and copies ran while one was open for 0% of the time, Pallas kernels for 8%

profile of v3, /device:TPU:0, one launch (start us, length us, event | category | flops | bytes accessed | tf_op | source)
XLA Modules:
  0.0 288.3 jit_solution(6684607687885153934)
XLA Ops:
  3.1 1.0 copy-done.59
  5.5 2.9 start.1
  8.4 33.3 %all_to_all.50 = bf16[32,2,4,16,128]{4,3,2,1,0:T(8,128)(2,1)S(1)} all-to-all(bf16[32,2,4,16,128]{4,3,2,1,0:T(8,128)(2,1)S(1)} %get-tuple-element.53), channel_id=1, replica_groups=mesh['grp'=1,'row'=16,'col'=2,'ch'=1] {'row','col'}, dimensions={0} | all-to-all | bytes 2097152 | tf_op jit(solution)/shard_map/all_to_all | solution.py:517
  41.8 1.1 outgoing.1
  42.9 3.7 %all-to-all-start.1 = ((bf16[32,4,16,128]{3,2,1,0:T(8,128)(2,1)}), bf16[32,4,16,128]{3,2,1,0:T(8,128)(2,1)}, u32[]{:S(2)}, u32[]{:S(2)}) async-start(bf16[32,4,16,128]{3,2,1,0:T(8,128)(2,1)} %bitcast.1), calls=%async_computation.1 | async-start | bytes 1048576 | tf_op jit(solution)/shard_map/all_to_all | solution.py:517
  46.7 1.0 copy-done.60
  47.7 1.6 out_gate.1
  49.4 12.3 %all-to-all-done.1.tri = bf16[32,4,16,128]{3,2,1,0:T(8,128)(2,1)} async-done(((bf16[32,4,16,128]{3,2,1,0:T(8,128)(2,1)}), bf16[32,4,16,128]{3,2,1,0:T(8,128)(2,1)}, u32[]{:S(2)}, u32[]{:S(2)}) %all-to-all-start.1) | async-done | bytes 524320 | tf_op jit(solution)/shard_map/all_to_all | solution.py:517
  61.7 5.2 %between.1 = (bf16[32,2,4,16,128]{4,3,2,1,0:T(8,128)(2,1)S(1)}, bf16[16,128,128]{2,1,0:T(8,128)(2,1)S(1)}, bf16[16,128,128]{2,1,0:T(8,128)(2,1)S(1)}, f32[16,128,128]{2,1,0:T(8,128)S(1)}, f32[16,128]{1,0:T(8,128)S(1)}) custom-call(s32[1]{0:T(128)S(6)} %copy.29.lengths, bf16[32,4,16,128]{3,2,1,0:T(8,128)(2,1)} %all-to-all-done.1.tri, ...), custom_call_target="tpu_custom_call" | custom-call | flops 335544320 | bytes 5582852 | tf_op jit(solution)/shard_map/between/pallas_call | solution.py:502
  69.5 29.7 %all_to_all.51 = bf16[32,2,4,16,128]{4,3,2,1,0:T(8,128)(2,1)S(1)} all-to-all(bf16[32,2,4,16,128]{4,3,2,1,0:T(8,128)(2,1)S(1)} %get-tuple-element.57), channel_id=1, replica_groups=mesh['grp'=1,'row'=16,'col'=2,'ch'=1] {'row','col'}, dimensions={0} | all-to-all | bytes 2097152 | tf_op jit(solution)/shard_map/all_to_all | solution.py:517
  100.3 3.7 %all-to-all-start.3 = ((bf16[32,4,16,128]{3,2,1,0:T(8,128)(2,1)}), bf16[32,4,16,128]{3,2,1,0:T(8,128)(2,1)}, u32[]{:S(2)}, u32[]{:S(2)}) async-start(bf16[32,4,16,128]{3,2,1,0:T(8,128)(2,1)} %bitcast.28), calls=%async_computation.3 | async-start | bytes 1048576 | tf_op jit(solution)/shard_map/all_to_all | solution.py:517
  104.1 1.0 copy-done.3
  105.1 1.0 copy-done.61
  106.2 2.6 upstream.1
  108.8 1.0 copy-done.5
  110.8 1.0 copy-done.45
  112.6 6.4 %all-to-all-done.3.tri = bf16[32,4,16,128]{3,2,1,0:T(8,128)(2,1)} async-done(((bf16[32,4,16,128]{3,2,1,0:T(8,128)(2,1)}), bf16[32,4,16,128]{3,2,1,0:T(8,128)(2,1)}, u32[]{:S(2)}, u32[]{:S(2)}) %all-to-all-start.3) | async-done | bytes 524320 | tf_op jit(solution)/shard_map/all_to_all | solution.py:517
  119.1 1.2 copy-done.9
  120.3 2.6 turn.1
  122.9 18.4 %all_to_all.52 = bf16[32,4,16,128]{3,2,1,0:T(8,128)(2,1)S(1)} all-to-all(bf16[32,4,16,128]{3,2,1,0:T(8,128)(2,1)S(1)} %turn.1), channel_id=1, replica_groups=mesh['grp'=1,'row'=16,'col'=2,'ch'=1] {'row','col'}, dimensions={0} | all-to-all | bytes 1048576 | tf_op jit(solution)/shard_map/all_to_all | solution.py:517
  142.8 3.7 %all-to-all-start.5 = ((bf16[32,2,4,16,128]{4,3,2,1,0:T(8,128)(2,1)}), bf16[32,2,4,16,128]{4,3,2,1,0:T(8,128)(2,1)}, u32[]{:S(2)}, u32[]{:S(2)}) async-start(bf16[32,2,4,16,128]{4,3,2,1,0:T(8,128)(2,1)} %bitcast.27), calls=%async_computation.5 | async-start | bytes 2097152 | tf_op jit(solution)/shard_map/all_to_all | solution.py:517
  146.6 2.3 edge_factors_upper.1
  149.9 1.4 copy-done.39
  151.3 1.3 copy-done.41
  153.2 1.2 copy-done.6
  154.4 1.2 copy-done.10
  155.7 1.2 copy-done.46
  156.9 1.0 copy-done.58
  157.9 5.2 %behind_turn.1 = (bf16[16,128,128]{2,1,0:T(8,128)(2,1)}, f32[16,128,128]{2,1,0:T(8,128)S(1)}, bf16[256,128]{1,0:T(8,128)(2,1)S(1)}, f32[2,128]{1,0:T(2,128)S(1)}) custom-call(bf16[32,4,16,128]{3,2,1,0:T(8,128)(2,1)} %all-to-all-done.3.tri, bf16[16,128,128]{2,1,0:T(8,128)(2,1)S(1)} %copy-done.31, bf16[16,128,128]{2,1,0:T(8,128)(2,1)S(1)} %copy-done.4, ...), custom_call_target="tpu_custom_call" | custom-call | flops 268435456 | bytes 7015424 | tf_op jit(solution)/shard_map/behind_turn/pallas_call | solution.py:502
  163.2 1.0 copy-done.47
  165.4 7.4 %all-to-all-done.5.d_edge = bf16[32,2,4,16,128]{4,3,2,1,0:T(8,128)(2,1)} async-done(((bf16[32,2,4,16,128]{4,3,2,1,0:T(8,128)(2,1)}), bf16[32,2,4,16,128]{4,3,2,1,0:T(8,128)(2,1)}, u32[]{:S(2)}, u32[]{:S(2)}) %all-to-all-start.5) | async-done | bytes 1048608 | tf_op jit(solution)/shard_map/all_to_all | solution.py:517
  172.8 1.2 copy-done.7
  174.0 1.2 copy-done.14
  175.3 1.2 copy-done.17
  176.5 1.6 copy-done.40
  178.1 1.6 copy-done.42
  179.7 1.2 copy-done.48
  182.3 6.5 %middle.1 = (bf16[32,4,16,128]{3,2,1,0:T(8,128)(2,1)S(1)}, f32[16,128,128]{2,1,0:T(8,128)S(1)}, bf16[16,512,128]{2,1,0:T(8,128)(2,1)S(1)}, f32[16,128,128]{2,1,0:T(8,128)S(1)}, f32[16,128,128]{2,1,0:T(8,128)S(1)}) custom-call(bf16[32,2,4,16,128]{4,3,2,1,0:T(8,128)(2,1)} %all-to-all-done.5.d_edge, f32[16,256,128]{2,1,0:T(8,128)S(1)} %copy-done.40, ...), custom_call_target="tpu_custom_call" | custom-call | flops 335544320 | bytes 16599040 | tf_op jit(solution)/shard_map/middle/pallas_call | solution.py:502
  188.8 1.1 copy-done.53
  190.9 18.4 %all_to_all.53 = bf16[32,4,16,128]{3,2,1,0:T(8,128)(2,1)S(1)} all-to-all(bf16[32,4,16,128]{3,2,1,0:T(8,128)(2,1)S(1)} %get-tuple-element.72), channel_id=1, replica_groups=mesh['grp'=1,'row'=16,'col'=2,'ch'=1] {'row','col'}, dimensions={0} | all-to-all | bytes 1048576 | tf_op jit(solution)/shard_map/all_to_all | solution.py:517
  210.8 3.8 %all-to-all-start.7 = ((bf16[32,2,4,16,128]{4,3,2,1,0:T(8,128)(2,1)}), bf16[32,2,4,16,128]{4,3,2,1,0:T(8,128)(2,1)}, u32[]{:S(2)}, u32[]{:S(2)}) async-start(bf16[32,2,4,16,128]{4,3,2,1,0:T(8,128)(2,1)} %bitcast.26), calls=%async_computation.7 | async-start | bytes 2097152 | tf_op jit(solution)/shard_map/all_to_all | solution.py:517
  214.6 1.0 copy-done.36
  215.6 2.3 edge_factors_lower.1
  217.9 1.3 copy-done.26
  219.2 1.4 copy-done.28
  222.2 1.2 copy-done.15
  223.4 1.2 copy-done.18
  224.6 1.2 copy-done.20
  225.8 1.6 copy-done.38
  227.4 1.2 copy-done.54
  228.7 1.2 copy-done.56
  229.9 4.5 %behind_middle.1 = (f32[16,128,128]{2,1,0:T(8,128)S(1)}, bf16[256,128]{1,0:T(8,128)(2,1)S(1)}, bf16[512,128]{1,0:T(8,128)(2,1)S(1)}, f32[4,128]{1,0:T(4,128)S(1)}) custom-call(f32[16,128,128]{2,1,0:T(8,128)S(1)} %copy-done.20, f32[16,128,128]{2,1,0:T(8,128)S(1)} %get-tuple-element.56.outgate, f32[16,128,128]{2,1,0:T(8,128)S(1)} %copy-done.15, ...), custom_call_target="tpu_custom_call" | custom-call | flops 536870912 | bytes 10817536 | tf_op jit(solution)/shard_map/behind_middle/pallas_call | solution.py:502
  236.7 4.1 %all-to-all-done.7.d_edge = bf16[32,2,4,16,128]{4,3,2,1,0:T(8,128)(2,1)} async-done(((bf16[32,2,4,16,128]{4,3,2,1,0:T(8,128)(2,1)}), bf16[32,2,4,16,128]{4,3,2,1,0:T(8,128)(2,1)}, u32[]{:S(2)}, u32[]{:S(2)}) %all-to-all-start.7) | async-done | bytes 1048608 | tf_op jit(solution)/shard_map/all_to_all | solution.py:517
  240.8 1.6 copy-done.27
  242.3 1.6 copy-done.29
  246.5 4.6 %finish.1 = (bf16[1536,128]{1,0:T(8,128)(2,1)}, bf16[16,512,128]{2,1,0:T(8,128)(2,1)S(1)}) custom-call(bf16[32,2,4,16,128]{4,3,2,1,0:T(8,128)(2,1)} %all-to-all-done.7.d_edge, f32[16,256,128]{2,1,0:T(8,128)S(1)} %copy-done.27, f32[16,256,128]{2,1,0:T(8,128)S(1)} %copy-done.29, bf16[16,128,128]{2,1,0:T(8,128)(2,1)S(1)} %copy-done.1, ...), custom_call_target="tpu_custom_call" | custom-call | flops 268435456 | bytes 8519680 | tf_op jit(solution)/shard_map/finish/pallas_call | solution.py:502
  251.2 1.3 copy-done.33
  252.5 3.6 %all-to-all-start.8 = ((bf16[32,48,128]{2,1,0:T(8,128)(2,1)}), bf16[32,48,128]{2,1,0:T(8,128)(2,1)S(1)}, u32[]{:S(2)}, u32[]{:S(2)}) async-start(bf16[32,48,128]{2,1,0:T(8,128)(2,1)} %bitcast.8), calls=%async_computation.8 | async-start | bytes 786432 | tf_op jit(solution)/shard_map/all_to_all | solution.py:517
  256.1 1.6 copy-done.34
  257.7 1.2 copy-done.50
  258.9 1.2 copy-done.52
  260.2 3.8 %behind_finish.1 = (bf16[16,128,128]{2,1,0:T(8,128)(2,1)}, f32[2,128]{1,0:T(2,128)S(1)}) custom-call(bf16[16,512,128]{2,1,0:T(8,128)(2,1)S(1)} %copy-done.34, f32[16,128,128]{2,1,0:T(8,128)S(1)} %copy-done.52, f32[16,128,128]{2,1,0:T(8,128)S(1)} %copy-done.21, f32[16,128,128]{2,1,0:T(8,128)S(1)} %copy-done.50, f32[16,128]{1,0:T(8,128)S(1)} %copy-done.73, ...), custom_call_target="tpu_custom_call" | custom-call | flops 268435456 | bytes 6039552 | tf_op jit(solution)/shard_map/behind_finish/pallas_call | solution.py:502
  263.9 4.9 %all-to-all-done.8.parts = bf16[32,48,128]{2,1,0:T(8,128)(2,1)S(1)} async-done(((bf16[32,48,128]{2,1,0:T(8,128)(2,1)}), bf16[32,48,128]{2,1,0:T(8,128)(2,1)S(1)}, u32[]{:S(2)}, u32[]{:S(2)}) %all-to-all-start.8) | async-done | bytes 393248 | tf_op jit(solution)/shard_map/all_to_all | solution.py:517
  268.9 17.9 %all_to_all.54.shared = bf16[32,64,128]{2,1,0:T(8,128)(2,1)S(1)} all-to-all(bf16[32,64,128]{2,1,0:T(8,128)(2,1)S(1)} %sum_weights.1), channel_id=1, replica_groups=mesh['grp'=1,'row'=16,'col'=2,'ch'=1] {'row','col'}, dimensions={0} | all-to-all | bytes 1048576 | tf_op jit(solution)/shard_map/all_to_all | solution.py:517
  (134 shorter events, 24.8 us)
Async XLA Ops:
  3.1 1.0 copy-start.59
  8.4 38.3 %copy-start = (bf16[16,128,128]{2,1,0:T(8,128)(2,1)}, bf16[16,128,128]{2,1,0:T(8,128)(2,1)S(1)}, u32[]{:S(2)}) copy-start(bf16[16,128,128]{2,1,0:T(8,128)(2,1)S(1)} %get-tuple-element.54.normed.normed0) | copy-start | bytes 1572868
  8.4 38.3 %copy-start.44 = (bf16[2,128,128]{2,1,0:T(8,128)(2,1)S(1)}, bf16[2,128,128]{2,1,0:T(8,128)(2,1)}, u32[]{:S(2)}) copy-start(bf16[2,128,128]{2,1,0:T(8,128)(2,1)} %outgate_w.7) | copy-start | bytes 196612
  41.7 19.9 %copy-start.23 = (bf16[2,2,128,128]{3,2,1,0:T(8,128)(2,1)S(1)}, bf16[2,2,128,128]{3,2,1,0:T(8,128)(2,1)}, u32[]{:S(2)}) copy-start(bf16[2,2,128,128]{3,2,1,0:T(8,128)(2,1)} %proj_w.9) | copy-start | bytes 393220
  41.7 19.9 %copy-start.25 = (bf16[2,2,128,128]{3,2,1,0:T(8,128)(2,1)S(1)}, bf16[2,2,128,128]{3,2,1,0:T(8,128)(2,1)}, u32[]{:S(2)}) copy-start(bf16[2,2,128,128]{3,2,1,0:T(8,128)(2,1)} %gate_w.9) | copy-start | bytes 393220
  41.7 19.9 %copy-start.43 = (bf16[2,128,128]{2,1,0:T(8,128)(2,1)S(1)}, bf16[2,128,128]{2,1,0:T(8,128)(2,1)}, u32[]{:S(2)}) copy-start(bf16[2,128,128]{2,1,0:T(8,128)(2,1)} %out_w.9) | copy-start | bytes 196612
  41.7 19.9 %copy-start.68 = (f32[2,128]{1,0:T(2,128)S(1)}, f32[2,128]{1,0:T(2,128)}, u32[]{:S(2)}) copy-start(f32[2,128]{1,0:T(2,128)} %mgain.9) | copy-start | bytes 3076
  41.8 19.9 %copy-start.70 = (f32[2,128]{1,0:T(2,128)S(1)}, f32[2,128]{1,0:T(2,128)}, u32[]{:S(2)}) copy-start(f32[2,128]{1,0:T(2,128)} %ngain.5) | copy-start | bytes 3076
  41.8 19.9 %copy-start.71 = (f32[2,128]{1,0:T(2,128)S(1)}, f32[2,128]{1,0:T(2,128)}, u32[]{:S(2)}) copy-start(f32[2,128]{1,0:T(2,128)} %mbias.5) | copy-start | bytes 3076
  41.8 19.9 %copy-start.79 = (f32[2,128]{1,0:T(2,128)S(1)}, f32[2,128]{1,0:T(2,128)}, u32[]{:S(2)}) copy-start(f32[2,128]{1,0:T(2,128)} %nbias.1) | copy-start | bytes 3076
  42.9 18.7 %all-to-all-start.1 = ((bf16[32,4,16,128]{3,2,1,0:T(8,128)(2,1)}), bf16[32,4,16,128]{3,2,1,0:T(8,128)(2,1)}, u32[]{:S(2)}, u32[]{:S(2)}) async-start(bf16[32,4,16,128]{3,2,1,0:T(8,128)(2,1)} %bitcast.1), calls=%async_computation.1 | async-start | bytes 1048576 | tf_op jit(solution)/shard_map/all_to_all | solution.py:517
  46.7 1.0 copy-start.60
  49.3 17.6 %copy-start.35 = (bf16[16,128,128]{2,1,0:T(8,128)(2,1)}, bf16[16,128,128]{2,1,0:T(8,128)(2,1)S(1)}, u32[]{:S(2)}) copy-start(bf16[16,128,128]{2,1,0:T(8,128)(2,1)S(1)} %get-tuple-element.55.pair_t.base) | copy-start | bytes 1572868
  69.5 30.0 %copy-start.74 = (f32[16,128]{1,0:T(8,128)}, f32[16,128]{1,0:T(8,128)S(1)}, u32[]{:S(2)}) copy-start(f32[16,128]{1,0:T(8,128)S(1)} %get-tuple-element.71.inverse_mid) | copy-start | bytes 24580
  100.3 18.7 %all-to-all-start.3 = ((bf16[32,4,16,128]{3,2,1,0:T(8,128)(2,1)}), bf16[32,4,16,128]{3,2,1,0:T(8,128)(2,1)}, u32[]{:S(2)}, u32[]{:S(2)}) async-start(bf16[32,4,16,128]{3,2,1,0:T(8,128)(2,1)} %bitcast.28), calls=%async_computation.3 | async-start | bytes 1048576 | tf_op jit(solution)/shard_map/all_to_all | solution.py:517
  104.1 1.0 copy-start.3
  105.1 1.0 copy-start.61
  108.8 1.0 copy-start.5
  109.8 1.0 copy-start.8
  110.8 1.0 copy-start.45
  119.1 1.2 copy-start.9
  141.8 1.0 copy-start.12
  142.8 3.8 %copy-start.4 = (bf16[16,128,128]{2,1,0:T(8,128)(2,1)S(1)}, bf16[16,128,128]{2,1,0:T(8,128)(2,1)}, u32[]{:S(2)}) copy-start(bf16[16,128,128]{2,1,0:T(8,128)(2,1)} %copy-done.2) | copy-start | bytes 1572868
  142.8 3.8 %copy-start.31 = (bf16[16,128,128]{2,1,0:T(8,128)(2,1)S(1)}, bf16[16,128,128]{2,1,0:T(8,128)(2,1)}, u32[]{:S(2)}) copy-start(bf16[16,128,128]{2,1,0:T(8,128)(2,1)} %copy-done.30) | copy-start | bytes 1572868
  142.8 30.0 %all-to-all-start.5 = ((bf16[32,2,4,16,128]{4,3,2,1,0:T(8,128)(2,1)}), bf16[32,2,4,16,128]{4,3,2,1,0:T(8,128)(2,1)}, u32[]{:S(2)}, u32[]{:S(2)}) async-start(bf16[32,2,4,16,128]{4,3,2,1,0:T(8,128)(2,1)} %bitcast.27), calls=%async_computation.5 | async-start | bytes 2097152 | tf_op jit(solution)/shard_map/all_to_all | solution.py:517
  148.9 1.0 copy-start.16
  149.9 1.4 copy-start.39
  151.3 1.3 copy-start.41
  153.2 1.2 copy-start.6
  154.4 1.2 copy-start.10
  155.7 1.2 copy-start.46
  156.9 1.0 copy-start.58
  163.2 1.0 copy-start.47
  172.8 1.2 copy-start.7
  174.0 1.2 copy-start.14
  175.2 1.2 copy-start.17
  176.5 1.6 copy-start.40
  178.1 1.6 copy-start.42
  179.7 1.2 copy-start.48
  188.8 1.1 copy-start.53
  190.9 18.9 %copy-start.19 = (f32[16,128,128]{2,1,0:T(8,128)}, f32[16,128,128]{2,1,0:T(8,128)S(1)}, u32[]{:S(2)}) copy-start(f32[16,128,128]{2,1,0:T(8,128)S(1)} %get-tuple-element.75.grad) | copy-start | bytes 3145732
  190.9 18.9 %copy-start.37 = (bf16[16,512,128]{2,1,0:T(8,128)(2,1)}, bf16[16,512,128]{2,1,0:T(8,128)(2,1)S(1)}, u32[]{:S(2)}) copy-start(bf16[16,512,128]{2,1,0:T(8,128)(2,1)S(1)} %get-tuple-element.77.d_in1) | copy-start | bytes 6291460
  209.3 5.2 %copy-start.1 = (bf16[16,128,128]{2,1,0:T(8,128)(2,1)S(1)}, bf16[16,128,128]{2,1,0:T(8,128)(2,1)}, u32[]{:S(2)}) copy-start(bf16[16,128,128]{2,1,0:T(8,128)(2,1)} %copy-done) | copy-start | bytes 1572868
  209.8 1.0 copy-start.11
  210.8 30.0 %all-to-all-start.7 = ((bf16[32,2,4,16,128]{4,3,2,1,0:T(8,128)(2,1)}), bf16[32,2,4,16,128]{4,3,2,1,0:T(8,128)(2,1)}, u32[]{:S(2)}, u32[]{:S(2)}) async-start(bf16[32,2,4,16,128]{4,3,2,1,0:T(8,128)(2,1)} %bitcast.26), calls=%async_computation.7 | async-start | bytes 2097152 | tf_op jit(solution)/shard_map/all_to_all | solution.py:517
  214.5 1.0 copy-start.36
  217.9 1.3 copy-start.26
  219.2 1.4 copy-start.28
  222.2 1.2 copy-start.15
  223.4 1.2 copy-start.18
  224.6 1.2 copy-start.20
  225.8 1.6 copy-start.38
  227.4 1.2 copy-start.54
  228.7 1.2 copy-start.56
  240.8 1.6 copy-start.27
  242.3 1.6 copy-start.29
  246.5 9.6 %copy-start.21 = (f32[16,128,128]{2,1,0:T(8,128)S(1)}, f32[16,128,128]{2,1,0:T(8,128)}, u32[]{:S(2)}) copy-start(f32[16,128,128]{2,1,0:T(8,128)} %copy-done.19) | copy-start | bytes 3145732
  246.5 9.6 %copy-start.73 = (f32[16,128]{1,0:T(8,128)S(1)}, f32[16,128]{1,0:T(8,128)}, u32[]{:S(2)}) copy-start(f32[16,128]{1,0:T(8,128)} %copy-done.72) | copy-start | bytes 24580
  251.2 1.3 copy-start.33
  252.5 16.4 %all-to-all-start.8 = ((bf16[32,48,128]{2,1,0:T(8,128)(2,1)}), bf16[32,48,128]{2,1,0:T(8,128)(2,1)S(1)}, u32[]{:S(2)}, u32[]{:S(2)}) async-start(bf16[32,48,128]{2,1,0:T(8,128)(2,1)} %bitcast.8), calls=%async_computation.8 | async-start | bytes 786432 | tf_op jit(solution)/shard_map/all_to_all | solution.py:517
  256.1 1.6 copy-start.34
  257.7 1.2 copy-start.50
  258.9 1.2 copy-start.52
  260.2 8.7 %copy-start.81 = (f32[2,128]{1,0:T(2,128)S(1)}, f32[2,128]{1,0:T(2,128)}, u32[]{:S(2)}) copy-start(f32[2,128]{1,0:T(2,128)} %copy-done.80) | copy-start | bytes 3076
  (23 other events, 17.9 us)

commit v4 on v3

--- a/solution.py
+++ b/solution.py
@@ -126,15 +126,28 @@
     return inverse * (weighted - first - scaled * second)
 
 
-def edges(normed, in_weights, mask):
+def save_norm(step, values, scaled_out, inverse_out):
+    scaled, inverse = norm_rows(values)
+    scaled_out[step] = scaled
+    inverse_out[pl.ds(step, 1), :] = inverse
+    return scaled
+
+
+def save_edges(step, normed, in_weights, mask, proj_out, gate_out):
     pre = dot(in_weights, normed)
     half = pre.shape[0] // 2
-    return pre[:half] * sigmoid(pre[half:]) * mask
+    gating = sigmoid(pre[half:])
+    factor = gating * mask
+    value = pre[:half] * factor
+    proj_out[step] = factor
+    gate_out[step] = value * (1.0 - gating)
+    return value
 
 
 def start_kernel(
     lengths, pair_far, ngain_far, nbias_far, proj_far, gate_far,
-    edge_out, normed_out, pair, ngain, nbias, proj_w, gate_w, sems, wts, scr,
+    edge_out, normed_out, proj_out, gate_out, scaled_out, inverse_out,
+    pair, ngain, nbias, proj_w, gate_w, sems, wts, scr,
 ):
     far = (proj_far.at[0], gate_far.at[0], ngain_far, nbias_far, pair_far)
     near = (proj_w.at[0], gate_w.at[0], ngain, nbias, pair)
@@ -151,32 +164,25 @@
     gain, bias = column(ngain, 0, lanes), column(nbias, 0, lanes)
 
     def body(step):
-        scaled, _ = norm_rows(jnp.transpose(pair[step].astype(F32)))
+        base = jnp.transpose(pair[step].astype(F32))
+        scaled = save_norm(step, base, scaled_out, inverse_out)
         normed = (scaled * gain + bias).astype(BF16)
         normed_out[step] = normed
-        put_rows(scr, edges(normed, wts[...], row_mask(lengths, step, rows, lanes)), step, rows)
+        mask = row_mask(lengths, step, rows, lanes)
+        put_rows(scr, save_edges(step, normed, wts[...], mask, proj_out, gate_out), step, rows)
 
     each_row(rows, 4, body)
     spread_edges(scr, edge_out)
 
 
-def out_gate_kernel(pair, normed, outgate_w, pair_out, gate_out):
-    outgate_t = turned(outgate_w[0])
-
-    def body(step):
-        pair_out[step] = jnp.transpose(pair[step].astype(F32)).astype(BF16)
-        gate_out[step] = sigmoid(dot(outgate_t, normed[step]))
-
-    each_row(pair.shape[0], 2, body)
-
-
 def between_kernel(
-    lengths, tri, pair_t, outgate, ngain, nbias, mgain, mbias, out_w, proj_w, gate_w,
-    edge_out, mid_out, normed_out, scaled_mid_out, inverse_mid_out, wts, scr,
+    lengths, tri, pair, normed0, ngain, nbias, mgain, mbias, out_w, outgate_w, proj_w, gate_w,
+    edge_out, mid_out, normed_out, proj_out, gate_out, scaled_out, inverse_out,
+    outgate_out, scaled_mid_out, inverse_mid_out, wts, scr,
 ):
-    rows, channels, lanes = pair_t.shape
+    rows, lanes, channels = pair.shape
     load_in_weights(proj_w, gate_w, 1, wts)
-    out_t = turned(out_w[0])
+    out_t, outgate_t = turned(out_w[0]), turned(outgate_w[0])
     gain, bias = column(ngain, 1, lanes), column(nbias, 1, lanes)
     gain_mid, bias_mid = column(mgain, 0, lanes), column(mbias, 0, lanes)
     collect_triangle(tri, scr)
@@ -187,44 +193,18 @@
         inverse_mid_out[pl.ds(step, 1), :] = inverse_mid
         unit = (scaled_mid * gain_mid + bias_mid).astype(BF16)
         outer = dot(out_t, unit)
-        mid = (pair_t[step].astype(F32) + outer * outgate[step]).astype(BF16)
+        outgate = sigmoid(dot(outgate_t, normed0[step]))
+        outgate_out[step] = outgate
+        mid = (jnp.transpose(pair[step].astype(F32)) + outer * outgate).astype(BF16)
         mid_out[step] = mid
-        scaled, _ = norm_rows(mid.astype(F32))
+        scaled = save_norm(step, mid.astype(F32), scaled_out, inverse_out)
         normed = (scaled * gain + bias).astype(BF16)
         normed_out[step] = normed
-        here = edges(normed, wts[...], row_mask(lengths, step, rows, lanes))
-        put_rows(scr, here, step, rows)
+        mask = row_mask(lengths, step, rows, lanes)
+        put_rows(scr, save_edges(step, normed, wts[...], mask, proj_out, gate_out), step, rows)
 
     each_row(rows, 4, body)
     spread_edges(scr, edge_out)
-
-
-def upstream_kernel(cot, normed, out_w, outgate_w, cot_out, gate_out, d_outer_out, d_unit_out):
-    outgate_t = turned(outgate_w[1])
-
-    def body(step):
-        grad = jnp.transpose(cot[step].astype(F32))
-        outgate = sigmoid(dot(outgate_t, normed[step]))
-        d_outer = (grad * outgate).astype(BF16)
-        cot_out[step] = grad
-        gate_out[step] = outgate
-        d_outer_out[step] = d_outer
-        d_unit_out[step] = dot(out_w[1], d_outer)
-
-    each_row(cot.shape[0], 2, body)
-
-
-def turn_kernel(tri, d_unit, mgain, d_tri_out, scr):
-    rows, channels, lanes = d_unit.shape
-    gain_mid = column(mgain, 1, lanes)
-    collect_triangle(tri, scr)
-
-    def body(step):
-        scaled_mid, inverse_mid = mid_norm(get_rows(scr, step, channels, rows))
-        put_rows(scr, norm_backward(d_unit[step] * gain_mid, scaled_mid, inverse_mid), step, rows)
-
-    each_row(rows, 4, body)
-    d_tri_out[...] = scr[...].reshape(d_tri_out.shape).astype(BF16)
 
 
 def out_weight_grads(unit, d_outer, normed, d_gatepre, out_ref):
@@ -233,63 +213,55 @@
     out_ref[width:, :] = dot_rt(normed[...], d_gatepre[...]).astype(out_ref.dtype)
 
 
+def in_weight_grads(normed_all, d_in_all, out_ref):
+    width = normed_all.shape[0]
+    for part in range(d_in_all.shape[0] // width):
+        block = slice(part * width, (part + 1) * width)
+        out_ref[block, :] = dot_rt(normed_all[...], d_in_all[block, :]).astype(out_ref.dtype)
+
+
 def lane_block(step, lanes):
     return pl.ds(pl.multiple_of(step * lanes, lanes), lanes)
 
 
-def behind_turn_kernel(
-    tri, mid, normed, outgate, grad, d_outer, d_unit, mgain, mbias, out_w, outgate_w,
-    new_out, d_normed_out, weights_out, small_out, scr, unit_all, outer_all, normed_all, gate_all,
-    sums,
+def turn_kernel(
+    tri, mid, normed, cot, mgain, mbias, out_w, outgate_w,
+    d_tri_out, new_out, grad_out, d_normed_out, weights_out, small_out,
+    scr, unit_all, outer_all, normed_all, gate_all, sums,
 ):
     rows, channels, lanes = mid.shape
-    out_t = turned(out_w[1])
+    out_t, outgate_t = turned(out_w[1]), turned(outgate_w[1])
     gain_mid, bias_mid = column(mgain, 1, lanes), column(mbias, 1, lanes)
     collect_triangle(tri, scr)
     sums[...] = jnp.zeros_like(sums)
 
     def body(step):
         here = lane_block(step, lanes)
-        scaled_mid, _ = mid_norm(get_rows(scr, step, channels, rows))
+        grad = jnp.transpose(cot[step].astype(F32))
+        grad_out[step] = grad
+        outgate = sigmoid(dot(outgate_t, normed[step]))
+        gated = grad * outgate
+        d_outer = gated.astype(BF16)
+        d_unit = dot(out_w[1], d_outer)
+        scaled_mid, inverse_mid = mid_norm(get_rows(scr, step, channels, rows))
+        put_rows(scr, norm_backward(d_unit * gain_mid, scaled_mid, inverse_mid), step, rows)
         unit = (scaled_mid * gain_mid + bias_mid).astype(BF16)
         outer = dot(out_t, unit)
-        gate = outgate[step]
-        update = outer * gate
-        new_out[step] = jnp.transpose(mid[step].astype(F32) + update).astype(BF16)
-        d_gatepre = (grad[step] * update * (1.0 - gate)).astype(BF16)
+        new_out[step] = jnp.transpose(mid[step].astype(F32) + outer * outgate).astype(BF16)
+        d_gatepre = (gated * outer * (1.0 - outgate)).astype(BF16)
         d_normed_out[step] = dot(outgate_w[1], d_gatepre)
         unit_all[:, here] = unit
-        outer_all[:, here] = d_outer[step]
+        outer_all[:, here] = d_outer
         normed_all[:, here] = normed[step]
         gate_all[:, here] = d_gatepre
-        sums[0] += d_unit[step] * scaled_mid
-        sums[1] += d_unit[step]
-
-    each_row(rows, 2, body)
+        sums[0] += d_unit * scaled_mid
+        sums[1] += d_unit
+
+    each_row(rows, 4, body)
+    d_tri_out[...] = scr[...].reshape(d_tri_out.shape).astype(BF16)
     out_weight_grads(unit_all, outer_all, normed_all, gate_all, weights_out)
     for index in range(2):
         small_out[index : index + 1, :] = as_row(sums[index])
-
-
-def edge_factor_kernel(
-    module, lengths, base, normed, proj_w, gate_w,
-    proj_out, gate_out, scaled_out, inverse_out, wts,
-):
-    rows, channels, lanes = base.shape
-    load_in_weights(proj_w, gate_w, module, wts)
-
-    def body(step):
-        pre = dot(wts[...], normed[step])
-        half = pre.shape[0] // 2
-        gating = sigmoid(pre[half:])
-        factor = gating * row_mask(lengths, step, rows, lanes)
-        proj_out[step] = factor
-        gate_out[step] = factor * pre[:half] * (1.0 - gating)
-        scaled, inverse = norm_rows(base[step].astype(F32))
-        scaled_out[step] = scaled
-        inverse_out[pl.ds(step, 1), :] = inverse
-
-    each_row(rows, 2, body)
 
 
 def in_normed(d_in, all_w, proj_w, gate_w):
@@ -303,97 +275,83 @@
 
 def middle_kernel(
     d_edge, proj_factor, gate_factor, d_normed_gate, scaled_in, inverse_in, cot, outgate,
-    scaled_mid, inverse_mid, ngain, mgain, proj_w, gate_w, out_w,
-    d_tri_out, grad_out, d_in_out, d_normed_out, d_unit_out, scr, scr_tri,
+    scaled_mid, inverse_mid, normed0, normed1, ngain, mgain, mbias, proj_w, gate_w, out_w,
+    outgate_w,
+    d_tri_out, grad_out, d_normed_out, out_weights, in_weights, small_out,
+    scr, scr_tri, unit_all, outer_all, normed_all, gate_all, upper_all, d_in_all, sums,
 ):
     rows, channels, lanes = cot.shape
-    gain, gain_mid = column(ngain, 1, lanes), column(mgain, 0, lanes)
+    out_t = turned(out_w[0])
+    gain = column(ngain, 1, lanes)
+    gain_mid, bias_mid = column(mgain, 0, lanes), column(mbias, 0, lanes)
     collect_edges(d_edge, scr)
+    sums[...] = jnp.zeros_like(sums)
     half = proj_factor.shape[1]
-
-    def body(step):
-        here = get_rows(scr, step, half, rows)
-        d_proj = (here * proj_factor[step]).astype(BF16)
-        d_gate = (here * gate_factor[step]).astype(BF16)
-        d_in = jnp.concatenate([d_proj, d_gate], axis=0)
-        d_in_out[step] = d_in
-        d_normed = in_normed(d_in, d_normed_gate[step], proj_w[1], gate_w[1])
-        d_normed_out[step] = d_normed
-        grad = cot[step] + norm_backward(
-            d_normed * gain, scaled_in[step], inverse_in[pl.ds(step, 1), :]
-        )
-        grad_out[step] = grad
-        d_unit = dot(out_w[0], (grad * outgate[step]).astype(BF16))
-        d_unit_out[step] = d_unit
-        d_tri = norm_backward(d_unit * gain_mid, scaled_mid[step], inverse_mid[pl.ds(step, 1), :])
-        put_rows(scr_tri, d_tri, step, rows)
-
-    each_row(rows, 4, body)
-    d_tri_out[...] = scr_tri[...].reshape(d_tri_out.shape).astype(BF16)
-
-
-def behind_middle_kernel(
-    grad, outgate, scaled_mid, d_unit, normed0, d_in1, normed1, d_normed1, scaled1,
-    mgain, mbias, out_w, outgate_w,
-    d_normed_out, out_weights, in_weights, small_out,
-    unit_all, outer_all, normed_all, gate_all, upper_all, d_in_all, sums,
-):
-    rows, channels, lanes = grad.shape
-    out_t = turned(out_w[0])
-    gain_mid, bias_mid = column(mgain, 0, lanes), column(mbias, 0, lanes)
-    sums[...] = jnp.zeros_like(sums)
-
-    def body(step):
-        here = lane_block(step, lanes)
-        scaled = scaled_mid[step]
-        unit = (scaled * gain_mid + bias_mid).astype(BF16)
-        outer = dot(out_t, unit)
-        gate = outgate[step]
-        gated = grad[step] * gate
-        d_gatepre = (gated * outer * (1.0 - gate)).astype(BF16)
-        d_normed_out[step] = dot(outgate_w[0], d_gatepre)
-        unit_all[:, here] = unit
-        outer_all[:, here] = gated.astype(BF16)
-        normed_all[:, here] = normed0[step]
-        gate_all[:, here] = d_gatepre
-        upper_all[:, here] = normed1[step]
-        d_in_all[:, here] = d_in1[step]
-        sums[0] += d_unit[step] * scaled
-        sums[1] += d_unit[step]
-        sums[2] += d_normed1[step] * scaled1[step]
-        sums[3] += d_normed1[step]
-
-    each_row(rows, 2, body)
-    out_weight_grads(unit_all, outer_all, normed_all, gate_all, out_weights)
-    in_weight_grads(upper_all, d_in_all, in_weights)
-    for index in range(4):
-        small_out[index : index + 1, :] = as_row(sums[index])
-
-
-def in_weight_grads(normed_all, d_in_all, out_ref):
-    width = normed_all.shape[0]
-    for part in range(d_in_all.shape[0] // width):
-        block = slice(part * width, (part + 1) * width)
-        out_ref[block, :] = dot_rt(normed_all[...], d_in_all[block, :]).astype(out_ref.dtype)
-
-
-def finish_kernel(
-    d_edge, proj_factor, gate_factor, normed, out0, in1, out1,
-    packed_out, d_in_out, scr, normed_all, d_in_all,
-):
-    rows, half, lanes = proj_factor.shape
-    collect_edges(d_edge, scr)
 
     def body(step):
         place = lane_block(step, lanes)
         here = get_rows(scr, step, half, rows)
         d_proj = (here * proj_factor[step]).astype(BF16)
         d_gate = (here * gate_factor[step]).astype(BF16)
-        d_in_out[step, 0:half] = d_proj
-        d_in_out[step, half:] = d_gate
-        d_in_all[0:half, place] = d_proj
-        d_in_all[half:, place] = d_gate
+        d_in = jnp.concatenate([d_proj, d_gate], axis=0)
+        d_in_all[:, place] = d_in
+        upper_all[:, place] = normed1[step]
+        d_normed = in_normed(d_in, d_normed_gate[step], proj_w[1], gate_w[1])
+        scaled = scaled_in[step]
+        sums[2] += d_normed * scaled
+        sums[3] += d_normed
+        grad = cot[step] + norm_backward(d_normed * gain, scaled, inverse_in[pl.ds(step, 1), :])
+        grad_out[step] = grad
+        gate = outgate[step]
+        gated = grad * gate
+        d_outer = gated.astype(BF16)
+        d_unit = dot(out_w[0], d_outer)
+        scaled = scaled_mid[step]
+        d_tri = norm_backward(d_unit * gain_mid, scaled, inverse_mid[pl.ds(step, 1), :])
+        put_rows(scr_tri, d_tri, step, rows)
+        unit = (scaled * gain_mid + bias_mid).astype(BF16)
+        outer = dot(out_t, unit)
+        d_gatepre = (gated * outer * (1.0 - gate)).astype(BF16)
+        d_normed_out[step] = dot(outgate_w[0], d_gatepre)
+        unit_all[:, place] = unit
+        outer_all[:, place] = d_outer
+        normed_all[:, place] = normed0[step]
+        gate_all[:, place] = d_gatepre
+        sums[0] += d_unit * scaled
+        sums[1] += d_unit
+
+    each_row(rows, 4, body)
+    d_tri_out[...] = scr_tri[...].reshape(d_tri_out.shape).astype(BF16)
+    out_weight_grads(unit_all, outer_all, normed_all, gate_all, out_weights)
+    in_weight_grads(upper_all, d_in_all, in_weights)
+    for index in range(4):
+        small_out[index : index + 1, :] = as_row(sums[index])
+
+
+def finish_kernel(
+    d_edge, proj_factor, gate_factor, d_normed_gate, scaled_in, inverse_in, grad, normed,
+    ngain, proj_w, gate_w, out0, in1, out1,
+    packed_out, grad_out, small_out, scr, normed_all, d_in_all, sums,
+):
+    rows, half, lanes = proj_factor.shape
+    gain = column(ngain, 0, lanes)
+    collect_edges(d_edge, scr)
+    sums[...] = jnp.zeros_like(sums)
+
+    def body(step):
+        place = lane_block(step, lanes)
+        here = get_rows(scr, step, half, rows)
+        d_proj = (here * proj_factor[step]).astype(BF16)
+        d_gate = (here * gate_factor[step]).astype(BF16)
+        d_in = jnp.concatenate([d_proj, d_gate], axis=0)
+        d_in_all[:, place] = d_in
         normed_all[:, place] = normed[step]
+        d_normed = in_normed(d_in, d_normed_gate[step], proj_w[0], gate_w[0])
+        scaled = scaled_in[step]
+        sums[0] += d_normed * scaled
+        sums[1] += d_normed
+        total = grad[step] + norm_backward(d_normed * gain, scaled, inverse_in[pl.ds(step, 1), :])
+        grad_out[step] = jnp.transpose(total).astype(BF16)
 
     each_row(rows, 4, body)
     first, second, third = d_in_all.shape[0], out0.shape[0], in1.shape[0]
@@ -401,25 +359,6 @@
     packed_out[first : first + second, :] = out0[...]
     packed_out[first + second : first + second + third, :] = in1[...]
     packed_out[first + second + third :, :] = out1[...]
-
-
-def behind_finish_kernel(
-    d_in, d_normed_gate, grad, scaled_in, inverse_in, ngain, proj_w, gate_w,
-    grad_out, small_out, sums,
-):
-    rows, channels, lanes = grad.shape
-    gain = column(ngain, 0, lanes)
-    sums[...] = jnp.zeros_like(sums)
-
-    def body(step):
-        d_normed = in_normed(d_in[step], d_normed_gate[step], proj_w[0], gate_w[0])
-        scaled = scaled_in[step]
-        sums[0] += d_normed * scaled
-        sums[1] += d_normed
-        total = grad[step] + norm_backward(d_normed * gain, scaled, inverse_in[pl.ds(step, 1), :])
-        grad_out[step] = jnp.transpose(total).astype(BF16)
-
-    each_row(rows, 2, body)
     for index in range(2):
         small_out[index : index + 1, :] = as_row(sums[index])
 
@@ -550,86 +489,63 @@
     def small(count):
         return ((count, H), F32)
 
-    sent, normed0 = call(
-        start_kernel, "start", [edge, tile], [lengths, pair, ngain, nbias, proj_w, gate_w],
+    saved = [tile, factor, factor, wide, row]
+    sent, normed0, *factors0 = call(
+        start_kernel, "start", [edge, *saved], [lengths, pair, ngain, nbias, proj_w, gate_w],
         [(pair.shape, BF16), (ngain.shape, F32), (nbias.shape, F32), (proj_w.shape, BF16),
          (gate_w.shape, BF16), pltpu.SemaphoreType.DMA((5,)), wts, big],
         4 * dense, 1, far=True,
     )
     edge0 = exchange(sent).reshape(grid[0])
-    pair_t, outgate0 = call(
-        out_gate_kernel, "out_gate", [tile, wide], [pair, normed0, outgate_w], (), dense,
-    )
     (here,) = call(
         functools.partial(triangle_kernel, False), "outgoing", [tri_grid], [edge0], (), triangle,
     )
     tri0 = exchange(here.reshape(tri[0]))
-    sent, mid_t, normed1, scaled_mid0, inverse_mid0 = call(
-        between_kernel, "between", [edge, tile, tile, wide, row],
-        [lengths, tri0, pair_t, outgate0, ngain, nbias, mgain, mbias, out_w, proj_w, gate_w],
-        [wts, big], 5 * dense, 1,
+    sent, mid_t, normed1, *factors1, outgate0, scaled_mid0, inverse_mid0 = call(
+        between_kernel, "between", [edge, tile, *saved, wide, wide, row],
+        [lengths, tri0, pair, normed0, ngain, nbias, mgain, mbias, out_w, outgate_w, proj_w,
+         gate_w],
+        [wts, big], 6 * dense, 1,
     )
     edge1 = exchange(sent).reshape(grid[0])
-    cot_t, outgate1, d_outer1, d_unit1 = call(
-        upstream_kernel, "upstream", [wide, wide, tile, wide],
-        [cotangent, normed1, out_w, outgate_w], (), 2 * dense,
-    )
     (here,) = call(
         functools.partial(triangle_kernel, True), "incoming", [tri_grid], [edge1], (), triangle,
     )
     tri1 = exchange(here.reshape(tri[0]))
-    (sent,) = call(turn_kernel, "turn", [tri], [tri1, d_unit1, mgain], [mid], dense)
+    sent, new_pair, cot_t, d_normed_gate1, out_grads1, small1 = call(
+        turn_kernel, "turn", [tri, (pair.shape, BF16), wide, wide, out_rows, small(2)],
+        [tri1, mid_t, normed1, cotangent, mgain, mbias, out_w, outgate_w],
+        [mid, flat, flat, flat, flat, sums(2)], 6 * dense,
+    )
     d_tri1 = exchange(sent).reshape(tri_grid[0])
-    new_pair, d_normed_gate1, out_grads1, small1 = call(
-        behind_turn_kernel, "behind_turn", [(pair.shape, BF16), wide, out_rows, small(2)],
-        [tri1, mid_t, normed1, outgate1, cot_t, d_outer1, d_unit1, mgain, mbias, out_w, outgate_w],
-        [mid, flat, flat, flat, flat, sums(2)], 4 * dense,
-    )
     (sent,) = call(
         functools.partial(edge_grad_kernel, True), "incoming_grad", [grid], [edge1, d_tri1],
         (), 2 * triangle,
     )
     d_edge1 = exchange(sent.reshape(edge[0]))
-    proj_factor1, gate_factor1, scaled1, inverse1 = call(
-        functools.partial(edge_factor_kernel, 1), "edge_factors_upper",
-        [factor, factor, wide, row], [lengths, mid_t, normed1, proj_w, gate_w], [wts],
-        4 * dense, 1,
-    )
-    sent, grad, d_in1, d_normed1, d_unit0 = call(
-        middle_kernel, "middle", [tri, wide, d_in, wide, wide],
+    proj_factor1, gate_factor1, scaled1, inverse1 = factors1
+    sent, grad, d_normed_gate0, out_grads0, in_grads1, small_middle = call(
+        middle_kernel, "middle", [tri, wide, wide, out_rows, in_rows, small(4)],
         [d_edge1, proj_factor1, gate_factor1, d_normed_gate1, scaled1, inverse1, cot_t, outgate0,
-         scaled_mid0, inverse_mid0, ngain, mgain, proj_w, gate_w, out_w],
-        [big, mid], 5 * dense, grant=24,
+         scaled_mid0, inverse_mid0, normed0, normed1, ngain, mgain, mbias, proj_w, gate_w, out_w,
+         outgate_w],
+        [big, mid, flat, flat, flat, flat, flat, flat_in, sums(4)], 13 * dense,
     )
     d_tri0 = exchange(sent).reshape(tri_grid[0])
-    d_normed_gate0, out_grads0, in_grads1, small_middle = call(
-        behind_middle_kernel, "behind_middle", [wide, out_rows, in_rows, small(4)],
-        [grad, outgate0, scaled_mid0, d_unit0, normed0, d_in1, normed1, d_normed1, scaled1,
-         mgain, mbias, out_w, outgate_w],
-        [flat, flat, flat, flat, flat, flat_in, sums(4)], 8 * dense, grant=24,
-    )
     (sent,) = call(
         functools.partial(edge_grad_kernel, False), "outgoing_grad", [grid], [edge0, d_tri0],
         (), 2 * triangle,
     )
     d_edge0 = exchange(sent.reshape(edge[0]))
-    proj_factor0, gate_factor0, scaled0, inverse0 = call(
-        functools.partial(edge_factor_kernel, 0), "edge_factors_lower",
-        [factor, factor, wide, row], [lengths, pair_t, normed0, proj_w, gate_w], [wts],
-        4 * dense, 1,
-    )
     share = 12 * H // shards
-    packed, d_in0 = call(
-        finish_kernel, "finish", [((12 * H, H), BF16), d_in],
-        [d_edge0, proj_factor0, gate_factor0, normed0, out_grads0, in_grads1, out_grads1],
-        [big, flat, flat_in], 4 * dense,
+    proj_factor0, gate_factor0, scaled0, inverse0 = factors0
+    packed, grad_pair, small0 = call(
+        finish_kernel, "finish", [((12 * H, H), BF16), (pair.shape, BF16), small(2)],
+        [d_edge0, proj_factor0, gate_factor0, d_normed_gate0, scaled0, inverse0, grad, normed0,
+         ngain, proj_w, gate_w, out_grads0, in_grads1, out_grads1],
+        [big, flat, flat_in, sums(2)], 8 * dense,
     )
     parts = exchange(packed.reshape(shards, share, H))
-    grad_pair, small0 = call(
-        behind_finish_kernel, "behind_finish", [(pair.shape, BF16), small(2)],
-        [d_in0, d_normed_gate0, grad, scaled0, inverse0, ngain, proj_w, gate_w], [sums(2)],
-        4 * dense,
-    )
     (shared,) = call(
         sum_kernel, "sum_weights", [((shards, share + 16, H), BF16)],
         [parts, small0, small_middle, small1],

time: 291 us -> 264 us (0.907)
  blocking collectives: 118 us -> 230 us
  local copies, waits for them, and re-layouts: 67.4 us -> 4.83 us
  waiting for transfers between devices: 35.2 us -> 0 us
  Pallas kernels: 47.6 us -> 27 us
  starting transfers between devices: 18.6 us -> 0 us
    all_to_all x5 -> x10, blocking collectives: 118 us -> 230 us  [exchange(): lax.all_to_all(values, ('row', 'col'), split_axis=0, concat_axis=0, tiled...]
    unnamed x164 -> x28, local copies, waits for them, and re-layouts: 66.9 us -> 4.25 us
    all_to_all x5 -> x0, waiting for transfers between devices: 35.2 us -> none  [exchange(): lax.all_to_all(values, ('row', 'col'), split_axis=0, concat_axis=0, tiled...]
    pallas_call x18 -> x11, Pallas kernels: 47.6 us -> 27 us  [call(): pl.pallas_call(kernel, name=name, out_shape=shapes, in_specs=[SCALARS] *...]
    all_to_all x5 -> x0, starting transfers between devices: 18.6 us -> none  [exchange(): lax.all_to_all(values, ('row', 'col'), split_axis=0, concat_axis=0, tiled...]
  transfers between devices with their start and end apart: 5 -> 0, of which waited for: 5 -> 0; matrix products, arithmetic and copies ran while one was open for 0% -> 0% of each run, Pallas kernels for 8% -> 0%
where the time goes in v4:
time: 264 us; the launch traced here: 263 us
  blocking collectives  230 us (87%)
  Pallas kernels  27 us (10%)
  local copies, waits for them, and re-layouts  4.83 us (2%)
    all_to_all x10, blocking collectives, exchange(): lax.all_to_all(values, ('row', 'col'), split_axis=0, concat_axis=0, tiled...  230 us
    pallas_call x11, Pallas kernels, call(): pl.pallas_call(kernel, name=name, out_shape=shapes, in_specs=[SCALARS] *...  27 us

profile of v4, /device:TPU:0, one launch (start us, length us, event | category | flops | bytes accessed | tf_op | source)
XLA Modules:
  0.0 263.3 jit_solution(7510310412174575718)
XLA Ops:
  1.3 0.0 copy-start
  1.3 0.9 copy-done
  2.2 0.0 copy-start.2
  2.2 0.9 copy-done.2
  3.1 0.0 copy-start.6
  3.1 1.0 copy-done.6
  4.1 0.0 copy-start.11
  4.1 0.7 copy-done.11
  4.8 0.0 copy-start.13
  4.8 0.7 copy-done.13
  5.5 3.1 %start.1 = (bf16[32,2,4,16,128]{4,3,2,1,0:T(8,128)(2,1)S(1)}, bf16[16,128,128]{2,1,0:T(8,128)(2,1)S(1)}, f32[16,256,128]{2,1,0:T(8,128)S(1)}, f32[16,256,128]{2,...) custom-call(s32[1]{0:T(128)S(6)} %copy.29.lengths, bf16[16,128,128]{2,1,0:T(8,128)(2,1)S(1)} %copy-done.6, ...), custom_call_target="tpu_custom_call" | custom-call | flops 268435456 | bytes 7612420 | tf_op jit(solution)/shard_map/start/pallas_call | solution.py:441
  8.6 0.0 copy-start.4
  8.6 0.0 copy-start.5
  8.6 0.0 copy-start.7
  8.6 0.0 copy-start.9
  8.7 0.0 copy-start.10
  8.7 33.3 %all_to_all.50 = bf16[32,2,4,16,128]{4,3,2,1,0:T(8,128)(2,1)S(1)} all-to-all(bf16[32,2,4,16,128]{4,3,2,1,0:T(8,128)(2,1)S(1)} %get-tuple-element.46), channel_id=1, replica_groups=mesh['grp'=1,'row'=16,'col'=2,'ch'=1] {'row','col'}, dimensions={0} | all-to-all | bytes 2097152 | tf_op jit(solution)/shard_map/all_to_all | solution.py:456
  42.0 0.3 outgoing.1
  42.3 18.4 %all_to_all.51.tri = bf16[32,4,16,128]{3,2,1,0:T(8,128)(2,1)S(1)} all-to-all(bf16[32,4,16,128]{3,2,1,0:T(8,128)(2,1)S(1)} %bitcast.30), channel_id=1, replica_groups=mesh['grp'=1,'row'=16,'col'=2,'ch'=1] {'row','col'}, dimensions={0} | all-to-all | bytes 1048576 | tf_op jit(solution)/shard_map/all_to_all | solution.py:456
  60.8 0.0 copy-done.4
  60.8 0.0 copy-done.5
  60.8 0.0 copy-done.7
  60.8 0.0 copy-done.9
  60.8 0.0 copy-done.10
  60.8 4.7 %between.1 = (bf16[32,2,4,16,128]{4,3,2,1,0:T(8,128)(2,1)S(1)}, bf16[16,128,128]{2,1,0:T(8,128)(2,1)S(1)}, bf16[16,128,128]{2,1,0:T(8,128)(2,1)S(1)}, f32[16,256...) custom-call(s32[1]{0:T(128)S(6)} %copy.29.lengths, ...), custom_call_target="tpu_custom_call" | custom-call | flops 402653184 | bytes 11423748 | tf_op jit(solution)/shard_map/between/pallas_call | solution.py:441
  65.6 0.0 copy-start.8
  65.6 29.7 %all_to_all.52 = bf16[32,2,4,16,128]{4,3,2,1,0:T(8,128)(2,1)S(1)} all-to-all(bf16[32,2,4,16,128]{4,3,2,1,0:T(8,128)(2,1)S(1)} %get-tuple-element.48), channel_id=1, replica_groups=mesh['grp'=1,'row'=16,'col'=2,'ch'=1] {'row','col'}, dimensions={0} | all-to-all | bytes 2097152 | tf_op jit(solution)/shard_map/all_to_all | solution.py:456
  95.2 0.3 incoming.1
  95.6 18.4 %all_to_all.53.tri = bf16[32,4,16,128]{3,2,1,0:T(8,128)(2,1)S(1)} all-to-all(bf16[32,4,16,128]{3,2,1,0:T(8,128)(2,1)S(1)} %bitcast.31), channel_id=1, replica_groups=mesh['grp'=1,'row'=16,'col'=2,'ch'=1] {'row','col'}, dimensions={0} | all-to-all | bytes 1048576 | tf_op jit(solution)/shard_map/all_to_all | solution.py:456
  114.0 0.0 copy-done.8
  114.0 3.6 %turn.1 = (bf16[32,4,16,128]{3,2,1,0:T(8,128)(2,1)S(1)}, bf16[16,128,128]{2,1,0:T(8,128)(2,1)}, f32[16,128,128]{2,1,0:T(8,128)S(1)}, f32[16,128,128]{2,1,0:T(8,1...) custom-call(bf16[32,4,16,128]{3,2,1,0:T(8,128)(2,1)S(1)} %all_to_all.53.tri, ...), custom_call_target="tpu_custom_call" | custom-call | flops 402653184 | bytes 5442560 | tf_op jit(solution)/shard_map/turn/pallas_call | solution.py:441
  117.6 18.4 %all_to_all.54 = bf16[32,4,16,128]{3,2,1,0:T(8,128)(2,1)S(1)} all-to-all(bf16[32,4,16,128]{3,2,1,0:T(8,128)(2,1)S(1)} %get-tuple-element.52), channel_id=1, replica_groups=mesh['grp'=1,'row'=16,'col'=2,'ch'=1] {'row','col'}, dimensions={0} | all-to-all | bytes 1048576 | tf_op jit(solution)/shard_map/all_to_all | solution.py:456
  136.0 0.0 copy-start.1
  136.0 0.0 copy-start.3
  136.0 0.0 copy-start.12
  136.0 0.4 incoming_grad.1
  136.5 29.7 %all_to_all.55.d_edge = bf16[32,2,4,16,128]{4,3,2,1,0:T(8,128)(2,1)S(1)} all-to-all(bf16[32,2,4,16,128]{4,3,2,1,0:T(8,128)(2,1)S(1)} %bitcast.26), channel_id=1, replica_groups=mesh['grp'=1,'row'=16,'col'=2,'ch'=1] {'row','col'}, dimensions={0} | all-to-all | bytes 2097152 | tf_op jit(solution)/shard_map/all_to_all | solution.py:456
  166.1 0.0 copy-done.1
  166.1 0.0 copy-done.3
  166.2 0.0 copy-done.12
  166.2 9.3 %middle.1 = (bf16[32,4,16,128]{3,2,1,0:T(8,128)(2,1)S(1)}, f32[16,128,128]{2,1,0:T(8,128)S(1)}, f32[16,128,128]{2,1,0:T(8,128)S(1)}, bf16[256,128]{1,0:T(8,128)(...) custom-call(bf16[32,2,4,16,128]{4,3,2,1,0:T(8,128)(2,1)S(1)} %all_to_all.55.d_edge, ...), custom_call_target="tpu_custom_call" | custom-call | flops 872415232 | bytes 14767104 | tf_op jit(solution)/shard_map/middle/pallas_call | solution.py:441
  175.4 18.4 %all_to_all.56 = bf16[32,4,16,128]{3,2,1,0:T(8,128)(2,1)S(1)} all-to-all(bf16[32,4,16,128]{3,2,1,0:T(8,128)(2,1)S(1)} %get-tuple-element.62), channel_id=1, replica_groups=mesh['grp'=1,'row'=16,'col'=2,'ch'=1] {'row','col'}, dimensions={0} | all-to-all | bytes 1048576 | tf_op jit(solution)/shard_map/all_to_all | solution.py:456
  193.9 0.5 outgoing_grad.1
  194.3 29.7 %all_to_all.57.d_edge = bf16[32,2,4,16,128]{4,3,2,1,0:T(8,128)(2,1)S(1)} all-to-all(bf16[32,2,4,16,128]{4,3,2,1,0:T(8,128)(2,1)S(1)} %bitcast.27), channel_id=1, replica_groups=mesh['grp'=1,'row'=16,'col'=2,'ch'=1] {'row','col'}, dimensions={0} | all-to-all | bytes 2097152 | tf_op jit(solution)/shard_map/all_to_all | solution.py:456
  224.0 3.7 %finish.1 = (bf16[1536,128]{1,0:T(8,128)(2,1)S(1)}, bf16[16,128,128]{2,1,0:T(8,128)(2,1)}, f32[2,128]{1,0:T(2,128)S(1)}) custom-call(bf16[32,2,4,16,128]{4,3,2,1,0:T(8,128)(2,1)S(1)} %all_to_all.57.d_edge, f32[16,256,128]{2,1,0:T(8,128)S(1)} %get-tuple-element.63.proj_factor, f32[16,256,128]{2,1,0:T(8,128)S(1)} %get-tuple-element.64.gate_factor, ...), custom_call_target="tpu_custom_call" | custom-call | flops 536870912 | bytes 10364928 | tf_op jit(solution)/shard_map/finish/pallas_call | solution.py:441
  227.7 16.2 %all_to_all.58.parts = bf16[32,48,128]{2,1,0:T(8,128)(2,1)S(1)} all-to-all(bf16[32,48,128]{2,1,0:T(8,128)(2,1)S(1)} %bitcast.32), channel_id=1, replica_groups=mesh['grp'=1,'row'=16,'col'=2,'ch'=1] {'row','col'}, dimensions={0} | all-to-all | bytes 786432 | tf_op jit(solution)/shard_map/all_to_all | solution.py:456
  243.9 0.1 sum_weights.1
  244.0 17.9 %all_to_all.59.shared = bf16[32,64,128]{2,1,0:T(8,128)(2,1)S(1)} all-to-all(bf16[32,64,128]{2,1,0:T(8,128)(2,1)S(1)} %sum_weights.1), channel_id=1, replica_groups=mesh['grp'=1,'row'=16,'col'=2,'ch'=1] {'row','col'}, dimensions={0} | all-to-all | bytes 1048576 | tf_op jit(solution)/shard_map/all_to_all | solution.py:456
  261.9 0.9 unpack.1
  262.8 0.6 fusion
Async XLA Ops:
  1.3 0.9 copy-start
  2.2 0.9 copy-start.2
  3.1 1.0 copy-start.6
  4.1 0.7 copy-start.11
  4.8 0.7 copy-start.13
  8.6 52.2 %copy-start.4 = (bf16[2,128,128]{2,1,0:T(8,128)(2,1)S(1)}, bf16[2,128,128]{2,1,0:T(8,128)(2,1)}, u32[]{:S(2)}) copy-start(bf16[2,128,128]{2,1,0:T(8,128)(2,1)} %out_w.5) | copy-start | bytes 196612
  8.6 52.2 %copy-start.5 = (bf16[2,128,128]{2,1,0:T(8,128)(2,1)S(1)}, bf16[2,128,128]{2,1,0:T(8,128)(2,1)}, u32[]{:S(2)}) copy-start(bf16[2,128,128]{2,1,0:T(8,128)(2,1)} %outgate_w.5) | copy-start | bytes 196612
  8.6 52.2 %copy-start.7 = (bf16[16,128,128]{2,1,0:T(8,128)(2,1)S(1)}, bf16[16,128,128]{2,1,0:T(8,128)(2,1)}, u32[]{:S(2)}) copy-start(bf16[16,128,128]{2,1,0:T(8,128)(2,1)} %pair.1) | copy-start | bytes 1572868
  8.6 52.1 %copy-start.9 = (f32[2,128]{1,0:T(2,128)S(1)}, f32[2,128]{1,0:T(2,128)}, u32[]{:S(2)}) copy-start(f32[2,128]{1,0:T(2,128)} %mgain.5) | copy-start | bytes 3076
  8.7 52.1 %copy-start.10 = (f32[2,128]{1,0:T(2,128)S(1)}, f32[2,128]{1,0:T(2,128)}, u32[]{:S(2)}) copy-start(f32[2,128]{1,0:T(2,128)} %mbias.5) | copy-start | bytes 3076
  65.6 48.5 %copy-start.8 = (bf16[16,128,128]{2,1,0:T(8,128)(2,1)S(1)}, bf16[16,128,128]{2,1,0:T(8,128)(2,1)}, u32[]{:S(2)}) copy-start(bf16[16,128,128]{2,1,0:T(8,128)(2,1)} %cot.1) | copy-start | bytes 1572868
  136.0 30.1 %copy-start.1 = (bf16[2,2,128,128]{3,2,1,0:T(8,128)(2,1)S(1)}, bf16[2,2,128,128]{3,2,1,0:T(8,128)(2,1)}, u32[]{:S(2)}) copy-start(bf16[2,2,128,128]{3,2,1,0:T(8,128)(2,1)} %proj_w.5) | copy-start | bytes 393220
  136.0 30.1 %copy-start.3 = (bf16[2,2,128,128]{3,2,1,0:T(8,128)(2,1)S(1)}, bf16[2,2,128,128]{3,2,1,0:T(8,128)(2,1)}, u32[]{:S(2)}) copy-start(bf16[2,2,128,128]{3,2,1,0:T(8,128)(2,1)} %gate_w.5) | copy-start | bytes 393220
  136.0 30.1 %copy-start.12 = (f32[2,128]{1,0:T(2,128)S(1)}, f32[2,128]{1,0:T(2,128)}, u32[]{:S(2)}) copy-start(f32[2,128]{1,0:T(2,128)} %ngain.5) | copy-start | bytes 3076

commit v5 on v4

--- a/solution.py
+++ b/solution.py
@@ -320,7 +320,7 @@
         sums[0] += d_unit * scaled
         sums[1] += d_unit
 
-    each_row(rows, 4, body)
+    each_row(rows, 2, body)
     d_tri_out[...] = scr_tri[...].reshape(d_tri_out.shape).astype(BF16)
     out_weight_grads(unit_all, outer_all, normed_all, gate_all, out_weights)
     in_weight_grads(upper_all, d_in_all, in_weights)
@@ -363,27 +363,34 @@
         small_out[index : index + 1, :] = as_row(sums[index])
 
 
-def sum_kernel(parts, small0, small_middle, small1, shared_out):
-    shards, share, width = parts.shape
-    own = jnp.sum(parts[...].astype(F32), axis=0).astype(BF16)
+def sum_kernel(parts, small0, small_middle, small1, own_out):
+    share = parts.shape[1]
+    own_out[0:share, :] = jnp.sum(parts[...].astype(F32), axis=0).astype(BF16)
     small = jnp.concatenate(
         [small0[...], small_middle[0:2], small_middle[2:4], small1[...]], axis=0
     )
     high = small.astype(BF16).astype(F32)
-    extra = jnp.concatenate([high, small - high], axis=0).astype(BF16)
+    own_out[share:, :] = jnp.concatenate([high, small - high], axis=0).astype(BF16)
+
+
+def unpack_kernel(
+    share, steps, few, shared, proj_out, gate_out, out_out, outgate_out, small_out, weights
+):
+    shards, _, width = shared.shape
+    me = lax.axis_index("row") * few + lax.axis_index("col")
+    total = jnp.zeros(small_out.shape, F32)
     for shard in range(shards):
-        shared_out[shard, 0:share] = own
-        shared_out[shard, share:] = extra
-
-
-def unpack_kernel(share, shared, proj_out, gate_out, out_out, outgate_out, small_out):
-    shards, _, width = shared.shape
-    total = jnp.sum(shared[:, share:, :].astype(F32), axis=0)
-    small_out[...] = total[0:8] + total[8:16]
-    weights = shared[:, 0:share, :].reshape(shards * share, width).astype(F32)
+        apart = me ^ shard
+        place = 0
+        for order, mask in enumerate(steps):
+            place = place + jnp.where((apart & mask) != 0, 1 << order, 0)
+        weights[shard * share : (shard + 1) * share, :] = shared[place, 0:share].astype(F32)
+        extra = shared[place, share:].astype(F32)
+        total = total + extra[0:8] + extra[8:16]
+    small_out[...] = total
     for module in range(2):
         blocks = [
-            weights[(6 * module + part) * width : (6 * module + part + 1) * width]
+            weights[(6 * module + part) * width : (6 * module + part + 1) * width, :]
             for part in range(6)
         ]
         for side in range(2):
@@ -454,6 +461,20 @@
 
 def exchange(values):
     return lax.all_to_all(values, ("row", "col"), split_axis=0, concat_axis=0, tiled=True)
+
+
+def doubling_steps(many, few):
+    far = [("row", 1 << bit) for bit in range(many.bit_length() - 2, 0, -1)]
+    return far + [("col", 1 << bit) for bit in range(few.bit_length() - 1)] + [("row", 1)]
+
+
+def gather_apart(own, many, few):
+    have = own[None]
+    for axis, mask in doubling_steps(many, few):
+        size = many if axis == "row" else few
+        pairs = [(index, index ^ mask) for index in range(size)]
+        have = jnp.concatenate([have, lax.ppermute(have, axis, pairs)], axis=0)
+    return have
 
 
 def grouped_device(
@@ -490,8 +511,12 @@
         return ((count, H), F32)
 
     saved = [tile, factor, factor, wide, row]
+    far = [
+        pltpu.with_memory_space_constraint(item, pltpu.HBM)
+        for item in (pair, ngain, nbias, proj_w, gate_w)
+    ]
     sent, normed0, *factors0 = call(
-        start_kernel, "start", [edge, *saved], [lengths, pair, ngain, nbias, proj_w, gate_w],
+        start_kernel, "start", [edge, *saved], [lengths, *far],
         [(pair.shape, BF16), (ngain.shape, F32), (nbias.shape, F32), (proj_w.shape, BF16),
          (gate_w.shape, BF16), pltpu.SemaphoreType.DMA((5,)), wts, big],
         4 * dense, 1, far=True,
@@ -546,16 +571,17 @@
         [big, flat, flat_in, sums(2)], 8 * dense,
     )
     parts = exchange(packed.reshape(shards, share, H))
-    (shared,) = call(
-        sum_kernel, "sum_weights", [((shards, share + 16, H), BF16)],
+    (own,) = call(
+        sum_kernel, "sum_weights", [((share + 16, H), BF16)],
         [parts, small0, small_middle, small1],
     )
-    shared = exchange(shared)
+    shared = gather_apart(own, many, few)
+    steps = [mask * few if axis == "row" else mask for axis, mask in doubling_steps(many, few)]
     grad_proj, grad_gate, grad_out, grad_outgate, small_all = call(
-        functools.partial(unpack_kernel, share), "unpack",
+        functools.partial(unpack_kernel, share, steps, few), "unpack",
         [(proj_w.shape, F32), (gate_w.shape, F32), (out_w.shape, F32), (outgate_w.shape, F32),
          small(8)],
-        [shared],
+        [shared], [((shards * share, H), F32)],
     )
     small_all = small_all.reshape(2, 4, H)
     return (
@@ -839,7 +865,7 @@
         P("grp", None, None),
     )
     many, few = mesh.shape["row"], mesh.shape["col"]
-    if mesh.shape["ch"] == 1 and H % (many * few) == 0:
+    if mesh.shape["ch"] == 1 and H % (many * few) == 0 and many & (many - 1) == 0:
         body = functools.partial(grouped_device, many=many, few=few)
     else:
         body = per_device

time: 264 us -> 263 us (level)
  blocking collectives: 230 us -> 212 us
  waiting for transfers between devices: 0 us -> 15.8 us
  local copies, waits for them, and re-layouts: 4.83 us -> 0.8 us
  starting transfers between devices: 0 us -> 3.94 us
    all_to_all x10 -> x9, blocking collectives: 230 us -> 212 us  [exchange(): lax.all_to_all(values, ('row', 'col'), split_axis=0, concat_axis=0, tiled...]
    ppermute x0 -> x5, waiting for transfers between devices: none -> 15.8 us  [gather_apart(): have = jnp.concatenate([have, lax.ppermute(have, axis, pairs)], axis=0)]
    unnamed x28 -> x24, local copies, waits for them, and re-layouts: 4.25 us -> 0.12 us
    ppermute x0 -> x5, starting transfers between devices: none -> 3.94 us  [gather_apart(): have = jnp.concatenate([have, lax.ppermute(have, axis, pairs)], axis=0)]
  transfers between devices with their start and end apart: 0 -> 5, of which waited for: 0 -> 5; matrix products, arithmetic and copies ran while one was open for 0% -> 0% of each run, Pallas kernels for 0% -> 0%
where the time goes in v5:
time: 263 us
  blocking collectives  212 us (81%)
  Pallas kernels  28.7 us (11%)
  waiting for transfers between devices  15.8 us (6%)
  starting transfers between devices  3.94 us (1%)
    all_to_all x9, blocking collectives, exchange(): lax.all_to_all(values, ('row', 'col'), split_axis=0, concat_axis=0, tiled...  212 us
    pallas_call x11, Pallas kernels, call(): pl.pallas_call(kernel, name=name, out_shape=shapes, in_specs=[SCALARS] *...  28.7 us
    ppermute x5, waiting for transfers between devices, gather_apart(): have = jnp.concatenate([have, lax.ppermute(have, axis, pairs)], axis=0)  15.8 us
  transfers between devices with their start and end apart: 5, of which 5 were waited for; matrix products, arithmetic and copies ran while one was open for 0% of the time, Pallas kernels for 0%

profile of v5, /device:TPU:0, one launch (start us, length us, event | category | flops | bytes accessed | tf_op | source)
XLA Modules:
  0.0 263.0 jit_solution(13704433377361186166)
XLA Ops:
  1.3 4.1 %start.1 = (bf16[32,2,4,16,128]{4,3,2,1,0:T(8,128)(2,1)S(1)}, bf16[16,128,128]{2,1,0:T(8,128)(2,1)S(1)}, f32[16,256,128]{2,1,0:T(8,128)S(1)}, f32[16,256,128]{2,...) custom-call(s32[1]{0:T(128)S(6)} %copy.38.lengths, bf16[16,128,128]{2,1,0:T(8,128)(2,1)} %pair.1, ...), custom_call_target="tpu_custom_call" | custom-call | flops 268435456 | bytes 7612420 | tf_op jit(solution)/shard_map/start/pallas_call | solution.py:448
  5.4 0.0 copy-start
  5.4 0.0 copy-start.1
  5.4 0.0 copy-start.2
  5.4 0.0 copy-start.3
  5.4 0.0 copy-start.4
  5.4 0.0 copy-start.6
  5.4 0.0 copy-start.7
  5.5 0.0 copy-start.8
  5.5 0.0 copy-start.9
  5.5 33.3 %all_to_all.45 = bf16[32,2,4,16,128]{4,3,2,1,0:T(8,128)(2,1)S(1)} all-to-all(bf16[32,2,4,16,128]{4,3,2,1,0:T(8,128)(2,1)S(1)} %get-tuple-element.46), channel_id=1, replica_groups=mesh['grp'=1,'row'=16,'col'=2,'ch'=1] {'row','col'}, dimensions={0} | all-to-all | bytes 2097152 | tf_op jit(solution)/shard_map/all_to_all | solution.py:463
  38.8 0.3 outgoing.1
  39.2 18.4 %all_to_all.46.tri = bf16[32,4,16,128]{3,2,1,0:T(8,128)(2,1)S(1)} all-to-all(bf16[32,4,16,128]{3,2,1,0:T(8,128)(2,1)S(1)} %bitcast.33), channel_id=1, replica_groups=mesh['grp'=1,'row'=16,'col'=2,'ch'=1] {'row','col'}, dimensions={0} | all-to-all | bytes 1048576 | tf_op jit(solution)/shard_map/all_to_all | solution.py:463
  57.6 0.0 copy-done
  57.6 0.0 copy-done.1
  57.6 0.0 copy-done.2
  57.6 0.0 copy-done.3
  57.6 0.0 copy-done.4
  57.6 0.0 copy-done.6
  57.6 0.0 copy-done.7
  57.6 0.0 copy-done.8
  57.7 0.0 copy-done.9
  57.7 4.7 %between.1 = (bf16[32,2,4,16,128]{4,3,2,1,0:T(8,128)(2,1)S(1)}, bf16[16,128,128]{2,1,0:T(8,128)(2,1)S(1)}, bf16[16,128,128]{2,1,0:T(8,128)(2,1)S(1)}, f32[16,256...) custom-call(s32[1]{0:T(128)S(6)} %copy.38.lengths, ...), custom_call_target="tpu_custom_call" | custom-call | flops 402653184 | bytes 11423748 | tf_op jit(solution)/shard_map/between/pallas_call | solution.py:448
  62.4 0.0 copy-start.5
  62.4 29.7 %all_to_all.47 = bf16[32,2,4,16,128]{4,3,2,1,0:T(8,128)(2,1)S(1)} all-to-all(bf16[32,2,4,16,128]{4,3,2,1,0:T(8,128)(2,1)S(1)} %get-tuple-element.48), channel_id=1, replica_groups=mesh['grp'=1,'row'=16,'col'=2,'ch'=1] {'row','col'}, dimensions={0} | all-to-all | bytes 2097152 | tf_op jit(solution)/shard_map/all_to_all | solution.py:463
  92.1 0.3 incoming.1
  92.4 18.4 %all_to_all.48.tri = bf16[32,4,16,128]{3,2,1,0:T(8,128)(2,1)S(1)} all-to-all(bf16[32,4,16,128]{3,2,1,0:T(8,128)(2,1)S(1)} %bitcast.34), channel_id=1, replica_groups=mesh['grp'=1,'row'=16,'col'=2,'ch'=1] {'row','col'}, dimensions={0} | all-to-all | bytes 1048576 | tf_op jit(solution)/shard_map/all_to_all | solution.py:463
  110.9 0.0 copy-done.5
  110.9 3.6 %turn.1 = (bf16[32,4,16,128]{3,2,1,0:T(8,128)(2,1)S(1)}, bf16[16,128,128]{2,1,0:T(8,128)(2,1)}, f32[16,128,128]{2,1,0:T(8,128)S(1)}, f32[16,128,128]{2,1,0:T(8,1...) custom-call(bf16[32,4,16,128]{3,2,1,0:T(8,128)(2,1)S(1)} %all_to_all.48.tri, ...), custom_call_target="tpu_custom_call" | custom-call | flops 402653184 | bytes 5442560 | tf_op jit(solution)/shard_map/turn/pallas_call | solution.py:448
  114.5 18.4 %all_to_all.49 = bf16[32,4,16,128]{3,2,1,0:T(8,128)(2,1)S(1)} all-to-all(bf16[32,4,16,128]{3,2,1,0:T(8,128)(2,1)S(1)} %get-tuple-element.52), channel_id=1, replica_groups=mesh['grp'=1,'row'=16,'col'=2,'ch'=1] {'row','col'}, dimensions={0} | all-to-all | bytes 1048576 | tf_op jit(solution)/shard_map/all_to_all | solution.py:463
  132.9 0.4 incoming_grad.1
  133.3 29.7 %all_to_all.50.d_edge = bf16[32,2,4,16,128]{4,3,2,1,0:T(8,128)(2,1)S(1)} all-to-all(bf16[32,2,4,16,128]{4,3,2,1,0:T(8,128)(2,1)S(1)} %bitcast.29), channel_id=1, replica_groups=mesh['grp'=1,'row'=16,'col'=2,'ch'=1] {'row','col'}, dimensions={0} | all-to-all | bytes 2097152 | tf_op jit(solution)/shard_map/all_to_all | solution.py:463
  163.0 9.8 %middle.1 = (bf16[32,4,16,128]{3,2,1,0:T(8,128)(2,1)S(1)}, f32[16,128,128]{2,1,0:T(8,128)S(1)}, f32[16,128,128]{2,1,0:T(8,128)S(1)}, bf16[256,128]{1,0:T(8,128)(...) custom-call(bf16[32,2,4,16,128]{4,3,2,1,0:T(8,128)(2,1)S(1)} %all_to_all.50.d_edge, ...), custom_call_target="tpu_custom_call" | custom-call | flops 872415232 | bytes 14767104 | tf_op jit(solution)/shard_map/middle/pallas_call | solution.py:448
  172.8 18.4 %all_to_all.51 = bf16[32,4,16,128]{3,2,1,0:T(8,128)(2,1)S(1)} all-to-all(bf16[32,4,16,128]{3,2,1,0:T(8,128)(2,1)S(1)} %get-tuple-element.62), channel_id=1, replica_groups=mesh['grp'=1,'row'=16,'col'=2,'ch'=1] {'row','col'}, dimensions={0} | all-to-all | bytes 1048576 | tf_op jit(solution)/shard_map/all_to_all | solution.py:463
  191.2 0.5 outgoing_grad.1
  191.7 29.7 %all_to_all.52.d_edge = bf16[32,2,4,16,128]{4,3,2,1,0:T(8,128)(2,1)S(1)} all-to-all(bf16[32,2,4,16,128]{4,3,2,1,0:T(8,128)(2,1)S(1)} %bitcast.30), channel_id=1, replica_groups=mesh['grp'=1,'row'=16,'col'=2,'ch'=1] {'row','col'}, dimensions={0} | all-to-all | bytes 2097152 | tf_op jit(solution)/shard_map/all_to_all | solution.py:463
  221.4 3.7 %finish.1 = (bf16[1536,128]{1,0:T(8,128)(2,1)S(1)}, bf16[16,128,128]{2,1,0:T(8,128)(2,1)}, f32[2,128]{1,0:T(2,128)S(1)}) custom-call(bf16[32,2,4,16,128]{4,3,2,1,0:T(8,128)(2,1)S(1)} %all_to_all.52.d_edge, f32[16,256,128]{2,1,0:T(8,128)S(1)} %get-tuple-element.63.proj_factor, f32[16,256,128]{2,1,0:T(8,128)S(1)} %get-tuple-element.64.gate_factor, ...), custom_call_target="tpu_custom_call" | custom-call | flops 536870912 | bytes 10364928 | tf_op jit(solution)/shard_map/finish/pallas_call | solution.py:448
  225.1 16.2 %all_to_all.53.parts = bf16[32,48,128]{2,1,0:T(8,128)(2,1)S(1)} all-to-all(bf16[32,48,128]{2,1,0:T(8,128)(2,1)S(1)} %bitcast.39), channel_id=1, replica_groups=mesh['grp'=1,'row'=16,'col'=2,'ch'=1] {'row','col'}, dimensions={0} | all-to-all | bytes 786432 | tf_op jit(solution)/shard_map/all_to_all | solution.py:463
  241.3 0.1 sum_weights.1
  241.3 1.7 collective-permute-start
  243.1 3.2 %collective-permute-done = bf16[1,64,128]{2,1,0:T(8,128)(2,1)S(1)} collective-permute-done((bf16[1,64,128]{2,1,0:T(8,128)(2,1)S(1)}, bf16[1,64,128]{2,1,0:T(8,128)(2,1)S(1)}, u32[]{:S(2)}, u32[]{:S(2)}) %collective-permute-start) | collective-permute-done | bytes 16416 | tf_op jit(solution)/shard_map/ppermute | solution.py:476
  246.3 0.2 collective-permute-start.1
  246.5 3.7 %collective-permute-done.1 = bf16[2,64,128]{2,1,0:T(8,128)(2,1)S(1)} collective-permute-done((bf16[2,64,128]{2,1,0:T(8,128)(2,1)S(1)}, bf16[2,64,128]{2,1,0:T(8,128)(2,1)S(1)}, u32[]{:S(2)}, u32[]{:S(2)}) %collective-permute-start.1) | collective-permute-done | bytes 32800 | tf_op jit(solution)/shard_map/ppermute | solution.py:476
  250.2 0.7 collective-permute-start.2
  251.0 3.6 %collective-permute-done.2 = bf16[4,64,128]{2,1,0:T(8,128)(2,1)S(1)} collective-permute-done((bf16[4,64,128]{2,1,0:T(8,128)(2,1)S(1)}, bf16[4,64,128]{2,1,0:T(8,128)(2,1)S(1)}, u32[]{:S(2)}, u32[]{:S(2)}) %collective-permute-start.2) | collective-permute-done | bytes 65568 | tf_op jit(solution)/shard_map/ppermute | solution.py:476
  254.6 1.2 collective-permute-start.3
  255.9 3.7 %collective-permute-done.3 = bf16[8,64,128]{2,1,0:T(8,128)(2,1)S(1)} collective-permute-done((bf16[8,64,128]{2,1,0:T(8,128)(2,1)S(1)}, bf16[8,64,128]{2,1,0:T(8,128)(2,1)S(1)}, u32[]{:S(2)}, u32[]{:S(2)}) %collective-permute-start.3) | collective-permute-done | bytes 131104 | tf_op jit(solution)/shard_map/ppermute | solution.py:476
  259.6 0.1 constant_dynamic-update-slice_fusion
  259.7 0.1 collective-permute-start.4
  259.8 1.5 collective-permute-done.4
  261.3 1.1 unpack.1
  262.4 0.6 fusion
  (8 shorter events, 0.1 us)
Async XLA Ops:
  5.4 52.2 %copy-start = (bf16[2,2,128,128]{3,2,1,0:T(8,128)(2,1)S(1)}, bf16[2,2,128,128]{3,2,1,0:T(8,128)(2,1)}, u32[]{:S(2)}) copy-start(bf16[2,2,128,128]{3,2,1,0:T(8,128)(2,1)} %proj_w.5) | copy-start | bytes 393220
  5.4 52.2 %copy-start.1 = (bf16[2,2,128,128]{3,2,1,0:T(8,128)(2,1)S(1)}, bf16[2,2,128,128]{3,2,1,0:T(8,128)(2,1)}, u32[]{:S(2)}) copy-start(bf16[2,2,128,128]{3,2,1,0:T(8,128)(2,1)} %gate_w.5) | copy-start | bytes 393220
  5.4 52.2 %copy-start.2 = (bf16[2,128,128]{2,1,0:T(8,128)(2,1)S(1)}, bf16[2,128,128]{2,1,0:T(8,128)(2,1)}, u32[]{:S(2)}) copy-start(bf16[2,128,128]{2,1,0:T(8,128)(2,1)} %out_w.5) | copy-start | bytes 196612
  5.4 52.2 %copy-start.3 = (bf16[2,128,128]{2,1,0:T(8,128)(2,1)S(1)}, bf16[2,128,128]{2,1,0:T(8,128)(2,1)}, u32[]{:S(2)}) copy-start(bf16[2,128,128]{2,1,0:T(8,128)(2,1)} %outgate_w.5) | copy-start | bytes 196612
  5.4 52.2 %copy-start.4 = (bf16[16,128,128]{2,1,0:T(8,128)(2,1)S(1)}, bf16[16,128,128]{2,1,0:T(8,128)(2,1)}, u32[]{:S(2)}) copy-start(bf16[16,128,128]{2,1,0:T(8,128)(2,1)} %pair.1) | copy-start | bytes 1572868
  5.4 52.2 %copy-start.6 = (f32[2,128]{1,0:T(2,128)S(1)}, f32[2,128]{1,0:T(2,128)}, u32[]{:S(2)}) copy-start(f32[2,128]{1,0:T(2,128)} %mgain.5) | copy-start | bytes 3076
  5.4 52.2 %copy-start.7 = (f32[2,128]{1,0:T(2,128)S(1)}, f32[2,128]{1,0:T(2,128)}, u32[]{:S(2)}) copy-start(f32[2,128]{1,0:T(2,128)} %mbias.5) | copy-start | bytes 3076
  5.5 52.2 %copy-start.8 = (f32[2,128]{1,0:T(2,128)S(1)}, f32[2,128]{1,0:T(2,128)}, u32[]{:S(2)}) copy-start(f32[2,128]{1,0:T(2,128)} %ngain.5) | copy-start | bytes 3076
  5.5 52.2 %copy-start.9 = (f32[2,128]{1,0:T(2,128)S(1)}, f32[2,128]{1,0:T(2,128)}, u32[]{:S(2)}) copy-start(f32[2,128]{1,0:T(2,128)} %nbias.1) | copy-start | bytes 3076
  62.4 48.5 %copy-start.5 = (bf16[16,128,128]{2,1,0:T(8,128)(2,1)S(1)}, bf16[16,128,128]{2,1,0:T(8,128)(2,1)}, u32[]{:S(2)}) copy-start(bf16[16,128,128]{2,1,0:T(8,128)(2,1)} %cot.1) | copy-start | bytes 1572868
  241.3 4.9 %collective-permute-start = (bf16[1,64,128]{2,1,0:T(8,128)(2,1)S(1)}, bf16[1,64,128]{2,1,0:T(8,128)(2,1)S(1)}, u32[]{:S(2)}, u32[]{:S(2)}) collective-permute-start(bf16[1,64,128]{2,1,0:T(8,128)(2,1)S(1)} %bitcast.35), channel_id=1, source_target_pairs={{0,16},{2,18},{4,20},{6,22},{8,24},{10,26},{12,28},{14,30},{16,0},... | collective-permute-start | bytes 49160 | tf_op jit(solution)/shard_map/ppermute | solution.py:476
  246.3 3.9 %collective-permute-start.1 = (bf16[2,64,128]{2,1,0:T(8,128)(2,1)S(1)}, bf16[2,64,128]{2,1,0:T(8,128)(2,1)S(1)}, u32[]{:S(2)}, u32[]{:S(2)}) collective-permute-start(bf16[2,64,128]{2,1,0:T(8,128)(2,1)S(1)} %pad_maximum_fusion.2), channel_id=1, source_target_pairs={{0,8},{2,10},{4,12},{6,14},{8,0},{10,2},{12,4},{14,6},{16,24},{18,... | collective-permute-start | bytes 98312 | tf_op jit(solution)/shard_map/ppermute | solution.py:476
  250.2 4.3 %collective-permute-start.2 = (bf16[4,64,128]{2,1,0:T(8,128)(2,1)S(1)}, bf16[4,64,128]{2,1,0:T(8,128)(2,1)S(1)}, u32[]{:S(2)}, u32[]{:S(2)}) collective-permute-start(bf16[4,64,128]{2,1,0:T(8,128)(2,1)S(1)} %pad_maximum_fusion.1), channel_id=1, source_target_pairs={{0,4},{2,6},{4,0},{6,2},{8,12},{10,14},{12,8},{14,10},{16,20},{18,... | collective-permute-start | bytes 196616 | tf_op jit(solution)/shard_map/ppermute | solution.py:476
  254.6 5.0 %collective-permute-start.3 = (bf16[8,64,128]{2,1,0:T(8,128)(2,1)S(1)}, bf16[8,64,128]{2,1,0:T(8,128)(2,1)S(1)}, u32[]{:S(2)}, u32[]{:S(2)}) collective-permute-start(bf16[8,64,128]{2,1,0:T(8,128)(2,1)S(1)} %pad_maximum_fusion), channel_id=1, source_target_pairs={{0,1},{1,0},{2,3},{3,2},{4,5},{5,4},{6,7},{7,6},{8,9},{9,8},{10,11... | collective-permute-start | bytes 393224 | tf_op jit(solution)/shard_map/ppermute | solution.py:476
  259.7 1.6 collective-permute-start.4

commit v6 on v4

--- a/solution.py
+++ b/solution.py
@@ -81,26 +81,63 @@
     return scratch[pl.ds(step, channels, stride=rows), :]
 
 
-def spread_edges(scratch, out_ref):
+def own_number(few):
+    return lax.axis_index("row") * few + lax.axis_index("col")
+
+
+def core_bit(few):
+    return few
+
+
+def chip_offsets(shards, few):
+    return [mask for mask in range(shards) if mask & core_bit(few) == 0]
+
+
+def sources(pieces, few):
+    me = own_number(few)
+    for offset, piece in zip(chip_offsets(2 * len(pieces), few), pieces):
+        for core in range(2):
+            yield me ^ (offset | core * core_bit(few)), piece.at[core]
+
+
+def rows_at(place, size):
+    return pl.ds(pl.multiple_of(place * size, size), size)
+
+
+def spread_edges(scratch, out_ref, few):
     shards, sides, group, rows, lanes = out_ref.shape
-    block = shards * group * rows
-    for side in range(sides):
-        part = scratch[side * block : (side + 1) * block, :]
-        out_ref[:, side] = part.reshape(shards, group, rows, lanes).astype(BF16)
-
-
-def collect_edges(in_ref, scratch):
-    shards, sides, group, rows, lanes = in_ref.shape
-    block = shards * group * rows
-    for side in range(sides):
-        scratch[side * block : (side + 1) * block, :] = (
-            in_ref[:, side].astype(F32).reshape(block, lanes)
+    size = group * rows
+    me = own_number(few)
+    for mask in range(shards):
+        for side in range(sides):
+            part = scratch[rows_at(side * shards + (me ^ mask), size), :]
+            out_ref[mask, side] = part.astype(BF16).reshape(group, rows, lanes)
+
+
+def collect_edges(pieces, scratch, few):
+    _, sides, group, rows, lanes = pieces[0].shape
+    size, shards = group * rows, 2 * len(pieces)
+    for source, part in sources(pieces, few):
+        for side in range(sides):
+            scratch[rows_at(side * shards + source, size), :] = (
+                part[side].astype(F32).reshape(size, lanes)
+            )
+
+
+def spread_triangle(scratch, out_ref, few):
+    shards, group, rows, lanes = out_ref.shape
+    me = own_number(few)
+    for mask in range(shards):
+        part = scratch[rows_at(me ^ mask, group * rows), :]
+        out_ref[mask] = part.astype(BF16).reshape(group, rows, lanes)
+
+
+def collect_triangle(pieces, scratch, few):
+    _, group, rows, lanes = pieces[0].shape
+    for source, part in sources(pieces, few):
+        scratch[rows_at(source, group * rows), :] = (
+            part[...].astype(F32).reshape(group * rows, lanes)
         )
-
-
-def collect_triangle(in_ref, scratch):
-    block = in_ref.size // in_ref.shape[-1]
-    scratch[0:block, :] = in_ref[...].astype(F32).reshape(block, in_ref.shape[-1])
 
 
 def each_row(rows, unroll, body):
@@ -145,7 +182,7 @@
 
 
 def start_kernel(
-    lengths, pair_far, ngain_far, nbias_far, proj_far, gate_far,
+    few, lengths, pair_far, ngain_far, nbias_far, proj_far, gate_far,
     edge_out, normed_out, proj_out, gate_out, scaled_out, inverse_out,
     pair, ngain, nbias, proj_w, gate_w, sems, wts, scr,
 ):
@@ -172,11 +209,18 @@
         put_rows(scr, save_edges(step, normed, wts[...], mask, proj_out, gate_out), step, rows)
 
     each_row(rows, 4, body)
-    spread_edges(scr, edge_out)
+    spread_edges(scr, edge_out, few)
 
 
 def between_kernel(
-    lengths, tri, pair, normed0, ngain, nbias, mgain, mbias, out_w, outgate_w, proj_w, gate_w,
+    few, count, lengths, *refs,
+):
+    tri, rest = refs[:count], refs[count:]
+    between_body(few, lengths, tri, *rest)
+
+
+def between_body(
+    few, lengths, tri, pair, normed0, ngain, nbias, mgain, mbias, out_w, outgate_w, proj_w, gate_w,
     edge_out, mid_out, normed_out, proj_out, gate_out, scaled_out, inverse_out,
     outgate_out, scaled_mid_out, inverse_mid_out, wts, scr,
 ):
@@ -185,7 +229,7 @@
     out_t, outgate_t = turned(out_w[0]), turned(outgate_w[0])
     gain, bias = column(ngain, 1, lanes), column(nbias, 1, lanes)
     gain_mid, bias_mid = column(mgain, 0, lanes), column(mbias, 0, lanes)
-    collect_triangle(tri, scr)
+    collect_triangle(tri, scr, few)
 
     def body(step):
         scaled_mid, inverse_mid = mid_norm(get_rows(scr, step, channels, rows))
@@ -204,7 +248,7 @@
         put_rows(scr, save_edges(step, normed, wts[...], mask, proj_out, gate_out), step, rows)
 
     each_row(rows, 4, body)
-    spread_edges(scr, edge_out)
+    spread_edges(scr, edge_out, few)
 
 
 def out_weight_grads(unit, d_outer, normed, d_gatepre, out_ref):
@@ -224,15 +268,19 @@
     return pl.ds(pl.multiple_of(step * lanes, lanes), lanes)
 
 
-def turn_kernel(
-    tri, mid, normed, cot, mgain, mbias, out_w, outgate_w,
+def turn_kernel(few, count, *refs):
+    turn_body(few, refs[:count], *refs[count:])
+
+
+def turn_body(
+    few, tri, mid, normed, cot, mgain, mbias, out_w, outgate_w,
     d_tri_out, new_out, grad_out, d_normed_out, weights_out, small_out,
     scr, unit_all, outer_all, normed_all, gate_all, sums,
 ):
     rows, channels, lanes = mid.shape
     out_t, outgate_t = turned(out_w[1]), turned(outgate_w[1])
     gain_mid, bias_mid = column(mgain, 1, lanes), column(mbias, 1, lanes)
-    collect_triangle(tri, scr)
+    collect_triangle(tri, scr, few)
     sums[...] = jnp.zeros_like(sums)
 
     def body(step):
@@ -258,7 +306,7 @@
         sums[1] += d_unit
 
     each_row(rows, 4, body)
-    d_tri_out[...] = scr[...].reshape(d_tri_out.shape).astype(BF16)
+    spread_triangle(scr, d_tri_out, few)
     out_weight_grads(unit_all, outer_all, normed_all, gate_all, weights_out)
     for index in range(2):
         small_out[index : index + 1, :] = as_row(sums[index])
@@ -273,8 +321,12 @@
     return total
 
 
-def middle_kernel(
-    d_edge, proj_factor, gate_factor, d_normed_gate, scaled_in, inverse_in, cot, outgate,
+def middle_kernel(few, count, *refs):
+    middle_body(few, refs[:count], *refs[count:])
+
+
+def middle_body(
+    few, d_edge, proj_factor, gate_factor, d_normed_gate, scaled_in, inverse_in, cot, outgate,
     scaled_mid, inverse_mid, normed0, normed1, ngain, mgain, mbias, proj_w, gate_w, out_w,
     outgate_w,
     d_tri_out, grad_out, d_normed_out, out_weights, in_weights, small_out,
@@ -284,7 +336,7 @@
     out_t = turned(out_w[0])
     gain = column(ngain, 1, lanes)
     gain_mid, bias_mid = column(mgain, 0, lanes), column(mbias, 0, lanes)
-    collect_edges(d_edge, scr)
+    collect_edges(d_edge, scr, few)
     sums[...] = jnp.zeros_like(sums)
     half = proj_factor.shape[1]
 
@@ -321,21 +373,25 @@
         sums[1] += d_unit
 
     each_row(rows, 4, body)
-    d_tri_out[...] = scr_tri[...].reshape(d_tri_out.shape).astype(BF16)
+    spread_triangle(scr_tri, d_tri_out, few)
     out_weight_grads(unit_all, outer_all, normed_all, gate_all, out_weights)
     in_weight_grads(upper_all, d_in_all, in_weights)
     for index in range(4):
         small_out[index : index + 1, :] = as_row(sums[index])
 
 
-def finish_kernel(
-    d_edge, proj_factor, gate_factor, d_normed_gate, scaled_in, inverse_in, grad, normed,
+def finish_kernel(few, count, *refs):
+    finish_body(few, refs[:count], *refs[count:])
+
+
+def finish_body(
+    few, d_edge, proj_factor, gate_factor, d_normed_gate, scaled_in, inverse_in, grad, normed,
     ngain, proj_w, gate_w, out0, in1, out1,
     packed_out, grad_out, small_out, scr, normed_all, d_in_all, sums,
 ):
     rows, half, lanes = proj_factor.shape
     gain = column(ngain, 0, lanes)
-    collect_edges(d_edge, scr)
+    collect_edges(d_edge, scr, few)
     sums[...] = jnp.zeros_like(sums)
 
     def body(step):
@@ -393,8 +449,13 @@
         outgate_out[module] = blocks[5]
 
 
-def triangle_kernel(incoming, edge, tri_out):
-    many, few, _, group, rows, lanes = edge.shape
+def triangle_kernel(incoming, few, count, *refs):
+    pieces, (edge_out, tri_out, tri_all) = refs[:count], refs[count:]
+    shards, _, group, rows, lanes = edge_out.shape
+    many = shards // few
+    for source, part in sources(pieces, few):
+        edge_out[source] = part[...]
+    edge = edge_out.reshape(many, few, 2, group, rows, lanes)
 
     def whole(side, channel):
         parts = [edge[:, c, side, channel].reshape(many * rows, lanes) for c in range(few)]
@@ -405,11 +466,21 @@
         tri = (dot_lt if incoming else dot_rt)(left, right).astype(BF16)
         for c in range(few):
             part = tri[:, c * lanes : (c + 1) * lanes]
-            tri_out[:, c, channel] = part.reshape(many, rows, lanes)
-
-
-def edge_grad_kernel(incoming, edge, d_tri, grad_out):
-    many, few, _, group, rows, lanes = edge.shape
+            tri_all[:, c, channel] = part.reshape(many, rows, lanes)
+    place = tri_all.reshape(shards, group, rows, lanes)
+    me = own_number(few)
+    for mask in range(shards):
+        tri_out[mask] = place[me ^ mask]
+
+
+def edge_grad_kernel(incoming, few, count, *refs):
+    pieces, (edge_all, grad_out, tri_all, grad_all) = refs[:count], refs[count:]
+    shards, _, group, rows, lanes = edge_all.shape
+    many = shards // few
+    for source, part in sources(pieces, few):
+        tri_all[source] = part[...]
+    edge = edge_all.reshape(many, few, 2, group, rows, lanes)
+    d_tri = tri_all.reshape(many, few, group, rows, lanes)
 
     def whole(ref, *index):
         parts = [ref[(slice(None), c) + index].reshape(many * rows, lanes) for c in range(few)]
@@ -426,7 +497,11 @@
             value = value.astype(BF16)
             for c in range(few):
                 part = value[:, c * lanes : (c + 1) * lanes]
-                grad_out[:, c, side, channel] = part.reshape(many, rows, lanes)
+                grad_all[:, c, side, channel] = part.reshape(many, rows, lanes)
+    place = grad_all.reshape(shards, 2, group, rows, lanes)
+    me = own_number(few)
+    for mask in range(shards):
+        grad_out[mask] = place[me ^ mask]
 
 
 SCALARS = pl.BlockSpec(memory_space=pltpu.SMEM)
@@ -454,6 +529,24 @@
 
 def exchange(values):
     return lax.all_to_all(values, ("row", "col"), split_axis=0, concat_axis=0, tiled=True)
+
+
+def swap(values, mask, shards):
+    pairs = [(index, index ^ mask) for index in range(shards)]
+    return lax.ppermute(values, ("row", "col"), pairs)
+
+
+def trade(sent, few):
+    shards = sent.shape[0]
+    core = core_bit(few)
+    offsets = chip_offsets(shards, few)
+    given = jnp.stack([sent[offset | core] for offset in offsets])
+    got = swap(given, core, shards)
+    pieces = {}
+    for place, offset in sorted(enumerate(offsets), key=lambda item: -item[1]):
+        both = jnp.stack([sent[offset], got[place]])
+        pieces[offset] = swap(both, offset, shards) if offset else both
+    return [pieces[offset] for offset in offsets]
 
 
 def grouped_device(
@@ -490,58 +583,65 @@
         return ((count, H), F32)
 
     saved = [tile, factor, factor, wide, row]
+    count = shards // 2
+    far = [
+        pltpu.with_memory_space_constraint(item, pltpu.HBM)
+        for item in (pair, ngain, nbias, proj_w, gate_w)
+    ]
     sent, normed0, *factors0 = call(
-        start_kernel, "start", [edge, *saved], [lengths, pair, ngain, nbias, proj_w, gate_w],
+        functools.partial(start_kernel, few), "start", [edge, *saved], [lengths, *far],
         [(pair.shape, BF16), (ngain.shape, F32), (nbias.shape, F32), (proj_w.shape, BF16),
          (gate_w.shape, BF16), pltpu.SemaphoreType.DMA((5,)), wts, big],
         4 * dense, 1, far=True,
     )
-    edge0 = exchange(sent).reshape(grid[0])
-    (here,) = call(
-        functools.partial(triangle_kernel, False), "outgoing", [tri_grid], [edge0], (), triangle,
-    )
-    tri0 = exchange(here.reshape(tri[0]))
+    edge0, sent = call(
+        functools.partial(triangle_kernel, False, few, count), "outgoing", [edge, tri],
+        trade(sent, few), [tri_grid], triangle,
+    )
+    tri0 = trade(sent, few)
     sent, mid_t, normed1, *factors1, outgate0, scaled_mid0, inverse_mid0 = call(
-        between_kernel, "between", [edge, tile, *saved, wide, wide, row],
-        [lengths, tri0, pair, normed0, ngain, nbias, mgain, mbias, out_w, outgate_w, proj_w,
+        functools.partial(between_kernel, few, count), "between",
+        [edge, tile, *saved, wide, wide, row],
+        [lengths, *tri0, pair, normed0, ngain, nbias, mgain, mbias, out_w, outgate_w, proj_w,
          gate_w],
         [wts, big], 6 * dense, 1,
     )
-    edge1 = exchange(sent).reshape(grid[0])
-    (here,) = call(
-        functools.partial(triangle_kernel, True), "incoming", [tri_grid], [edge1], (), triangle,
-    )
-    tri1 = exchange(here.reshape(tri[0]))
+    edge1, sent = call(
+        functools.partial(triangle_kernel, True, few, count), "incoming", [edge, tri],
+        trade(sent, few), [tri_grid], triangle,
+    )
+    tri1 = trade(sent, few)
     sent, new_pair, cot_t, d_normed_gate1, out_grads1, small1 = call(
-        turn_kernel, "turn", [tri, (pair.shape, BF16), wide, wide, out_rows, small(2)],
-        [tri1, mid_t, normed1, cotangent, mgain, mbias, out_w, outgate_w],
+        functools.partial(turn_kernel, few, count), "turn",
+        [tri, (pair.shape, BF16), wide, wide, out_rows, small(2)],
+        [*tri1, mid_t, normed1, cotangent, mgain, mbias, out_w, outgate_w],
         [mid, flat, flat, flat, flat, sums(2)], 6 * dense,
     )
-    d_tri1 = exchange(sent).reshape(tri_grid[0])
     (sent,) = call(
-        functools.partial(edge_grad_kernel, True), "incoming_grad", [grid], [edge1, d_tri1],
-        (), 2 * triangle,
-    )
-    d_edge1 = exchange(sent.reshape(edge[0]))
+        functools.partial(edge_grad_kernel, True, few, count), "incoming_grad", [edge],
+        [*trade(sent, few), edge1], [tri, grid], 2 * triangle,
+    )
+    d_edge1 = trade(sent, few)
     proj_factor1, gate_factor1, scaled1, inverse1 = factors1
     sent, grad, d_normed_gate0, out_grads0, in_grads1, small_middle = call(
-        middle_kernel, "middle", [tri, wide, wide, out_rows, in_rows, small(4)],
-        [d_edge1, proj_factor1, gate_factor1, d_normed_gate1, scaled1, inverse1, cot_t, outgate0,
+        functools.partial(middle_kernel, few, count), "middle",
+        [tri, wide, wide, out_rows, in_rows, small(4)],
+        [*d_edge1, proj_factor1, gate_factor1, d_normed_gate1, scaled1, inverse1, cot_t, outgate0,
          scaled_mid0, inverse_mid0, normed0, normed1, ngain, mgain, mbias, proj_w, gate_w, out_w,
          outgate_w],
         [big, mid, flat, flat, flat, flat, flat, flat_in, sums(4)], 13 * dense,
     )
-    d_tri0 = exchange(sent).reshape(tri_grid[0])
     (sent,) = call(
-        functools.partial(edge_grad_kernel, False), "outgoing_grad", [grid], [edge0, d_tri0],
-        (), 2 * triangle,
-    )
-    d_edge0 = exchange(sent.reshape(edge[0]))
+        functools.partial(edge_grad_kernel, False, few, count), "outgoing_grad", [edge],
+        [*trade(sent, few), edge0], [tri, grid], 2 * triangle,
+    )
+    d_edge0 = trade(sent, few)
     share = 12 * H // shards
     proj_factor0, gate_factor0, scaled0, inverse0 = factors0
     packed, grad_pair, small0 = call(
-        finish_kernel, "finish", [((12 * H, H), BF16), (pair.shape, BF16), small(2)],
-        [d_edge0, proj_factor0, gate_factor0, d_normed_gate0, scaled0, inverse0, grad, normed0,
+        functools.partial(finish_kernel, few, count), "finish",
+        [((12 * H, H), BF16), (pair.shape, BF16), small(2)],
+        [*d_edge0, proj_factor0, gate_factor0, d_normed_gate0, scaled0, inverse0, grad, normed0,
          ngain, proj_w, gate_w, out_grads0, in_grads1, out_grads1],
         [big, flat, flat_in, sums(2)], 8 * dense,
     )
@@ -812,6 +912,10 @@
     )
 
 
+def power_of_two(many, few):
+    return many > 1 and many & (many - 1) == 0 and few & (few - 1) == 0
+
+
 def solution(mesh):
     in_specs = (
         P(("grp", "row"), "col", None),
@@ -839,7 +943,7 @@
         P("grp", None, None),
     )
     many, few = mesh.shape["row"], mesh.shape["col"]
-    if mesh.shape["ch"] == 1 and H % (many * few) == 0:
+    if mesh.shape["ch"] == 1 and H % (many * few) == 0 and power_of_two(many, few):
         body = functools.partial(grouped_device, many=many, few=few)
     else:
         body = per_device

time: 264 us -> 350 us (1.33)
  starting transfers between devices: 0 us -> 220 us
  blocking collectives: 230 us -> 35.4 us
  waiting for transfers between devices: 0 us -> 59.6 us
    ppermute x0 -> x128, starting transfers between devices: none -> 220 us  [swap(): return lax.ppermute(values, ('row', 'col'), pairs)]
    all_to_all x10 -> x2, blocking collectives: 230 us -> 35.4 us  [exchange(): lax.all_to_all(values, ('row', 'col'), split_axis=0, concat_axis=0, tiled...]
    ppermute x0 -> x128, waiting for transfers between devices: none -> 59.6 us  [swap(): return lax.ppermute(values, ('row', 'col'), pairs)]
    unnamed x28 -> x76, local copies, waits for them, and re-layouts: 4.25 us -> 0.72 us
  transfers between devices with their start and end apart: 0 -> 128, of which waited for: 0 -> 33; matrix products, arithmetic and copies ran while one was open for 0% -> 0% of each run, Pallas kernels for 0% -> 0%
where the time goes in v6:
time: 350 us; the launch traced here: 349 us
  starting transfers between devices  220 us (63%)
  waiting for transfers between devices  59.6 us (17%)
  blocking collectives  35.4 us (10%)
  Pallas kernels  28.8 us (8%)
    ppermute x128, starting transfers between devices, swap(): return lax.ppermute(values, ('row', 'col'), pairs)  220 us
    ppermute x128, waiting for transfers between devices, swap(): return lax.ppermute(values, ('row', 'col'), pairs)  59.6 us
    all_to_all x2, blocking collectives, exchange(): lax.all_to_all(values, ('row', 'col'), split_axis=0, concat_axis=0, tiled...  35.4 us
    pallas_call x11, Pallas kernels, call(): pl.pallas_call(kernel, name=name, out_shape=shapes, in_specs=[SCALARS] *...  28.8 us
  transfers between devices with their start and end apart: 128, of which 33 were waited for; matrix products, arithmetic and copies ran while one was open for 0% of the time, Pallas kernels for 0%

profile of v6, /device:TPU:0, one launch (start us, length us, event | category | flops | bytes accessed | tf_op | source)
XLA Modules:
  0.0 349.2 jit_solution(16461286771632822357)
XLA Ops:
  1.3 4.1 %start.1 = (bf16[32,2,4,16,128]{4,3,2,1,0:T(8,128)(2,1)S(1)}, bf16[16,128,128]{2,1,0:T(8,128)(2,1)S(1)}, f32[16,256,128]{2,1,0:T(8,128)S(1)}, f32[16,256,128]{2,...) custom-call(s32[1]{0:T(128)S(6)} %copy.85.lengths, bf16[16,128,128]{2,1,0:T(8,128)(2,1)} %refs_16_.1, ...), custom_call_target="tpu_custom_call" | custom-call | flops 268435456 | bytes 7612420 | tf_op jit(solution)/shard_map/start/pallas_call | solution.py:516
  7.6 2.9 collective-permute-start.1
  12.2 2.1 collective-permute-start.4
  16.0 2.6 collective-permute-start.6
  18.7 2.9 collective-permute-start.8
  22.9 3.5 %collective-permute-start.10 = (bf16[2,2,4,16,128]{4,3,2,1,0:T(8,128)(2,1)S(1)}, bf16[2,2,4,16,128]{4,3,2,1,0:T(8,128)(2,1)S(1)}, u32[]{:S(2)}, u32[]{:S(2)}) collective-permute-start(bf16[2,2,4,16,128]{4,3,2,1,0:T(8,128)(2,1)S(1)} %pad_maximum_fusion.10), channel_id=1, source_target_pairs={{0,20},{1,21},{2,22},{3,23},{4,16},{5,17},{6,18},{7,19},{8,28},{9,... | collective-permute-start | bytes 196616 | tf_op jit(solution)/shard_map/ppermute | solution.py:536
  26.5 3.8 %collective-permute-start.12 = (bf16[2,2,4,16,128]{4,3,2,1,0:T(8,128)(2,1)S(1)}, bf16[2,2,4,16,128]{4,3,2,1,0:T(8,128)(2,1)S(1)}, u32[]{:S(2)}, u32[]{:S(2)}) collective-permute-start(bf16[2,2,4,16,128]{4,3,2,1,0:T(8,128)(2,1)S(1)} %pad_maximum_fusion.12), channel_id=1, source_target_pairs={{0,24},{1,25},{2,26},{3,27},{4,28},{5,29},{6,30},{7,31},{8,16},{9,... | collective-permute-start | bytes 196616 | tf_op jit(solution)/shard_map/ppermute | solution.py:536
  30.4 4.5 %collective-permute-start.13 = (bf16[2,2,4,16,128]{4,3,2,1,0:T(8,128)(2,1)S(1)}, bf16[2,2,4,16,128]{4,3,2,1,0:T(8,128)(2,1)S(1)}, u32[]{:S(2)}, u32[]{:S(2)}) collective-permute-start(bf16[2,2,4,16,128]{4,3,2,1,0:T(8,128)(2,1)S(1)} %pad_maximum_fusion.13), channel_id=1, source_target_pairs={{0,25},{1,24},{2,27},{3,26},{4,29},{5,28},{6,31},{7,30},{8,17},{9,... | collective-permute-start | bytes 196616 | tf_op jit(solution)/shard_map/ppermute | solution.py:536
  36.8 3.9 %collective-permute-start.15 = (bf16[2,2,4,16,128]{4,3,2,1,0:T(8,128)(2,1)S(1)}, bf16[2,2,4,16,128]{4,3,2,1,0:T(8,128)(2,1)S(1)}, u32[]{:S(2)}, u32[]{:S(2)}) collective-permute-start(bf16[2,2,4,16,128]{4,3,2,1,0:T(8,128)(2,1)S(1)} %pad_maximum_fusion.15), channel_id=1, source_target_pairs={{0,29},{1,28},{2,31},{3,30},{4,25},{5,24},{6,27},{7,26},{8,21},{9,... | collective-permute-start | bytes 196616 | tf_op jit(solution)/shard_map/ppermute | solution.py:536
  41.9 2.9 collective-permute-done.15.refs_15_
  56.6 2.8 collective-permute-start.24
  62.0 2.4 collective-permute-start.27
  64.4 3.0 collective-permute-start.28
  68.7 3.3 collective-permute-start.30
  75.3 4.2 %collective-permute-done.31.refs_15_ = bf16[2,4,16,128]{3,2,1,0:T(8,128)(2,1)S(1)} collective-permute-done((bf16[2,4,16,128]{3,2,1,0:T(8,128)(2,1)S(1)}, bf16[2,4,16,128]{3,2,1,0:T(8,128)(2,1)S(1)}, u32[]{:S(2)}, u32[]{:S(2)}) %collective-permute-start.31) | collective-permute-done | bytes 32800 | tf_op jit(solution)/shard_map/ppermute | solution.py:536
  79.6 4.8 %between.1 = (bf16[32,2,4,16,128]{4,3,2,1,0:T(8,128)(2,1)S(1)}, bf16[16,128,128]{2,1,0:T(8,128)(2,1)S(1)}, bf16[16,128,128]{2,1,0:T(8,128)(2,1)S(1)}, f32[16,256...) custom-call(s32[1]{0:T(128)S(6)} %copy.85.lengths, ...), custom_call_target="tpu_custom_call" | custom-call | flops 402653184 | bytes 11423748 | tf_op jit(solution)/shard_map/between/pallas_call | solution.py:516
  93.7 2.8 collective-permute-start.39
  96.5 2.8 collective-permute-start.41
  100.5 3.7 %collective-permute-start.43 = (bf16[2,2,4,16,128]{4,3,2,1,0:T(8,128)(2,1)S(1)}, bf16[2,2,4,16,128]{4,3,2,1,0:T(8,128)(2,1)S(1)}, u32[]{:S(2)}, u32[]{:S(2)}) collective-permute-start(bf16[2,2,4,16,128]{4,3,2,1,0:T(8,128)(2,1)S(1)} %pad_maximum_fusion.27), channel_id=1, source_target_pairs={{0,21},{1,20},{2,23},{3,22},{4,17},{5,16},{6,19},{7,18},{8,29},{9,... | collective-permute-start | bytes 196616 | tf_op jit(solution)/shard_map/ppermute | solution.py:536
  105.4 2.6 collective-permute-start.45
  109.3 3.8 %collective-permute-start.46 = (bf16[2,2,4,16,128]{4,3,2,1,0:T(8,128)(2,1)S(1)}, bf16[2,2,4,16,128]{4,3,2,1,0:T(8,128)(2,1)S(1)}, u32[]{:S(2)}, u32[]{:S(2)}) collective-permute-start(bf16[2,2,4,16,128]{4,3,2,1,0:T(8,128)(2,1)S(1)} %pad_maximum_fusion.30), channel_id=1, source_target_pairs={{0,28},{1,29},{2,30},{3,31},{4,24},{5,25},{6,26},{7,27},{8,20},{9,... | collective-permute-start | bytes 196616 | tf_op jit(solution)/shard_map/ppermute | solution.py:536
  116.4 4.7 %collective-permute-done.47.refs_15_ = bf16[2,2,4,16,128]{4,3,2,1,0:T(8,128)(2,1)S(1)} collective-permute-done((bf16[2,2,4,16,128]{4,3,2,1,0:T(8,128)(2,1)S(1)}, bf16[2,2,4,16,128]{4,3,2,1,0:T(8,128)(2,1)S(1)}, u32[]{:S(2)}, u32[]{:S(2)}) %collective-permute-start.47) | collective-permute-done | bytes 65568 | tf_op jit(solution)/shard_map/ppermute | solution.py:536
  127.7 2.2 collective-permute-start.53
  130.4 2.5 collective-permute-start.55
  133.9 2.9 collective-permute-start.57
  137.9 2.8 collective-permute-start.59
  141.6 3.9 %collective-permute-start.61 = (bf16[2,4,16,128]{3,2,1,0:T(8,128)(2,1)S(1)}, bf16[2,4,16,128]{3,2,1,0:T(8,128)(2,1)S(1)}, u32[]{:S(2)}, u32[]{:S(2)}) collective-permute-start(bf16[2,4,16,128]{3,2,1,0:T(8,128)(2,1)S(1)} %pad_maximum_fusion.93), channel_id=1, source_target_pairs={{0,25},{1,24},{2,27},{3,26},{4,29},{5,28},{6,31},{7,30},{8,17},{9,... | collective-permute-start | bytes 98312 | tf_op jit(solution)/shard_map/ppermute | solution.py:536
  146.2 3.9 %collective-permute-start.63 = (bf16[2,4,16,128]{3,2,1,0:T(8,128)(2,1)S(1)}, bf16[2,4,16,128]{3,2,1,0:T(8,128)(2,1)S(1)}, u32[]{:S(2)}, u32[]{:S(2)}) collective-permute-start(bf16[2,4,16,128]{3,2,1,0:T(8,128)(2,1)S(1)} %pad_maximum_fusion.95), channel_id=1, source_target_pairs={{0,29},{1,28},{2,31},{3,30},{4,25},{5,24},{6,27},{7,26},{8,21},{9,... | collective-permute-start | bytes 98312 | tf_op jit(solution)/shard_map/ppermute | solution.py:536
  150.2 2.0 collective-permute-done.62.refs_14_
  153.7 3.9 %turn.1 = (bf16[32,4,16,128]{3,2,1,0:T(8,128)(2,1)S(1)}, bf16[16,128,128]{2,1,0:T(8,128)(2,1)}, f32[16,128,128]{2,1,0:T(8,128)S(1)}, f32[16,128,128]{2,1,0:T(8,1...) custom-call(bf16[2,4,16,128]{3,2,1,0:T(8,128)(2,1)S(1)} %pad_maximum_fusion.80.refs_0_, ...), custom_call_target="tpu_custom_call" | custom-call | flops 402653184 | bytes 5442560 | tf_op jit(solution)/shard_map/turn/pallas_call | solution.py:516
  162.9 3.2 collective-permute-start.69
  166.5 2.5 collective-permute-start.71
  170.9 2.2 collective-permute-start.73
  174.5 2.2 collective-permute-start.75
  176.7 3.3 collective-permute-start.76
  181.7 2.7 collective-permute-start.78
  188.4 3.6 %collective-permute-done.79.refs_15_ = bf16[2,4,16,128]{3,2,1,0:T(8,128)(2,1)S(1)} collective-permute-done((bf16[2,4,16,128]{3,2,1,0:T(8,128)(2,1)S(1)}, bf16[2,4,16,128]{3,2,1,0:T(8,128)(2,1)S(1)}, u32[]{:S(2)}, u32[]{:S(2)}) %collective-permute-start.79) | collective-permute-done | bytes 32800 | tf_op jit(solution)/shard_map/ppermute | solution.py:536
  198.5 3.1 collective-permute-start.85
  202.0 2.6 collective-permute-start.87
  204.6 3.9 %collective-permute-start.89 = (bf16[2,2,4,16,128]{4,3,2,1,0:T(8,128)(2,1)S(1)}, bf16[2,2,4,16,128]{4,3,2,1,0:T(8,128)(2,1)S(1)}, u32[]{:S(2)}, u32[]{:S(2)}) collective-permute-start(bf16[2,2,4,16,128]{4,3,2,1,0:T(8,128)(2,1)S(1)} %pad_maximum_fusion.41), channel_id=1, source_target_pairs={{0,17},{1,16},{2,19},{3,18},{4,21},{5,20},{6,23},{7,22},{8,25},{9,... | collective-permute-start | bytes 196616 | tf_op jit(solution)/shard_map/ppermute | solution.py:536
  208.9 3.5 %collective-permute-start.91 = (bf16[2,2,4,16,128]{4,3,2,1,0:T(8,128)(2,1)S(1)}, bf16[2,2,4,16,128]{4,3,2,1,0:T(8,128)(2,1)S(1)}, u32[]{:S(2)}, u32[]{:S(2)}) collective-permute-start(bf16[2,2,4,16,128]{4,3,2,1,0:T(8,128)(2,1)S(1)} %pad_maximum_fusion.43), channel_id=1, source_target_pairs={{0,21},{1,20},{2,23},{3,22},{4,17},{5,16},{6,19},{7,18},{8,29},{9,... | collective-permute-start | bytes 196616 | tf_op jit(solution)/shard_map/ppermute | solution.py:536
  214.6 2.6 collective-permute-start.93
  218.6 2.8 collective-permute-done.90.refs_10_
  221.4 2.8 collective-permute-start.95
  225.2 4.1 %collective-permute-done.95.refs_15_ = bf16[2,2,4,16,128]{4,3,2,1,0:T(8,128)(2,1)S(1)} collective-permute-done((bf16[2,2,4,16,128]{4,3,2,1,0:T(8,128)(2,1)S(1)}, bf16[2,2,4,16,128]{4,3,2,1,0:T(8,128)(2,1)S(1)}, u32[]{:S(2)}, u32[]{:S(2)}) %collective-permute-start.95) | collective-permute-done | bytes 65568 | tf_op jit(solution)/shard_map/ppermute | solution.py:536
  229.3 9.3 %middle.1 = (bf16[32,4,16,128]{3,2,1,0:T(8,128)(2,1)S(1)}, f32[16,128,128]{2,1,0:T(8,128)S(1)}, f32[16,128,128]{2,1,0:T(8,128)S(1)}, bf16[256,128]{1,0:T(8,128)(...) custom-call(bf16[2,2,4,16,128]{4,3,2,1,0:T(8,128)(2,1)S(1)} %pad_maximum_fusion.32.refs_0_, ...), custom_call_target="tpu_custom_call" | custom-call | flops 872415232 | bytes 14767104 | tf_op jit(solution)/shard_map/middle/pallas_call | solution.py:516
  241.5 2.0 collective-permute-start.98
  251.3 2.1 collective-permute-start.105
  255.4 2.4 collective-permute-start.107
  259.1 2.9 collective-permute-start.109
  262.1 2.4 collective-permute-start.110
  264.4 2.8 collective-permute-start.111
  268.7 3.3 collective-permute-done.111.refs_15_
  276.3 2.1 collective-permute-start.115
  281.1 3.4 collective-permute-start.119
  287.1 2.0 collective-permute-start.122
  289.2 3.1 collective-permute-start.123
  292.3 2.9 collective-permute-start.124
  296.5 3.2 collective-permute-start.126
  300.7 4.5 %collective-permute-start.127 = (bf16[2,2,4,16,128]{4,3,2,1,0:T(8,128)(2,1)S(1)}, bf16[2,2,4,16,128]{4,3,2,1,0:T(8,128)(2,1)S(1)}, u32[]{:S(2)}, u32[]{:S(2)}) collective-permute-start(bf16[2,2,4,16,128]{4,3,2,1,0:T(8,128)(2,1)S(1)} %pad_maximum_fusion.63), channel_id=1, source_target_pairs={{0,29},{1,28},{2,31},{3,30},{4,25},{5,24},{6,27},{7,26},{8,21},{9,... | collective-permute-start | bytes 196616 | tf_op jit(solution)/shard_map/ppermute | solution.py:536
  305.2 3.3 collective-permute-done.127.refs_15_
  308.6 3.7 %finish.1 = (bf16[1536,128]{1,0:T(8,128)(2,1)S(1)}, bf16[16,128,128]{2,1,0:T(8,128)(2,1)}, f32[2,128]{1,0:T(2,128)S(1)}) custom-call(bf16[2,2,4,16,128]{4,3,2,1,0:T(8,128)(2,1)S(1)} %pad_maximum_fusion.48.refs_0_, bf16[2,2,4,16,128]{4,3,2,1,0:T(8,128)(2,1)S(1)} %collective-permute-done.113.refs_1_, ...), custom_call_target="tpu_custom_call" | custom-call | flops 536870912 | bytes 10364928 | tf_op jit(solution)/shard_map/finish/pallas_call | solution.py:516
  312.3 17.5 %all_to_all.10.parts = bf16[32,48,128]{2,1,0:T(8,128)(2,1)S(1)} all-to-all(bf16[32,48,128]{2,1,0:T(8,128)(2,1)S(1)} %bitcast.14), channel_id=1, replica_groups=mesh['grp'=1,'row'=16,'col'=2,'ch'=1] {'row','col'}, dimensions={0} | all-to-all | bytes 786432 | tf_op jit(solution)/shard_map/all_to_all | solution.py:531
  329.9 17.9 %all_to_all.11.shared = bf16[32,64,128]{2,1,0:T(8,128)(2,1)S(1)} all-to-all(bf16[32,64,128]{2,1,0:T(8,128)(2,1)S(1)} %sum_weights.1), channel_id=1, replica_groups=mesh['grp'=1,'row'=16,'col'=2,'ch'=1] {'row','col'}, dimensions={0} | all-to-all | bytes 1048576 | tf_op jit(solution)/shard_map/all_to_all | solution.py:531
  (434 shorter events, 112.4 us)
Async XLA Ops:
  12.2 9.4 %collective-permute-start.4 = (bf16[2,2,4,16,128]{4,3,2,1,0:T(8,128)(2,1)S(1)}, bf16[2,2,4,16,128]{4,3,2,1,0:T(8,128)(2,1)S(1)}, u32[]{:S(2)}, u32[]{:S(2)}) collective-permute-start(bf16[2,2,4,16,128]{4,3,2,1,0:T(8,128)(2,1)S(1)} %pad_maximum_fusion.4), channel_id=1, source_target_pairs={{0,8},{1,9},{2,10},{3,11},{4,12},{5,13},{6,14},{7,15},{8,0},{9,1},... | collective-permute-start | bytes 196616 | tf_op jit(solution)/shard_map/ppermute | solution.py:536
  14.3 8.5 %collective-permute-start.5 = (bf16[2,2,4,16,128]{4,3,2,1,0:T(8,128)(2,1)S(1)}, bf16[2,2,4,16,128]{4,3,2,1,0:T(8,128)(2,1)S(1)}, u32[]{:S(2)}, u32[]{:S(2)}) collective-permute-start(bf16[2,2,4,16,128]{4,3,2,1,0:T(8,128)(2,1)S(1)} %pad_maximum_fusion.5), channel_id=1, source_target_pairs={{0,9},{1,8},{2,11},{3,10},{4,13},{5,12},{6,15},{7,14},{8,1},{9,0},... | collective-permute-start | bytes 196616 | tf_op jit(solution)/shard_map/ppermute | solution.py:536
  16.0 10.4 %collective-permute-start.6 = (bf16[2,2,4,16,128]{4,3,2,1,0:T(8,128)(2,1)S(1)}, bf16[2,2,4,16,128]{4,3,2,1,0:T(8,128)(2,1)S(1)}, u32[]{:S(2)}, u32[]{:S(2)}) collective-permute-start(bf16[2,2,4,16,128]{4,3,2,1,0:T(8,128)(2,1)S(1)} %pad_maximum_fusion.6), channel_id=1, source_target_pairs={{0,12},{1,13},{2,14},{3,15},{4,8},{5,9},{6,10},{7,11},{8,4},{9,5},... | collective-permute-start | bytes 196616 | tf_op jit(solution)/shard_map/ppermute | solution.py:536
  18.7 11.7 %collective-permute-start.8 = (bf16[2,2,4,16,128]{4,3,2,1,0:T(8,128)(2,1)S(1)}, bf16[2,2,4,16,128]{4,3,2,1,0:T(8,128)(2,1)S(1)}, u32[]{:S(2)}, u32[]{:S(2)}) collective-permute-start(bf16[2,2,4,16,128]{4,3,2,1,0:T(8,128)(2,1)S(1)} %pad_maximum_fusion.8), channel_id=1, source_target_pairs={{0,16},{1,17},{2,18},{3,19},{4,20},{5,21},{6,22},{7,23},{8,24},{9,... | collective-permute-start | bytes 196616 | tf_op jit(solution)/shard_map/ppermute | solution.py:536
  21.6 13.3 %collective-permute-start.9 = (bf16[2,2,4,16,128]{4,3,2,1,0:T(8,128)(2,1)S(1)}, bf16[2,2,4,16,128]{4,3,2,1,0:T(8,128)(2,1)S(1)}, u32[]{:S(2)}, u32[]{:S(2)}) collective-permute-start(bf16[2,2,4,16,128]{4,3,2,1,0:T(8,128)(2,1)S(1)} %pad_maximum_fusion.9), channel_id=1, source_target_pairs={{0,17},{1,16},{2,19},{3,18},{4,21},{5,20},{6,23},{7,22},{8,25},{9,... | collective-permute-start | bytes 196616 | tf_op jit(solution)/shard_map/ppermute | solution.py:536
  22.9 14.0 %collective-permute-start.10 = (bf16[2,2,4,16,128]{4,3,2,1,0:T(8,128)(2,1)S(1)}, bf16[2,2,4,16,128]{4,3,2,1,0:T(8,128)(2,1)S(1)}, u32[]{:S(2)}, u32[]{:S(2)}) collective-permute-start(bf16[2,2,4,16,128]{4,3,2,1,0:T(8,128)(2,1)S(1)} %pad_maximum_fusion.10), channel_id=1, source_target_pairs={{0,20},{1,21},{2,22},{3,23},{4,16},{5,17},{6,18},{7,19},{8,28},{9,... | collective-permute-start | bytes 196616 | tf_op jit(solution)/shard_map/ppermute | solution.py:536
  26.4 14.3 %collective-permute-start.11 = (bf16[2,2,4,16,128]{4,3,2,1,0:T(8,128)(2,1)S(1)}, bf16[2,2,4,16,128]{4,3,2,1,0:T(8,128)(2,1)S(1)}, u32[]{:S(2)}, u32[]{:S(2)}) collective-permute-start(bf16[2,2,4,16,128]{4,3,2,1,0:T(8,128)(2,1)S(1)} %pad_maximum_fusion.11), channel_id=1, source_target_pairs={{0,21},{1,20},{2,23},{3,22},{4,17},{5,16},{6,19},{7,18},{8,29},{9,... | collective-permute-start | bytes 196616 | tf_op jit(solution)/shard_map/ppermute | solution.py:536
  26.5 14.2 %collective-permute-start.12 = (bf16[2,2,4,16,128]{4,3,2,1,0:T(8,128)(2,1)S(1)}, bf16[2,2,4,16,128]{4,3,2,1,0:T(8,128)(2,1)S(1)}, u32[]{:S(2)}, u32[]{:S(2)}) collective-permute-start(bf16[2,2,4,16,128]{4,3,2,1,0:T(8,128)(2,1)S(1)} %pad_maximum_fusion.12), channel_id=1, source_target_pairs={{0,24},{1,25},{2,26},{3,27},{4,28},{5,29},{6,30},{7,31},{8,16},{9,... | collective-permute-start | bytes 196616 | tf_op jit(solution)/shard_map/ppermute | solution.py:536
  30.4 10.4 %collective-permute-start.13 = (bf16[2,2,4,16,128]{4,3,2,1,0:T(8,128)(2,1)S(1)}, bf16[2,2,4,16,128]{4,3,2,1,0:T(8,128)(2,1)S(1)}, u32[]{:S(2)}, u32[]{:S(2)}) collective-permute-start(bf16[2,2,4,16,128]{4,3,2,1,0:T(8,128)(2,1)S(1)} %pad_maximum_fusion.13), channel_id=1, source_target_pairs={{0,25},{1,24},{2,27},{3,26},{4,29},{5,28},{6,31},{7,30},{8,17},{9,... | collective-permute-start | bytes 196616 | tf_op jit(solution)/shard_map/ppermute | solution.py:536
  50.6 8.9 %collective-permute-start.20 = (bf16[2,4,16,128]{3,2,1,0:T(8,128)(2,1)S(1)}, bf16[2,4,16,128]{3,2,1,0:T(8,128)(2,1)S(1)}, u32[]{:S(2)}, u32[]{:S(2)}) collective-permute-start(bf16[2,4,16,128]{3,2,1,0:T(8,128)(2,1)S(1)} %pad_maximum_fusion.68), channel_id=1, source_target_pairs={{0,8},{1,9},{2,10},{3,11},{4,12},{5,13},{6,14},{7,15},{8,0},{9,1},... | collective-permute-start | bytes 98312 | tf_op jit(solution)/shard_map/ppermute | solution.py:536
  53.2 8.7 %collective-permute-start.22 = (bf16[2,4,16,128]{3,2,1,0:T(8,128)(2,1)S(1)}, bf16[2,4,16,128]{3,2,1,0:T(8,128)(2,1)S(1)}, u32[]{:S(2)}, u32[]{:S(2)}) collective-permute-start(bf16[2,4,16,128]{3,2,1,0:T(8,128)(2,1)S(1)} %pad_maximum_fusion.70), channel_id=1, source_target_pairs={{0,12},{1,13},{2,14},{3,15},{4,8},{5,9},{6,10},{7,11},{8,4},{9,5},... | collective-permute-start | bytes 98312 | tf_op jit(solution)/shard_map/ppermute | solution.py:536
  55.1 9.3 %collective-permute-start.23 = (bf16[2,4,16,128]{3,2,1,0:T(8,128)(2,1)S(1)}, bf16[2,4,16,128]{3,2,1,0:T(8,128)(2,1)S(1)}, u32[]{:S(2)}, u32[]{:S(2)}) collective-permute-start(bf16[2,4,16,128]{3,2,1,0:T(8,128)(2,1)S(1)} %pad_maximum_fusion.71), channel_id=1, source_target_pairs={{0,13},{1,12},{2,15},{3,14},{4,9},{5,8},{6,11},{7,10},{8,5},{9,4},... | collective-permute-start | bytes 98312 | tf_op jit(solution)/shard_map/ppermute | solution.py:536
  56.6 10.7 %collective-permute-start.24 = (bf16[2,4,16,128]{3,2,1,0:T(8,128)(2,1)S(1)}, bf16[2,4,16,128]{3,2,1,0:T(8,128)(2,1)S(1)}, u32[]{:S(2)}, u32[]{:S(2)}) collective-permute-start(bf16[2,4,16,128]{3,2,1,0:T(8,128)(2,1)S(1)} %pad_maximum_fusion.72), channel_id=1, source_target_pairs={{0,16},{1,17},{2,18},{3,19},{4,20},{5,21},{6,22},{7,23},{8,24},{9,... | collective-permute-start | bytes 98312 | tf_op jit(solution)/shard_map/ppermute | solution.py:536
  59.5 9.2 %collective-permute-start.25 = (bf16[2,4,16,128]{3,2,1,0:T(8,128)(2,1)S(1)}, bf16[2,4,16,128]{3,2,1,0:T(8,128)(2,1)S(1)}, u32[]{:S(2)}, u32[]{:S(2)}) collective-permute-start(bf16[2,4,16,128]{3,2,1,0:T(8,128)(2,1)S(1)} %pad_maximum_fusion.73), channel_id=1, source_target_pairs={{0,17},{1,16},{2,19},{3,18},{4,21},{5,20},{6,23},{7,22},{8,25},{9,... | collective-permute-start | bytes 98312 | tf_op jit(solution)/shard_map/ppermute | solution.py:536
  60.1 11.9 %collective-permute-start.26 = (bf16[2,4,16,128]{3,2,1,0:T(8,128)(2,1)S(1)}, bf16[2,4,16,128]{3,2,1,0:T(8,128)(2,1)S(1)}, u32[]{:S(2)}, u32[]{:S(2)}) collective-permute-start(bf16[2,4,16,128]{3,2,1,0:T(8,128)(2,1)S(1)} %pad_maximum_fusion.74), channel_id=1, source_target_pairs={{0,20},{1,21},{2,22},{3,23},{4,16},{5,17},{6,18},{7,19},{8,28},{9,... | collective-permute-start | bytes 98312 | tf_op jit(solution)/shard_map/ppermute | solution.py:536
  62.0 11.9 %collective-permute-start.27 = (bf16[2,4,16,128]{3,2,1,0:T(8,128)(2,1)S(1)}, bf16[2,4,16,128]{3,2,1,0:T(8,128)(2,1)S(1)}, u32[]{:S(2)}, u32[]{:S(2)}) collective-permute-start(bf16[2,4,16,128]{3,2,1,0:T(8,128)(2,1)S(1)} %pad_maximum_fusion.75), channel_id=1, source_target_pairs={{0,21},{1,20},{2,23},{3,22},{4,17},{5,16},{6,19},{7,18},{8,29},{9,... | collective-permute-start | bytes 98312 | tf_op jit(solution)/shard_map/ppermute | solution.py:536
  64.4 9.5 %collective-permute-start.28 = (bf16[2,4,16,128]{3,2,1,0:T(8,128)(2,1)S(1)}, bf16[2,4,16,128]{3,2,1,0:T(8,128)(2,1)S(1)}, u32[]{:S(2)}, u32[]{:S(2)}) collective-permute-start(bf16[2,4,16,128]{3,2,1,0:T(8,128)(2,1)S(1)} %pad_maximum_fusion.76), channel_id=1, source_target_pairs={{0,24},{1,25},{2,26},{3,27},{4,28},{5,29},{6,30},{7,31},{8,16},{9,... | collective-permute-start | bytes 98312 | tf_op jit(solution)/shard_map/ppermute | solution.py:536
  90.3 9.0 %collective-permute-start.37 = (bf16[2,2,4,16,128]{4,3,2,1,0:T(8,128)(2,1)S(1)}, bf16[2,2,4,16,128]{4,3,2,1,0:T(8,128)(2,1)S(1)}, u32[]{:S(2)}, u32[]{:S(2)}) collective-permute-start(bf16[2,2,4,16,128]{4,3,2,1,0:T(8,128)(2,1)S(1)} %pad_maximum_fusion.21), channel_id=1, source_target_pairs={{0,9},{1,8},{2,11},{3,10},{4,13},{5,12},{6,15},{7,14},{8,1},{9,0},... | collective-permute-start | bytes 196616 | tf_op jit(solution)/shard_map/ppermute | solution.py:536
  93.7 10.5 %collective-permute-start.39 = (bf16[2,2,4,16,128]{4,3,2,1,0:T(8,128)(2,1)S(1)}, bf16[2,2,4,16,128]{4,3,2,1,0:T(8,128)(2,1)S(1)}, u32[]{:S(2)}, u32[]{:S(2)}) collective-permute-start(bf16[2,2,4,16,128]{4,3,2,1,0:T(8,128)(2,1)S(1)} %pad_maximum_fusion.23), channel_id=1, source_target_pairs={{0,13},{1,12},{2,15},{3,14},{4,9},{5,8},{6,11},{7,10},{8,5},{9,4},... | collective-permute-start | bytes 196616 | tf_op jit(solution)/shard_map/ppermute | solution.py:536
  96.5 8.9 %collective-permute-start.40 = (bf16[2,2,4,16,128]{4,3,2,1,0:T(8,128)(2,1)S(1)}, bf16[2,2,4,16,128]{4,3,2,1,0:T(8,128)(2,1)S(1)}, u32[]{:S(2)}, u32[]{:S(2)}) collective-permute-start(bf16[2,2,4,16,128]{4,3,2,1,0:T(8,128)(2,1)S(1)} %pad_maximum_fusion.24), channel_id=1, source_target_pairs={{0,16},{1,17},{2,18},{3,19},{4,20},{5,21},{6,22},{7,23},{8,24},{9,... | collective-permute-start | bytes 196616 | tf_op jit(solution)/shard_map/ppermute | solution.py:536
  96.5 12.9 %collective-permute-start.41 = (bf16[2,2,4,16,128]{4,3,2,1,0:T(8,128)(2,1)S(1)}, bf16[2,2,4,16,128]{4,3,2,1,0:T(8,128)(2,1)S(1)}, u32[]{:S(2)}, u32[]{:S(2)}) collective-permute-start(bf16[2,2,4,16,128]{4,3,2,1,0:T(8,128)(2,1)S(1)} %pad_maximum_fusion.25), channel_id=1, source_target_pairs={{0,17},{1,16},{2,19},{3,18},{4,21},{5,20},{6,23},{7,22},{8,25},{9,... | collective-permute-start | bytes 196616 | tf_op jit(solution)/shard_map/ppermute | solution.py:536
  99.3 13.8 %collective-permute-start.42 = (bf16[2,2,4,16,128]{4,3,2,1,0:T(8,128)(2,1)S(1)}, bf16[2,2,4,16,128]{4,3,2,1,0:T(8,128)(2,1)S(1)}, u32[]{:S(2)}, u32[]{:S(2)}) collective-permute-start(bf16[2,2,4,16,128]{4,3,2,1,0:T(8,128)(2,1)S(1)} %pad_maximum_fusion.26), channel_id=1, source_target_pairs={{0,20},{1,21},{2,22},{3,23},{4,16},{5,17},{6,18},{7,19},{8,28},{9,... | collective-permute-start | bytes 196616 | tf_op jit(solution)/shard_map/ppermute | solution.py:536
  100.5 15.0 %collective-permute-start.43 = (bf16[2,2,4,16,128]{4,3,2,1,0:T(8,128)(2,1)S(1)}, bf16[2,2,4,16,128]{4,3,2,1,0:T(8,128)(2,1)S(1)}, u32[]{:S(2)}, u32[]{:S(2)}) collective-permute-start(bf16[2,2,4,16,128]{4,3,2,1,0:T(8,128)(2,1)S(1)} %pad_maximum_fusion.27), channel_id=1, source_target_pairs={{0,21},{1,20},{2,23},{3,22},{4,17},{5,16},{6,19},{7,18},{8,29},{9,... | collective-permute-start | bytes 196616 | tf_op jit(solution)/shard_map/ppermute | solution.py:536
  104.2 11.3 %collective-permute-start.44 = (bf16[2,2,4,16,128]{4,3,2,1,0:T(8,128)(2,1)S(1)}, bf16[2,2,4,16,128]{4,3,2,1,0:T(8,128)(2,1)S(1)}, u32[]{:S(2)}, u32[]{:S(2)}) collective-permute-start(bf16[2,2,4,16,128]{4,3,2,1,0:T(8,128)(2,1)S(1)} %pad_maximum_fusion.28), channel_id=1, source_target_pairs={{0,24},{1,25},{2,26},{3,27},{4,28},{5,29},{6,30},{7,31},{8,16},{9,... | collective-permute-start | bytes 196616 | tf_op jit(solution)/shard_map/ppermute | solution.py:536
  105.4 10.2 %collective-permute-start.45 = (bf16[2,2,4,16,128]{4,3,2,1,0:T(8,128)(2,1)S(1)}, bf16[2,2,4,16,128]{4,3,2,1,0:T(8,128)(2,1)S(1)}, u32[]{:S(2)}, u32[]{:S(2)}) collective-permute-start(bf16[2,2,4,16,128]{4,3,2,1,0:T(8,128)(2,1)S(1)} %pad_maximum_fusion.29), channel_id=1, source_target_pairs={{0,25},{1,24},{2,27},{3,26},{4,29},{5,28},{6,31},{7,30},{8,17},{9,... | collective-permute-start | bytes 196616 | tf_op jit(solution)/shard_map/ppermute | solution.py:536
  127.7 9.1 %collective-permute-start.53 = (bf16[2,4,16,128]{3,2,1,0:T(8,128)(2,1)S(1)}, bf16[2,4,16,128]{3,2,1,0:T(8,128)(2,1)S(1)}, u32[]{:S(2)}, u32[]{:S(2)}) collective-permute-start(bf16[2,4,16,128]{3,2,1,0:T(8,128)(2,1)S(1)} %pad_maximum_fusion.85), channel_id=1, source_target_pairs={{0,9},{1,8},{2,11},{3,10},{4,13},{5,12},{6,15},{7,14},{8,1},{9,0},... | collective-permute-start | bytes 98312 | tf_op jit(solution)/shard_map/ppermute | solution.py:536
  130.4 10.3 %collective-permute-start.55 = (bf16[2,4,16,128]{3,2,1,0:T(8,128)(2,1)S(1)}, bf16[2,4,16,128]{3,2,1,0:T(8,128)(2,1)S(1)}, u32[]{:S(2)}, u32[]{:S(2)}) collective-permute-start(bf16[2,4,16,128]{3,2,1,0:T(8,128)(2,1)S(1)} %pad_maximum_fusion.87), channel_id=1, source_target_pairs={{0,13},{1,12},{2,15},{3,14},{4,9},{5,8},{6,11},{7,10},{8,5},{9,4},... | collective-permute-start | bytes 98312 | tf_op jit(solution)/shard_map/ppermute | solution.py:536
  132.9 8.7 %collective-permute-start.56 = (bf16[2,4,16,128]{3,2,1,0:T(8,128)(2,1)S(1)}, bf16[2,4,16,128]{3,2,1,0:T(8,128)(2,1)S(1)}, u32[]{:S(2)}, u32[]{:S(2)}) collective-permute-start(bf16[2,4,16,128]{3,2,1,0:T(8,128)(2,1)S(1)} %pad_maximum_fusion.88), channel_id=1, source_target_pairs={{0,16},{1,17},{2,18},{3,19},{4,20},{5,21},{6,22},{7,23},{8,24},{9,... | collective-permute-start | bytes 98312 | tf_op jit(solution)/shard_map/ppermute | solution.py:536
  133.9 11.6 %collective-permute-start.57 = (bf16[2,4,16,128]{3,2,1,0:T(8,128)(2,1)S(1)}, bf16[2,4,16,128]{3,2,1,0:T(8,128)(2,1)S(1)}, u32[]{:S(2)}, u32[]{:S(2)}) collective-permute-start(bf16[2,4,16,128]{3,2,1,0:T(8,128)(2,1)S(1)} %pad_maximum_fusion.89), channel_id=1, source_target_pairs={{0,17},{1,16},{2,19},{3,18},{4,21},{5,20},{6,23},{7,22},{8,25},{9,... | collective-permute-start | bytes 98312 | tf_op jit(solution)/shard_map/ppermute | solution.py:536
  136.9 9.3 %collective-permute-start.58 = (bf16[2,4,16,128]{3,2,1,0:T(8,128)(2,1)S(1)}, bf16[2,4,16,128]{3,2,1,0:T(8,128)(2,1)S(1)}, u32[]{:S(2)}, u32[]{:S(2)}) collective-permute-start(bf16[2,4,16,128]{3,2,1,0:T(8,128)(2,1)S(1)} %pad_maximum_fusion.90), channel_id=1, source_target_pairs={{0,20},{1,21},{2,22},{3,23},{4,16},{5,17},{6,18},{7,19},{8,28},{9,... | collective-permute-start | bytes 98312 | tf_op jit(solution)/shard_map/ppermute | solution.py:536
  137.9 12.2 %collective-permute-start.59 = (bf16[2,4,16,128]{3,2,1,0:T(8,128)(2,1)S(1)}, bf16[2,4,16,128]{3,2,1,0:T(8,128)(2,1)S(1)}, u32[]{:S(2)}, u32[]{:S(2)}) collective-permute-start(bf16[2,4,16,128]{3,2,1,0:T(8,128)(2,1)S(1)} %pad_maximum_fusion.91), channel_id=1, source_target_pairs={{0,21},{1,20},{2,23},{3,22},{4,17},{5,16},{6,19},{7,18},{8,29},{9,... | collective-permute-start | bytes 98312 | tf_op jit(solution)/shard_map/ppermute | solution.py:536
  140.7 9.5 %collective-permute-start.60 = (bf16[2,4,16,128]{3,2,1,0:T(8,128)(2,1)S(1)}, bf16[2,4,16,128]{3,2,1,0:T(8,128)(2,1)S(1)}, u32[]{:S(2)}, u32[]{:S(2)}) collective-permute-start(bf16[2,4,16,128]{3,2,1,0:T(8,128)(2,1)S(1)} %pad_maximum_fusion.92), channel_id=1, source_target_pairs={{0,24},{1,25},{2,26},{3,27},{4,28},{5,29},{6,30},{7,31},{8,16},{9,... | collective-permute-start | bytes 98312 | tf_op jit(solution)/shard_map/ppermute | solution.py:536
  162.9 10.2 %collective-permute-start.69 = (bf16[2,4,16,128]{3,2,1,0:T(8,128)(2,1)S(1)}, bf16[2,4,16,128]{3,2,1,0:T(8,128)(2,1)S(1)}, u32[]{:S(2)}, u32[]{:S(2)}) collective-permute-start(bf16[2,4,16,128]{3,2,1,0:T(8,128)(2,1)S(1)} %pad_maximum_fusion.101), channel_id=1, source_target_pairs={{0,9},{1,8},{2,11},{3,10},{4,13},{5,12},{6,15},{7,14},{8,1},{9,0},... | collective-permute-start | bytes 98312 | tf_op jit(solution)/shard_map/ppermute | solution.py:536
  166.5 10.2 %collective-permute-start.71 = (bf16[2,4,16,128]{3,2,1,0:T(8,128)(2,1)S(1)}, bf16[2,4,16,128]{3,2,1,0:T(8,128)(2,1)S(1)}, u32[]{:S(2)}, u32[]{:S(2)}) collective-permute-start(bf16[2,4,16,128]{3,2,1,0:T(8,128)(2,1)S(1)} %pad_maximum_fusion.103), channel_id=1, source_target_pairs={{0,13},{1,12},{2,15},{3,14},{4,9},{5,8},{6,11},{7,10},{8,5},{9,4},... | collective-permute-start | bytes 98312 | tf_op jit(solution)/shard_map/ppermute | solution.py:536
  169.0 11.1 %collective-permute-start.72 = (bf16[2,4,16,128]{3,2,1,0:T(8,128)(2,1)S(1)}, bf16[2,4,16,128]{3,2,1,0:T(8,128)(2,1)S(1)}, u32[]{:S(2)}, u32[]{:S(2)}) collective-permute-start(bf16[2,4,16,128]{3,2,1,0:T(8,128)(2,1)S(1)} %pad_maximum_fusion.104), channel_id=1, source_target_pairs={{0,16},{1,17},{2,18},{3,19},{4,20},{5,21},{6,22},{7,23},{8,24},{9,... | collective-permute-start | bytes 98312 | tf_op jit(solution)/shard_map/ppermute | solution.py:536
  170.9 10.8 %collective-permute-start.73 = (bf16[2,4,16,128]{3,2,1,0:T(8,128)(2,1)S(1)}, bf16[2,4,16,128]{3,2,1,0:T(8,128)(2,1)S(1)}, u32[]{:S(2)}, u32[]{:S(2)}) collective-permute-start(bf16[2,4,16,128]{3,2,1,0:T(8,128)(2,1)S(1)} %pad_maximum_fusion.105), channel_id=1, source_target_pairs={{0,17},{1,16},{2,19},{3,18},{4,21},{5,20},{6,23},{7,22},{8,25},{9,... | collective-permute-start | bytes 98312 | tf_op jit(solution)/shard_map/ppermute | solution.py:536
  173.1 11.3 %collective-permute-start.74 = (bf16[2,4,16,128]{3,2,1,0:T(8,128)(2,1)S(1)}, bf16[2,4,16,128]{3,2,1,0:T(8,128)(2,1)S(1)}, u32[]{:S(2)}, u32[]{:S(2)}) collective-permute-start(bf16[2,4,16,128]{3,2,1,0:T(8,128)(2,1)S(1)} %pad_maximum_fusion.106), channel_id=1, source_target_pairs={{0,20},{1,21},{2,22},{3,23},{4,16},{5,17},{6,18},{7,19},{8,28},{9,... | collective-permute-start | bytes 98312 | tf_op jit(solution)/shard_map/ppermute | solution.py:536
  174.5 11.7 %collective-permute-start.75 = (bf16[2,4,16,128]{3,2,1,0:T(8,128)(2,1)S(1)}, bf16[2,4,16,128]{3,2,1,0:T(8,128)(2,1)S(1)}, u32[]{:S(2)}, u32[]{:S(2)}) collective-permute-start(bf16[2,4,16,128]{3,2,1,0:T(8,128)(2,1)S(1)} %pad_maximum_fusion.107), channel_id=1, source_target_pairs={{0,21},{1,20},{2,23},{3,22},{4,17},{5,16},{6,19},{7,18},{8,29},{9,... | collective-permute-start | bytes 98312 | tf_op jit(solution)/shard_map/ppermute | solution.py:536
  176.7 9.5 %collective-permute-start.76 = (bf16[2,4,16,128]{3,2,1,0:T(8,128)(2,1)S(1)}, bf16[2,4,16,128]{3,2,1,0:T(8,128)(2,1)S(1)}, u32[]{:S(2)}, u32[]{:S(2)}) collective-permute-start(bf16[2,4,16,128]{3,2,1,0:T(8,128)(2,1)S(1)} %pad_maximum_fusion.108), channel_id=1, source_target_pairs={{0,24},{1,25},{2,26},{3,27},{4,28},{5,29},{6,30},{7,31},{8,16},{9,... | collective-permute-start | bytes 98312 | tf_op jit(solution)/shard_map/ppermute | solution.py:536
  198.5 10.1 %collective-permute-start.85 = (bf16[2,2,4,16,128]{4,3,2,1,0:T(8,128)(2,1)S(1)}, bf16[2,2,4,16,128]{4,3,2,1,0:T(8,128)(2,1)S(1)}, u32[]{:S(2)}, u32[]{:S(2)}) collective-permute-start(bf16[2,2,4,16,128]{4,3,2,1,0:T(8,128)(2,1)S(1)} %pad_maximum_fusion.37), channel_id=1, source_target_pairs={{0,9},{1,8},{2,11},{3,10},{4,13},{5,12},{6,15},{7,14},{8,1},{9,0},... | collective-permute-start | bytes 196616 | tf_op jit(solution)/shard_map/ppermute | solution.py:536
  202.0 10.3 %collective-permute-start.87 = (bf16[2,2,4,16,128]{4,3,2,1,0:T(8,128)(2,1)S(1)}, bf16[2,2,4,16,128]{4,3,2,1,0:T(8,128)(2,1)S(1)}, u32[]{:S(2)}, u32[]{:S(2)}) collective-permute-start(bf16[2,2,4,16,128]{4,3,2,1,0:T(8,128)(2,1)S(1)} %pad_maximum_fusion.39), channel_id=1, source_target_pairs={{0,13},{1,12},{2,15},{3,14},{4,9},{5,8},{6,11},{7,10},{8,5},{9,4},... | collective-permute-start | bytes 196616 | tf_op jit(solution)/shard_map/ppermute | solution.py:536
  204.6 10.0 %collective-permute-start.88 = (bf16[2,2,4,16,128]{4,3,2,1,0:T(8,128)(2,1)S(1)}, bf16[2,2,4,16,128]{4,3,2,1,0:T(8,128)(2,1)S(1)}, u32[]{:S(2)}, u32[]{:S(2)}) collective-permute-start(bf16[2,2,4,16,128]{4,3,2,1,0:T(8,128)(2,1)S(1)} %pad_maximum_fusion.40), channel_id=1, source_target_pairs={{0,16},{1,17},{2,18},{3,19},{4,20},{5,21},{6,22},{7,23},{8,24},{9,... | collective-permute-start | bytes 196616 | tf_op jit(solution)/shard_map/ppermute | solution.py:536
  204.6 13.5 %collective-permute-start.89 = (bf16[2,2,4,16,128]{4,3,2,1,0:T(8,128)(2,1)S(1)}, bf16[2,2,4,16,128]{4,3,2,1,0:T(8,128)(2,1)S(1)}, u32[]{:S(2)}, u32[]{:S(2)}) collective-permute-start(bf16[2,2,4,16,128]{4,3,2,1,0:T(8,128)(2,1)S(1)} %pad_maximum_fusion.41), channel_id=1, source_target_pairs={{0,17},{1,16},{2,19},{3,18},{4,21},{5,20},{6,23},{7,22},{8,25},{9,... | collective-permute-start | bytes 196616 | tf_op jit(solution)/shard_map/ppermute | solution.py:536
  208.6 12.8 %collective-permute-start.90 = (bf16[2,2,4,16,128]{4,3,2,1,0:T(8,128)(2,1)S(1)}, bf16[2,2,4,16,128]{4,3,2,1,0:T(8,128)(2,1)S(1)}, u32[]{:S(2)}, u32[]{:S(2)}) collective-permute-start(bf16[2,2,4,16,128]{4,3,2,1,0:T(8,128)(2,1)S(1)} %pad_maximum_fusion.42), channel_id=1, source_target_pairs={{0,20},{1,21},{2,22},{3,23},{4,16},{5,17},{6,18},{7,19},{8,28},{9,... | collective-permute-start | bytes 196616 | tf_op jit(solution)/shard_map/ppermute | solution.py:536
  208.9 15.3 %collective-permute-start.91 = (bf16[2,2,4,16,128]{4,3,2,1,0:T(8,128)(2,1)S(1)}, bf16[2,2,4,16,128]{4,3,2,1,0:T(8,128)(2,1)S(1)}, u32[]{:S(2)}, u32[]{:S(2)}) collective-permute-start(bf16[2,2,4,16,128]{4,3,2,1,0:T(8,128)(2,1)S(1)} %pad_maximum_fusion.43), channel_id=1, source_target_pairs={{0,21},{1,20},{2,23},{3,22},{4,17},{5,16},{6,19},{7,18},{8,29},{9,... | collective-permute-start | bytes 196616 | tf_op jit(solution)/shard_map/ppermute | solution.py:536
  212.4 11.8 %collective-permute-start.92 = (bf16[2,2,4,16,128]{4,3,2,1,0:T(8,128)(2,1)S(1)}, bf16[2,2,4,16,128]{4,3,2,1,0:T(8,128)(2,1)S(1)}, u32[]{:S(2)}, u32[]{:S(2)}) collective-permute-start(bf16[2,2,4,16,128]{4,3,2,1,0:T(8,128)(2,1)S(1)} %pad_maximum_fusion.44), channel_id=1, source_target_pairs={{0,24},{1,25},{2,26},{3,27},{4,28},{5,29},{6,30},{7,31},{8,16},{9,... | collective-permute-start | bytes 196616 | tf_op jit(solution)/shard_map/ppermute | solution.py:536
  214.6 9.6 %collective-permute-start.93 = (bf16[2,2,4,16,128]{4,3,2,1,0:T(8,128)(2,1)S(1)}, bf16[2,2,4,16,128]{4,3,2,1,0:T(8,128)(2,1)S(1)}, u32[]{:S(2)}, u32[]{:S(2)}) collective-permute-start(bf16[2,2,4,16,128]{4,3,2,1,0:T(8,128)(2,1)S(1)} %pad_maximum_fusion.45), channel_id=1, source_target_pairs={{0,25},{1,24},{2,27},{3,26},{4,29},{5,28},{6,31},{7,30},{8,17},{9,... | collective-permute-start | bytes 196616 | tf_op jit(solution)/shard_map/ppermute | solution.py:536
  246.6 8.8 %collective-permute-start.102 = (bf16[2,4,16,128]{3,2,1,0:T(8,128)(2,1)S(1)}, bf16[2,4,16,128]{3,2,1,0:T(8,128)(2,1)S(1)}, u32[]{:S(2)}, u32[]{:S(2)}) collective-permute-start(bf16[2,4,16,128]{3,2,1,0:T(8,128)(2,1)S(1)} %pad_maximum_fusion.118), channel_id=1, source_target_pairs={{0,12},{1,13},{2,14},{3,15},{4,8},{5,9},{6,10},{7,11},{8,4},{9,5},... | collective-permute-start | bytes 98312 | tf_op jit(solution)/shard_map/ppermute | solution.py:536
  248.1 9.6 %collective-permute-start.103 = (bf16[2,4,16,128]{3,2,1,0:T(8,128)(2,1)S(1)}, bf16[2,4,16,128]{3,2,1,0:T(8,128)(2,1)S(1)}, u32[]{:S(2)}, u32[]{:S(2)}) collective-permute-start(bf16[2,4,16,128]{3,2,1,0:T(8,128)(2,1)S(1)} %pad_maximum_fusion.119), channel_id=1, source_target_pairs={{0,13},{1,12},{2,15},{3,14},{4,9},{5,8},{6,11},{7,10},{8,5},{9,4},... | collective-permute-start | bytes 98312 | tf_op jit(solution)/shard_map/ppermute | solution.py:536
  250.0 9.1 %collective-permute-start.104 = (bf16[2,4,16,128]{3,2,1,0:T(8,128)(2,1)S(1)}, bf16[2,4,16,128]{3,2,1,0:T(8,128)(2,1)S(1)}, u32[]{:S(2)}, u32[]{:S(2)}) collective-permute-start(bf16[2,4,16,128]{3,2,1,0:T(8,128)(2,1)S(1)} %pad_maximum_fusion.120), channel_id=1, source_target_pairs={{0,16},{1,17},{2,18},{3,19},{4,20},{5,21},{6,22},{7,23},{8,24},{9,... | collective-permute-start | bytes 98312 | tf_op jit(solution)/shard_map/ppermute | solution.py:536
  251.3 10.7 %collective-permute-start.105 = (bf16[2,4,16,128]{3,2,1,0:T(8,128)(2,1)S(1)}, bf16[2,4,16,128]{3,2,1,0:T(8,128)(2,1)S(1)}, u32[]{:S(2)}, u32[]{:S(2)}) collective-permute-start(bf16[2,4,16,128]{3,2,1,0:T(8,128)(2,1)S(1)} %pad_maximum_fusion.121), channel_id=1, source_target_pairs={{0,17},{1,16},{2,19},{3,18},{4,21},{5,20},{6,23},{7,22},{8,25},{9,... | collective-permute-start | bytes 98312 | tf_op jit(solution)/shard_map/ppermute | solution.py:536
  253.4 11.0 %collective-permute-start.106 = (bf16[2,4,16,128]{3,2,1,0:T(8,128)(2,1)S(1)}, bf16[2,4,16,128]{3,2,1,0:T(8,128)(2,1)S(1)}, u32[]{:S(2)}, u32[]{:S(2)}) collective-permute-start(bf16[2,4,16,128]{3,2,1,0:T(8,128)(2,1)S(1)} %pad_maximum_fusion.122), channel_id=1, source_target_pairs={{0,20},{1,21},{2,22},{3,23},{4,16},{5,17},{6,18},{7,19},{8,28},{9,... | collective-permute-start | bytes 98312 | tf_op jit(solution)/shard_map/ppermute | solution.py:536
  255.4 11.8 %collective-permute-start.107 = (bf16[2,4,16,128]{3,2,1,0:T(8,128)(2,1)S(1)}, bf16[2,4,16,128]{3,2,1,0:T(8,128)(2,1)S(1)}, u32[]{:S(2)}, u32[]{:S(2)}) collective-permute-start(bf16[2,4,16,128]{3,2,1,0:T(8,128)(2,1)S(1)} %pad_maximum_fusion.123), channel_id=1, source_target_pairs={{0,21},{1,20},{2,23},{3,22},{4,17},{5,16},{6,19},{7,18},{8,29},{9,... | collective-permute-start | bytes 98312 | tf_op jit(solution)/shard_map/ppermute | solution.py:536
  257.8 9.5 %collective-permute-start.108 = (bf16[2,4,16,128]{3,2,1,0:T(8,128)(2,1)S(1)}, bf16[2,4,16,128]{3,2,1,0:T(8,128)(2,1)S(1)}, u32[]{:S(2)}, u32[]{:S(2)}) collective-permute-start(bf16[2,4,16,128]{3,2,1,0:T(8,128)(2,1)S(1)} %pad_maximum_fusion.124), channel_id=1, source_target_pairs={{0,24},{1,25},{2,26},{3,27},{4,28},{5,29},{6,30},{7,31},{8,16},{9,... | collective-permute-start | bytes 98312 | tf_op jit(solution)/shard_map/ppermute | solution.py:536
  278.5 8.7 %collective-permute-start.117 = (bf16[2,2,4,16,128]{4,3,2,1,0:T(8,128)(2,1)S(1)}, bf16[2,2,4,16,128]{4,3,2,1,0:T(8,128)(2,1)S(1)}, u32[]{:S(2)}, u32[]{:S(2)}) collective-permute-start(bf16[2,2,4,16,128]{4,3,2,1,0:T(8,128)(2,1)S(1)} %pad_maximum_fusion.53), channel_id=1, source_target_pairs={{0,9},{1,8},{2,11},{3,10},{4,13},{5,12},{6,15},{7,14},{8,1},{9,0},... | collective-permute-start | bytes 196616 | tf_op jit(solution)/shard_map/ppermute | solution.py:536
  280.3 8.9 %collective-permute-start.118 = (bf16[2,2,4,16,128]{4,3,2,1,0:T(8,128)(2,1)S(1)}, bf16[2,2,4,16,128]{4,3,2,1,0:T(8,128)(2,1)S(1)}, u32[]{:S(2)}, u32[]{:S(2)}) collective-permute-start(bf16[2,2,4,16,128]{4,3,2,1,0:T(8,128)(2,1)S(1)} %pad_maximum_fusion.54), channel_id=1, source_target_pairs={{0,12},{1,13},{2,14},{3,15},{4,8},{5,9},{6,10},{7,11},{8,4},{9,5},... | collective-permute-start | bytes 196616 | tf_op jit(solution)/shard_map/ppermute | solution.py:536
  281.1 11.2 %collective-permute-start.119 = (bf16[2,2,4,16,128]{4,3,2,1,0:T(8,128)(2,1)S(1)}, bf16[2,2,4,16,128]{4,3,2,1,0:T(8,128)(2,1)S(1)}, u32[]{:S(2)}, u32[]{:S(2)}) collective-permute-start(bf16[2,2,4,16,128]{4,3,2,1,0:T(8,128)(2,1)S(1)} %pad_maximum_fusion.55), channel_id=1, source_target_pairs={{0,13},{1,12},{2,15},{3,14},{4,9},{5,8},{6,11},{7,10},{8,5},{9,4},... | collective-permute-start | bytes 196616 | tf_op jit(solution)/shard_map/ppermute | solution.py:536
  284.6 10.8 %collective-permute-start.120 = (bf16[2,2,4,16,128]{4,3,2,1,0:T(8,128)(2,1)S(1)}, bf16[2,2,4,16,128]{4,3,2,1,0:T(8,128)(2,1)S(1)}, u32[]{:S(2)}, u32[]{:S(2)}) collective-permute-start(bf16[2,2,4,16,128]{4,3,2,1,0:T(8,128)(2,1)S(1)} %pad_maximum_fusion.56), channel_id=1, source_target_pairs={{0,16},{1,17},{2,18},{3,19},{4,20},{5,21},{6,22},{7,23},{8,24},{9,... | collective-permute-start | bytes 196616 | tf_op jit(solution)/shard_map/ppermute | solution.py:536
  286.0 10.5 %collective-permute-start.121 = (bf16[2,2,4,16,128]{4,3,2,1,0:T(8,128)(2,1)S(1)}, bf16[2,2,4,16,128]{4,3,2,1,0:T(8,128)(2,1)S(1)}, u32[]{:S(2)}, u32[]{:S(2)}) collective-permute-start(bf16[2,2,4,16,128]{4,3,2,1,0:T(8,128)(2,1)S(1)} %pad_maximum_fusion.57), channel_id=1, source_target_pairs={{0,17},{1,16},{2,19},{3,18},{4,21},{5,20},{6,23},{7,22},{8,25},{9,... | collective-permute-start | bytes 196616 | tf_op jit(solution)/shard_map/ppermute | solution.py:536
  287.1 13.5 %collective-permute-start.122 = (bf16[2,2,4,16,128]{4,3,2,1,0:T(8,128)(2,1)S(1)}, bf16[2,2,4,16,128]{4,3,2,1,0:T(8,128)(2,1)S(1)}, u32[]{:S(2)}, u32[]{:S(2)}) collective-permute-start(bf16[2,2,4,16,128]{4,3,2,1,0:T(8,128)(2,1)S(1)} %pad_maximum_fusion.58), channel_id=1, source_target_pairs={{0,20},{1,21},{2,22},{3,23},{4,16},{5,17},{6,18},{7,19},{8,28},{9,... | collective-permute-start | bytes 196616 | tf_op jit(solution)/shard_map/ppermute | solution.py:536
  289.2 16.0 %collective-permute-start.123 = (bf16[2,2,4,16,128]{4,3,2,1,0:T(8,128)(2,1)S(1)}, bf16[2,2,4,16,128]{4,3,2,1,0:T(8,128)(2,1)S(1)}, u32[]{:S(2)}, u32[]{:S(2)}) collective-permute-start(bf16[2,2,4,16,128]{4,3,2,1,0:T(8,128)(2,1)S(1)} %pad_maximum_fusion.59), channel_id=1, source_target_pairs={{0,21},{1,20},{2,23},{3,22},{4,17},{5,16},{6,19},{7,18},{8,29},{9,... | collective-permute-start | bytes 196616 | tf_op jit(solution)/shard_map/ppermute | solution.py:536
  292.3 12.9 %collective-permute-start.124 = (bf16[2,2,4,16,128]{4,3,2,1,0:T(8,128)(2,1)S(1)}, bf16[2,2,4,16,128]{4,3,2,1,0:T(8,128)(2,1)S(1)}, u32[]{:S(2)}, u32[]{:S(2)}) collective-permute-start(bf16[2,2,4,16,128]{4,3,2,1,0:T(8,128)(2,1)S(1)} %pad_maximum_fusion.60), channel_id=1, source_target_pairs={{0,24},{1,25},{2,26},{3,27},{4,28},{5,29},{6,30},{7,31},{8,16},{9,... | collective-permute-start | bytes 196616 | tf_op jit(solution)/shard_map/ppermute | solution.py:536
  295.3 9.9 %collective-permute-start.125 = (bf16[2,2,4,16,128]{4,3,2,1,0:T(8,128)(2,1)S(1)}, bf16[2,2,4,16,128]{4,3,2,1,0:T(8,128)(2,1)S(1)}, u32[]{:S(2)}, u32[]{:S(2)}) collective-permute-start(bf16[2,2,4,16,128]{4,3,2,1,0:T(8,128)(2,1)S(1)} %pad_maximum_fusion.61), channel_id=1, source_target_pairs={{0,25},{1,24},{2,27},{3,26},{4,29},{5,28},{6,31},{7,30},{8,17},{9,... | collective-permute-start | bytes 196616 | tf_op jit(solution)/shard_map/ppermute | solution.py:536
  296.5 8.7 %collective-permute-start.126 = (bf16[2,2,4,16,128]{4,3,2,1,0:T(8,128)(2,1)S(1)}, bf16[2,2,4,16,128]{4,3,2,1,0:T(8,128)(2,1)S(1)}, u32[]{:S(2)}, u32[]{:S(2)}) collective-permute-start(bf16[2,2,4,16,128]{4,3,2,1,0:T(8,128)(2,1)S(1)} %pad_maximum_fusion.62), channel_id=1, source_target_pairs={{0,28},{1,29},{2,30},{3,31},{4,24},{5,25},{6,26},{7,27},{8,20},{9,... | collective-permute-start | bytes 196616 | tf_op jit(solution)/shard_map/ppermute | solution.py:536
  (74 other events, 1047.4 us)

commit v7 on v4

--- a/solution.py
+++ b/solution.py
@@ -288,7 +288,7 @@
     sums[...] = jnp.zeros_like(sums)
     half = proj_factor.shape[1]
 
-    def body(step):
+    def upper(step):
         place = lane_block(step, lanes)
         here = get_rows(scr, step, half, rows)
         d_proj = (here * proj_factor[step]).astype(BF16)
@@ -300,10 +300,14 @@
         scaled = scaled_in[step]
         sums[2] += d_normed * scaled
         sums[3] += d_normed
-        grad = cot[step] + norm_backward(d_normed * gain, scaled, inverse_in[pl.ds(step, 1), :])
-        grad_out[step] = grad
+        grad_out[step] = cot[step] + norm_backward(
+            d_normed * gain, scaled, inverse_in[pl.ds(step, 1), :]
+        )
+
+    def lower(step):
+        place = lane_block(step, lanes)
         gate = outgate[step]
-        gated = grad * gate
+        gated = grad_out[step] * gate
         d_outer = gated.astype(BF16)
         d_unit = dot(out_w[0], d_outer)
         scaled = scaled_mid[step]
@@ -320,7 +324,8 @@
         sums[0] += d_unit * scaled
         sums[1] += d_unit
 
-    each_row(rows, 4, body)
+    each_row(rows, 4, upper)
+    each_row(rows, 4, lower)
     d_tri_out[...] = scr_tri[...].reshape(d_tri_out.shape).astype(BF16)
     out_weight_grads(unit_all, outer_all, normed_all, gate_all, out_weights)
     in_weight_grads(upper_all, d_in_all, in_weights)
@@ -328,15 +333,20 @@
         small_out[index : index + 1, :] = as_row(sums[index])
 
 
+def split_cores(all_rows, own_out, other_out, few):
+    chips, share, width = own_out.shape
+    view = all_rows.reshape(chips // few, 2, few, share, width)
+    core = lax.rem(lax.axis_index("row"), 2)
+    own_out[...] = view[:, core].reshape(own_out.shape)
+    other_out[...] = view[:, 1 - core].reshape(other_out.shape)
+
+
 def finish_kernel(
-    d_edge, proj_factor, gate_factor, d_normed_gate, scaled_in, inverse_in, grad, normed,
-    ngain, proj_w, gate_w, out0, in1, out1,
-    packed_out, grad_out, small_out, scr, normed_all, d_in_all, sums,
+    few, d_edge, proj_factor, gate_factor, normed, out0, in1, out1,
+    own_out, other_out, d_in_out, scr, normed_all, d_in_all, packed,
 ):
     rows, half, lanes = proj_factor.shape
-    gain = column(ngain, 0, lanes)
     collect_edges(d_edge, scr)
-    sums[...] = jnp.zeros_like(sums)
 
     def body(step):
         place = lane_block(step, lanes)
@@ -344,9 +354,29 @@
         d_proj = (here * proj_factor[step]).astype(BF16)
         d_gate = (here * gate_factor[step]).astype(BF16)
         d_in = jnp.concatenate([d_proj, d_gate], axis=0)
+        d_in_out[step] = d_in
         d_in_all[:, place] = d_in
         normed_all[:, place] = normed[step]
-        d_normed = in_normed(d_in, d_normed_gate[step], proj_w[0], gate_w[0])
+
+    each_row(rows, 4, body)
+    first, second, third = d_in_all.shape[0], out0.shape[0], in1.shape[0]
+    in_weight_grads(normed_all, d_in_all, packed.at[0:first])
+    packed[first : first + second, :] = out0[...]
+    packed[first + second : first + second + third, :] = in1[...]
+    packed[first + second + third :, :] = out1[...]
+    split_cores(packed, own_out, other_out, few)
+
+
+def behind_finish_kernel(
+    d_in, d_normed_gate, scaled_in, inverse_in, grad, ngain, proj_w, gate_w,
+    grad_out, small_out, sums,
+):
+    rows, channels, lanes = grad.shape
+    gain = column(ngain, 0, lanes)
+    sums[...] = jnp.zeros_like(sums)
+
+    def body(step):
+        d_normed = in_normed(d_in[step], d_normed_gate[step], proj_w[0], gate_w[0])
         scaled = scaled_in[step]
         sums[0] += d_normed * scaled
         sums[1] += d_normed
@@ -354,36 +384,47 @@
         grad_out[step] = jnp.transpose(total).astype(BF16)
 
     each_row(rows, 4, body)
-    first, second, third = d_in_all.shape[0], out0.shape[0], in1.shape[0]
-    in_weight_grads(normed_all, d_in_all, packed_out.at[0:first])
-    packed_out[first : first + second, :] = out0[...]
-    packed_out[first + second : first + second + third, :] = in1[...]
-    packed_out[first + second + third :, :] = out1[...]
     for index in range(2):
         small_out[index : index + 1, :] = as_row(sums[index])
 
 
+def add_kernel(first, second, out_ref):
+    out_ref[...] = (first[...].astype(F32) + second[...].astype(F32)).astype(BF16)
+
+
 def sum_kernel(parts, small0, small_middle, small1, shared_out):
-    shards, share, width = parts.shape
+    chips, share, width = parts.shape
     own = jnp.sum(parts[...].astype(F32), axis=0).astype(BF16)
     small = jnp.concatenate(
         [small0[...], small_middle[0:2], small_middle[2:4], small1[...]], axis=0
     )
     high = small.astype(BF16).astype(F32)
     extra = jnp.concatenate([high, small - high], axis=0).astype(BF16)
-    for shard in range(shards):
-        shared_out[shard, 0:share] = own
-        shared_out[shard, share:] = extra
-
-
-def unpack_kernel(share, shared, proj_out, gate_out, out_out, outgate_out, small_out):
-    shards, _, width = shared.shape
-    total = jnp.sum(shared[:, share:, :].astype(F32), axis=0)
-    small_out[...] = total[0:8] + total[8:16]
-    weights = shared[:, 0:share, :].reshape(shards * share, width).astype(F32)
+    for chip in range(chips):
+        shared_out[chip, 0:share] = own
+        shared_out[chip, share:] = extra
+
+
+def unpack_kernel(
+    share, few, own, other, proj_out, gate_out, out_out, outgate_out,
+    norm_gain_out, norm_bias_out, mid_gain_out, mid_bias_out, weights,
+):
+    chips, _, width = own.shape
+    core = lax.rem(lax.axis_index("row"), 2)
+    view = weights.reshape(chips // few, 2, few, share, width)
+    block = (chips // few, few, share, width)
+    view[:, core] = own[:, 0:share].astype(F32).reshape(block)
+    view[:, 1 - core] = other[:, 0:share].astype(F32).reshape(block)
+    mine = jnp.sum(own[:, share:].astype(F32), axis=0)
+    theirs = jnp.sum(other[:, share:].astype(F32), axis=0)
+    total = mine + theirs
+    total = total[0:8] + total[8:16]
     for module in range(2):
+        for index, out in enumerate((norm_gain_out, norm_bias_out, mid_gain_out, mid_bias_out)):
+            at = 4 * module + index
+            out[module : module + 1, :] = total[at : at + 1]
         blocks = [
-            weights[(6 * module + part) * width : (6 * module + part + 1) * width]
+            weights[(6 * module + part) * width : (6 * module + part + 1) * width, :]
             for part in range(6)
         ]
         for side in range(2):
@@ -454,6 +495,20 @@
 
 def exchange(values):
     return lax.all_to_all(values, ("row", "col"), split_axis=0, concat_axis=0, tiled=True)
+
+
+def swap_cores(values, many, few):
+    pairs = [(index, index ^ few) for index in range(many * few)]
+    return lax.ppermute(values, ("row", "col"), pairs)
+
+
+def exchange_chips(values, many, few):
+    groups = [
+        [row * few + col for row in range(core, many, 2) for col in range(few)] for core in range(2)
+    ]
+    return lax.all_to_all(
+        values, ("row", "col"), split_axis=0, concat_axis=0, axis_index_groups=groups, tiled=True
+    )
 
 
 def grouped_device(
@@ -490,8 +545,12 @@
         return ((count, H), F32)
 
     saved = [tile, factor, factor, wide, row]
+    far = [
+        pltpu.with_memory_space_constraint(item, pltpu.HBM)
+        for item in (pair, ngain, nbias, proj_w, gate_w)
+    ]
     sent, normed0, *factors0 = call(
-        start_kernel, "start", [edge, *saved], [lengths, pair, ngain, nbias, proj_w, gate_w],
+        start_kernel, "start", [edge, *saved], [lengths, *far],
         [(pair.shape, BF16), (ngain.shape, F32), (nbias.shape, F32), (proj_w.shape, BF16),
          (gate_w.shape, BF16), pltpu.SemaphoreType.DMA((5,)), wts, big],
         4 * dense, 1, far=True,
@@ -538,35 +597,43 @@
     )
     d_edge0 = exchange(sent.reshape(edge[0]))
     share = 12 * H // shards
+    chips = shards // 2
     proj_factor0, gate_factor0, scaled0, inverse0 = factors0
-    packed, grad_pair, small0 = call(
-        finish_kernel, "finish", [((12 * H, H), BF16), (pair.shape, BF16), small(2)],
-        [d_edge0, proj_factor0, gate_factor0, d_normed_gate0, scaled0, inverse0, grad, normed0,
-         ngain, proj_w, gate_w, out_grads0, in_grads1, out_grads1],
-        [big, flat, flat_in, sums(2)], 8 * dense,
-    )
-    parts = exchange(packed.reshape(shards, share, H))
+    held = ((chips, share, H), BF16)
+    own, other, d_in0 = call(
+        functools.partial(finish_kernel, few), "finish", [held, held, d_in],
+        [d_edge0, proj_factor0, gate_factor0, normed0, out_grads0, in_grads1, out_grads1],
+        [big, flat, flat_in, ((12 * H, H), BF16)], 4 * dense,
+    )
+    other = swap_cores(other, many, few)
+    grad_pair, small0 = call(
+        behind_finish_kernel, "behind_finish", [(pair.shape, BF16), small(2)],
+        [d_in0, d_normed_gate0, scaled0, inverse0, grad, ngain, proj_w, gate_w], [sums(2)],
+        4 * dense,
+    )
+    (own,) = call(add_kernel, "add_cores", [held], [own, other])
+    parts = exchange_chips(own, many, few)
     (shared,) = call(
-        sum_kernel, "sum_weights", [((shards, share + 16, H), BF16)],
+        sum_kernel, "sum_weights", [((chips, share + 16, H), BF16)],
         [parts, small0, small_middle, small1],
     )
-    shared = exchange(shared)
-    grad_proj, grad_gate, grad_out, grad_outgate, small_all = call(
-        functools.partial(unpack_kernel, share), "unpack",
+    shared = exchange_chips(shared, many, few)
+    other = swap_cores(shared, many, few)
+    grad_proj, grad_gate, grad_out, grad_outgate, *vectors = call(
+        functools.partial(unpack_kernel, share, few), "unpack",
         [(proj_w.shape, F32), (gate_w.shape, F32), (out_w.shape, F32), (outgate_w.shape, F32),
-         small(8)],
-        [shared],
-    )
-    small_all = small_all.reshape(2, 4, H)
+         (ngain.shape, F32), (nbias.shape, F32), (mgain.shape, F32), (mbias.shape, F32)],
+        [shared, other], [((12 * H, H), F32)],
+    )
     return (
         new_pair,
         grad_pair,
-        small_all[:, 0],
-        small_all[:, 1],
+        vectors[0],
+        vectors[1],
         grad_proj,
         grad_gate,
-        small_all[:, 2],
-        small_all[:, 3],
+        vectors[2],
+        vectors[3],
         grad_out,
         grad_outgate,
     )
@@ -839,7 +906,7 @@
         P("grp", None, None),
     )
     many, few = mesh.shape["row"], mesh.shape["col"]
-    if mesh.shape["ch"] == 1 and H % (many * few) == 0:
+    if mesh.shape["ch"] == 1 and H % (many * few) == 0 and many % 2 == 0 and few & (few - 1) == 0:
         body = functools.partial(grouped_device, many=many, few=few)
     else:
         body = per_device

time: 264 us -> 254 us (0.962)
  blocking collectives: 230 us -> 209 us
  waiting for transfers between devices: 0 us -> 6.88 us
  starting transfers between devices: 0 us -> 4.76 us
    all_to_all x10 -> x8, blocking collectives: 230 us -> 196 us  [exchange(): lax.all_to_all(values, ('row', 'col'), split_axis=0, concat_axis=0, tiled...]
    all_to_all x0 -> x1, blocking collectives: none -> 12.6 us  [exchange_chips(): lax.all_to_all(values, ('row', 'col'), split_axis=0, concat_axis=0, axis_...]
    all_to_all x0 -> x1, starting transfers between devices: none -> 4.68 us  [exchange_chips(): lax.all_to_all(values, ('row', 'col'), split_axis=0, concat_axis=0, axis_...]
    all_to_all x0 -> x1, waiting for transfers between devices: none -> 3.92 us  [exchange_chips(): lax.all_to_all(values, ('row', 'col'), split_axis=0, concat_axis=0, axis_...]
    ppermute x0 -> x2, waiting for transfers between devices: none -> 2.96 us  [swap_cores(): return lax.ppermute(values, ('row', 'col'), pairs)]
    pallas_call x11 -> x13, Pallas kernels: 27 us -> 28.3 us  [call(): pl.pallas_call(kernel, name=name, out_shape=shapes, in_specs=[SCALARS] *...]
  transfers between devices with their start and end apart: 0 -> 3, of which waited for: 0 -> 3; matrix products, arithmetic and copies ran while one was open for 0% -> 0% of each run, Pallas kernels for 0% -> 1%
where the time goes in v7:
time: 254 us; the launch traced here: 253 us
  blocking collectives  209 us (82%)
  Pallas kernels  28.3 us (11%)
  waiting for transfers between devices  6.88 us (3%)
  starting transfers between devices  4.76 us (2%)
  local copies, waits for them, and re-layouts  3.19 us (1%)
    all_to_all x8, blocking collectives, exchange(): lax.all_to_all(values, ('row', 'col'), split_axis=0, concat_axis=0, tiled...  196 us
    pallas_call x13, Pallas kernels, call(): pl.pallas_call(kernel, name=name, out_shape=shapes, in_specs=[SCALARS] *...  28.3 us
    all_to_all x1, blocking collectives, exchange_chips(): lax.all_to_all(values, ('row', 'col'), split_axis=0, concat_axis=0, axis_...  12.6 us
  transfers between devices with their start and end apart: 3, of which 3 were waited for; matrix products, arithmetic and copies ran while one was open for 0% of the time, Pallas kernels for 1%

profile of v7, /device:TPU:0, one launch (start us, length us, event | category | flops | bytes accessed | tf_op | source)
XLA Modules:
  0.0 253.3 jit_solution(15803612923265772434)
XLA Ops:
  1.3 4.1 %start.1 = (bf16[32,2,4,16,128]{4,3,2,1,0:T(8,128)(2,1)S(1)}, bf16[16,128,128]{2,1,0:T(8,128)(2,1)S(1)}, f32[16,256,128]{2,1,0:T(8,128)S(1)}, f32[16,256,128]{2,...) custom-call(s32[1]{0:T(128)S(6)} %copy.21.lengths, bf16[16,128,128]{2,1,0:T(8,128)(2,1)} %pair.1, ...), custom_call_target="tpu_custom_call" | custom-call | flops 268435456 | bytes 7612420 | tf_op jit(solution)/shard_map/start/pallas_call | solution.py:482
  5.4 0.0 copy-start
  5.4 0.0 copy-start.1
  5.4 0.0 copy-start.7
  5.4 0.0 copy-start.8
  5.4 0.0 copy-start.9
  5.4 0.0 copy-start.11
  5.4 0.0 copy-start.12
  5.5 0.0 copy-start.13
  5.5 0.0 copy-start.14
  5.5 33.3 %all_to_all.50 = bf16[32,2,4,16,128]{4,3,2,1,0:T(8,128)(2,1)S(1)} all-to-all(bf16[32,2,4,16,128]{4,3,2,1,0:T(8,128)(2,1)S(1)} %get-tuple-element.51), channel_id=1, replica_groups=mesh['grp'=1,'row'=16,'col'=2,'ch'=1] {'row','col'}, dimensions={0} | all-to-all | bytes 2097152 | tf_op jit(solution)/shard_map/all_to_all | solution.py:497
  38.8 0.3 outgoing.1
  39.2 18.4 %all_to_all.51.tri = bf16[32,4,16,128]{3,2,1,0:T(8,128)(2,1)S(1)} all-to-all(bf16[32,4,16,128]{3,2,1,0:T(8,128)(2,1)S(1)} %bitcast.16), channel_id=1, replica_groups=mesh['grp'=1,'row'=16,'col'=2,'ch'=1] {'row','col'}, dimensions={0} | all-to-all | bytes 1048576 | tf_op jit(solution)/shard_map/all_to_all | solution.py:497
  57.6 0.0 copy-done
  57.6 0.0 copy-done.1
  57.6 0.0 copy-done.7
  57.6 0.0 copy-done.8
  57.6 0.0 copy-done.9
  57.6 0.0 copy-done.11
  57.6 0.0 copy-done.12
  57.6 0.0 copy-done.13
  57.7 0.0 copy-done.14
  57.7 4.7 %between.1 = (bf16[32,2,4,16,128]{4,3,2,1,0:T(8,128)(2,1)S(1)}, bf16[16,128,128]{2,1,0:T(8,128)(2,1)S(1)}, bf16[16,128,128]{2,1,0:T(8,128)(2,1)S(1)}, f32[16,256...) custom-call(s32[1]{0:T(128)S(6)} %copy.21.lengths, ...), custom_call_target="tpu_custom_call" | custom-call | flops 402653184 | bytes 11423748 | tf_op jit(solution)/shard_map/between/pallas_call | solution.py:482
  62.4 0.0 copy-start.10
  62.4 29.7 %all_to_all.52 = bf16[32,2,4,16,128]{4,3,2,1,0:T(8,128)(2,1)S(1)} all-to-all(bf16[32,2,4,16,128]{4,3,2,1,0:T(8,128)(2,1)S(1)} %get-tuple-element.53), channel_id=1, replica_groups=mesh['grp'=1,'row'=16,'col'=2,'ch'=1] {'row','col'}, dimensions={0} | all-to-all | bytes 2097152 | tf_op jit(solution)/shard_map/all_to_all | solution.py:497
  92.1 0.3 incoming.1
  92.4 18.4 %all_to_all.53.tri = bf16[32,4,16,128]{3,2,1,0:T(8,128)(2,1)S(1)} all-to-all(bf16[32,4,16,128]{3,2,1,0:T(8,128)(2,1)S(1)} %bitcast.17), channel_id=1, replica_groups=mesh['grp'=1,'row'=16,'col'=2,'ch'=1] {'row','col'}, dimensions={0} | all-to-all | bytes 1048576 | tf_op jit(solution)/shard_map/all_to_all | solution.py:497
  110.9 0.0 copy-done.10
  110.9 3.5 %turn.1 = (bf16[32,4,16,128]{3,2,1,0:T(8,128)(2,1)S(1)}, bf16[16,128,128]{2,1,0:T(8,128)(2,1)}, f32[16,128,128]{2,1,0:T(8,128)S(1)}, f32[16,128,128]{2,1,0:T(8,1...) custom-call(bf16[32,4,16,128]{3,2,1,0:T(8,128)(2,1)S(1)} %all_to_all.53.tri, ...), custom_call_target="tpu_custom_call" | custom-call | flops 402653184 | bytes 5442560 | tf_op jit(solution)/shard_map/turn/pallas_call | solution.py:482
  114.4 18.4 %all_to_all.54 = bf16[32,4,16,128]{3,2,1,0:T(8,128)(2,1)S(1)} all-to-all(bf16[32,4,16,128]{3,2,1,0:T(8,128)(2,1)S(1)} %get-tuple-element.57), channel_id=1, replica_groups=mesh['grp'=1,'row'=16,'col'=2,'ch'=1] {'row','col'}, dimensions={0} | all-to-all | bytes 1048576 | tf_op jit(solution)/shard_map/all_to_all | solution.py:497
  132.8 0.4 incoming_grad.1
  133.3 29.7 %all_to_all.55.d_edge = bf16[32,2,4,16,128]{4,3,2,1,0:T(8,128)(2,1)S(1)} all-to-all(bf16[32,2,4,16,128]{4,3,2,1,0:T(8,128)(2,1)S(1)} %bitcast.12), channel_id=1, replica_groups=mesh['grp'=1,'row'=16,'col'=2,'ch'=1] {'row','col'}, dimensions={0} | all-to-all | bytes 2097152 | tf_op jit(solution)/shard_map/all_to_all | solution.py:497
  163.0 7.2 %middle.1 = (bf16[32,4,16,128]{3,2,1,0:T(8,128)(2,1)S(1)}, f32[16,128,128]{2,1,0:T(8,128)S(1)}, f32[16,128,128]{2,1,0:T(8,128)S(1)}, bf16[256,128]{1,0:T(8,128)(...) custom-call(bf16[32,2,4,16,128]{4,3,2,1,0:T(8,128)(2,1)S(1)} %all_to_all.55.d_edge, ...), custom_call_target="tpu_custom_call" | custom-call | flops 872415232 | bytes 14767104 | tf_op jit(solution)/shard_map/middle/pallas_call | solution.py:482
  170.1 0.0 copy-start.2
  170.1 0.0 copy-start.4
  170.1 18.4 %all_to_all.56 = bf16[32,4,16,128]{3,2,1,0:T(8,128)(2,1)S(1)} all-to-all(bf16[32,4,16,128]{3,2,1,0:T(8,128)(2,1)S(1)} %get-tuple-element.67), channel_id=1, replica_groups=mesh['grp'=1,'row'=16,'col'=2,'ch'=1] {'row','col'}, dimensions={0} | all-to-all | bytes 1048576 | tf_op jit(solution)/shard_map/all_to_all | solution.py:497
  188.6 0.5 outgoing_grad.1
  189.0 29.7 %all_to_all.57.d_edge = bf16[32,2,4,16,128]{4,3,2,1,0:T(8,128)(2,1)S(1)} all-to-all(bf16[32,2,4,16,128]{4,3,2,1,0:T(8,128)(2,1)S(1)} %bitcast.13), channel_id=1, replica_groups=mesh['grp'=1,'row'=16,'col'=2,'ch'=1] {'row','col'}, dimensions={0} | all-to-all | bytes 2097152 | tf_op jit(solution)/shard_map/all_to_all | solution.py:497
  218.7 0.0 copy-done.2
  218.7 0.0 copy-done.4
  218.7 2.6 %finish.1 = (bf16[16,48,128]{2,1,0:T(8,128)(2,1)S(1)}, bf16[16,48,128]{2,1,0:T(8,128)(2,1)S(1)}, bf16[16,512,128]{2,1,0:T(8,128)(2,1)S(1)}) custom-call(bf16[32,2,4,16,128]{4,3,2,1,0:T(8,128)(2,1)S(1)} %all_to_all.57.d_edge, f32[16,256,128]{2,1,0:T(8,128)S(1)} %get-tuple-element.68.proj_factor, f32[16,256,128]{2,1,0:T(8,128)S(1)} %get-tuple-element.69.gate_factor, ...), custom_call_target="tpu_custom_call" | custom-call | flops 268435456 | bytes 8519680 | tf_op jit(solution)/shard_map/finish/pallas_call | solution.py:482
  221.3 0.1 collective-permute-start
  221.4 1.4 collective-permute-done.second
  222.8 0.0 copy-start.6
  222.9 0.7 copy-done.6
  223.5 4.7 %all-to-all-start.8 = ((bf16[16,48,128]{2,1,0:T(8,128)(2,1)}), bf16[16,48,128]{2,1,0:T(8,128)(2,1)}, u32[]{:S(2)}, u32[]{:S(2)}) async-start(bf16[16,48,128]{2,1,0:T(8,128)(2,1)} %copy-done.6), calls=%async_computation.8 | async-start | bytes 393216 | tf_op jit(solution)/shard_map/all_to_all | solution.py:509
  228.2 0.0 copy-start.3
  228.2 1.2 copy-done.3
  229.4 0.0 copy-start.5
  229.4 1.2 copy-done.5
  230.7 2.6 %behind_finish.1 = (bf16[16,128,128]{2,1,0:T(8,128)(2,1)}, f32[2,128]{1,0:T(2,128)S(1)}) custom-call(bf16[16,512,128]{2,1,0:T(8,128)(2,1)S(1)} %get-tuple-element.73.d_in, f32[16,128,128]{2,1,0:T(8,128)S(1)} %copy-done.5, f32[16,128,128]{2,1,0:T(8,128)S(1)} %get-tuple-element.75.scaled_in, f32[16,128]{1,0:T(8,128)S(1)} %get-tuple-element.76.inverse_in, ...), custom_call_target="tpu_custom_call" | custom-call | flops 268435456 | bytes 6039552 | tf_op jit(solution)/shard_map/behind_finish/pallas_call | solution.py:482
  233.3 3.9 %all-to-all-done.8.parts = bf16[16,48,128]{2,1,0:T(8,128)(2,1)} async-done(((bf16[16,48,128]{2,1,0:T(8,128)(2,1)}), bf16[16,48,128]{2,1,0:T(8,128)(2,1)}, u32[]{:S(2)}, u32[]{:S(2)}) %all-to-all-start.8) | async-done | bytes 196640 | tf_op jit(solution)/shard_map/all_to_all | solution.py:509
  237.2 1.0 sum_weights.1
  238.2 12.6 %all_to_all.58.own = bf16[16,64,128]{2,1,0:T(8,128)(2,1)S(1)} all-to-all(bf16[16,64,128]{2,1,0:T(8,128)(2,1)S(1)} %sum_weights.1), channel_id=1, replica_groups={{0,1,4,5,8,9,12,13,16,17,20,21,24,25,28,29},{2,3,6,7,10,11,14,15,18,19,..., dimensions={0} | all-to-all | bytes 524288 | tf_op jit(solution)/shard_map/all_to_all | solution.py:509
  250.8 0.0 collective-permute-start.1
  250.8 1.5 collective-permute-done.1.other
  252.4 1.0 unpack.1
  (1 shorter events, 0.0 us)
Async XLA Ops:
  5.4 52.2 %copy-start = (bf16[2,2,128,128]{3,2,1,0:T(8,128)(2,1)S(1)}, bf16[2,2,128,128]{3,2,1,0:T(8,128)(2,1)}, u32[]{:S(2)}) copy-start(bf16[2,2,128,128]{3,2,1,0:T(8,128)(2,1)} %proj_w.5) | copy-start | bytes 393220
  5.4 52.2 %copy-start.1 = (bf16[2,2,128,128]{3,2,1,0:T(8,128)(2,1)S(1)}, bf16[2,2,128,128]{3,2,1,0:T(8,128)(2,1)}, u32[]{:S(2)}) copy-start(bf16[2,2,128,128]{3,2,1,0:T(8,128)(2,1)} %gate_w.5) | copy-start | bytes 393220
  5.4 52.2 %copy-start.7 = (bf16[2,128,128]{2,1,0:T(8,128)(2,1)S(1)}, bf16[2,128,128]{2,1,0:T(8,128)(2,1)}, u32[]{:S(2)}) copy-start(bf16[2,128,128]{2,1,0:T(8,128)(2,1)} %out_w.5) | copy-start | bytes 196612
  5.4 52.2 %copy-start.8 = (bf16[2,128,128]{2,1,0:T(8,128)(2,1)S(1)}, bf16[2,128,128]{2,1,0:T(8,128)(2,1)}, u32[]{:S(2)}) copy-start(bf16[2,128,128]{2,1,0:T(8,128)(2,1)} %outgate_w.5) | copy-start | bytes 196612
  5.4 52.2 %copy-start.9 = (bf16[16,128,128]{2,1,0:T(8,128)(2,1)S(1)}, bf16[16,128,128]{2,1,0:T(8,128)(2,1)}, u32[]{:S(2)}) copy-start(bf16[16,128,128]{2,1,0:T(8,128)(2,1)} %pair.1) | copy-start | bytes 1572868
  5.4 52.2 %copy-start.11 = (f32[2,128]{1,0:T(2,128)S(1)}, f32[2,128]{1,0:T(2,128)}, u32[]{:S(2)}) copy-start(f32[2,128]{1,0:T(2,128)} %mgain.5) | copy-start | bytes 3076
  5.4 52.2 %copy-start.12 = (f32[2,128]{1,0:T(2,128)S(1)}, f32[2,128]{1,0:T(2,128)}, u32[]{:S(2)}) copy-start(f32[2,128]{1,0:T(2,128)} %mbias.5) | copy-start | bytes 3076
  5.5 52.2 %copy-start.13 = (f32[2,128]{1,0:T(2,128)S(1)}, f32[2,128]{1,0:T(2,128)}, u32[]{:S(2)}) copy-start(f32[2,128]{1,0:T(2,128)} %ngain.5) | copy-start | bytes 3076
  5.5 52.2 %copy-start.14 = (f32[2,128]{1,0:T(2,128)S(1)}, f32[2,128]{1,0:T(2,128)}, u32[]{:S(2)}) copy-start(f32[2,128]{1,0:T(2,128)} %nbias.1) | copy-start | bytes 3076
  62.4 48.5 %copy-start.10 = (bf16[16,128,128]{2,1,0:T(8,128)(2,1)S(1)}, bf16[16,128,128]{2,1,0:T(8,128)(2,1)}, u32[]{:S(2)}) copy-start(bf16[16,128,128]{2,1,0:T(8,128)(2,1)} %cot.1) | copy-start | bytes 1572868
  170.1 48.6 %copy-start.2 = (f32[16,128,128]{2,1,0:T(8,128)}, f32[16,128,128]{2,1,0:T(8,128)S(1)}, u32[]{:S(2)}) copy-start(f32[16,128,128]{2,1,0:T(8,128)S(1)} %get-tuple-element.77.grad) | copy-start | bytes 3145732
  170.1 48.6 %copy-start.4 = (f32[16,128,128]{2,1,0:T(8,128)}, f32[16,128,128]{2,1,0:T(8,128)S(1)}, u32[]{:S(2)}) copy-start(f32[16,128,128]{2,1,0:T(8,128)S(1)} %get-tuple-element.74.d_normed_gate) | copy-start | bytes 3145732
  221.3 1.5 collective-permute-start
  222.8 0.7 copy-start.6
  223.5 13.7 %all-to-all-start.8 = ((bf16[16,48,128]{2,1,0:T(8,128)(2,1)}), bf16[16,48,128]{2,1,0:T(8,128)(2,1)}, u32[]{:S(2)}, u32[]{:S(2)}) async-start(bf16[16,48,128]{2,1,0:T(8,128)(2,1)} %copy-done.6), calls=%async_computation.8 | async-start | bytes 393216 | tf_op jit(solution)/shard_map/all_to_all | solution.py:509
  228.2 1.2 copy-start.3
  229.4 1.2 copy-start.5
  250.8 1.5 collective-permute-start.1

commit v8 on v7

--- a/solution.py
+++ b/solution.py
@@ -34,7 +34,7 @@
 
 
 def sigmoid(values):
-    return 1.0 / (1.0 + jnp.exp(-values))
+    return 0.5 * jnp.tanh(0.5 * values) + 0.5
 
 
 def norm_rows(values):
@@ -103,12 +103,17 @@
     scratch[0:block, :] = in_ref[...].astype(F32).reshape(block, in_ref.shape[-1])
 
 
-def each_row(rows, unroll, body):
-    def step_body(step, carry):
-        body(step)
+def each_row(rows, unroll, body, sums=None):
+    def several(block, carry):
+        parts = [body(block * unroll + step) for step in range(unroll)]
+        for index in range(0 if sums is None else sums.shape[0]):
+            total = parts[0][index]
+            for part in parts[1:]:
+                total = total + part[index]
+            sums[index] += total
         return carry
 
-    lax.fori_loop(0, rows, step_body, 0, unroll=unroll)
+    lax.fori_loop(0, rows // unroll, several, 0)
 
 
 def mid_norm(tri):
@@ -146,7 +151,7 @@
 
 def start_kernel(
     lengths, pair_far, ngain_far, nbias_far, proj_far, gate_far,
-    edge_out, normed_out, proj_out, gate_out, scaled_out, inverse_out,
+    edge_out, normed_out, proj_out, gate_out, scaled_out, inverse_out, mask_out,
     pair, ngain, nbias, proj_w, gate_w, sems, wts, scr,
 ):
     far = (proj_far.at[0], gate_far.at[0], ngain_far, nbias_far, pair_far)
@@ -169,6 +174,7 @@
         normed = (scaled * gain + bias).astype(BF16)
         normed_out[step] = normed
         mask = row_mask(lengths, step, rows, lanes)
+        mask_out[pl.ds(step, 1), :] = mask
         put_rows(scr, save_edges(step, normed, wts[...], mask, proj_out, gate_out), step, rows)
 
     each_row(rows, 4, body)
@@ -176,7 +182,7 @@
 
 
 def between_kernel(
-    lengths, tri, pair, normed0, ngain, nbias, mgain, mbias, out_w, outgate_w, proj_w, gate_w,
+    mask_all, tri, pair, normed0, ngain, nbias, mgain, mbias, out_w, outgate_w, proj_w, gate_w,
     edge_out, mid_out, normed_out, proj_out, gate_out, scaled_out, inverse_out,
     outgate_out, scaled_mid_out, inverse_mid_out, wts, scr,
 ):
@@ -200,7 +206,7 @@
         scaled = save_norm(step, mid.astype(F32), scaled_out, inverse_out)
         normed = (scaled * gain + bias).astype(BF16)
         normed_out[step] = normed
-        mask = row_mask(lengths, step, rows, lanes)
+        mask = mask_all[pl.ds(step, 1), :]
         put_rows(scr, save_edges(step, normed, wts[...], mask, proj_out, gate_out), step, rows)
 
     each_row(rows, 4, body)
@@ -254,10 +260,9 @@
         outer_all[:, here] = d_outer
         normed_all[:, here] = normed[step]
         gate_all[:, here] = d_gatepre
-        sums[0] += d_unit * scaled_mid
-        sums[1] += d_unit
-
-    each_row(rows, 4, body)
+        return d_unit * scaled_mid, d_unit
+
+    each_row(rows, 4, body, sums)
     d_tri_out[...] = scr[...].reshape(d_tri_out.shape).astype(BF16)
     out_weight_grads(unit_all, outer_all, normed_all, gate_all, weights_out)
     for index in range(2):
@@ -298,11 +303,10 @@
         upper_all[:, place] = normed1[step]
         d_normed = in_normed(d_in, d_normed_gate[step], proj_w[1], gate_w[1])
         scaled = scaled_in[step]
-        sums[2] += d_normed * scaled
-        sums[3] += d_normed
         grad_out[step] = cot[step] + norm_backward(
             d_normed * gain, scaled, inverse_in[pl.ds(step, 1), :]
         )
+        return d_normed * scaled, d_normed
 
     def lower(step):
         place = lane_block(step, lanes)
@@ -321,11 +325,10 @@
         outer_all[:, place] = d_outer
         normed_all[:, place] = normed0[step]
         gate_all[:, place] = d_gatepre
-        sums[0] += d_unit * scaled
-        sums[1] += d_unit
-
-    each_row(rows, 4, upper)
-    each_row(rows, 4, lower)
+        return d_unit * scaled, d_unit
+
+    each_row(rows, 4, upper, sums.at[2:4])
+    each_row(rows, 4, lower, sums.at[0:2])
     d_tri_out[...] = scr_tri[...].reshape(d_tri_out.shape).astype(BF16)
     out_weight_grads(unit_all, outer_all, normed_all, gate_all, out_weights)
     in_weight_grads(upper_all, d_in_all, in_weights)
@@ -367,46 +370,58 @@
     split_cores(packed, own_out, other_out, few)
 
 
-def behind_finish_kernel(
-    d_in, d_normed_gate, scaled_in, inverse_in, grad, ngain, proj_w, gate_w,
-    grad_out, small_out, sums,
+def norm_sums_kernel(
+    d_in, d_normed_gate, scaled_in, proj_w, gate_w, small_middle, small1,
+    d_normed_out, extra_out, sums,
+):
+    rows = d_in.shape[0]
+    sums[...] = jnp.zeros_like(sums)
+
+    def body(step):
+        d_normed = in_normed(d_in[step], d_normed_gate[step], proj_w[0], gate_w[0])
+        d_normed_out[step] = d_normed
+        return d_normed * scaled_in[step], d_normed
+
+    each_row(rows, 4, body, sums)
+    small = jnp.concatenate(
+        [as_row(sums[0]), as_row(sums[1]), small_middle[0:2], small_middle[2:4], small1[...]],
+        axis=0,
+    )
+    high = small.astype(BF16).astype(F32)
+    extra_out[...] = jnp.concatenate([high, small - high], axis=0).astype(BF16)
+
+
+def add_kernel(first, second, extra, out_ref, extra_out):
+    out_ref[...] = (first[...].astype(F32) + second[...].astype(F32)).astype(BF16)
+    extra_out[...] = extra[...]
+
+
+def sum_kernel(parts, extra, shared_out):
+    chips, share, width = parts.shape
+    own = jnp.sum(parts[...].astype(F32), axis=0).astype(BF16)
+    for chip in range(chips):
+        shared_out[chip, 0:share] = own
+        shared_out[chip, share:] = extra[...]
+
+
+def grad_pair_kernel(
+    share, shared, d_normed, scaled_in, inverse_in, grad, ngain, grad_out, mine_out
 ):
     rows, channels, lanes = grad.shape
     gain = column(ngain, 0, lanes)
-    sums[...] = jnp.zeros_like(sums)
+    mine_out[...] = jnp.sum(shared[:, share:].astype(F32), axis=0)
 
     def body(step):
-        d_normed = in_normed(d_in[step], d_normed_gate[step], proj_w[0], gate_w[0])
-        scaled = scaled_in[step]
-        sums[0] += d_normed * scaled
-        sums[1] += d_normed
-        total = grad[step] + norm_backward(d_normed * gain, scaled, inverse_in[pl.ds(step, 1), :])
+        total = grad[step] + norm_backward(
+            d_normed[step] * gain, scaled_in[step], inverse_in[pl.ds(step, 1), :]
+        )
         grad_out[step] = jnp.transpose(total).astype(BF16)
 
     each_row(rows, 4, body)
-    for index in range(2):
-        small_out[index : index + 1, :] = as_row(sums[index])
-
-
-def add_kernel(first, second, out_ref):
-    out_ref[...] = (first[...].astype(F32) + second[...].astype(F32)).astype(BF16)
-
-
-def sum_kernel(parts, small0, small_middle, small1, shared_out):
-    chips, share, width = parts.shape
-    own = jnp.sum(parts[...].astype(F32), axis=0).astype(BF16)
-    small = jnp.concatenate(
-        [small0[...], small_middle[0:2], small_middle[2:4], small1[...]], axis=0
-    )
-    high = small.astype(BF16).astype(F32)
-    extra = jnp.concatenate([high, small - high], axis=0).astype(BF16)
-    for chip in range(chips):
-        shared_out[chip, 0:share] = own
-        shared_out[chip, share:] = extra
 
 
 def unpack_kernel(
-    share, few, own, other, proj_out, gate_out, out_out, outgate_out,
+    share, few, own, other, mine, proj_out, gate_out, out_out, outgate_out,
     norm_gain_out, norm_bias_out, mid_gain_out, mid_bias_out, weights,
 ):
     chips, _, width = own.shape
@@ -415,9 +430,7 @@
     block = (chips // few, few, share, width)
     view[:, core] = own[:, 0:share].astype(F32).reshape(block)
     view[:, 1 - core] = other[:, 0:share].astype(F32).reshape(block)
-    mine = jnp.sum(own[:, share:].astype(F32), axis=0)
-    theirs = jnp.sum(other[:, share:].astype(F32), axis=0)
-    total = mine + theirs
+    total = mine[...] + jnp.sum(other[:, share:].astype(F32), axis=0)
     total = total[0:8] + total[8:16]
     for module in range(2):
         for index, out in enumerate((norm_gain_out, norm_bias_out, mid_gain_out, mid_bias_out)):
@@ -475,15 +488,14 @@
 FAR = pl.BlockSpec(memory_space=pltpu.HBM)
 
 
-def call(kernel, name, outs, args, scratch=(), flops=0, scalars=0, grant=16, far=False):
+def call(kernel, name, outs, args, scratch=(), flops=0, grant=16, specs=None):
     shapes = [jax.ShapeDtypeStruct(shape, dtype) for shape, dtype in outs]
     moved = sum(a.size * a.dtype.itemsize for a in list(args) + shapes)
-    rest = FAR if far else VECTORS
     return pl.pallas_call(
         kernel,
         name=name,
         out_shape=shapes,
-        in_specs=[SCALARS] * scalars + [rest] * (len(args) - scalars),
+        in_specs=specs or [VECTORS] * len(args),
         out_specs=[VECTORS] * len(shapes),
         scratch_shapes=[
             pltpu.VMEM(*item) if isinstance(item, tuple) else item for item in scratch
@@ -549,11 +561,11 @@
         pltpu.with_memory_space_constraint(item, pltpu.HBM)
         for item in (pair, ngain, nbias, proj_w, gate_w)
     ]
-    sent, normed0, *factors0 = call(
-        start_kernel, "start", [edge, *saved], [lengths, *far],
+    sent, normed0, *factors0, mask = call(
+        start_kernel, "start", [edge, *saved, row], [lengths, *far],
         [(pair.shape, BF16), (ngain.shape, F32), (nbias.shape, F32), (proj_w.shape, BF16),
          (gate_w.shape, BF16), pltpu.SemaphoreType.DMA((5,)), wts, big],
-        4 * dense, 1, far=True,
+        4 * dense, specs=[SCALARS] + [FAR] * len(far),
     )
     edge0 = exchange(sent).reshape(grid[0])
     (here,) = call(
@@ -562,9 +574,9 @@
     tri0 = exchange(here.reshape(tri[0]))
     sent, mid_t, normed1, *factors1, outgate0, scaled_mid0, inverse_mid0 = call(
         between_kernel, "between", [edge, tile, *saved, wide, wide, row],
-        [lengths, tri0, pair, normed0, ngain, nbias, mgain, mbias, out_w, outgate_w, proj_w,
+        [mask, tri0, pair, normed0, ngain, nbias, mgain, mbias, out_w, outgate_w, proj_w,
          gate_w],
-        [wts, big], 6 * dense, 1,
+        [wts, big], 6 * dense,
     )
     edge1 = exchange(sent).reshape(grid[0])
     (here,) = call(
@@ -606,24 +618,28 @@
         [big, flat, flat_in, ((12 * H, H), BF16)], 4 * dense,
     )
     other = swap_cores(other, many, few)
-    grad_pair, small0 = call(
-        behind_finish_kernel, "behind_finish", [(pair.shape, BF16), small(2)],
-        [d_in0, d_normed_gate0, scaled0, inverse0, grad, ngain, proj_w, gate_w], [sums(2)],
+    d_normed0, extra = call(
+        norm_sums_kernel, "norm_sums", [wide, ((16, H), BF16)],
+        [d_in0, d_normed_gate0, scaled0, proj_w, gate_w, small_middle, small1], [sums(2)],
         4 * dense,
     )
-    (own,) = call(add_kernel, "add_cores", [held], [own, other])
+    own, extra = call(add_kernel, "add_cores", [held, ((16, H), BF16)], [own, other, extra])
     parts = exchange_chips(own, many, few)
     (shared,) = call(
-        sum_kernel, "sum_weights", [((chips, share + 16, H), BF16)],
-        [parts, small0, small_middle, small1],
+        sum_kernel, "sum_weights", [((chips, share + 16, H), BF16)], [parts, extra]
     )
     shared = exchange_chips(shared, many, few)
     other = swap_cores(shared, many, few)
+    grad_pair, mine = call(
+        functools.partial(grad_pair_kernel, share), "grad_pair",
+        [(pair.shape, BF16), ((16, H), F32)],
+        [shared, d_normed0, scaled0, inverse0, grad, ngain],
+    )
     grad_proj, grad_gate, grad_out, grad_outgate, *vectors = call(
         functools.partial(unpack_kernel, share, few), "unpack",
         [(proj_w.shape, F32), (gate_w.shape, F32), (out_w.shape, F32), (outgate_w.shape, F32),
          (ngain.shape, F32), (nbias.shape, F32), (mgain.shape, F32), (mbias.shape, F32)],
-        [shared, other], [((12 * H, H), F32)],
+        [shared, other, mine], [((12 * H, H), F32)],
     )
     return (
         new_pair,

time: 254 us -> 252 us (level)
  blocking collectives: 209 us -> 222 us
  waiting for transfers between devices: 6.88 us -> 0.04 us
  starting transfers between devices: 4.76 us -> 0.08 us
  local copies, waits for them, and re-layouts: 3.19 us -> 0.06 us
    all_to_all x1 -> x2, blocking collectives: 12.6 us -> 26.5 us  [exchange_chips(): lax.all_to_all(values, ('row', 'col'), split_axis=0, concat_axis=0, axis_...]
    all_to_all x1 -> x0, starting transfers between devices: 4.68 us -> none  [exchange_chips(): lax.all_to_all(values, ('row', 'col'), split_axis=0, concat_axis=0, axis_...]
    all_to_all x1 -> x0, waiting for transfers between devices: 3.92 us -> none  [exchange_chips(): lax.all_to_all(values, ('row', 'col'), split_axis=0, concat_axis=0, axis_...]
    unnamed x30 -> x20, local copies, waits for them, and re-layouts: 3.19 us -> 0.06 us
    ppermute x2, waiting for transfers between devices: 2.96 us -> 0.04 us  [swap_cores(): return lax.ppermute(values, ('row', 'col'), pairs)]
    pallas_call x13 -> x14, Pallas kernels: 28.3 us -> 27.8 us  [call(): pl.pallas_call(kernel, name=name, out_shape=shapes, in_specs=specs or [VE...]
  transfers between devices with their start and end apart: 3 -> 2, of which waited for: 3 -> 0; matrix products, arithmetic and copies ran while one was open for 0% -> 0% of each run, Pallas kernels for 1% -> 1%
where the time goes in v8:
time: 252 us
  blocking collectives  222 us (88%)
  Pallas kernels  27.8 us (11%)
    all_to_all x8, blocking collectives, exchange(): lax.all_to_all(values, ('row', 'col'), split_axis=0, concat_axis=0, tiled...  196 us
    pallas_call x14, Pallas kernels, call(): pl.pallas_call(kernel, name=name, out_shape=shapes, in_specs=specs or [VE...  27.8 us
    all_to_all x2, blocking collectives, exchange_chips(): lax.all_to_all(values, ('row', 'col'), split_axis=0, concat_axis=0, axis_...  26.5 us
  transfers between devices with their start and end apart: 2, of which 0 were waited for; matrix products, arithmetic and copies ran while one was open for 0% of the time, Pallas kernels for 1%

profile of v8, /device:TPU:0, one launch (start us, length us, event | category | flops | bytes accessed | tf_op | source)
XLA Modules:
  0.0 251.9 jit_solution(8587870410994980876)
XLA Ops:
  1.3 4.1 %start.1 = (bf16[32,2,4,16,128]{4,3,2,1,0:T(8,128)(2,1)S(1)}, bf16[16,128,128]{2,1,0:T(8,128)(2,1)S(1)}, f32[16,256,128]{2,1,0:T(8,128)S(1)}, f32[16,256,128]{2,...) custom-call(s32[1]{0:T(128)S(6)} %copy.21.lengths, ...), custom_call_target="tpu_custom_call" | custom-call | flops 268435456 | bytes 7620612 | tf_op jit(solution)/shard_map/start/pallas_call | solution.py:494
  5.3 0.0 copy-start
  5.4 0.0 copy-start.1
  5.4 0.0 copy-start.2
  5.4 0.0 copy-start.3
  5.4 0.0 copy-start.5
  5.4 0.0 copy-start.6
  5.4 0.0 copy-start.7
  5.4 0.0 copy-start.8
  5.4 0.0 copy-start.9
  5.5 33.3 %all_to_all.50 = bf16[32,2,4,16,128]{4,3,2,1,0:T(8,128)(2,1)S(1)} all-to-all(bf16[32,2,4,16,128]{4,3,2,1,0:T(8,128)(2,1)S(1)} %get-tuple-element.57), channel_id=1, replica_groups=mesh['grp'=1,'row'=16,'col'=2,'ch'=1] {'row','col'}, dimensions={0} | all-to-all | bytes 2097152 | tf_op jit(solution)/shard_map/all_to_all | solution.py:509
  38.8 0.3 outgoing.1
  39.1 18.4 %all_to_all.51.tri = bf16[32,4,16,128]{3,2,1,0:T(8,128)(2,1)S(1)} all-to-all(bf16[32,4,16,128]{3,2,1,0:T(8,128)(2,1)S(1)} %bitcast.16), channel_id=1, replica_groups=mesh['grp'=1,'row'=16,'col'=2,'ch'=1] {'row','col'}, dimensions={0} | all-to-all | bytes 1048576 | tf_op jit(solution)/shard_map/all_to_all | solution.py:509
  57.6 0.0 copy-done
  57.6 0.0 copy-done.1
  57.6 0.0 copy-done.2
  57.6 0.0 copy-done.3
  57.6 0.0 copy-done.5
  57.6 0.0 copy-done.6
  57.6 0.0 copy-done.7
  57.6 0.0 copy-done.8
  57.6 0.0 copy-done.9
  57.6 4.7 %between.1 = (bf16[32,2,4,16,128]{4,3,2,1,0:T(8,128)(2,1)S(1)}, bf16[16,128,128]{2,1,0:T(8,128)(2,1)S(1)}, bf16[16,128,128]{2,1,0:T(8,128)(2,1)S(1)}, f32[16,256...) custom-call(f32[16,128]{1,0:T(8,128)S(1)} %get-tuple-element.56.mask, ...), custom_call_target="tpu_custom_call" | custom-call | flops 402653184 | bytes 11431936 | tf_op jit(solution)/shard_map/between/pallas_call | solution.py:494
  62.3 0.0 copy-start.4
  62.3 29.7 %all_to_all.52 = bf16[32,2,4,16,128]{4,3,2,1,0:T(8,128)(2,1)S(1)} all-to-all(bf16[32,2,4,16,128]{4,3,2,1,0:T(8,128)(2,1)S(1)} %get-tuple-element.59), channel_id=1, replica_groups=mesh['grp'=1,'row'=16,'col'=2,'ch'=1] {'row','col'}, dimensions={0} | all-to-all | bytes 2097152 | tf_op jit(solution)/shard_map/all_to_all | solution.py:509
  92.0 0.3 incoming.1
  92.3 18.4 %all_to_all.53.tri = bf16[32,4,16,128]{3,2,1,0:T(8,128)(2,1)S(1)} all-to-all(bf16[32,4,16,128]{3,2,1,0:T(8,128)(2,1)S(1)} %bitcast.17), channel_id=1, replica_groups=mesh['grp'=1,'row'=16,'col'=2,'ch'=1] {'row','col'}, dimensions={0} | all-to-all | bytes 1048576 | tf_op jit(solution)/shard_map/all_to_all | solution.py:509
  110.8 0.0 copy-done.4
  110.8 3.6 %turn.1 = (bf16[32,4,16,128]{3,2,1,0:T(8,128)(2,1)S(1)}, bf16[16,128,128]{2,1,0:T(8,128)(2,1)}, f32[16,128,128]{2,1,0:T(8,128)S(1)}, f32[16,128,128]{2,1,0:T(8,1...) custom-call(bf16[32,4,16,128]{3,2,1,0:T(8,128)(2,1)S(1)} %all_to_all.53.tri, ...), custom_call_target="tpu_custom_call" | custom-call | flops 402653184 | bytes 5442560 | tf_op jit(solution)/shard_map/turn/pallas_call | solution.py:494
  114.3 18.4 %all_to_all.54 = bf16[32,4,16,128]{3,2,1,0:T(8,128)(2,1)S(1)} all-to-all(bf16[32,4,16,128]{3,2,1,0:T(8,128)(2,1)S(1)} %get-tuple-element.63), channel_id=1, replica_groups=mesh['grp'=1,'row'=16,'col'=2,'ch'=1] {'row','col'}, dimensions={0} | all-to-all | bytes 1048576 | tf_op jit(solution)/shard_map/all_to_all | solution.py:509
  132.7 0.4 incoming_grad.1
  133.2 29.7 %all_to_all.55.d_edge = bf16[32,2,4,16,128]{4,3,2,1,0:T(8,128)(2,1)S(1)} all-to-all(bf16[32,2,4,16,128]{4,3,2,1,0:T(8,128)(2,1)S(1)} %bitcast.12), channel_id=1, replica_groups=mesh['grp'=1,'row'=16,'col'=2,'ch'=1] {'row','col'}, dimensions={0} | all-to-all | bytes 2097152 | tf_op jit(solution)/shard_map/all_to_all | solution.py:509
  162.9 7.2 %middle.1 = (bf16[32,4,16,128]{3,2,1,0:T(8,128)(2,1)S(1)}, f32[16,128,128]{2,1,0:T(8,128)S(1)}, f32[16,128,128]{2,1,0:T(8,128)S(1)}, bf16[256,128]{1,0:T(8,128)(...) custom-call(bf16[32,2,4,16,128]{4,3,2,1,0:T(8,128)(2,1)S(1)} %all_to_all.55.d_edge, ...), custom_call_target="tpu_custom_call" | custom-call | flops 872415232 | bytes 14767104 | tf_op jit(solution)/shard_map/middle/pallas_call | solution.py:494
  170.1 18.4 %all_to_all.56 = bf16[32,4,16,128]{3,2,1,0:T(8,128)(2,1)S(1)} all-to-all(bf16[32,4,16,128]{3,2,1,0:T(8,128)(2,1)S(1)} %get-tuple-element.73), channel_id=1, replica_groups=mesh['grp'=1,'row'=16,'col'=2,'ch'=1] {'row','col'}, dimensions={0} | all-to-all | bytes 1048576 | tf_op jit(solution)/shard_map/all_to_all | solution.py:509
  188.5 0.5 outgoing_grad.1
  189.0 29.7 %all_to_all.57.d_edge = bf16[32,2,4,16,128]{4,3,2,1,0:T(8,128)(2,1)S(1)} all-to-all(bf16[32,2,4,16,128]{4,3,2,1,0:T(8,128)(2,1)S(1)} %bitcast.13), channel_id=1, replica_groups=mesh['grp'=1,'row'=16,'col'=2,'ch'=1] {'row','col'}, dimensions={0} | all-to-all | bytes 2097152 | tf_op jit(solution)/shard_map/all_to_all | solution.py:509
  218.7 2.6 %finish.1 = (bf16[16,48,128]{2,1,0:T(8,128)(2,1)S(1)}, bf16[16,48,128]{2,1,0:T(8,128)(2,1)S(1)}, bf16[16,512,128]{2,1,0:T(8,128)(2,1)S(1)}) custom-call(bf16[32,2,4,16,128]{4,3,2,1,0:T(8,128)(2,1)S(1)} %all_to_all.57.d_edge, f32[16,256,128]{2,1,0:T(8,128)S(1)} %get-tuple-element.74.proj_factor, f32[16,256,128]{2,1,0:T(8,128)S(1)} %get-tuple-element.75.gate_factor, ...), custom_call_target="tpu_custom_call" | custom-call | flops 268435456 | bytes 8519680 | tf_op jit(solution)/shard_map/finish/pallas_call | solution.py:494
  221.3 0.1 collective-permute-start
  221.3 1.4 norm_sums.1
  222.7 0.0 collective-permute-done.second
  222.8 13.4 %all_to_all.58.parts = bf16[16,48,128]{2,1,0:T(8,128)(2,1)S(1)} all-to-all(bf16[16,48,128]{2,1,0:T(8,128)(2,1)S(1)} %get-tuple-element.87), channel_id=1, replica_groups={{0,1,4,5,8,9,12,13,16,17,20,21,24,25,28,29},{2,3,6,7,10,11,14,15,18,19,..., dimensions={0} | all-to-all | bytes 393216 | tf_op jit(solution)/shard_map/all_to_all | solution.py:521
  236.2 13.1 %all_to_all.59.shared.own = bf16[16,64,128]{2,1,0:T(8,128)(2,1)S(1)} all-to-all(bf16[16,64,128]{2,1,0:T(8,128)(2,1)S(1)} %sum_weights.1), channel_id=1, replica_groups={{0,1,4,5,8,9,12,13,16,17,20,21,24,25,28,29},{2,3,6,7,10,11,14,15,18,19,..., dimensions={0} | all-to-all | bytes 524288 | tf_op jit(solution)/shard_map/all_to_all | solution.py:521
  249.3 0.0 collective-permute-start.1
  249.3 1.6 grad_pair.1
  250.9 0.0 collective-permute-done.1.other
  250.9 1.0 unpack.1
  (2 shorter events, 0.1 us)
Async XLA Ops:
  5.3 52.2 %copy-start = (bf16[2,2,128,128]{3,2,1,0:T(8,128)(2,1)S(1)}, bf16[2,2,128,128]{3,2,1,0:T(8,128)(2,1)}, u32[]{:S(2)}) copy-start(bf16[2,2,128,128]{3,2,1,0:T(8,128)(2,1)} %proj_w.5) | copy-start | bytes 393220
  5.4 52.2 %copy-start.1 = (bf16[2,2,128,128]{3,2,1,0:T(8,128)(2,1)S(1)}, bf16[2,2,128,128]{3,2,1,0:T(8,128)(2,1)}, u32[]{:S(2)}) copy-start(bf16[2,2,128,128]{3,2,1,0:T(8,128)(2,1)} %gate_w.5) | copy-start | bytes 393220
  5.4 52.2 %copy-start.2 = (bf16[2,128,128]{2,1,0:T(8,128)(2,1)S(1)}, bf16[2,128,128]{2,1,0:T(8,128)(2,1)}, u32[]{:S(2)}) copy-start(bf16[2,128,128]{2,1,0:T(8,128)(2,1)} %out_w.5) | copy-start | bytes 196612
  5.4 52.2 %copy-start.3 = (bf16[2,128,128]{2,1,0:T(8,128)(2,1)S(1)}, bf16[2,128,128]{2,1,0:T(8,128)(2,1)}, u32[]{:S(2)}) copy-start(bf16[2,128,128]{2,1,0:T(8,128)(2,1)} %outgate_w.5) | copy-start | bytes 196612
  5.4 52.2 %copy-start.5 = (bf16[16,128,128]{2,1,0:T(8,128)(2,1)S(1)}, bf16[16,128,128]{2,1,0:T(8,128)(2,1)}, u32[]{:S(2)}) copy-start(bf16[16,128,128]{2,1,0:T(8,128)(2,1)} %pair.1) | copy-start | bytes 1572868
  5.4 52.2 %copy-start.6 = (f32[2,128]{1,0:T(2,128)S(1)}, f32[2,128]{1,0:T(2,128)}, u32[]{:S(2)}) copy-start(f32[2,128]{1,0:T(2,128)} %mgain.5) | copy-start | bytes 3076
  5.4 52.2 %copy-start.7 = (f32[2,128]{1,0:T(2,128)S(1)}, f32[2,128]{1,0:T(2,128)}, u32[]{:S(2)}) copy-start(f32[2,128]{1,0:T(2,128)} %mbias.5) | copy-start | bytes 3076
  5.4 52.2 %copy-start.8 = (f32[2,128]{1,0:T(2,128)S(1)}, f32[2,128]{1,0:T(2,128)}, u32[]{:S(2)}) copy-start(f32[2,128]{1,0:T(2,128)} %ngain.5) | copy-start | bytes 3076
  5.4 52.2 %copy-start.9 = (f32[2,128]{1,0:T(2,128)S(1)}, f32[2,128]{1,0:T(2,128)}, u32[]{:S(2)}) copy-start(f32[2,128]{1,0:T(2,128)} %nbias.1) | copy-start | bytes 3076
  62.3 48.5 %copy-start.4 = (bf16[16,128,128]{2,1,0:T(8,128)(2,1)S(1)}, bf16[16,128,128]{2,1,0:T(8,128)(2,1)}, u32[]{:S(2)}) copy-start(bf16[16,128,128]{2,1,0:T(8,128)(2,1)} %cot.1) | copy-start | bytes 1572868
  221.3 1.5 collective-permute-start
  249.3 1.6 collective-permute-start.1

commit v9 on v8

--- a/solution.py
+++ b/solution.py
@@ -73,34 +73,58 @@
         scratch[(2 + side) * width : (3 + side) * width, :] = turned(gate_ref[module, side])
 
 
-def put_rows(scratch, values, step, rows):
-    scratch[pl.ds(step, values.shape[0], stride=rows), :] = values
-
-
-def get_rows(scratch, step, channels, rows):
-    return scratch[pl.ds(step, channels, stride=rows), :]
+BLOCK = 16
+
+
+def turn_matrix(rows):
+    size = BLOCK * rows
+    out = lax.broadcasted_iota(jnp.int32, (size, size), 0)
+    source = lax.broadcasted_iota(jnp.int32, (size, size), 1)
+    return jnp.where(source == (out % rows) * BLOCK + out // rows, 1.0, 0.0).astype(BF16)
+
+
+def spread_block(matrix, scratch, start, group):
+    rows, _, lanes = scratch.shape
+    block = scratch[:, start : start + BLOCK, :].reshape(rows * BLOCK, lanes)
+    return dot(matrix, block).astype(BF16).reshape(BLOCK // group, group, rows, lanes)
+
+
+def collect_block(matrix, values, scratch, start):
+    rows, _, lanes = scratch.shape
+    turned_block = dot(matrix, values.reshape(BLOCK * rows, lanes)).astype(BF16)
+    scratch[:, start : start + BLOCK, :] = turned_block.reshape(rows, BLOCK, lanes)
 
 
 def spread_edges(scratch, out_ref):
     shards, sides, group, rows, lanes = out_ref.shape
-    block = shards * group * rows
+    matrix, step = turn_matrix(rows), BLOCK // group
     for side in range(sides):
-        part = scratch[side * block : (side + 1) * block, :]
-        out_ref[:, side] = part.reshape(shards, group, rows, lanes).astype(BF16)
+        for shard in range(0, shards, step):
+            start = (side * shards + shard) * group
+            out_ref[shard : shard + step, side] = spread_block(matrix, scratch, start, group)
 
 
 def collect_edges(in_ref, scratch):
     shards, sides, group, rows, lanes = in_ref.shape
-    block = shards * group * rows
+    matrix, step = turn_matrix(rows), BLOCK // group
     for side in range(sides):
-        scratch[side * block : (side + 1) * block, :] = (
-            in_ref[:, side].astype(F32).reshape(block, lanes)
-        )
+        for shard in range(0, shards, step):
+            start = (side * shards + shard) * group
+            collect_block(matrix, in_ref[shard : shard + step, side], scratch, start)
+
+
+def spread_triangle(scratch, out_ref):
+    shards, group, rows, lanes = out_ref.shape
+    matrix, step = turn_matrix(rows), BLOCK // group
+    for shard in range(0, shards, step):
+        out_ref[shard : shard + step] = spread_block(matrix, scratch, shard * group, group)
 
 
 def collect_triangle(in_ref, scratch):
-    block = in_ref.size // in_ref.shape[-1]
-    scratch[0:block, :] = in_ref[...].astype(F32).reshape(block, in_ref.shape[-1])
+    shards, group, rows, lanes = in_ref.shape
+    matrix, step = turn_matrix(rows), BLOCK // group
+    for shard in range(0, shards, step):
+        collect_block(matrix, in_ref[shard : shard + step], scratch, shard * group)
 
 
 def each_row(rows, unroll, body, sums=None):
@@ -175,7 +199,7 @@
         normed_out[step] = normed
         mask = row_mask(lengths, step, rows, lanes)
         mask_out[pl.ds(step, 1), :] = mask
-        put_rows(scr, save_edges(step, normed, wts[...], mask, proj_out, gate_out), step, rows)
+        scr[step] = save_edges(step, normed, wts[...], mask, proj_out, gate_out).astype(BF16)
 
     each_row(rows, 4, body)
     spread_edges(scr, edge_out)
@@ -194,7 +218,7 @@
     collect_triangle(tri, scr)
 
     def body(step):
-        scaled_mid, inverse_mid = mid_norm(get_rows(scr, step, channels, rows))
+        scaled_mid, inverse_mid = mid_norm(scr[step, 0:channels].astype(F32))
         scaled_mid_out[step] = scaled_mid
         inverse_mid_out[pl.ds(step, 1), :] = inverse_mid
         unit = (scaled_mid * gain_mid + bias_mid).astype(BF16)
@@ -207,7 +231,7 @@
         normed = (scaled * gain + bias).astype(BF16)
         normed_out[step] = normed
         mask = mask_all[pl.ds(step, 1), :]
-        put_rows(scr, save_edges(step, normed, wts[...], mask, proj_out, gate_out), step, rows)
+        scr[step] = save_edges(step, normed, wts[...], mask, proj_out, gate_out).astype(BF16)
 
     each_row(rows, 4, body)
     spread_edges(scr, edge_out)
@@ -249,8 +273,8 @@
         gated = grad * outgate
         d_outer = gated.astype(BF16)
         d_unit = dot(out_w[1], d_outer)
-        scaled_mid, inverse_mid = mid_norm(get_rows(scr, step, channels, rows))
-        put_rows(scr, norm_backward(d_unit * gain_mid, scaled_mid, inverse_mid), step, rows)
+        scaled_mid, inverse_mid = mid_norm(scr[step, 0:channels].astype(F32))
+        scr[step] = norm_backward(d_unit * gain_mid, scaled_mid, inverse_mid).astype(BF16)
         unit = (scaled_mid * gain_mid + bias_mid).astype(BF16)
         outer = dot(out_t, unit)
         new_out[step] = jnp.transpose(mid[step].astype(F32) + outer * outgate).astype(BF16)
@@ -263,7 +287,7 @@
         return d_unit * scaled_mid, d_unit
 
     each_row(rows, 4, body, sums)
-    d_tri_out[...] = scr[...].reshape(d_tri_out.shape).astype(BF16)
+    spread_triangle(scr, d_tri_out)
     out_weight_grads(unit_all, outer_all, normed_all, gate_all, weights_out)
     for index in range(2):
         small_out[index : index + 1, :] = as_row(sums[index])
@@ -295,7 +319,7 @@
 
     def upper(step):
         place = lane_block(step, lanes)
-        here = get_rows(scr, step, half, rows)
+        here = scr[step].astype(F32)
         d_proj = (here * proj_factor[step]).astype(BF16)
         d_gate = (here * gate_factor[step]).astype(BF16)
         d_in = jnp.concatenate([d_proj, d_gate], axis=0)
@@ -316,7 +340,7 @@
         d_unit = dot(out_w[0], d_outer)
         scaled = scaled_mid[step]
         d_tri = norm_backward(d_unit * gain_mid, scaled, inverse_mid[pl.ds(step, 1), :])
-        put_rows(scr_tri, d_tri, step, rows)
+        scr_tri[step] = d_tri.astype(BF16)
         unit = (scaled * gain_mid + bias_mid).astype(BF16)
         outer = dot(out_t, unit)
         d_gatepre = (gated * outer * (1.0 - gate)).astype(BF16)
@@ -329,7 +353,7 @@
 
     each_row(rows, 4, upper, sums.at[2:4])
     each_row(rows, 4, lower, sums.at[0:2])
-    d_tri_out[...] = scr_tri[...].reshape(d_tri_out.shape).astype(BF16)
+    spread_triangle(scr_tri, d_tri_out)
     out_weight_grads(unit_all, outer_all, normed_all, gate_all, out_weights)
     in_weight_grads(upper_all, d_in_all, in_weights)
     for index in range(4):
@@ -353,7 +377,7 @@
 
     def body(step):
         place = lane_block(step, lanes)
-        here = get_rows(scr, step, half, rows)
+        here = scr[step].astype(F32)
         d_proj = (here * proj_factor[step]).astype(BF16)
         d_gate = (here * gate_factor[step]).astype(BF16)
         d_in = jnp.concatenate([d_proj, d_gate], axis=0)
@@ -540,8 +564,8 @@
     factor = ((rows, 2 * H, lanes), F32)
     d_in = ((rows, 4 * H, lanes), BF16)
     wts = ((4 * H, channels), BF16)
-    big = ((2 * H * rows, lanes), F32)
-    mid = ((H * rows, lanes), F32)
+    big = ((rows, 2 * H, lanes), BF16)
+    mid = ((rows, H, lanes), BF16)
     positions = rows * lanes
     flat = ((H, positions), BF16)
     flat_in = ((4 * H, positions), BF16)
@@ -895,6 +919,16 @@
     )
 
 
+def on_device(pair, *rest, many, few, split):
+    rows, lanes, channels = pair.shape
+    shards = many * few
+    whole_channels = split == 1 and H % shards == 0 and BLOCK % (H // shards) == 0
+    tiles = rows == BLOCK and lanes % 128 == 0 and channels == H
+    if whole_channels and tiles and many % 2 == 0 and few & (few - 1) == 0:
+        return grouped_device(pair, *rest, many=many, few=few)
+    return per_device(pair, *rest)
+
+
 def solution(mesh):
     in_specs = (
         P(("grp", "row"), "col", None),
@@ -921,11 +955,9 @@
         P("grp", None, None),
         P("grp", None, None),
     )
-    many, few = mesh.shape["row"], mesh.shape["col"]
-    if mesh.shape["ch"] == 1 and H % (many * few) == 0 and many % 2 == 0 and few & (few - 1) == 0:
-        body = functools.partial(grouped_device, many=many, few=few)
-    else:
-        body = per_device
+    body = functools.partial(
+        on_device, many=mesh.shape["row"], few=mesh.shape["col"], split=mesh.shape["ch"]
+    )
     return jax.shard_map(
         body, mesh=mesh, in_specs=in_specs, out_specs=out_specs, check_vma=False
     )

time: 252 us -> 252 us (level)
  no operation moved by 1% of the time
where the time goes in v9:
time: 252 us
  blocking collectives  223 us (88%)
  Pallas kernels  27.4 us (11%)
    all_to_all x8, blocking collectives, exchange(): lax.all_to_all(values, ('row', 'col'), split_axis=0, concat_axis=0, tiled...  196 us
    pallas_call x14, Pallas kernels, call(): pl.pallas_call(kernel, name=name, out_shape=shapes, in_specs=specs or [VE...  27.4 us
    all_to_all x2, blocking collectives, exchange_chips(): lax.all_to_all(values, ('row', 'col'), split_axis=0, concat_axis=0, axis_...  26.5 us
  transfers between devices with their start and end apart: 2, of which 0 were waited for; matrix products, arithmetic and copies ran while one was open for 0% of the time, Pallas kernels for 1%

profile of v9, /device:TPU:0, one launch (start us, length us, event | category | flops | bytes accessed | tf_op | source)
XLA Modules:
  0.0 251.6 jit_solution(14980116274857555247)
XLA Ops:
  1.3 4.2 %start.1 = (bf16[32,2,4,16,128]{4,3,2,1,0:T(8,128)(2,1)S(1)}, bf16[16,128,128]{2,1,0:T(8,128)(2,1)S(1)}, f32[16,256,128]{2,1,0:T(8,128)S(1)}, f32[16,256,128]{2,...) custom-call(s32[1]{0:T(128)S(6)} %copy.21.lengths, ...), custom_call_target="tpu_custom_call" | custom-call | flops 268435456 | bytes 7620612 | tf_op jit(solution)/shard_map/start/pallas_call | solution.py:518
  5.4 0.0 copy-start
  5.5 0.0 copy-start.1
  5.5 0.0 copy-start.2
  5.5 0.0 copy-start.3
  5.5 0.0 copy-start.5
  5.5 0.0 copy-start.6
  5.5 0.0 copy-start.7
  5.5 0.0 copy-start.8
  5.5 0.0 copy-start.9
  5.6 33.3 %all_to_all.50 = bf16[32,2,4,16,128]{4,3,2,1,0:T(8,128)(2,1)S(1)} all-to-all(bf16[32,2,4,16,128]{4,3,2,1,0:T(8,128)(2,1)S(1)} %get-tuple-element.57), channel_id=1, replica_groups=mesh['grp'=1,'row'=16,'col'=2,'ch'=1] {'row','col'}, dimensions={0} | all-to-all | bytes 2097152 | tf_op jit(solution)/shard_map/all_to_all | solution.py:533
  38.9 0.3 outgoing.1
  39.2 18.4 %all_to_all.51.tri = bf16[32,4,16,128]{3,2,1,0:T(8,128)(2,1)S(1)} all-to-all(bf16[32,4,16,128]{3,2,1,0:T(8,128)(2,1)S(1)} %bitcast.16), channel_id=1, replica_groups=mesh['grp'=1,'row'=16,'col'=2,'ch'=1] {'row','col'}, dimensions={0} | all-to-all | bytes 1048576 | tf_op jit(solution)/shard_map/all_to_all | solution.py:533
  57.7 0.0 copy-done
  57.7 0.0 copy-done.1
  57.7 0.0 copy-done.2
  57.7 0.0 copy-done.3
  57.7 0.0 copy-done.5
  57.7 0.0 copy-done.6
  57.7 0.0 copy-done.7
  57.7 0.0 copy-done.8
  57.7 0.0 copy-done.9
  57.7 4.9 %between.1 = (bf16[32,2,4,16,128]{4,3,2,1,0:T(8,128)(2,1)S(1)}, bf16[16,128,128]{2,1,0:T(8,128)(2,1)S(1)}, bf16[16,128,128]{2,1,0:T(8,128)(2,1)S(1)}, f32[16,256...) custom-call(f32[16,128]{1,0:T(8,128)S(1)} %get-tuple-element.56.mask, ...), custom_call_target="tpu_custom_call" | custom-call | flops 402653184 | bytes 11431936 | tf_op jit(solution)/shard_map/between/pallas_call | solution.py:518
  62.6 0.0 copy-start.4
  62.6 29.7 %all_to_all.52 = bf16[32,2,4,16,128]{4,3,2,1,0:T(8,128)(2,1)S(1)} all-to-all(bf16[32,2,4,16,128]{4,3,2,1,0:T(8,128)(2,1)S(1)} %get-tuple-element.59), channel_id=1, replica_groups=mesh['grp'=1,'row'=16,'col'=2,'ch'=1] {'row','col'}, dimensions={0} | all-to-all | bytes 2097152 | tf_op jit(solution)/shard_map/all_to_all | solution.py:533
  92.3 0.4 incoming.1
  92.7 18.4 %all_to_all.53.tri = bf16[32,4,16,128]{3,2,1,0:T(8,128)(2,1)S(1)} all-to-all(bf16[32,4,16,128]{3,2,1,0:T(8,128)(2,1)S(1)} %bitcast.17), channel_id=1, replica_groups=mesh['grp'=1,'row'=16,'col'=2,'ch'=1] {'row','col'}, dimensions={0} | all-to-all | bytes 1048576 | tf_op jit(solution)/shard_map/all_to_all | solution.py:533
  111.1 0.0 copy-done.4
  111.1 3.2 %turn.1 = (bf16[32,4,16,128]{3,2,1,0:T(8,128)(2,1)S(1)}, bf16[16,128,128]{2,1,0:T(8,128)(2,1)}, f32[16,128,128]{2,1,0:T(8,128)S(1)}, f32[16,128,128]{2,1,0:T(8,1...) custom-call(bf16[32,4,16,128]{3,2,1,0:T(8,128)(2,1)S(1)} %all_to_all.53.tri, ...), custom_call_target="tpu_custom_call" | custom-call | flops 402653184 | bytes 5442560 | tf_op jit(solution)/shard_map/turn/pallas_call | solution.py:518
  114.3 18.4 %all_to_all.54 = bf16[32,4,16,128]{3,2,1,0:T(8,128)(2,1)S(1)} all-to-all(bf16[32,4,16,128]{3,2,1,0:T(8,128)(2,1)S(1)} %get-tuple-element.63), channel_id=1, replica_groups=mesh['grp'=1,'row'=16,'col'=2,'ch'=1] {'row','col'}, dimensions={0} | all-to-all | bytes 1048576 | tf_op jit(solution)/shard_map/all_to_all | solution.py:533
  132.8 0.4 incoming_grad.1
  133.2 29.7 %all_to_all.55.d_edge = bf16[32,2,4,16,128]{4,3,2,1,0:T(8,128)(2,1)S(1)} all-to-all(bf16[32,2,4,16,128]{4,3,2,1,0:T(8,128)(2,1)S(1)} %bitcast.12), channel_id=1, replica_groups=mesh['grp'=1,'row'=16,'col'=2,'ch'=1] {'row','col'}, dimensions={0} | all-to-all | bytes 2097152 | tf_op jit(solution)/shard_map/all_to_all | solution.py:533
  162.9 7.0 %middle.1 = (bf16[32,4,16,128]{3,2,1,0:T(8,128)(2,1)S(1)}, f32[16,128,128]{2,1,0:T(8,128)S(1)}, f32[16,128,128]{2,1,0:T(8,128)S(1)}, bf16[256,128]{1,0:T(8,128)(...) custom-call(bf16[32,2,4,16,128]{4,3,2,1,0:T(8,128)(2,1)S(1)} %all_to_all.55.d_edge, ...), custom_call_target="tpu_custom_call" | custom-call | flops 872415232 | bytes 14767104 | tf_op jit(solution)/shard_map/middle/pallas_call | solution.py:518
  169.9 18.4 %all_to_all.56 = bf16[32,4,16,128]{3,2,1,0:T(8,128)(2,1)S(1)} all-to-all(bf16[32,4,16,128]{3,2,1,0:T(8,128)(2,1)S(1)} %get-tuple-element.73), channel_id=1, replica_groups=mesh['grp'=1,'row'=16,'col'=2,'ch'=1] {'row','col'}, dimensions={0} | all-to-all | bytes 1048576 | tf_op jit(solution)/shard_map/all_to_all | solution.py:533
  188.4 0.5 outgoing_grad.1
  188.8 29.7 %all_to_all.57.d_edge = bf16[32,2,4,16,128]{4,3,2,1,0:T(8,128)(2,1)S(1)} all-to-all(bf16[32,2,4,16,128]{4,3,2,1,0:T(8,128)(2,1)S(1)} %bitcast.13), channel_id=1, replica_groups=mesh['grp'=1,'row'=16,'col'=2,'ch'=1] {'row','col'}, dimensions={0} | all-to-all | bytes 2097152 | tf_op jit(solution)/shard_map/all_to_all | solution.py:533
  218.5 2.4 finish.1
  220.9 0.1 collective-permute-start
  221.0 1.4 norm_sums.1
  222.4 0.0 collective-permute-done.second
  222.5 13.4 %all_to_all.58.parts = bf16[16,48,128]{2,1,0:T(8,128)(2,1)S(1)} all-to-all(bf16[16,48,128]{2,1,0:T(8,128)(2,1)S(1)} %get-tuple-element.87), channel_id=1, replica_groups={{0,1,4,5,8,9,12,13,16,17,20,21,24,25,28,29},{2,3,6,7,10,11,14,15,18,19,..., dimensions={0} | all-to-all | bytes 393216 | tf_op jit(solution)/shard_map/all_to_all | solution.py:545
  235.9 13.1 %all_to_all.59.shared.own = bf16[16,64,128]{2,1,0:T(8,128)(2,1)S(1)} all-to-all(bf16[16,64,128]{2,1,0:T(8,128)(2,1)S(1)} %sum_weights.1), channel_id=1, replica_groups={{0,1,4,5,8,9,12,13,16,17,20,21,24,25,28,29},{2,3,6,7,10,11,14,15,18,19,..., dimensions={0} | all-to-all | bytes 524288 | tf_op jit(solution)/shard_map/all_to_all | solution.py:545
  249.0 0.0 collective-permute-start.1
  249.0 1.6 grad_pair.1
  250.6 0.0 collective-permute-done.1.other
  250.6 1.0 unpack.1
  (2 shorter events, 0.1 us)
Async XLA Ops:
  5.4 52.2 %copy-start = (bf16[2,2,128,128]{3,2,1,0:T(8,128)(2,1)S(1)}, bf16[2,2,128,128]{3,2,1,0:T(8,128)(2,1)}, u32[]{:S(2)}) copy-start(bf16[2,2,128,128]{3,2,1,0:T(8,128)(2,1)} %proj_w.5) | copy-start | bytes 393220
  5.5 52.2 %copy-start.1 = (bf16[2,2,128,128]{3,2,1,0:T(8,128)(2,1)S(1)}, bf16[2,2,128,128]{3,2,1,0:T(8,128)(2,1)}, u32[]{:S(2)}) copy-start(bf16[2,2,128,128]{3,2,1,0:T(8,128)(2,1)} %gate_w.5) | copy-start | bytes 393220
  5.5 52.2 %copy-start.2 = (bf16[2,128,128]{2,1,0:T(8,128)(2,1)S(1)}, bf16[2,128,128]{2,1,0:T(8,128)(2,1)}, u32[]{:S(2)}) copy-start(bf16[2,128,128]{2,1,0:T(8,128)(2,1)} %out_w.5) | copy-start | bytes 196612
  5.5 52.2 %copy-start.3 = (bf16[2,128,128]{2,1,0:T(8,128)(2,1)S(1)}, bf16[2,128,128]{2,1,0:T(8,128)(2,1)}, u32[]{:S(2)}) copy-start(bf16[2,128,128]{2,1,0:T(8,128)(2,1)} %outgate_w.5) | copy-start | bytes 196612
  5.5 52.2 %copy-start.5 = (bf16[16,128,128]{2,1,0:T(8,128)(2,1)S(1)}, bf16[16,128,128]{2,1,0:T(8,128)(2,1)}, u32[]{:S(2)}) copy-start(bf16[16,128,128]{2,1,0:T(8,128)(2,1)} %pair.1) | copy-start | bytes 1572868
  5.5 52.2 %copy-start.6 = (f32[2,128]{1,0:T(2,128)S(1)}, f32[2,128]{1,0:T(2,128)}, u32[]{:S(2)}) copy-start(f32[2,128]{1,0:T(2,128)} %mgain.5) | copy-start | bytes 3076
  5.5 52.2 %copy-start.7 = (f32[2,128]{1,0:T(2,128)S(1)}, f32[2,128]{1,0:T(2,128)}, u32[]{:S(2)}) copy-start(f32[2,128]{1,0:T(2,128)} %mbias.5) | copy-start | bytes 3076
  5.5 52.2 %copy-start.8 = (f32[2,128]{1,0:T(2,128)S(1)}, f32[2,128]{1,0:T(2,128)}, u32[]{:S(2)}) copy-start(f32[2,128]{1,0:T(2,128)} %ngain.5) | copy-start | bytes 3076
  5.5 52.2 %copy-start.9 = (f32[2,128]{1,0:T(2,128)S(1)}, f32[2,128]{1,0:T(2,128)}, u32[]{:S(2)}) copy-start(f32[2,128]{1,0:T(2,128)} %nbias.1) | copy-start | bytes 3076
  62.6 48.5 %copy-start.4 = (bf16[16,128,128]{2,1,0:T(8,128)(2,1)S(1)}, bf16[16,128,128]{2,1,0:T(8,128)(2,1)}, u32[]{:S(2)}) copy-start(bf16[16,128,128]{2,1,0:T(8,128)(2,1)} %cot.1) | copy-start | bytes 1572868
  220.9 1.5 collective-permute-start
  249.0 1.6 collective-permute-start.1

commit v10 on v9

--- a/solution.py
+++ b/solution.py
@@ -66,11 +66,24 @@
     return jnp.where((row_id < limit) & (col_id < limit), 1.0, 0.0).astype(F32)
 
 
+EDGE_BLOCK = 64
+
+
 def load_in_weights(proj_ref, gate_ref, module, scratch):
     width = proj_ref.shape[-1]
     for side in range(2):
-        scratch[side * width : (side + 1) * width, :] = turned(proj_ref[module, side])
-        scratch[(2 + side) * width : (3 + side) * width, :] = turned(gate_ref[module, side])
+        proj, gate = turned(proj_ref[module, side]), turned(gate_ref[module, side])
+        for start in range(0, width, EDGE_BLOCK):
+            at = 2 * (side * width + start)
+            scratch[at : at + EDGE_BLOCK, :] = proj[start : start + EDGE_BLOCK]
+            scratch[at + EDGE_BLOCK : at + 2 * EDGE_BLOCK, :] = gate[start : start + EDGE_BLOCK]
+
+
+def load_back_weights(proj_ref, gate_ref, module, scratch):
+    width = proj_ref.shape[-1]
+    for side in range(2):
+        scratch[:, side * width : (side + 1) * width] = proj_ref[module, side]
+        scratch[:, (2 + side) * width : (3 + side) * width] = gate_ref[module, side]
 
 
 BLOCK = 16
@@ -162,15 +175,16 @@
     return scaled
 
 
-def save_edges(step, normed, in_weights, mask, proj_out, gate_out):
-    pre = dot(in_weights, normed)
-    half = pre.shape[0] // 2
-    gating = sigmoid(pre[half:])
-    factor = gating * mask
-    value = pre[:half] * factor
-    proj_out[step] = factor
-    gate_out[step] = value * (1.0 - gating)
-    return value
+def save_edges(step, normed, wts, mask, proj_out, gate_out, edge_scr):
+    for start in range(0, proj_out.shape[1], EDGE_BLOCK):
+        block = slice(start, start + EDGE_BLOCK)
+        pre = dot(wts[2 * start : 2 * (start + EDGE_BLOCK), :], normed)
+        gating = sigmoid(pre[EDGE_BLOCK:])
+        factor = gating * mask
+        value = pre[:EDGE_BLOCK] * factor
+        proj_out[step, block] = factor
+        gate_out[step, block] = value * (1.0 - gating)
+        edge_scr[step, block] = value.astype(BF16)
 
 
 def start_kernel(
@@ -199,7 +213,7 @@
         normed_out[step] = normed
         mask = row_mask(lengths, step, rows, lanes)
         mask_out[pl.ds(step, 1), :] = mask
-        scr[step] = save_edges(step, normed, wts[...], mask, proj_out, gate_out).astype(BF16)
+        save_edges(step, normed, wts, mask, proj_out, gate_out, scr)
 
     each_row(rows, 4, body)
     spread_edges(scr, edge_out)
@@ -231,7 +245,7 @@
         normed = (scaled * gain + bias).astype(BF16)
         normed_out[step] = normed
         mask = mask_all[pl.ds(step, 1), :]
-        scr[step] = save_edges(step, normed, wts[...], mask, proj_out, gate_out).astype(BF16)
+        save_edges(step, normed, wts, mask, proj_out, gate_out, scr)
 
     each_row(rows, 4, body)
     spread_edges(scr, edge_out)
@@ -293,13 +307,15 @@
         small_out[index : index + 1, :] = as_row(sums[index])
 
 
-def in_normed(d_in, all_w, proj_w, gate_w):
-    width = proj_w.shape[-1]
-    total = all_w
-    for side in range(2):
-        total = total + dot(proj_w[side], d_in[side * width : (side + 1) * width])
-        total = total + dot(gate_w[side], d_in[(2 + side) * width : (3 + side) * width])
-    return total
+def edge_backward(step, scratch, proj_factor, gate_factor, d_in_out):
+    half = proj_factor.shape[1]
+    for start in range(0, half, EDGE_BLOCK):
+        block = slice(start, start + EDGE_BLOCK)
+        here = scratch[step, block].astype(F32)
+        d_in_out[start : start + EDGE_BLOCK, :] = (here * proj_factor[step, block]).astype(BF16)
+        d_in_out[half + start : half + start + EDGE_BLOCK, :] = (
+            here * gate_factor[step, block]
+        ).astype(BF16)
 
 
 def middle_kernel(
@@ -307,7 +323,7 @@
     scaled_mid, inverse_mid, normed0, normed1, ngain, mgain, mbias, proj_w, gate_w, out_w,
     outgate_w,
     d_tri_out, grad_out, d_normed_out, out_weights, in_weights, small_out,
-    scr, scr_tri, unit_all, outer_all, normed_all, gate_all, upper_all, d_in_all, sums,
+    scr, scr_tri, unit_all, outer_all, normed_all, gate_all, upper_all, d_in_all, back, sums,
 ):
     rows, channels, lanes = cot.shape
     out_t = turned(out_w[0])
@@ -315,17 +331,13 @@
     gain_mid, bias_mid = column(mgain, 0, lanes), column(mbias, 0, lanes)
     collect_edges(d_edge, scr)
     sums[...] = jnp.zeros_like(sums)
-    half = proj_factor.shape[1]
+    load_back_weights(proj_w, gate_w, 1, back)
 
     def upper(step):
         place = lane_block(step, lanes)
-        here = scr[step].astype(F32)
-        d_proj = (here * proj_factor[step]).astype(BF16)
-        d_gate = (here * gate_factor[step]).astype(BF16)
-        d_in = jnp.concatenate([d_proj, d_gate], axis=0)
-        d_in_all[:, place] = d_in
+        edge_backward(step, scr, proj_factor, gate_factor, d_in_all.at[:, place])
         upper_all[:, place] = normed1[step]
-        d_normed = in_normed(d_in, d_normed_gate[step], proj_w[1], gate_w[1])
+        d_normed = d_normed_gate[step] + dot(back[...], d_in_all[:, place])
         scaled = scaled_in[step]
         grad_out[step] = cot[step] + norm_backward(
             d_normed * gain, scaled, inverse_in[pl.ds(step, 1), :]
@@ -370,19 +382,14 @@
 
 def finish_kernel(
     few, d_edge, proj_factor, gate_factor, normed, out0, in1, out1,
-    own_out, other_out, d_in_out, scr, normed_all, d_in_all, packed,
+    own_out, other_out, d_in_all, scr, normed_all, packed,
 ):
     rows, half, lanes = proj_factor.shape
     collect_edges(d_edge, scr)
 
     def body(step):
         place = lane_block(step, lanes)
-        here = scr[step].astype(F32)
-        d_proj = (here * proj_factor[step]).astype(BF16)
-        d_gate = (here * gate_factor[step]).astype(BF16)
-        d_in = jnp.concatenate([d_proj, d_gate], axis=0)
-        d_in_out[step] = d_in
-        d_in_all[:, place] = d_in
+        edge_backward(step, scr, proj_factor, gate_factor, d_in_all.at[:, place])
         normed_all[:, place] = normed[step]
 
     each_row(rows, 4, body)
@@ -396,13 +403,14 @@
 
 def norm_sums_kernel(
     d_in, d_normed_gate, scaled_in, proj_w, gate_w, small_middle, small1,
-    d_normed_out, extra_out, sums,
+    d_normed_out, extra_out, back, sums,
 ):
-    rows = d_in.shape[0]
+    rows, channels, lanes = scaled_in.shape
     sums[...] = jnp.zeros_like(sums)
+    load_back_weights(proj_w, gate_w, 0, back)
 
     def body(step):
-        d_normed = in_normed(d_in[step], d_normed_gate[step], proj_w[0], gate_w[0])
+        d_normed = d_normed_gate[step] + dot(back[...], d_in[:, lane_block(step, lanes)])
         d_normed_out[step] = d_normed
         return d_normed * scaled_in[step], d_normed
 
@@ -562,7 +570,7 @@
     wide = ((rows, channels, lanes), F32)
     row = ((rows, lanes), F32)
     factor = ((rows, 2 * H, lanes), F32)
-    d_in = ((rows, 4 * H, lanes), BF16)
+    back = ((channels, 4 * H), BF16)
     wts = ((4 * H, channels), BF16)
     big = ((rows, 2 * H, lanes), BF16)
     mid = ((rows, H, lanes), BF16)
@@ -624,7 +632,7 @@
         [d_edge1, proj_factor1, gate_factor1, d_normed_gate1, scaled1, inverse1, cot_t, outgate0,
          scaled_mid0, inverse_mid0, normed0, normed1, ngain, mgain, mbias, proj_w, gate_w, out_w,
          outgate_w],
-        [big, mid, flat, flat, flat, flat, flat, flat_in, sums(4)], 13 * dense,
+        [big, mid, flat, flat, flat, flat, flat, flat_in, back, sums(4)], 13 * dense,
     )
     d_tri0 = exchange(sent).reshape(tri_grid[0])
     (sent,) = call(
@@ -637,14 +645,14 @@
     proj_factor0, gate_factor0, scaled0, inverse0 = factors0
     held = ((chips, share, H), BF16)
     own, other, d_in0 = call(
-        functools.partial(finish_kernel, few), "finish", [held, held, d_in],
+        functools.partial(finish_kernel, few), "finish", [held, held, flat_in],
         [d_edge0, proj_factor0, gate_factor0, normed0, out_grads0, in_grads1, out_grads1],
-        [big, flat, flat_in, ((12 * H, H), BF16)], 4 * dense,
+        [big, flat, ((12 * H, H), BF16)], 4 * dense,
     )
     other = swap_cores(other, many, few)
     d_normed0, extra = call(
         norm_sums_kernel, "norm_sums", [wide, ((16, H), BF16)],
-        [d_in0, d_normed_gate0, scaled0, proj_w, gate_w, small_middle, small1], [sums(2)],
+        [d_in0, d_normed_gate0, scaled0, proj_w, gate_w, small_middle, small1], [back, sums(2)],
         4 * dense,
     )
     own, extra = call(add_kernel, "add_cores", [held, ((16, H), BF16)], [own, other, extra])

time: 252 us -> 253 us (level)
  no operation moved by 1% of the time
where the time goes in v10:
time: 253 us
  blocking collectives  223 us (88%)
  Pallas kernels  28.8 us (11%)
    all_to_all x8, blocking collectives, exchange(): lax.all_to_all(values, ('row', 'col'), split_axis=0, concat_axis=0, tiled...  196 us
    pallas_call x14, Pallas kernels, call(): pl.pallas_call(kernel, name=name, out_shape=shapes, in_specs=specs or [VE...  28.8 us
    all_to_all x2, blocking collectives, exchange_chips(): lax.all_to_all(values, ('row', 'col'), split_axis=0, concat_axis=0, axis_...  26.5 us
  transfers between devices with their start and end apart: 2, of which 0 were waited for; matrix products, arithmetic and copies ran while one was open for 0% of the time, Pallas kernels for 1%

profile of v10, /device:TPU:0, one launch (start us, length us, event | category | flops | bytes accessed | tf_op | source)
XLA Modules:
  0.0 253.0 jit_solution(3440895544279440558)
XLA Ops:
  1.3 4.1 %start.1 = (bf16[32,2,4,16,128]{4,3,2,1,0:T(8,128)(2,1)S(1)}, bf16[16,128,128]{2,1,0:T(8,128)(2,1)S(1)}, f32[16,256,128]{2,1,0:T(8,128)S(1)}, f32[16,256,128]{2,...) custom-call(s32[1]{0:T(128)S(6)} %copy.21.lengths, ...), custom_call_target="tpu_custom_call" | custom-call | flops 268435456 | bytes 7620612 | tf_op jit(solution)/shard_map/start/pallas_call | solution.py:526
  5.4 0.0 copy-start
  5.4 0.0 copy-start.1
  5.4 0.0 copy-start.2
  5.5 0.0 copy-start.3
  5.5 0.0 copy-start.5
  5.5 0.0 copy-start.6
  5.5 0.0 copy-start.7
  5.5 0.0 copy-start.8
  5.5 0.0 copy-start.9
  5.5 33.3 %all_to_all.50 = bf16[32,2,4,16,128]{4,3,2,1,0:T(8,128)(2,1)S(1)} all-to-all(bf16[32,2,4,16,128]{4,3,2,1,0:T(8,128)(2,1)S(1)} %get-tuple-element.57), channel_id=1, replica_groups=mesh['grp'=1,'row'=16,'col'=2,'ch'=1] {'row','col'}, dimensions={0} | all-to-all | bytes 2097152 | tf_op jit(solution)/shard_map/all_to_all | solution.py:541
  38.9 0.3 outgoing.1
  39.2 18.4 %all_to_all.51.tri = bf16[32,4,16,128]{3,2,1,0:T(8,128)(2,1)S(1)} all-to-all(bf16[32,4,16,128]{3,2,1,0:T(8,128)(2,1)S(1)} %bitcast.16), channel_id=1, replica_groups=mesh['grp'=1,'row'=16,'col'=2,'ch'=1] {'row','col'}, dimensions={0} | all-to-all | bytes 1048576 | tf_op jit(solution)/shard_map/all_to_all | solution.py:541
  57.6 0.0 copy-done
  57.6 0.0 copy-done.1
  57.6 0.0 copy-done.2
  57.6 0.0 copy-done.3
  57.7 0.0 copy-done.5
  57.7 0.0 copy-done.6
  57.7 0.0 copy-done.7
  57.7 0.0 copy-done.8
  57.7 0.0 copy-done.9
  57.7 6.3 %between.1 = (bf16[32,2,4,16,128]{4,3,2,1,0:T(8,128)(2,1)S(1)}, bf16[16,128,128]{2,1,0:T(8,128)(2,1)S(1)}, bf16[16,128,128]{2,1,0:T(8,128)(2,1)S(1)}, f32[16,256...) custom-call(f32[16,128]{1,0:T(8,128)S(1)} %get-tuple-element.56.mask, ...), custom_call_target="tpu_custom_call" | custom-call | flops 402653184 | bytes 11431936 | tf_op jit(solution)/shard_map/between/pallas_call | solution.py:526
  64.0 0.0 copy-start.4
  64.0 29.7 %all_to_all.52 = bf16[32,2,4,16,128]{4,3,2,1,0:T(8,128)(2,1)S(1)} all-to-all(bf16[32,2,4,16,128]{4,3,2,1,0:T(8,128)(2,1)S(1)} %get-tuple-element.59), channel_id=1, replica_groups=mesh['grp'=1,'row'=16,'col'=2,'ch'=1] {'row','col'}, dimensions={0} | all-to-all | bytes 2097152 | tf_op jit(solution)/shard_map/all_to_all | solution.py:541
  93.7 0.3 incoming.1
  94.0 18.4 %all_to_all.53.tri = bf16[32,4,16,128]{3,2,1,0:T(8,128)(2,1)S(1)} all-to-all(bf16[32,4,16,128]{3,2,1,0:T(8,128)(2,1)S(1)} %bitcast.17), channel_id=1, replica_groups=mesh['grp'=1,'row'=16,'col'=2,'ch'=1] {'row','col'}, dimensions={0} | all-to-all | bytes 1048576 | tf_op jit(solution)/shard_map/all_to_all | solution.py:541
  112.5 0.0 copy-done.4
  112.5 3.2 %turn.1 = (bf16[32,4,16,128]{3,2,1,0:T(8,128)(2,1)S(1)}, bf16[16,128,128]{2,1,0:T(8,128)(2,1)}, f32[16,128,128]{2,1,0:T(8,128)S(1)}, f32[16,128,128]{2,1,0:T(8,1...) custom-call(bf16[32,4,16,128]{3,2,1,0:T(8,128)(2,1)S(1)} %all_to_all.53.tri, ...), custom_call_target="tpu_custom_call" | custom-call | flops 402653184 | bytes 5442560 | tf_op jit(solution)/shard_map/turn/pallas_call | solution.py:526
  115.7 18.4 %all_to_all.54 = bf16[32,4,16,128]{3,2,1,0:T(8,128)(2,1)S(1)} all-to-all(bf16[32,4,16,128]{3,2,1,0:T(8,128)(2,1)S(1)} %get-tuple-element.63), channel_id=1, replica_groups=mesh['grp'=1,'row'=16,'col'=2,'ch'=1] {'row','col'}, dimensions={0} | all-to-all | bytes 1048576 | tf_op jit(solution)/shard_map/all_to_all | solution.py:541
  134.1 0.4 incoming_grad.1
  134.6 29.7 %all_to_all.55.d_edge = bf16[32,2,4,16,128]{4,3,2,1,0:T(8,128)(2,1)S(1)} all-to-all(bf16[32,2,4,16,128]{4,3,2,1,0:T(8,128)(2,1)S(1)} %bitcast.12), channel_id=1, replica_groups=mesh['grp'=1,'row'=16,'col'=2,'ch'=1] {'row','col'}, dimensions={0} | all-to-all | bytes 2097152 | tf_op jit(solution)/shard_map/all_to_all | solution.py:541
  164.2 7.3 %middle.1 = (bf16[32,4,16,128]{3,2,1,0:T(8,128)(2,1)S(1)}, f32[16,128,128]{2,1,0:T(8,128)S(1)}, f32[16,128,128]{2,1,0:T(8,128)S(1)}, bf16[256,128]{1,0:T(8,128)(...) custom-call(bf16[32,2,4,16,128]{4,3,2,1,0:T(8,128)(2,1)S(1)} %all_to_all.55.d_edge, ...), custom_call_target="tpu_custom_call" | custom-call | flops 872415232 | bytes 14767104 | tf_op jit(solution)/shard_map/middle/pallas_call | solution.py:526
  171.6 18.4 %all_to_all.56 = bf16[32,4,16,128]{3,2,1,0:T(8,128)(2,1)S(1)} all-to-all(bf16[32,4,16,128]{3,2,1,0:T(8,128)(2,1)S(1)} %get-tuple-element.73), channel_id=1, replica_groups=mesh['grp'=1,'row'=16,'col'=2,'ch'=1] {'row','col'}, dimensions={0} | all-to-all | bytes 1048576 | tf_op jit(solution)/shard_map/all_to_all | solution.py:541
  190.0 0.5 outgoing_grad.1
  190.5 29.7 %all_to_all.57.d_edge = bf16[32,2,4,16,128]{4,3,2,1,0:T(8,128)(2,1)S(1)} all-to-all(bf16[32,2,4,16,128]{4,3,2,1,0:T(8,128)(2,1)S(1)} %bitcast.13), channel_id=1, replica_groups=mesh['grp'=1,'row'=16,'col'=2,'ch'=1] {'row','col'}, dimensions={0} | all-to-all | bytes 2097152 | tf_op jit(solution)/shard_map/all_to_all | solution.py:541
  220.2 2.1 finish.1
  222.2 0.1 collective-permute-start
  222.3 1.5 norm_sums.1
  223.8 0.0 collective-permute-done.second
  223.8 0.1 add_cores.1
  223.9 13.4 %all_to_all.58.parts = bf16[16,48,128]{2,1,0:T(8,128)(2,1)S(1)} all-to-all(bf16[16,48,128]{2,1,0:T(8,128)(2,1)S(1)} %get-tuple-element.87), channel_id=1, replica_groups={{0,1,4,5,8,9,12,13,16,17,20,21,24,25,28,29},{2,3,6,7,10,11,14,15,18,19,..., dimensions={0} | all-to-all | bytes 393216 | tf_op jit(solution)/shard_map/all_to_all | solution.py:553
  237.3 13.1 %all_to_all.59.shared.own = bf16[16,64,128]{2,1,0:T(8,128)(2,1)S(1)} all-to-all(bf16[16,64,128]{2,1,0:T(8,128)(2,1)S(1)} %sum_weights.1), channel_id=1, replica_groups={{0,1,4,5,8,9,12,13,16,17,20,21,24,25,28,29},{2,3,6,7,10,11,14,15,18,19,..., dimensions={0} | all-to-all | bytes 524288 | tf_op jit(solution)/shard_map/all_to_all | solution.py:553
  250.4 0.0 collective-permute-start.1
  250.4 1.6 grad_pair.1
  252.0 0.0 collective-permute-done.1.other
  252.0 1.0 unpack.1
  (1 shorter events, 0.0 us)
Async XLA Ops:
  5.4 52.2 %copy-start = (bf16[2,2,128,128]{3,2,1,0:T(8,128)(2,1)S(1)}, bf16[2,2,128,128]{3,2,1,0:T(8,128)(2,1)}, u32[]{:S(2)}) copy-start(bf16[2,2,128,128]{3,2,1,0:T(8,128)(2,1)} %proj_w.5) | copy-start | bytes 393220
  5.4 52.2 %copy-start.1 = (bf16[2,2,128,128]{3,2,1,0:T(8,128)(2,1)S(1)}, bf16[2,2,128,128]{3,2,1,0:T(8,128)(2,1)}, u32[]{:S(2)}) copy-start(bf16[2,2,128,128]{3,2,1,0:T(8,128)(2,1)} %gate_w.5) | copy-start | bytes 393220
  5.4 52.2 %copy-start.2 = (bf16[2,128,128]{2,1,0:T(8,128)(2,1)S(1)}, bf16[2,128,128]{2,1,0:T(8,128)(2,1)}, u32[]{:S(2)}) copy-start(bf16[2,128,128]{2,1,0:T(8,128)(2,1)} %out_w.5) | copy-start | bytes 196612
  5.5 52.2 %copy-start.3 = (bf16[2,128,128]{2,1,0:T(8,128)(2,1)S(1)}, bf16[2,128,128]{2,1,0:T(8,128)(2,1)}, u32[]{:S(2)}) copy-start(bf16[2,128,128]{2,1,0:T(8,128)(2,1)} %outgate_w.5) | copy-start | bytes 196612
  5.5 52.2 %copy-start.5 = (bf16[16,128,128]{2,1,0:T(8,128)(2,1)S(1)}, bf16[16,128,128]{2,1,0:T(8,128)(2,1)}, u32[]{:S(2)}) copy-start(bf16[16,128,128]{2,1,0:T(8,128)(2,1)} %pair.1) | copy-start | bytes 1572868
  5.5 52.2 %copy-start.6 = (f32[2,128]{1,0:T(2,128)S(1)}, f32[2,128]{1,0:T(2,128)}, u32[]{:S(2)}) copy-start(f32[2,128]{1,0:T(2,128)} %mgain.5) | copy-start | bytes 3076
  5.5 52.2 %copy-start.7 = (f32[2,128]{1,0:T(2,128)S(1)}, f32[2,128]{1,0:T(2,128)}, u32[]{:S(2)}) copy-start(f32[2,128]{1,0:T(2,128)} %mbias.5) | copy-start | bytes 3076
  5.5 52.2 %copy-start.8 = (f32[2,128]{1,0:T(2,128)S(1)}, f32[2,128]{1,0:T(2,128)}, u32[]{:S(2)}) copy-start(f32[2,128]{1,0:T(2,128)} %ngain.5) | copy-start | bytes 3076
  5.5 52.2 %copy-start.9 = (f32[2,128]{1,0:T(2,128)S(1)}, f32[2,128]{1,0:T(2,128)}, u32[]{:S(2)}) copy-start(f32[2,128]{1,0:T(2,128)} %nbias.1) | copy-start | bytes 3076
  64.0 48.5 %copy-start.4 = (bf16[16,128,128]{2,1,0:T(8,128)(2,1)S(1)}, bf16[16,128,128]{2,1,0:T(8,128)(2,1)}, u32[]{:S(2)}) copy-start(bf16[16,128,128]{2,1,0:T(8,128)(2,1)} %cot.1) | copy-start | bytes 1572868
  222.2 1.6 collective-permute-start
  250.4 1.6 collective-permute-start.1

commit v11 on v10

--- a/solution.py
+++ b/solution.py
@@ -66,17 +66,11 @@
     return jnp.where((row_id < limit) & (col_id < limit), 1.0, 0.0).astype(F32)
 
 
-EDGE_BLOCK = 64
-
-
 def load_in_weights(proj_ref, gate_ref, module, scratch):
     width = proj_ref.shape[-1]
     for side in range(2):
-        proj, gate = turned(proj_ref[module, side]), turned(gate_ref[module, side])
-        for start in range(0, width, EDGE_BLOCK):
-            at = 2 * (side * width + start)
-            scratch[at : at + EDGE_BLOCK, :] = proj[start : start + EDGE_BLOCK]
-            scratch[at + EDGE_BLOCK : at + 2 * EDGE_BLOCK, :] = gate[start : start + EDGE_BLOCK]
+        scratch[side * width : (side + 1) * width, :] = turned(proj_ref[module, side])
+        scratch[(2 + side) * width : (3 + side) * width, :] = turned(gate_ref[module, side])
 
 
 def load_back_weights(proj_ref, gate_ref, module, scratch):
@@ -141,16 +135,13 @@
 
 
 def each_row(rows, unroll, body, sums=None):
-    def several(block, carry):
-        parts = [body(block * unroll + step) for step in range(unroll)]
+    for block in range(0, rows, unroll):
+        parts = [body(block + step) for step in range(unroll)]
         for index in range(0 if sums is None else sums.shape[0]):
             total = parts[0][index]
             for part in parts[1:]:
                 total = total + part[index]
             sums[index] += total
-        return carry
-
-    lax.fori_loop(0, rows // unroll, several, 0)
 
 
 def mid_norm(tri):
@@ -175,16 +166,15 @@
     return scaled
 
 
-def save_edges(step, normed, wts, mask, proj_out, gate_out, edge_scr):
-    for start in range(0, proj_out.shape[1], EDGE_BLOCK):
-        block = slice(start, start + EDGE_BLOCK)
-        pre = dot(wts[2 * start : 2 * (start + EDGE_BLOCK), :], normed)
-        gating = sigmoid(pre[EDGE_BLOCK:])
-        factor = gating * mask
-        value = pre[:EDGE_BLOCK] * factor
-        proj_out[step, block] = factor
-        gate_out[step, block] = value * (1.0 - gating)
-        edge_scr[step, block] = value.astype(BF16)
+def save_edges(step, normed, in_weights, mask, proj_out, gate_out):
+    pre = dot(in_weights, normed)
+    half = pre.shape[0] // 2
+    gating = sigmoid(pre[half:])
+    factor = gating * mask
+    value = pre[:half] * factor
+    proj_out[step] = factor
+    gate_out[step] = value * (1.0 - gating)
+    return value.astype(BF16)
 
 
 def start_kernel(
@@ -213,7 +203,7 @@
         normed_out[step] = normed
         mask = row_mask(lengths, step, rows, lanes)
         mask_out[pl.ds(step, 1), :] = mask
-        save_edges(step, normed, wts, mask, proj_out, gate_out, scr)
+        scr[step] = save_edges(step, normed, wts[...], mask, proj_out, gate_out)
 
     each_row(rows, 4, body)
     spread_edges(scr, edge_out)
@@ -222,17 +212,17 @@
 def between_kernel(
     mask_all, tri, pair, normed0, ngain, nbias, mgain, mbias, out_w, outgate_w, proj_w, gate_w,
     edge_out, mid_out, normed_out, proj_out, gate_out, scaled_out, inverse_out,
-    outgate_out, scaled_mid_out, inverse_mid_out, wts, scr,
+    outgate_out, scaled_mid_out, inverse_mid_out, wts, tri_in, scr,
 ):
     rows, lanes, channels = pair.shape
     load_in_weights(proj_w, gate_w, 1, wts)
     out_t, outgate_t = turned(out_w[0]), turned(outgate_w[0])
     gain, bias = column(ngain, 1, lanes), column(nbias, 1, lanes)
     gain_mid, bias_mid = column(mgain, 0, lanes), column(mbias, 0, lanes)
-    collect_triangle(tri, scr)
+    collect_triangle(tri, tri_in)
 
     def body(step):
-        scaled_mid, inverse_mid = mid_norm(scr[step, 0:channels].astype(F32))
+        scaled_mid, inverse_mid = mid_norm(tri_in[step].astype(F32))
         scaled_mid_out[step] = scaled_mid
         inverse_mid_out[pl.ds(step, 1), :] = inverse_mid
         unit = (scaled_mid * gain_mid + bias_mid).astype(BF16)
@@ -245,7 +235,7 @@
         normed = (scaled * gain + bias).astype(BF16)
         normed_out[step] = normed
         mask = mask_all[pl.ds(step, 1), :]
-        save_edges(step, normed, wts, mask, proj_out, gate_out, scr)
+        scr[step] = save_edges(step, normed, wts[...], mask, proj_out, gate_out)
 
     each_row(rows, 4, body)
     spread_edges(scr, edge_out)
@@ -265,18 +255,18 @@
 
 
 def lane_block(step, lanes):
-    return pl.ds(pl.multiple_of(step * lanes, lanes), lanes)
+    return pl.ds(step * lanes, lanes)
 
 
 def turn_kernel(
     tri, mid, normed, cot, mgain, mbias, out_w, outgate_w,
     d_tri_out, new_out, grad_out, d_normed_out, weights_out, small_out,
-    scr, unit_all, outer_all, normed_all, gate_all, sums,
+    tri_in, scr, unit_all, outer_all, normed_all, gate_all, sums,
 ):
     rows, channels, lanes = mid.shape
     out_t, outgate_t = turned(out_w[1]), turned(outgate_w[1])
     gain_mid, bias_mid = column(mgain, 1, lanes), column(mbias, 1, lanes)
-    collect_triangle(tri, scr)
+    collect_triangle(tri, tri_in)
     sums[...] = jnp.zeros_like(sums)
 
     def body(step):
@@ -287,7 +277,7 @@
         gated = grad * outgate
         d_outer = gated.astype(BF16)
         d_unit = dot(out_w[1], d_outer)
-        scaled_mid, inverse_mid = mid_norm(scr[step, 0:channels].astype(F32))
+        scaled_mid, inverse_mid = mid_norm(tri_in[step].astype(F32))
         scr[step] = norm_backward(d_unit * gain_mid, scaled_mid, inverse_mid).astype(BF16)
         unit = (scaled_mid * gain_mid + bias_mid).astype(BF16)
         outer = dot(out_t, unit)
@@ -307,15 +297,11 @@
         small_out[index : index + 1, :] = as_row(sums[index])
 
 
-def edge_backward(step, scratch, proj_factor, gate_factor, d_in_out):
-    half = proj_factor.shape[1]
-    for start in range(0, half, EDGE_BLOCK):
-        block = slice(start, start + EDGE_BLOCK)
-        here = scratch[step, block].astype(F32)
-        d_in_out[start : start + EDGE_BLOCK, :] = (here * proj_factor[step, block]).astype(BF16)
-        d_in_out[half + start : half + start + EDGE_BLOCK, :] = (
-            here * gate_factor[step, block]
-        ).astype(BF16)
+def edge_backward(step, scratch, proj_factor, gate_factor):
+    here = scratch[step].astype(F32)
+    d_proj = (here * proj_factor[step]).astype(BF16)
+    d_gate = (here * gate_factor[step]).astype(BF16)
+    return jnp.concatenate([d_proj, d_gate], axis=0)
 
 
 def middle_kernel(
@@ -335,9 +321,10 @@
 
     def upper(step):
         place = lane_block(step, lanes)
-        edge_backward(step, scr, proj_factor, gate_factor, d_in_all.at[:, place])
+        d_in = edge_backward(step, scr, proj_factor, gate_factor)
+        d_in_all[:, place] = d_in
         upper_all[:, place] = normed1[step]
-        d_normed = d_normed_gate[step] + dot(back[...], d_in_all[:, place])
+        d_normed = d_normed_gate[step] + dot(back[...], d_in)
         scaled = scaled_in[step]
         grad_out[step] = cot[step] + norm_backward(
             d_normed * gain, scaled, inverse_in[pl.ds(step, 1), :]
@@ -389,7 +376,7 @@
 
     def body(step):
         place = lane_block(step, lanes)
-        edge_backward(step, scr, proj_factor, gate_factor, d_in_all.at[:, place])
+        d_in_all[:, place] = edge_backward(step, scr, proj_factor, gate_factor)
         normed_all[:, place] = normed[step]
 
     each_row(rows, 4, body)
@@ -608,7 +595,7 @@
         between_kernel, "between", [edge, tile, *saved, wide, wide, row],
         [mask, tri0, pair, normed0, ngain, nbias, mgain, mbias, out_w, outgate_w, proj_w,
          gate_w],
-        [wts, big], 6 * dense,
+        [wts, mid, big], 6 * dense,
     )
     edge1 = exchange(sent).reshape(grid[0])
     (here,) = call(
@@ -618,7 +605,7 @@
     sent, new_pair, cot_t, d_normed_gate1, out_grads1, small1 = call(
         turn_kernel, "turn", [tri, (pair.shape, BF16), wide, wide, out_rows, small(2)],
         [tri1, mid_t, normed1, cotangent, mgain, mbias, out_w, outgate_w],
-        [mid, flat, flat, flat, flat, sums(2)], 6 * dense,
+        [mid, mid, flat, flat, flat, flat, sums(2)], 6 * dense,
     )
     d_tri1 = exchange(sent).reshape(tri_grid[0])
     (sent,) = call(

time: 253 us -> 247 us (0.976)
  Pallas kernels: 28.8 us -> 22.3 us
    pallas_call x14, Pallas kernels: 28.8 us -> 22.3 us  [call(): pl.pallas_call(kernel, name=name, out_shape=shapes, in_specs=specs or [VE...]
  transfers between devices with their start and end apart: 2 -> 2, of which waited for: 0 -> 2; matrix products, arithmetic and copies ran while one was open for 0% -> 0% of each run, Pallas kernels for 1% -> 1%
where the time goes in v11:
time: 247 us
  blocking collectives  222 us (90%)
  Pallas kernels  22.3 us (9%)
    all_to_all x8, blocking collectives, exchange(): lax.all_to_all(values, ('row', 'col'), split_axis=0, concat_axis=0, tiled...  196 us
    all_to_all x2, blocking collectives, exchange_chips(): lax.all_to_all(values, ('row', 'col'), split_axis=0, concat_axis=0, axis_...  26 us
    pallas_call x14, Pallas kernels, call(): pl.pallas_call(kernel, name=name, out_shape=shapes, in_specs=specs or [VE...  22.3 us
  transfers between devices with their start and end apart: 2, of which 2 were waited for; matrix products, arithmetic and copies ran while one was open for 0% of the time, Pallas kernels for 1%

profile of v11, /device:TPU:0, one launch (start us, length us, event | category | flops | bytes accessed | tf_op | source)
XLA Modules:
  0.0 246.6 jit_solution(18014817809868339946)
XLA Ops:
  1.3 3.2 %start.1 = (bf16[32,2,4,16,128]{4,3,2,1,0:T(8,128)(2,1)S(1)}, bf16[16,128,128]{2,1,0:T(8,128)(2,1)S(1)}, f32[16,256,128]{2,1,0:T(8,128)S(1)}, f32[16,256,128]{2,...) custom-call(s32[1]{0:T(128)S(6)} %copy.21.lengths, ...), custom_call_target="tpu_custom_call" | custom-call | flops 268435456 | bytes 7620612 | tf_op jit(solution)/shard_map/start/pallas_call | solution.py:513
  4.5 0.0 copy-start
  4.5 0.0 copy-start.1
  4.5 0.0 copy-start.2
  4.5 0.0 copy-start.3
  4.6 0.0 copy-start.5
  4.6 0.0 copy-start.6
  4.6 0.0 copy-start.7
  4.6 0.0 copy-start.8
  4.6 0.0 copy-start.9
  4.6 33.3 %all_to_all.50 = bf16[32,2,4,16,128]{4,3,2,1,0:T(8,128)(2,1)S(1)} all-to-all(bf16[32,2,4,16,128]{4,3,2,1,0:T(8,128)(2,1)S(1)} %get-tuple-element.57), channel_id=1, replica_groups=mesh['grp'=1,'row'=16,'col'=2,'ch'=1] {'row','col'}, dimensions={0} | all-to-all | bytes 2097152 | tf_op jit(solution)/shard_map/all_to_all | solution.py:528
  38.0 0.3 outgoing.1
  38.3 18.4 %all_to_all.51.tri = bf16[32,4,16,128]{3,2,1,0:T(8,128)(2,1)S(1)} all-to-all(bf16[32,4,16,128]{3,2,1,0:T(8,128)(2,1)S(1)} %bitcast.16), channel_id=1, replica_groups=mesh['grp'=1,'row'=16,'col'=2,'ch'=1] {'row','col'}, dimensions={0} | all-to-all | bytes 1048576 | tf_op jit(solution)/shard_map/all_to_all | solution.py:528
  56.7 0.0 copy-done
  56.7 0.0 copy-done.1
  56.7 0.0 copy-done.2
  56.7 0.0 copy-done.3
  56.7 0.0 copy-done.5
  56.8 0.0 copy-done.6
  56.8 0.0 copy-done.7
  56.8 0.0 copy-done.8
  56.8 0.0 copy-done.9
  56.8 4.0 %between.1 = (bf16[32,2,4,16,128]{4,3,2,1,0:T(8,128)(2,1)S(1)}, bf16[16,128,128]{2,1,0:T(8,128)(2,1)S(1)}, bf16[16,128,128]{2,1,0:T(8,128)(2,1)S(1)}, f32[16,256...) custom-call(f32[16,128]{1,0:T(8,128)S(1)} %get-tuple-element.56.mask, ...), custom_call_target="tpu_custom_call" | custom-call | flops 402653184 | bytes 11431936 | tf_op jit(solution)/shard_map/between/pallas_call | solution.py:513
  60.8 0.0 copy-start.4
  60.8 29.7 %all_to_all.52 = bf16[32,2,4,16,128]{4,3,2,1,0:T(8,128)(2,1)S(1)} all-to-all(bf16[32,2,4,16,128]{4,3,2,1,0:T(8,128)(2,1)S(1)} %get-tuple-element.59), channel_id=1, replica_groups=mesh['grp'=1,'row'=16,'col'=2,'ch'=1] {'row','col'}, dimensions={0} | all-to-all | bytes 2097152 | tf_op jit(solution)/shard_map/all_to_all | solution.py:528
  90.5 0.3 incoming.1
  90.9 18.4 %all_to_all.53.tri = bf16[32,4,16,128]{3,2,1,0:T(8,128)(2,1)S(1)} all-to-all(bf16[32,4,16,128]{3,2,1,0:T(8,128)(2,1)S(1)} %bitcast.17), channel_id=1, replica_groups=mesh['grp'=1,'row'=16,'col'=2,'ch'=1] {'row','col'}, dimensions={0} | all-to-all | bytes 1048576 | tf_op jit(solution)/shard_map/all_to_all | solution.py:528
  109.3 0.0 copy-done.4
  109.3 3.3 %turn.1 = (bf16[32,4,16,128]{3,2,1,0:T(8,128)(2,1)S(1)}, bf16[16,128,128]{2,1,0:T(8,128)(2,1)}, f32[16,128,128]{2,1,0:T(8,128)S(1)}, f32[16,128,128]{2,1,0:T(8,1...) custom-call(bf16[32,4,16,128]{3,2,1,0:T(8,128)(2,1)S(1)} %all_to_all.53.tri, ...), custom_call_target="tpu_custom_call" | custom-call | flops 402653184 | bytes 5442560 | tf_op jit(solution)/shard_map/turn/pallas_call | solution.py:513
  112.6 18.4 %all_to_all.54 = bf16[32,4,16,128]{3,2,1,0:T(8,128)(2,1)S(1)} all-to-all(bf16[32,4,16,128]{3,2,1,0:T(8,128)(2,1)S(1)} %get-tuple-element.63), channel_id=1, replica_groups=mesh['grp'=1,'row'=16,'col'=2,'ch'=1] {'row','col'}, dimensions={0} | all-to-all | bytes 1048576 | tf_op jit(solution)/shard_map/all_to_all | solution.py:528
  131.0 0.4 incoming_grad.1
  131.4 29.7 %all_to_all.55.d_edge = bf16[32,2,4,16,128]{4,3,2,1,0:T(8,128)(2,1)S(1)} all-to-all(bf16[32,2,4,16,128]{4,3,2,1,0:T(8,128)(2,1)S(1)} %bitcast.12), channel_id=1, replica_groups=mesh['grp'=1,'row'=16,'col'=2,'ch'=1] {'row','col'}, dimensions={0} | all-to-all | bytes 2097152 | tf_op jit(solution)/shard_map/all_to_all | solution.py:528
  161.1 5.4 %middle.1 = (bf16[32,4,16,128]{3,2,1,0:T(8,128)(2,1)S(1)}, f32[16,128,128]{2,1,0:T(8,128)S(1)}, f32[16,128,128]{2,1,0:T(8,128)S(1)}, bf16[256,128]{1,0:T(8,128)(...) custom-call(bf16[32,2,4,16,128]{4,3,2,1,0:T(8,128)(2,1)S(1)} %all_to_all.55.d_edge, ...), custom_call_target="tpu_custom_call" | custom-call | flops 872415232 | bytes 14767104 | tf_op jit(solution)/shard_map/middle/pallas_call | solution.py:513
  166.5 18.4 %all_to_all.56 = bf16[32,4,16,128]{3,2,1,0:T(8,128)(2,1)S(1)} all-to-all(bf16[32,4,16,128]{3,2,1,0:T(8,128)(2,1)S(1)} %get-tuple-element.73), channel_id=1, replica_groups=mesh['grp'=1,'row'=16,'col'=2,'ch'=1] {'row','col'}, dimensions={0} | all-to-all | bytes 1048576 | tf_op jit(solution)/shard_map/all_to_all | solution.py:528
  184.9 0.5 outgoing_grad.1
  185.4 29.7 %all_to_all.57.d_edge = bf16[32,2,4,16,128]{4,3,2,1,0:T(8,128)(2,1)S(1)} all-to-all(bf16[32,2,4,16,128]{4,3,2,1,0:T(8,128)(2,1)S(1)} %bitcast.13), channel_id=1, replica_groups=mesh['grp'=1,'row'=16,'col'=2,'ch'=1] {'row','col'}, dimensions={0} | all-to-all | bytes 2097152 | tf_op jit(solution)/shard_map/all_to_all | solution.py:528
  215.1 1.4 finish.1
  216.5 0.1 collective-permute-start
  216.5 1.0 norm_sums.1
  217.5 0.4 collective-permute-done.second
  218.0 13.4 %all_to_all.58.parts = bf16[16,48,128]{2,1,0:T(8,128)(2,1)S(1)} all-to-all(bf16[16,48,128]{2,1,0:T(8,128)(2,1)S(1)} %get-tuple-element.87), channel_id=1, replica_groups={{0,1,4,5,8,9,12,13,16,17,20,21,24,25,28,29},{2,3,6,7,10,11,14,15,18,19,..., dimensions={0} | all-to-all | bytes 393216 | tf_op jit(solution)/shard_map/all_to_all | solution.py:540
  231.4 12.6 %all_to_all.59.shared.own = bf16[16,64,128]{2,1,0:T(8,128)(2,1)S(1)} all-to-all(bf16[16,64,128]{2,1,0:T(8,128)(2,1)S(1)} %sum_weights.1), channel_id=1, replica_groups={{0,1,4,5,8,9,12,13,16,17,20,21,24,25,28,29},{2,3,6,7,10,11,14,15,18,19,..., dimensions={0} | all-to-all | bytes 524288 | tf_op jit(solution)/shard_map/all_to_all | solution.py:540
  244.1 0.0 collective-permute-start.1
  244.1 1.4 grad_pair.1
  245.5 0.1 collective-permute-done.1.other
  245.6 1.0 unpack.1
  (2 shorter events, 0.1 us)
Async XLA Ops:
  4.5 52.2 %copy-start = (bf16[2,2,128,128]{3,2,1,0:T(8,128)(2,1)S(1)}, bf16[2,2,128,128]{3,2,1,0:T(8,128)(2,1)}, u32[]{:S(2)}) copy-start(bf16[2,2,128,128]{3,2,1,0:T(8,128)(2,1)} %proj_w.5) | copy-start | bytes 393220
  4.5 52.2 %copy-start.1 = (bf16[2,2,128,128]{3,2,1,0:T(8,128)(2,1)S(1)}, bf16[2,2,128,128]{3,2,1,0:T(8,128)(2,1)}, u32[]{:S(2)}) copy-start(bf16[2,2,128,128]{3,2,1,0:T(8,128)(2,1)} %gate_w.5) | copy-start | bytes 393220
  4.5 52.2 %copy-start.2 = (bf16[2,128,128]{2,1,0:T(8,128)(2,1)S(1)}, bf16[2,128,128]{2,1,0:T(8,128)(2,1)}, u32[]{:S(2)}) copy-start(bf16[2,128,128]{2,1,0:T(8,128)(2,1)} %out_w.5) | copy-start | bytes 196612
  4.5 52.2 %copy-start.3 = (bf16[2,128,128]{2,1,0:T(8,128)(2,1)S(1)}, bf16[2,128,128]{2,1,0:T(8,128)(2,1)}, u32[]{:S(2)}) copy-start(bf16[2,128,128]{2,1,0:T(8,128)(2,1)} %outgate_w.5) | copy-start | bytes 196612
  4.6 52.2 %copy-start.5 = (bf16[16,128,128]{2,1,0:T(8,128)(2,1)S(1)}, bf16[16,128,128]{2,1,0:T(8,128)(2,1)}, u32[]{:S(2)}) copy-start(bf16[16,128,128]{2,1,0:T(8,128)(2,1)} %pair.1) | copy-start | bytes 1572868
  4.6 52.2 %copy-start.6 = (f32[2,128]{1,0:T(2,128)S(1)}, f32[2,128]{1,0:T(2,128)}, u32[]{:S(2)}) copy-start(f32[2,128]{1,0:T(2,128)} %mgain.5) | copy-start | bytes 3076
  4.6 52.2 %copy-start.7 = (f32[2,128]{1,0:T(2,128)S(1)}, f32[2,128]{1,0:T(2,128)}, u32[]{:S(2)}) copy-start(f32[2,128]{1,0:T(2,128)} %mbias.5) | copy-start | bytes 3076
  4.6 52.2 %copy-start.8 = (f32[2,128]{1,0:T(2,128)S(1)}, f32[2,128]{1,0:T(2,128)}, u32[]{:S(2)}) copy-start(f32[2,128]{1,0:T(2,128)} %ngain.5) | copy-start | bytes 3076
  4.6 52.2 %copy-start.9 = (f32[2,128]{1,0:T(2,128)S(1)}, f32[2,128]{1,0:T(2,128)}, u32[]{:S(2)}) copy-start(f32[2,128]{1,0:T(2,128)} %nbias.1) | copy-start | bytes 3076
  60.8 48.5 %copy-start.4 = (bf16[16,128,128]{2,1,0:T(8,128)(2,1)S(1)}, bf16[16,128,128]{2,1,0:T(8,128)(2,1)}, u32[]{:S(2)}) copy-start(bf16[16,128,128]{2,1,0:T(8,128)(2,1)} %cot.1) | copy-start | bytes 1572868
  216.5 1.5 collective-permute-start
  244.1 1.5 collective-permute-start.1

commit v12 on v11

--- a/solution.py
+++ b/solution.py
@@ -52,7 +52,43 @@
 
 def column(ref, module, lanes):
     row = ref[module : module + 1, :]
-    return jnp.transpose(jnp.broadcast_to(row, (lanes, row.shape[1])))
+    return beside(*[jnp.transpose(jnp.broadcast_to(row, (lanes, row.shape[1])))] * 2)
+
+
+def beside(left, right):
+    return jnp.concatenate([left, right], axis=-1)
+
+
+def pair_of(ref, step):
+    return beside(ref[2 * step], ref[2 * step + 1])
+
+
+def put_pair(ref, step, values):
+    lanes = ref.shape[-1]
+    ref[2 * step] = values[:, :lanes]
+    ref[2 * step + 1] = values[:, lanes:]
+
+
+def pair_of_rows(ref, step):
+    return beside(ref[2 * step : 2 * step + 1, :], ref[2 * step + 1 : 2 * step + 2, :])
+
+
+def put_pair_of_rows(ref, step, values):
+    lanes = ref.shape[-1]
+    ref[2 * step : 2 * step + 1, :] = values[:, :lanes]
+    ref[2 * step + 1 : 2 * step + 2, :] = values[:, lanes:]
+
+
+def turned_pair(ref, step):
+    return beside(
+        jnp.transpose(ref[2 * step].astype(F32)), jnp.transpose(ref[2 * step + 1].astype(F32))
+    )
+
+
+def put_turned_pair(ref, step, values):
+    lanes = ref.shape[1]
+    ref[2 * step] = jnp.transpose(values[:, :lanes]).astype(BF16)
+    ref[2 * step + 1] = jnp.transpose(values[:, lanes:]).astype(BF16)
 
 
 def as_row(total):
@@ -90,58 +126,67 @@
     return jnp.where(source == (out % rows) * BLOCK + out // rows, 1.0, 0.0).astype(BF16)
 
 
-def spread_block(matrix, scratch, start, group):
+def spread_blocks(matrix, scratch, start, group):
     rows, _, lanes = scratch.shape
-    block = scratch[:, start : start + BLOCK, :].reshape(rows * BLOCK, lanes)
-    return dot(matrix, block).astype(BF16).reshape(BLOCK // group, group, rows, lanes)
-
-
-def collect_block(matrix, values, scratch, start):
+    blocks = [
+        scratch[:, at : at + BLOCK, :].reshape(rows * BLOCK, lanes)
+        for at in (start, start + BLOCK)
+    ]
+    both = dot(matrix, beside(*blocks)).astype(BF16)
+    parts = [
+        part.reshape(BLOCK // group, group, rows, lanes)
+        for part in (both[:, :lanes], both[:, lanes:])
+    ]
+    return jnp.concatenate(parts, axis=0)
+
+
+def collect_blocks(matrix, values, scratch, start):
     rows, _, lanes = scratch.shape
-    turned_block = dot(matrix, values.reshape(BLOCK * rows, lanes)).astype(BF16)
-    scratch[:, start : start + BLOCK, :] = turned_block.reshape(rows, BLOCK, lanes)
+    flat = values.reshape(2, BLOCK * rows, lanes)
+    both = dot(matrix, beside(flat[0], flat[1])).astype(BF16)
+    for at, part in ((start, both[:, :lanes]), (start + BLOCK, both[:, lanes:])):
+        scratch[:, at : at + BLOCK, :] = part.reshape(rows, BLOCK, lanes)
 
 
 def spread_edges(scratch, out_ref):
     shards, sides, group, rows, lanes = out_ref.shape
-    matrix, step = turn_matrix(rows), BLOCK // group
+    matrix, step = turn_matrix(rows), 2 * BLOCK // group
     for side in range(sides):
         for shard in range(0, shards, step):
             start = (side * shards + shard) * group
-            out_ref[shard : shard + step, side] = spread_block(matrix, scratch, start, group)
+            out_ref[shard : shard + step, side] = spread_blocks(matrix, scratch, start, group)
 
 
 def collect_edges(in_ref, scratch):
     shards, sides, group, rows, lanes = in_ref.shape
-    matrix, step = turn_matrix(rows), BLOCK // group
+    matrix, step = turn_matrix(rows), 2 * BLOCK // group
     for side in range(sides):
         for shard in range(0, shards, step):
             start = (side * shards + shard) * group
-            collect_block(matrix, in_ref[shard : shard + step, side], scratch, start)
+            collect_blocks(matrix, in_ref[shard : shard + step, side], scratch, start)
 
 
 def spread_triangle(scratch, out_ref):
     shards, group, rows, lanes = out_ref.shape
-    matrix, step = turn_matrix(rows), BLOCK // group
+    matrix, step = turn_matrix(rows), 2 * BLOCK // group
     for shard in range(0, shards, step):
-        out_ref[shard : shard + step] = spread_block(matrix, scratch, shard * group, group)
+        out_ref[shard : shard + step] = spread_blocks(matrix, scratch, shard * group, group)
 
 
 def collect_triangle(in_ref, scratch):
     shards, group, rows, lanes = in_ref.shape
-    matrix, step = turn_matrix(rows), BLOCK // group
+    matrix, step = turn_matrix(rows), 2 * BLOCK // group
     for shard in range(0, shards, step):
-        collect_block(matrix, in_ref[shard : shard + step], scratch, shard * group)
-
-
-def each_row(rows, unroll, body, sums=None):
-    for block in range(0, rows, unroll):
-        parts = [body(block + step) for step in range(unroll)]
+        collect_blocks(matrix, in_ref[shard : shard + step], scratch, shard * group)
+
+
+def each_pair(rows, body, sums=None):
+    for block in range(0, rows // 2, 2):
+        parts = [body(block + step) for step in range(2)]
         for index in range(0 if sums is None else sums.shape[0]):
-            total = parts[0][index]
-            for part in parts[1:]:
-                total = total + part[index]
-            sums[index] += total
+            total = parts[0][index] + parts[1][index]
+            lanes = sums.shape[-1]
+            sums[index] += total[:, :lanes] + total[:, lanes:]
 
 
 def mid_norm(tri):
@@ -161,8 +206,8 @@
 
 def save_norm(step, values, scaled_out, inverse_out):
     scaled, inverse = norm_rows(values)
-    scaled_out[step] = scaled
-    inverse_out[pl.ds(step, 1), :] = inverse
+    put_pair(scaled_out, step, scaled)
+    put_pair_of_rows(inverse_out, step, inverse)
     return scaled
 
 
@@ -172,8 +217,8 @@
     gating = sigmoid(pre[half:])
     factor = gating * mask
     value = pre[:half] * factor
-    proj_out[step] = factor
-    gate_out[step] = value * (1.0 - gating)
+    put_pair(proj_out, step, factor)
+    put_pair(gate_out, step, value * (1.0 - gating))
     return value.astype(BF16)
 
 
@@ -197,15 +242,15 @@
     gain, bias = column(ngain, 0, lanes), column(nbias, 0, lanes)
 
     def body(step):
-        base = jnp.transpose(pair[step].astype(F32))
+        base = turned_pair(pair, step)
         scaled = save_norm(step, base, scaled_out, inverse_out)
         normed = (scaled * gain + bias).astype(BF16)
-        normed_out[step] = normed
-        mask = row_mask(lengths, step, rows, lanes)
-        mask_out[pl.ds(step, 1), :] = mask
-        scr[step] = save_edges(step, normed, wts[...], mask, proj_out, gate_out)
-
-    each_row(rows, 4, body)
+        put_pair(normed_out, step, normed)
+        mask = beside(*[row_mask(lengths, 2 * step + row, rows, lanes) for row in range(2)])
+        put_pair_of_rows(mask_out, step, mask)
+        put_pair(scr, step, save_edges(step, normed, wts[...], mask, proj_out, gate_out))
+
+    each_pair(rows, body)
     spread_edges(scr, edge_out)
 
 
@@ -222,22 +267,22 @@
     collect_triangle(tri, tri_in)
 
     def body(step):
-        scaled_mid, inverse_mid = mid_norm(tri_in[step].astype(F32))
-        scaled_mid_out[step] = scaled_mid
-        inverse_mid_out[pl.ds(step, 1), :] = inverse_mid
+        scaled_mid, inverse_mid = mid_norm(pair_of(tri_in, step).astype(F32))
+        put_pair(scaled_mid_out, step, scaled_mid)
+        put_pair_of_rows(inverse_mid_out, step, inverse_mid)
         unit = (scaled_mid * gain_mid + bias_mid).astype(BF16)
         outer = dot(out_t, unit)
-        outgate = sigmoid(dot(outgate_t, normed0[step]))
-        outgate_out[step] = outgate
-        mid = (jnp.transpose(pair[step].astype(F32)) + outer * outgate).astype(BF16)
-        mid_out[step] = mid
+        outgate = sigmoid(dot(outgate_t, pair_of(normed0, step)))
+        put_pair(outgate_out, step, outgate)
+        mid = (turned_pair(pair, step) + outer * outgate).astype(BF16)
+        put_pair(mid_out, step, mid)
         scaled = save_norm(step, mid.astype(F32), scaled_out, inverse_out)
         normed = (scaled * gain + bias).astype(BF16)
-        normed_out[step] = normed
-        mask = mask_all[pl.ds(step, 1), :]
-        scr[step] = save_edges(step, normed, wts[...], mask, proj_out, gate_out)
-
-    each_row(rows, 4, body)
+        put_pair(normed_out, step, normed)
+        mask = pair_of_rows(mask_all, step)
+        put_pair(scr, step, save_edges(step, normed, wts[...], mask, proj_out, gate_out))
+
+    each_pair(rows, body)
     spread_edges(scr, edge_out)
 
 
@@ -255,7 +300,7 @@
 
 
 def lane_block(step, lanes):
-    return pl.ds(step * lanes, lanes)
+    return pl.ds(2 * step * lanes, 2 * lanes)
 
 
 def turn_kernel(
@@ -271,26 +316,28 @@
 
     def body(step):
         here = lane_block(step, lanes)
-        grad = jnp.transpose(cot[step].astype(F32))
-        grad_out[step] = grad
-        outgate = sigmoid(dot(outgate_t, normed[step]))
+        grad = turned_pair(cot, step)
+        put_pair(grad_out, step, grad)
+        here_normed = pair_of(normed, step)
+        outgate = sigmoid(dot(outgate_t, here_normed))
         gated = grad * outgate
         d_outer = gated.astype(BF16)
         d_unit = dot(out_w[1], d_outer)
-        scaled_mid, inverse_mid = mid_norm(tri_in[step].astype(F32))
-        scr[step] = norm_backward(d_unit * gain_mid, scaled_mid, inverse_mid).astype(BF16)
+        scaled_mid, inverse_mid = mid_norm(pair_of(tri_in, step).astype(F32))
+        d_tri = norm_backward(d_unit * gain_mid, scaled_mid, inverse_mid)
+        put_pair(scr, step, d_tri.astype(BF16))
         unit = (scaled_mid * gain_mid + bias_mid).astype(BF16)
         outer = dot(out_t, unit)
-        new_out[step] = jnp.transpose(mid[step].astype(F32) + outer * outgate).astype(BF16)
+        put_turned_pair(new_out, step, pair_of(mid, step).astype(F32) + outer * outgate)
         d_gatepre = (gated * outer * (1.0 - outgate)).astype(BF16)
-        d_normed_out[step] = dot(outgate_w[1], d_gatepre)
+        put_pair(d_normed_out, step, dot(outgate_w[1], d_gatepre))
         unit_all[:, here] = unit
         outer_all[:, here] = d_outer
-        normed_all[:, here] = normed[step]
+        normed_all[:, here] = here_normed
         gate_all[:, here] = d_gatepre
         return d_unit * scaled_mid, d_unit
 
-    each_row(rows, 4, body, sums)
+    each_pair(rows, body, sums)
     spread_triangle(scr, d_tri_out)
     out_weight_grads(unit_all, outer_all, normed_all, gate_all, weights_out)
     for index in range(2):
@@ -298,9 +345,9 @@
 
 
 def edge_backward(step, scratch, proj_factor, gate_factor):
-    here = scratch[step].astype(F32)
-    d_proj = (here * proj_factor[step]).astype(BF16)
-    d_gate = (here * gate_factor[step]).astype(BF16)
+    here = pair_of(scratch, step).astype(F32)
+    d_proj = (here * pair_of(proj_factor, step)).astype(BF16)
+    d_gate = (here * pair_of(gate_factor, step)).astype(BF16)
     return jnp.concatenate([d_proj, d_gate], axis=0)
 
 
@@ -323,35 +370,36 @@
         place = lane_block(step, lanes)
         d_in = edge_backward(step, scr, proj_factor, gate_factor)
         d_in_all[:, place] = d_in
-        upper_all[:, place] = normed1[step]
-        d_normed = d_normed_gate[step] + dot(back[...], d_in)
-        scaled = scaled_in[step]
-        grad_out[step] = cot[step] + norm_backward(
-            d_normed * gain, scaled, inverse_in[pl.ds(step, 1), :]
+        upper_all[:, place] = pair_of(normed1, step)
+        d_normed = pair_of(d_normed_gate, step) + dot(back[...], d_in)
+        scaled = pair_of(scaled_in, step)
+        grad = pair_of(cot, step) + norm_backward(
+            d_normed * gain, scaled, pair_of_rows(inverse_in, step)
         )
+        put_pair(grad_out, step, grad)
         return d_normed * scaled, d_normed
 
     def lower(step):
         place = lane_block(step, lanes)
-        gate = outgate[step]
-        gated = grad_out[step] * gate
+        gate = pair_of(outgate, step)
+        gated = pair_of(grad_out, step) * gate
         d_outer = gated.astype(BF16)
         d_unit = dot(out_w[0], d_outer)
-        scaled = scaled_mid[step]
-        d_tri = norm_backward(d_unit * gain_mid, scaled, inverse_mid[pl.ds(step, 1), :])
-        scr_tri[step] = d_tri.astype(BF16)
+        scaled = pair_of(scaled_mid, step)
+        d_tri = norm_backward(d_unit * gain_mid, scaled, pair_of_rows(inverse_mid, step))
+        put_pair(scr_tri, step, d_tri.astype(BF16))
         unit = (scaled * gain_mid + bias_mid).astype(BF16)
         outer = dot(out_t, unit)
         d_gatepre = (gated * outer * (1.0 - gate)).astype(BF16)
-        d_normed_out[step] = dot(outgate_w[0], d_gatepre)
+        put_pair(d_normed_out, step, dot(outgate_w[0], d_gatepre))
         unit_all[:, place] = unit
         outer_all[:, place] = d_outer
-        normed_all[:, place] = normed0[step]
+        normed_all[:, place] = pair_of(normed0, step)
         gate_all[:, place] = d_gatepre
         return d_unit * scaled, d_unit
 
-    each_row(rows, 4, upper, sums.at[2:4])
-    each_row(rows, 4, lower, sums.at[0:2])
+    each_pair(rows, upper, sums.at[2:4])
+    each_pair(rows, lower, sums.at[0:2])
     spread_triangle(scr_tri, d_tri_out)
     out_weight_grads(unit_all, outer_all, normed_all, gate_all, out_weights)
     in_weight_grads(upper_all, d_in_all, in_weights)
@@ -377,9 +425,9 @@
     def body(step):
         place = lane_block(step, lanes)
         d_in_all[:, place] = edge_backward(step, scr, proj_factor, gate_factor)
-        normed_all[:, place] = normed[step]
-
-    each_row(rows, 4, body)
+        normed_all[:, place] = pair_of(normed, step)
+
+    each_pair(rows, body)
     first, second, third = d_in_all.shape[0], out0.shape[0], in1.shape[0]
     in_weight_grads(normed_all, d_in_all, packed.at[0:first])
     packed[first : first + second, :] = out0[...]
@@ -397,11 +445,12 @@
     load_back_weights(proj_w, gate_w, 0, back)
 
     def body(step):
-        d_normed = d_normed_gate[step] + dot(back[...], d_in[:, lane_block(step, lanes)])
-        d_normed_out[step] = d_normed
-        return d_normed * scaled_in[step], d_normed
-
-    each_row(rows, 4, body, sums)
+        here = d_in[:, lane_block(step, lanes)]
+        d_normed = pair_of(d_normed_gate, step) + dot(back[...], here)
+        put_pair(d_normed_out, step, d_normed)
+        return d_normed * pair_of(scaled_in, step), d_normed
+
+    each_pair(rows, body, sums)
     small = jnp.concatenate(
         [as_row(sums[0]), as_row(sums[1]), small_middle[0:2], small_middle[2:4], small1[...]],
         axis=0,
@@ -431,12 +480,13 @@
     mine_out[...] = jnp.sum(shared[:, share:].astype(F32), axis=0)
 
     def body(step):
-        total = grad[step] + norm_backward(
-            d_normed[step] * gain, scaled_in[step], inverse_in[pl.ds(step, 1), :]
+        total = pair_of(grad, step) + norm_backward(
+            pair_of(d_normed, step) * gain, pair_of(scaled_in, step),
+            pair_of_rows(inverse_in, step),
         )
-        grad_out[step] = jnp.transpose(total).astype(BF16)
-
-    each_row(rows, 4, body)
+        put_turned_pair(grad_out, step, total)
+
+    each_pair(rows, body)
 
 
 def unpack_kernel(
@@ -917,7 +967,7 @@
 def on_device(pair, *rest, many, few, split):
     rows, lanes, channels = pair.shape
     shards = many * few
-    whole_channels = split == 1 and H % shards == 0 and BLOCK % (H // shards) == 0
+    whole_channels = split == 1 and H % shards == 0 and BLOCK % (H // shards) == 0 and H % (2 * BLOCK) == 0
     tiles = rows == BLOCK and lanes % 128 == 0 and channels == H
     if whole_channels and tiles and many % 2 == 0 and few & (few - 1) == 0:
         return grouped_device(pair, *rest, many=many, few=few)

time: 247 us -> 244 us (0.988)
  Pallas kernels: 22.3 us -> 19 us
    pallas_call x14, Pallas kernels: 22.3 us -> 19 us  [call(): pl.pallas_call(kernel, name=name, out_shape=shapes, in_specs=specs or [VE...]
where the time goes in v12:
time: 244 us
  blocking collectives  222 us (91%)
  Pallas kernels  19 us (8%)
    all_to_all x8, blocking collectives, exchange(): lax.all_to_all(values, ('row', 'col'), split_axis=0, concat_axis=0, tiled...  196 us
    all_to_all x2, blocking collectives, exchange_chips(): lax.all_to_all(values, ('row', 'col'), split_axis=0, concat_axis=0, axis_...  26 us
    pallas_call x14, Pallas kernels, call(): pl.pallas_call(kernel, name=name, out_shape=shapes, in_specs=specs or [VE...  19 us
  transfers between devices with their start and end apart: 2, of which 2 were waited for; matrix products, arithmetic and copies ran while one was open for 0% of the time, Pallas kernels for 1%

profile of v12, /device:TPU:0, one launch (start us, length us, event | category | flops | bytes accessed | tf_op | source)
XLA Modules:
  0.0 243.6 jit_solution(13620692098769147649)
XLA Ops:
  1.3 2.9 %start.1 = (bf16[32,2,4,16,128]{4,3,2,1,0:T(8,128)(2,1)S(1)}, bf16[16,128,128]{2,1,0:T(8,128)(2,1)S(1)}, f32[16,256,128]{2,1,0:T(8,128)S(1)}, f32[16,256,128]{2,...) custom-call(s32[1]{0:T(128)S(6)} %copy.21.lengths, ...), custom_call_target="tpu_custom_call" | custom-call | flops 268435456 | bytes 7620612 | tf_op jit(solution)/shard_map/start/pallas_call | solution.py:563
  4.2 0.0 copy-start
  4.3 0.0 copy-start.1
  4.3 0.0 copy-start.2
  4.3 0.0 copy-start.3
  4.3 0.0 copy-start.5
  4.3 0.0 copy-start.6
  4.3 0.0 copy-start.7
  4.3 0.0 copy-start.8
  4.3 0.0 copy-start.9
  4.3 33.3 %all_to_all.50 = bf16[32,2,4,16,128]{4,3,2,1,0:T(8,128)(2,1)S(1)} all-to-all(bf16[32,2,4,16,128]{4,3,2,1,0:T(8,128)(2,1)S(1)} %get-tuple-element.57), channel_id=1, replica_groups=mesh['grp'=1,'row'=16,'col'=2,'ch'=1] {'row','col'}, dimensions={0} | all-to-all | bytes 2097152 | tf_op jit(solution)/shard_map/all_to_all | solution.py:578
  37.7 0.3 outgoing.1
  38.0 18.4 %all_to_all.51.tri = bf16[32,4,16,128]{3,2,1,0:T(8,128)(2,1)S(1)} all-to-all(bf16[32,4,16,128]{3,2,1,0:T(8,128)(2,1)S(1)} %bitcast.16), channel_id=1, replica_groups=mesh['grp'=1,'row'=16,'col'=2,'ch'=1] {'row','col'}, dimensions={0} | all-to-all | bytes 1048576 | tf_op jit(solution)/shard_map/all_to_all | solution.py:578
  56.5 0.0 copy-done
  56.5 0.0 copy-done.1
  56.5 0.0 copy-done.2
  56.5 0.0 copy-done.3
  56.5 0.0 copy-done.5
  56.5 0.0 copy-done.6
  56.5 0.0 copy-done.7
  56.5 0.0 copy-done.8
  56.5 0.0 copy-done.9
  56.5 3.0 %between.1 = (bf16[32,2,4,16,128]{4,3,2,1,0:T(8,128)(2,1)S(1)}, bf16[16,128,128]{2,1,0:T(8,128)(2,1)S(1)}, bf16[16,128,128]{2,1,0:T(8,128)(2,1)S(1)}, f32[16,256...) custom-call(f32[16,128]{1,0:T(8,128)S(1)} %get-tuple-element.56.mask, ...), custom_call_target="tpu_custom_call" | custom-call | flops 402653184 | bytes 11431936 | tf_op jit(solution)/shard_map/between/pallas_call | solution.py:563
  59.5 0.0 copy-start.4
  59.5 29.7 %all_to_all.52 = bf16[32,2,4,16,128]{4,3,2,1,0:T(8,128)(2,1)S(1)} all-to-all(bf16[32,2,4,16,128]{4,3,2,1,0:T(8,128)(2,1)S(1)} %get-tuple-element.59), channel_id=1, replica_groups=mesh['grp'=1,'row'=16,'col'=2,'ch'=1] {'row','col'}, dimensions={0} | all-to-all | bytes 2097152 | tf_op jit(solution)/shard_map/all_to_all | solution.py:578
  89.2 0.3 incoming.1
  89.5 18.4 %all_to_all.53.tri = bf16[32,4,16,128]{3,2,1,0:T(8,128)(2,1)S(1)} all-to-all(bf16[32,4,16,128]{3,2,1,0:T(8,128)(2,1)S(1)} %bitcast.17), channel_id=1, replica_groups=mesh['grp'=1,'row'=16,'col'=2,'ch'=1] {'row','col'}, dimensions={0} | all-to-all | bytes 1048576 | tf_op jit(solution)/shard_map/all_to_all | solution.py:578
  107.9 0.0 copy-done.4
  107.9 3.1 %turn.1 = (bf16[32,4,16,128]{3,2,1,0:T(8,128)(2,1)S(1)}, bf16[16,128,128]{2,1,0:T(8,128)(2,1)}, f32[16,128,128]{2,1,0:T(8,128)S(1)}, f32[16,128,128]{2,1,0:T(8,1...) custom-call(bf16[32,4,16,128]{3,2,1,0:T(8,128)(2,1)S(1)} %all_to_all.53.tri, ...), custom_call_target="tpu_custom_call" | custom-call | flops 402653184 | bytes 5442560 | tf_op jit(solution)/shard_map/turn/pallas_call | solution.py:563
  111.1 18.4 %all_to_all.54 = bf16[32,4,16,128]{3,2,1,0:T(8,128)(2,1)S(1)} all-to-all(bf16[32,4,16,128]{3,2,1,0:T(8,128)(2,1)S(1)} %get-tuple-element.63), channel_id=1, replica_groups=mesh['grp'=1,'row'=16,'col'=2,'ch'=1] {'row','col'}, dimensions={0} | all-to-all | bytes 1048576 | tf_op jit(solution)/shard_map/all_to_all | solution.py:578
  129.5 0.4 incoming_grad.1
  129.9 29.7 %all_to_all.55.d_edge = bf16[32,2,4,16,128]{4,3,2,1,0:T(8,128)(2,1)S(1)} all-to-all(bf16[32,2,4,16,128]{4,3,2,1,0:T(8,128)(2,1)S(1)} %bitcast.12), channel_id=1, replica_groups=mesh['grp'=1,'row'=16,'col'=2,'ch'=1] {'row','col'}, dimensions={0} | all-to-all | bytes 2097152 | tf_op jit(solution)/shard_map/all_to_all | solution.py:578
  159.6 3.9 %middle.1 = (bf16[32,4,16,128]{3,2,1,0:T(8,128)(2,1)S(1)}, f32[16,128,128]{2,1,0:T(8,128)S(1)}, f32[16,128,128]{2,1,0:T(8,128)S(1)}, bf16[256,128]{1,0:T(8,128)(...) custom-call(bf16[32,2,4,16,128]{4,3,2,1,0:T(8,128)(2,1)S(1)} %all_to_all.55.d_edge, ...), custom_call_target="tpu_custom_call" | custom-call | flops 872415232 | bytes 14767104 | tf_op jit(solution)/shard_map/middle/pallas_call | solution.py:563
  163.5 18.4 %all_to_all.56 = bf16[32,4,16,128]{3,2,1,0:T(8,128)(2,1)S(1)} all-to-all(bf16[32,4,16,128]{3,2,1,0:T(8,128)(2,1)S(1)} %get-tuple-element.73), channel_id=1, replica_groups=mesh['grp'=1,'row'=16,'col'=2,'ch'=1] {'row','col'}, dimensions={0} | all-to-all | bytes 1048576 | tf_op jit(solution)/shard_map/all_to_all | solution.py:578
  181.9 0.5 outgoing_grad.1
  182.4 29.7 %all_to_all.57.d_edge = bf16[32,2,4,16,128]{4,3,2,1,0:T(8,128)(2,1)S(1)} all-to-all(bf16[32,2,4,16,128]{4,3,2,1,0:T(8,128)(2,1)S(1)} %bitcast.13), channel_id=1, replica_groups=mesh['grp'=1,'row'=16,'col'=2,'ch'=1] {'row','col'}, dimensions={0} | all-to-all | bytes 2097152 | tf_op jit(solution)/shard_map/all_to_all | solution.py:578
  212.1 1.3 finish.1
  213.4 0.1 collective-permute-start
  213.5 0.6 norm_sums.1
  214.1 0.8 collective-permute-done.second
  215.0 13.4 %all_to_all.58.parts = bf16[16,48,128]{2,1,0:T(8,128)(2,1)S(1)} all-to-all(bf16[16,48,128]{2,1,0:T(8,128)(2,1)S(1)} %get-tuple-element.87), channel_id=1, replica_groups={{0,1,4,5,8,9,12,13,16,17,20,21,24,25,28,29},{2,3,6,7,10,11,14,15,18,19,..., dimensions={0} | all-to-all | bytes 393216 | tf_op jit(solution)/shard_map/all_to_all | solution.py:590
  228.4 12.6 %all_to_all.59.shared.own = bf16[16,64,128]{2,1,0:T(8,128)(2,1)S(1)} all-to-all(bf16[16,64,128]{2,1,0:T(8,128)(2,1)S(1)} %sum_weights.1), channel_id=1, replica_groups={{0,1,4,5,8,9,12,13,16,17,20,21,24,25,28,29},{2,3,6,7,10,11,14,15,18,19,..., dimensions={0} | all-to-all | bytes 524288 | tf_op jit(solution)/shard_map/all_to_all | solution.py:590
  241.0 0.0 collective-permute-start.1
  241.0 1.4 grad_pair.1
  242.5 0.1 collective-permute-done.1.other
  242.6 1.0 unpack.1
  (2 shorter events, 0.1 us)
Async XLA Ops:
  4.2 52.2 %copy-start = (bf16[2,2,128,128]{3,2,1,0:T(8,128)(2,1)S(1)}, bf16[2,2,128,128]{3,2,1,0:T(8,128)(2,1)}, u32[]{:S(2)}) copy-start(bf16[2,2,128,128]{3,2,1,0:T(8,128)(2,1)} %proj_w.5) | copy-start | bytes 393220
  4.3 52.2 %copy-start.1 = (bf16[2,2,128,128]{3,2,1,0:T(8,128)(2,1)S(1)}, bf16[2,2,128,128]{3,2,1,0:T(8,128)(2,1)}, u32[]{:S(2)}) copy-start(bf16[2,2,128,128]{3,2,1,0:T(8,128)(2,1)} %gate_w.5) | copy-start | bytes 393220
  4.3 52.2 %copy-start.2 = (bf16[2,128,128]{2,1,0:T(8,128)(2,1)S(1)}, bf16[2,128,128]{2,1,0:T(8,128)(2,1)}, u32[]{:S(2)}) copy-start(bf16[2,128,128]{2,1,0:T(8,128)(2,1)} %out_w.5) | copy-start | bytes 196612
  4.3 52.2 %copy-start.3 = (bf16[2,128,128]{2,1,0:T(8,128)(2,1)S(1)}, bf16[2,128,128]{2,1,0:T(8,128)(2,1)}, u32[]{:S(2)}) copy-start(bf16[2,128,128]{2,1,0:T(8,128)(2,1)} %outgate_w.5) | copy-start | bytes 196612
  4.3 52.2 %copy-start.5 = (bf16[16,128,128]{2,1,0:T(8,128)(2,1)S(1)}, bf16[16,128,128]{2,1,0:T(8,128)(2,1)}, u32[]{:S(2)}) copy-start(bf16[16,128,128]{2,1,0:T(8,128)(2,1)} %pair.1) | copy-start | bytes 1572868
  4.3 52.2 %copy-start.6 = (f32[2,128]{1,0:T(2,128)S(1)}, f32[2,128]{1,0:T(2,128)}, u32[]{:S(2)}) copy-start(f32[2,128]{1,0:T(2,128)} %mgain.5) | copy-start | bytes 3076
  4.3 52.2 %copy-start.7 = (f32[2,128]{1,0:T(2,128)S(1)}, f32[2,128]{1,0:T(2,128)}, u32[]{:S(2)}) copy-start(f32[2,128]{1,0:T(2,128)} %mbias.5) | copy-start | bytes 3076
  4.3 52.2 %copy-start.8 = (f32[2,128]{1,0:T(2,128)S(1)}, f32[2,128]{1,0:T(2,128)}, u32[]{:S(2)}) copy-start(f32[2,128]{1,0:T(2,128)} %ngain.5) | copy-start | bytes 3076
  4.3 52.2 %copy-start.9 = (f32[2,128]{1,0:T(2,128)S(1)}, f32[2,128]{1,0:T(2,128)}, u32[]{:S(2)}) copy-start(f32[2,128]{1,0:T(2,128)} %nbias.1) | copy-start | bytes 3076
  59.5 48.5 %copy-start.4 = (bf16[16,128,128]{2,1,0:T(8,128)(2,1)S(1)}, bf16[16,128,128]{2,1,0:T(8,128)(2,1)}, u32[]{:S(2)}) copy-start(bf16[16,128,128]{2,1,0:T(8,128)(2,1)} %cot.1) | copy-start | bytes 1572868
  213.4 1.5 collective-permute-start
  241.0 1.5 collective-permute-start.1

commit v13 on v12

--- a/solution.py
+++ b/solution.py
@@ -79,16 +79,28 @@
     ref[2 * step + 1 : 2 * step + 2, :] = values[:, lanes:]
 
 
-def turned_pair(ref, step):
-    return beside(
-        jnp.transpose(ref[2 * step].astype(F32)), jnp.transpose(ref[2 * step + 1].astype(F32))
-    )
-
-
-def put_turned_pair(ref, step, values):
+def identity(size):
+    down = lax.broadcasted_iota(jnp.int32, (size, size), 0)
+    across = lax.broadcasted_iota(jnp.int32, (size, size), 1)
+    return jnp.where(down == across, 1.0, 0.0).astype(BF16)
+
+
+def turned_pair(unit_matrix, ref, step):
+    lanes, channels = ref.shape[1:]
+    both = ref[2 * step : 2 * step + 2].reshape(2 * lanes, channels)
+    return dot_rt(unit_matrix, both)
+
+
+def put_turned_pair(unit_matrix, ref, step, values):
     lanes = ref.shape[1]
-    ref[2 * step] = jnp.transpose(values[:, :lanes]).astype(BF16)
-    ref[2 * step + 1] = jnp.transpose(values[:, lanes:]).astype(BF16)
+    values = values.astype(BF16)
+    ref[2 * step] = dot_rt(unit_matrix, values[:, :lanes]).astype(BF16)
+    ref[2 * step + 1] = dot_rt(unit_matrix, values[:, lanes:]).astype(BF16)
+
+
+def copy_pair_out(near, far, sems, step):
+    here = pl.ds(2 * step, 2)
+    return pltpu.make_async_copy(near.at[here], far.at[here], sems.at[step])
 
 
 def as_row(total):
@@ -239,10 +251,11 @@
         copy.wait()
     rows, lanes, channels = pair.shape
     load_in_weights(proj_w, gate_w, 0, wts)
+    unit_matrix = identity(channels)
     gain, bias = column(ngain, 0, lanes), column(nbias, 0, lanes)
 
     def body(step):
-        base = turned_pair(pair, step)
+        base = turned_pair(unit_matrix, pair, step)
         scaled = save_norm(step, base, scaled_out, inverse_out)
         normed = (scaled * gain + bias).astype(BF16)
         put_pair(normed_out, step, normed)
@@ -261,6 +274,7 @@
 ):
     rows, lanes, channels = pair.shape
     load_in_weights(proj_w, gate_w, 1, wts)
+    unit_matrix = identity(channels)
     out_t, outgate_t = turned(out_w[0]), turned(outgate_w[0])
     gain, bias = column(ngain, 1, lanes), column(nbias, 1, lanes)
     gain_mid, bias_mid = column(mgain, 0, lanes), column(mbias, 0, lanes)
@@ -274,7 +288,7 @@
         outer = dot(out_t, unit)
         outgate = sigmoid(dot(outgate_t, pair_of(normed0, step)))
         put_pair(outgate_out, step, outgate)
-        mid = (turned_pair(pair, step) + outer * outgate).astype(BF16)
+        mid = (turned_pair(unit_matrix, pair, step) + outer * outgate).astype(BF16)
         put_pair(mid_out, step, mid)
         scaled = save_norm(step, mid.astype(F32), scaled_out, inverse_out)
         normed = (scaled * gain + bias).astype(BF16)
@@ -306,9 +320,10 @@
 def turn_kernel(
     tri, mid, normed, cot, mgain, mbias, out_w, outgate_w,
     d_tri_out, new_out, grad_out, d_normed_out, weights_out, small_out,
-    tri_in, scr, unit_all, outer_all, normed_all, gate_all, sums,
+    new_near, sems, tri_in, scr, unit_all, outer_all, normed_all, gate_all, sums,
 ):
     rows, channels, lanes = mid.shape
+    unit_matrix = identity(channels)
     out_t, outgate_t = turned(out_w[1]), turned(outgate_w[1])
     gain_mid, bias_mid = column(mgain, 1, lanes), column(mbias, 1, lanes)
     collect_triangle(tri, tri_in)
@@ -316,7 +331,7 @@
 
     def body(step):
         here = lane_block(step, lanes)
-        grad = turned_pair(cot, step)
+        grad = turned_pair(unit_matrix, cot, step)
         put_pair(grad_out, step, grad)
         here_normed = pair_of(normed, step)
         outgate = sigmoid(dot(outgate_t, here_normed))
@@ -328,7 +343,9 @@
         put_pair(scr, step, d_tri.astype(BF16))
         unit = (scaled_mid * gain_mid + bias_mid).astype(BF16)
         outer = dot(out_t, unit)
-        put_turned_pair(new_out, step, pair_of(mid, step).astype(F32) + outer * outgate)
+        update = pair_of(mid, step).astype(F32) + outer * outgate
+        put_turned_pair(unit_matrix, new_near, step, update)
+        copy_pair_out(new_near, new_out, sems, step).start()
         d_gatepre = (gated * outer * (1.0 - outgate)).astype(BF16)
         put_pair(d_normed_out, step, dot(outgate_w[1], d_gatepre))
         unit_all[:, here] = unit
@@ -342,6 +359,8 @@
     out_weight_grads(unit_all, outer_all, normed_all, gate_all, weights_out)
     for index in range(2):
         small_out[index : index + 1, :] = as_row(sums[index])
+    for step in range(rows // 2):
+        copy_pair_out(new_near, new_out, sems, step).wait()
 
 
 def edge_backward(step, scratch, proj_factor, gate_factor):
@@ -473,9 +492,11 @@
 
 
 def grad_pair_kernel(
-    share, shared, d_normed, scaled_in, inverse_in, grad, ngain, grad_out, mine_out
+    share, shared, d_normed, scaled_in, inverse_in, grad, ngain, grad_out, mine_out,
+    grad_near, sems,
 ):
     rows, channels, lanes = grad.shape
+    unit_matrix = identity(channels)
     gain = column(ngain, 0, lanes)
     mine_out[...] = jnp.sum(shared[:, share:].astype(F32), axis=0)
 
@@ -484,9 +505,12 @@
             pair_of(d_normed, step) * gain, pair_of(scaled_in, step),
             pair_of_rows(inverse_in, step),
         )
-        put_turned_pair(grad_out, step, total)
+        put_turned_pair(unit_matrix, grad_near, step, total)
+        copy_pair_out(grad_near, grad_out, sems, step).start()
 
     each_pair(rows, body)
+    for step in range(rows // 2):
+        copy_pair_out(grad_near, grad_out, sems, step).wait()
 
 
 def unpack_kernel(
@@ -557,7 +581,7 @@
 FAR = pl.BlockSpec(memory_space=pltpu.HBM)
 
 
-def call(kernel, name, outs, args, scratch=(), flops=0, grant=16, specs=None):
+def call(kernel, name, outs, args, scratch=(), flops=0, grant=16, specs=None, out_specs=None):
     shapes = [jax.ShapeDtypeStruct(shape, dtype) for shape, dtype in outs]
     moved = sum(a.size * a.dtype.itemsize for a in list(args) + shapes)
     return pl.pallas_call(
@@ -565,7 +589,7 @@
         name=name,
         out_shape=shapes,
         in_specs=specs or [VECTORS] * len(args),
-        out_specs=[VECTORS] * len(shapes),
+        out_specs=out_specs or [VECTORS] * len(shapes),
         scratch_shapes=[
             pltpu.VMEM(*item) if isinstance(item, tuple) else item for item in scratch
         ],
@@ -655,7 +679,9 @@
     sent, new_pair, cot_t, d_normed_gate1, out_grads1, small1 = call(
         turn_kernel, "turn", [tri, (pair.shape, BF16), wide, wide, out_rows, small(2)],
         [tri1, mid_t, normed1, cotangent, mgain, mbias, out_w, outgate_w],
-        [mid, mid, flat, flat, flat, flat, sums(2)], 6 * dense,
+        [(pair.shape, BF16), pltpu.SemaphoreType.DMA((rows // 2,)), mid, mid, flat, flat, flat,
+         flat, sums(2)],
+        6 * dense, out_specs=[VECTORS, FAR] + [VECTORS] * 4,
     )
     d_tri1 = exchange(sent).reshape(tri_grid[0])
     (sent,) = call(
@@ -703,6 +729,7 @@
         functools.partial(grad_pair_kernel, share), "grad_pair",
         [(pair.shape, BF16), ((16, H), F32)],
         [shared, d_normed0, scaled0, inverse0, grad, ngain],
+        [(pair.shape, BF16), pltpu.SemaphoreType.DMA((rows // 2,))], out_specs=[FAR, VECTORS],
     )
     grad_proj, grad_gate, grad_out, grad_outgate, *vectors = call(
         functools.partial(unpack_kernel, share, few), "unpack",
@@ -968,7 +995,7 @@
     rows, lanes, channels = pair.shape
     shards = many * few
     whole_channels = split == 1 and H % shards == 0 and BLOCK % (H // shards) == 0 and H % (2 * BLOCK) == 0
-    tiles = rows == BLOCK and lanes % 128 == 0 and channels == H
+    tiles = rows == BLOCK and lanes == H and channels == H
     if whole_channels and tiles and many % 2 == 0 and few & (few - 1) == 0:
         return grouped_device(pair, *rest, many=many, few=few)
     return per_device(pair, *rest)

time: 244 us -> 245 us (level)
  transfers between devices with their start and end apart: 2 -> 2, of which waited for: 2 -> 1; matrix products, arithmetic and copies ran while one was open for 0% -> 0% of each run, Pallas kernels for 1% -> 1%
where the time goes in v13:
time: 245 us; the launch traced here: 244 us
  blocking collectives  222 us (91%)
  Pallas kernels  19.7 us (8%)
    all_to_all x8, blocking collectives, exchange(): lax.all_to_all(values, ('row', 'col'), split_axis=0, concat_axis=0, tiled...  196 us
    all_to_all x2, blocking collectives, exchange_chips(): lax.all_to_all(values, ('row', 'col'), split_axis=0, concat_axis=0, axis_...  26 us
    pallas_call x14, Pallas kernels, call(): pl.pallas_call(kernel, name=name, out_shape=shapes, in_specs=specs or [VE...  19.7 us
  transfers between devices with their start and end apart: 2, of which 1 were waited for; matrix products, arithmetic and copies ran while one was open for 0% of the time, Pallas kernels for 1%

profile of v13, /device:TPU:0, one launch (start us, length us, event | category | flops | bytes accessed | tf_op | source)
XLA Modules:
  0.0 244.2 jit_solution(11150461463350998441)
XLA Ops:
  1.3 3.5 %start.1 = (bf16[32,2,4,16,128]{4,3,2,1,0:T(8,128)(2,1)S(1)}, bf16[16,128,128]{2,1,0:T(8,128)(2,1)S(1)}, f32[16,256,128]{2,1,0:T(8,128)S(1)}, f32[16,256,128]{2,...) custom-call(s32[1]{0:T(128)S(6)} %copy.21.lengths, ...), custom_call_target="tpu_custom_call" | custom-call | flops 268435456 | bytes 7620612 | tf_op jit(solution)/shard_map/start/pallas_call | solution.py:587
  4.8 0.0 copy-start
  4.8 0.0 copy-start.1
  4.9 0.0 copy-start.2
  4.9 0.0 copy-start.3
  4.9 0.0 copy-start.5
  4.9 0.0 copy-start.6
  4.9 0.0 copy-start.7
  4.9 0.0 copy-start.8
  4.9 0.0 copy-start.9
  4.9 33.3 %all_to_all.50 = bf16[32,2,4,16,128]{4,3,2,1,0:T(8,128)(2,1)S(1)} all-to-all(bf16[32,2,4,16,128]{4,3,2,1,0:T(8,128)(2,1)S(1)} %get-tuple-element.57), channel_id=1, replica_groups=mesh['grp'=1,'row'=16,'col'=2,'ch'=1] {'row','col'}, dimensions={0} | all-to-all | bytes 2097152 | tf_op jit(solution)/shard_map/all_to_all | solution.py:602
  38.3 0.3 outgoing.1
  38.6 18.4 %all_to_all.51.tri = bf16[32,4,16,128]{3,2,1,0:T(8,128)(2,1)S(1)} all-to-all(bf16[32,4,16,128]{3,2,1,0:T(8,128)(2,1)S(1)} %bitcast.16), channel_id=1, replica_groups=mesh['grp'=1,'row'=16,'col'=2,'ch'=1] {'row','col'}, dimensions={0} | all-to-all | bytes 1048576 | tf_op jit(solution)/shard_map/all_to_all | solution.py:602
  57.0 0.0 copy-done
  57.1 0.0 copy-done.1
  57.1 0.0 copy-done.2
  57.1 0.0 copy-done.3
  57.1 0.0 copy-done.5
  57.1 0.0 copy-done.6
  57.1 0.0 copy-done.7
  57.1 0.0 copy-done.8
  57.1 0.0 copy-done.9
  57.1 2.9 %between.1 = (bf16[32,2,4,16,128]{4,3,2,1,0:T(8,128)(2,1)S(1)}, bf16[16,128,128]{2,1,0:T(8,128)(2,1)S(1)}, bf16[16,128,128]{2,1,0:T(8,128)(2,1)S(1)}, f32[16,256...) custom-call(f32[16,128]{1,0:T(8,128)S(1)} %get-tuple-element.56.mask, ...), custom_call_target="tpu_custom_call" | custom-call | flops 402653184 | bytes 11431936 | tf_op jit(solution)/shard_map/between/pallas_call | solution.py:587
  60.0 0.0 copy-start.4
  60.0 29.7 %all_to_all.52 = bf16[32,2,4,16,128]{4,3,2,1,0:T(8,128)(2,1)S(1)} all-to-all(bf16[32,2,4,16,128]{4,3,2,1,0:T(8,128)(2,1)S(1)} %get-tuple-element.59), channel_id=1, replica_groups=mesh['grp'=1,'row'=16,'col'=2,'ch'=1] {'row','col'}, dimensions={0} | all-to-all | bytes 2097152 | tf_op jit(solution)/shard_map/all_to_all | solution.py:602
  89.7 0.3 incoming.1
  90.0 18.4 %all_to_all.53.tri = bf16[32,4,16,128]{3,2,1,0:T(8,128)(2,1)S(1)} all-to-all(bf16[32,4,16,128]{3,2,1,0:T(8,128)(2,1)S(1)} %bitcast.17), channel_id=1, replica_groups=mesh['grp'=1,'row'=16,'col'=2,'ch'=1] {'row','col'}, dimensions={0} | all-to-all | bytes 1048576 | tf_op jit(solution)/shard_map/all_to_all | solution.py:602
  108.5 0.0 copy-done.4
  108.5 3.3 %turn.1 = (bf16[32,4,16,128]{3,2,1,0:T(8,128)(2,1)S(1)}, bf16[16,128,128]{2,1,0:T(8,128)(2,1)}, f32[16,128,128]{2,1,0:T(8,128)S(1)}, f32[16,128,128]{2,1,0:T(8,1...) custom-call(bf16[32,4,16,128]{3,2,1,0:T(8,128)(2,1)S(1)} %all_to_all.53.tri, ...), custom_call_target="tpu_custom_call" | custom-call | flops 402653184 | bytes 5442560 | tf_op jit(solution)/shard_map/turn/pallas_call | solution.py:587
  111.7 18.4 %all_to_all.54 = bf16[32,4,16,128]{3,2,1,0:T(8,128)(2,1)S(1)} all-to-all(bf16[32,4,16,128]{3,2,1,0:T(8,128)(2,1)S(1)} %get-tuple-element.63), channel_id=1, replica_groups=mesh['grp'=1,'row'=16,'col'=2,'ch'=1] {'row','col'}, dimensions={0} | all-to-all | bytes 1048576 | tf_op jit(solution)/shard_map/all_to_all | solution.py:602
  130.2 0.4 incoming_grad.1
  130.6 29.7 %all_to_all.55.d_edge = bf16[32,2,4,16,128]{4,3,2,1,0:T(8,128)(2,1)S(1)} all-to-all(bf16[32,2,4,16,128]{4,3,2,1,0:T(8,128)(2,1)S(1)} %bitcast.12), channel_id=1, replica_groups=mesh['grp'=1,'row'=16,'col'=2,'ch'=1] {'row','col'}, dimensions={0} | all-to-all | bytes 2097152 | tf_op jit(solution)/shard_map/all_to_all | solution.py:602
  160.3 3.9 %middle.1 = (bf16[32,4,16,128]{3,2,1,0:T(8,128)(2,1)S(1)}, f32[16,128,128]{2,1,0:T(8,128)S(1)}, f32[16,128,128]{2,1,0:T(8,128)S(1)}, bf16[256,128]{1,0:T(8,128)(...) custom-call(bf16[32,2,4,16,128]{4,3,2,1,0:T(8,128)(2,1)S(1)} %all_to_all.55.d_edge, ...), custom_call_target="tpu_custom_call" | custom-call | flops 872415232 | bytes 14767104 | tf_op jit(solution)/shard_map/middle/pallas_call | solution.py:587
  164.2 18.4 %all_to_all.56 = bf16[32,4,16,128]{3,2,1,0:T(8,128)(2,1)S(1)} all-to-all(bf16[32,4,16,128]{3,2,1,0:T(8,128)(2,1)S(1)} %get-tuple-element.73), channel_id=1, replica_groups=mesh['grp'=1,'row'=16,'col'=2,'ch'=1] {'row','col'}, dimensions={0} | all-to-all | bytes 1048576 | tf_op jit(solution)/shard_map/all_to_all | solution.py:602
  182.6 0.5 outgoing_grad.1
  183.1 29.7 %all_to_all.57.d_edge = bf16[32,2,4,16,128]{4,3,2,1,0:T(8,128)(2,1)S(1)} all-to-all(bf16[32,2,4,16,128]{4,3,2,1,0:T(8,128)(2,1)S(1)} %bitcast.13), channel_id=1, replica_groups=mesh['grp'=1,'row'=16,'col'=2,'ch'=1] {'row','col'}, dimensions={0} | all-to-all | bytes 2097152 | tf_op jit(solution)/shard_map/all_to_all | solution.py:602
  212.7 1.3 finish.1
  214.1 0.1 collective-permute-start
  214.2 0.6 norm_sums.1
  214.8 0.8 collective-permute-done.second
  215.6 13.4 %all_to_all.58.parts = bf16[16,48,128]{2,1,0:T(8,128)(2,1)S(1)} all-to-all(bf16[16,48,128]{2,1,0:T(8,128)(2,1)S(1)} %get-tuple-element.87), channel_id=1, replica_groups={{0,1,4,5,8,9,12,13,16,17,20,21,24,25,28,29},{2,3,6,7,10,11,14,15,18,19,..., dimensions={0} | all-to-all | bytes 393216 | tf_op jit(solution)/shard_map/all_to_all | solution.py:614
  229.1 12.6 %all_to_all.59.shared.own = bf16[16,64,128]{2,1,0:T(8,128)(2,1)S(1)} all-to-all(bf16[16,64,128]{2,1,0:T(8,128)(2,1)S(1)} %sum_weights.1), channel_id=1, replica_groups={{0,1,4,5,8,9,12,13,16,17,20,21,24,25,28,29},{2,3,6,7,10,11,14,15,18,19,..., dimensions={0} | all-to-all | bytes 524288 | tf_op jit(solution)/shard_map/all_to_all | solution.py:614
  241.7 0.0 collective-permute-start.1
  241.7 1.5 grad_pair.1
  243.2 0.0 collective-permute-done.1.other
  243.2 1.0 unpack.1
  (2 shorter events, 0.1 us)
Async XLA Ops:
  4.8 52.2 %copy-start = (bf16[2,2,128,128]{3,2,1,0:T(8,128)(2,1)S(1)}, bf16[2,2,128,128]{3,2,1,0:T(8,128)(2,1)}, u32[]{:S(2)}) copy-start(bf16[2,2,128,128]{3,2,1,0:T(8,128)(2,1)} %proj_w.5) | copy-start | bytes 393220
  4.8 52.2 %copy-start.1 = (bf16[2,2,128,128]{3,2,1,0:T(8,128)(2,1)S(1)}, bf16[2,2,128,128]{3,2,1,0:T(8,128)(2,1)}, u32[]{:S(2)}) copy-start(bf16[2,2,128,128]{3,2,1,0:T(8,128)(2,1)} %gate_w.5) | copy-start | bytes 393220
  4.9 52.2 %copy-start.2 = (bf16[2,128,128]{2,1,0:T(8,128)(2,1)S(1)}, bf16[2,128,128]{2,1,0:T(8,128)(2,1)}, u32[]{:S(2)}) copy-start(bf16[2,128,128]{2,1,0:T(8,128)(2,1)} %out_w.5) | copy-start | bytes 196612
  4.9 52.2 %copy-start.3 = (bf16[2,128,128]{2,1,0:T(8,128)(2,1)S(1)}, bf16[2,128,128]{2,1,0:T(8,128)(2,1)}, u32[]{:S(2)}) copy-start(bf16[2,128,128]{2,1,0:T(8,128)(2,1)} %outgate_w.5) | copy-start | bytes 196612
  4.9 52.2 %copy-start.5 = (bf16[16,128,128]{2,1,0:T(8,128)(2,1)S(1)}, bf16[16,128,128]{2,1,0:T(8,128)(2,1)}, u32[]{:S(2)}) copy-start(bf16[16,128,128]{2,1,0:T(8,128)(2,1)} %pair.1) | copy-start | bytes 1572868
  4.9 52.2 %copy-start.6 = (f32[2,128]{1,0:T(2,128)S(1)}, f32[2,128]{1,0:T(2,128)}, u32[]{:S(2)}) copy-start(f32[2,128]{1,0:T(2,128)} %mgain.5) | copy-start | bytes 3076
  4.9 52.2 %copy-start.7 = (f32[2,128]{1,0:T(2,128)S(1)}, f32[2,128]{1,0:T(2,128)}, u32[]{:S(2)}) copy-start(f32[2,128]{1,0:T(2,128)} %mbias.5) | copy-start | bytes 3076
  4.9 52.2 %copy-start.8 = (f32[2,128]{1,0:T(2,128)S(1)}, f32[2,128]{1,0:T(2,128)}, u32[]{:S(2)}) copy-start(f32[2,128]{1,0:T(2,128)} %ngain.5) | copy-start | bytes 3076
  4.9 52.2 %copy-start.9 = (f32[2,128]{1,0:T(2,128)S(1)}, f32[2,128]{1,0:T(2,128)}, u32[]{:S(2)}) copy-start(f32[2,128]{1,0:T(2,128)} %nbias.1) | copy-start | bytes 3076
  60.0 48.5 %copy-start.4 = (bf16[16,128,128]{2,1,0:T(8,128)(2,1)S(1)}, bf16[16,128,128]{2,1,0:T(8,128)(2,1)}, u32[]{:S(2)}) copy-start(bf16[16,128,128]{2,1,0:T(8,128)(2,1)} %cot.1) | copy-start | bytes 1572868
  214.1 1.5 collective-permute-start
  241.7 1.5 collective-permute-start.1

commit v14 on v12

--- a/solution.py
+++ b/solution.py
@@ -227,21 +227,26 @@
     edge_out, normed_out, proj_out, gate_out, scaled_out, inverse_out, mask_out,
     pair, ngain, nbias, proj_w, gate_w, sems, wts, scr,
 ):
-    far = (proj_far.at[0], gate_far.at[0], ngain_far, nbias_far, pair_far)
-    near = (proj_w.at[0], gate_w.at[0], ngain, nbias, pair)
+    rows, lanes, channels = pair.shape
+    blocks = [pl.ds(start, 4) for start in range(0, rows, 4)]
+    far = [proj_far.at[0], gate_far.at[0], ngain_far, nbias_far]
+    near = [proj_w.at[0], gate_w.at[0], ngain, nbias]
+    far += [pair_far.at[block] for block in blocks]
+    near += [pair.at[block] for block in blocks]
     copies = [
         pltpu.make_async_copy(source, target, sems.at[index])
         for index, (source, target) in enumerate(zip(far, near))
     ]
     for copy in copies:
         copy.start()
-    for copy in copies:
+    for copy in copies[:4]:
         copy.wait()
-    rows, lanes, channels = pair.shape
     load_in_weights(proj_w, gate_w, 0, wts)
     gain, bias = column(ngain, 0, lanes), column(nbias, 0, lanes)
 
     def body(step):
+        if step % 2 == 0:
+            copies[4 + step // 2].wait()
         base = turned_pair(pair, step)
         scaled = save_norm(step, base, scaled_out, inverse_out)
         normed = (scaled * gain + bias).astype(BF16)
@@ -328,7 +333,7 @@
         put_pair(scr, step, d_tri.astype(BF16))
         unit = (scaled_mid * gain_mid + bias_mid).astype(BF16)
         outer = dot(out_t, unit)
-        put_turned_pair(new_out, step, pair_of(mid, step).astype(F32) + outer * outgate)
+        put_pair(new_out, step, (pair_of(mid, step).astype(F32) + outer * outgate).astype(BF16))
         d_gatepre = (gated * outer * (1.0 - outgate)).astype(BF16)
         put_pair(d_normed_out, step, dot(outgate_w[1], d_gatepre))
         unit_all[:, here] = unit
@@ -437,8 +442,8 @@
 
 
 def norm_sums_kernel(
-    d_in, d_normed_gate, scaled_in, proj_w, gate_w, small_middle, small1,
-    d_normed_out, extra_out, back, sums,
+    d_in, d_normed_gate, scaled_in, proj_w, gate_w, small_middle, small1, new_t,
+    d_normed_out, small_out, new_out, back, sums,
 ):
     rows, channels, lanes = scaled_in.shape
     sums[...] = jnp.zeros_like(sums)
@@ -448,28 +453,31 @@
         here = d_in[:, lane_block(step, lanes)]
         d_normed = pair_of(d_normed_gate, step) + dot(back[...], here)
         put_pair(d_normed_out, step, d_normed)
+        put_turned_pair(new_out, step, pair_of(new_t, step).astype(F32))
         return d_normed * pair_of(scaled_in, step), d_normed
 
     each_pair(rows, body, sums)
-    small = jnp.concatenate(
+    small_out[...] = jnp.concatenate(
         [as_row(sums[0]), as_row(sums[1]), small_middle[0:2], small_middle[2:4], small1[...]],
         axis=0,
     )
-    high = small.astype(BF16).astype(F32)
-    extra_out[...] = jnp.concatenate([high, small - high], axis=0).astype(BF16)
-
-
-def add_kernel(first, second, extra, out_ref, extra_out):
+
+
+def add_kernel(first, second, small, out_ref, small_out):
     out_ref[...] = (first[...].astype(F32) + second[...].astype(F32)).astype(BF16)
-    extra_out[...] = extra[...]
-
-
-def sum_kernel(parts, extra, shared_out):
+    small_out[...] = small[...]
+
+
+def sum_kernel(parts, small, small_other, shared_out):
     chips, share, width = parts.shape
     own = jnp.sum(parts[...].astype(F32), axis=0).astype(BF16)
+    both = small[...] + small_other[...]
+    high = both.astype(BF16).astype(F32)
+    core = lax.rem(lax.axis_index("row"), 2)
+    mine = jnp.where(core == 0, high, both - high).astype(BF16)
     for chip in range(chips):
         shared_out[chip, 0:share] = own
-        shared_out[chip, share:] = extra[...]
+        shared_out[chip, share:] = mine
 
 
 def grad_pair_kernel(
@@ -500,7 +508,6 @@
     view[:, core] = own[:, 0:share].astype(F32).reshape(block)
     view[:, 1 - core] = other[:, 0:share].astype(F32).reshape(block)
     total = mine[...] + jnp.sum(other[:, share:].astype(F32), axis=0)
-    total = total[0:8] + total[8:16]
     for module in range(2):
         for index, out in enumerate((norm_gain_out, norm_bias_out, mid_gain_out, mid_bias_out)):
             at = 4 * module + index
@@ -633,7 +640,7 @@
     sent, normed0, *factors0, mask = call(
         start_kernel, "start", [edge, *saved, row], [lengths, *far],
         [(pair.shape, BF16), (ngain.shape, F32), (nbias.shape, F32), (proj_w.shape, BF16),
-         (gate_w.shape, BF16), pltpu.SemaphoreType.DMA((5,)), wts, big],
+         (gate_w.shape, BF16), pltpu.SemaphoreType.DMA((4 + rows // 4,)), wts, big],
         4 * dense, specs=[SCALARS] + [FAR] * len(far),
     )
     edge0 = exchange(sent).reshape(grid[0])
@@ -652,8 +659,8 @@
         functools.partial(triangle_kernel, True), "incoming", [tri_grid], [edge1], (), triangle,
     )
     tri1 = exchange(here.reshape(tri[0]))
-    sent, new_pair, cot_t, d_normed_gate1, out_grads1, small1 = call(
-        turn_kernel, "turn", [tri, (pair.shape, BF16), wide, wide, out_rows, small(2)],
+    sent, new_t, cot_t, d_normed_gate1, out_grads1, small1 = call(
+        turn_kernel, "turn", [tri, tile, wide, wide, out_rows, small(2)],
         [tri1, mid_t, normed1, cotangent, mgain, mbias, out_w, outgate_w],
         [mid, mid, flat, flat, flat, flat, sums(2)], 6 * dense,
     )
@@ -687,21 +694,24 @@
         [big, flat, ((12 * H, H), BF16)], 4 * dense,
     )
     other = swap_cores(other, many, few)
-    d_normed0, extra = call(
-        norm_sums_kernel, "norm_sums", [wide, ((16, H), BF16)],
-        [d_in0, d_normed_gate0, scaled0, proj_w, gate_w, small_middle, small1], [back, sums(2)],
+    d_normed0, sums_here, new_pair = call(
+        norm_sums_kernel, "norm_sums", [wide, small(8), (pair.shape, BF16)],
+        [d_in0, d_normed_gate0, scaled0, proj_w, gate_w, small_middle, small1, new_t],
+        [back, sums(2)],
         4 * dense,
     )
-    own, extra = call(add_kernel, "add_cores", [held, ((16, H), BF16)], [own, other, extra])
+    own, sums_here = call(add_kernel, "add_cores", [held, small(8)], [own, other, sums_here])
+    sums_other = swap_cores(sums_here, many, few)
     parts = exchange_chips(own, many, few)
     (shared,) = call(
-        sum_kernel, "sum_weights", [((chips, share + 16, H), BF16)], [parts, extra]
+        sum_kernel, "sum_weights", [((chips, share + 8, H), BF16)],
+        [parts, sums_here, sums_other],
     )
     shared = exchange_chips(shared, many, few)
     other = swap_cores(shared, many, few)
     grad_pair, mine = call(
         functools.partial(grad_pair_kernel, share), "grad_pair",
-        [(pair.shape, BF16), ((16, H), F32)],
+        [(pair.shape, BF16), small(8)],
         [shared, d_normed0, scaled0, inverse0, grad, ngain],
     )
     grad_proj, grad_gate, grad_out, grad_outgate, *vectors = call(

time: 244 us -> 245 us (level)
  blocking collectives: 222 us -> 209 us
  waiting for transfers between devices: 0.9 us -> 8.86 us
  starting transfers between devices: 0.07 us -> 4.95 us
    all_to_all x2 -> x1, blocking collectives: 26 us -> 12.5 us  [exchange_chips(): lax.all_to_all(values, ('row', 'col'), split_axis=0, concat_axis=0, axis_...]
    all_to_all x0 -> x1, waiting for transfers between devices: none -> 7.69 us  [exchange_chips(): lax.all_to_all(values, ('row', 'col'), split_axis=0, concat_axis=0, axis_...]
    all_to_all x0 -> x1, starting transfers between devices: none -> 4.64 us  [exchange_chips(): lax.all_to_all(values, ('row', 'col'), split_axis=0, concat_axis=0, axis_...]
  transfers between devices with their start and end apart: 2 -> 4, of which waited for: 2 -> 4; matrix products, arithmetic and copies ran while one was open for 0% -> 0% of each run, Pallas kernels for 1% -> 1%
where the time goes in v14:
time: 245 us; the launch traced here: 244 us
  blocking collectives  209 us (85%)
  Pallas kernels  20.5 us (8%)
  waiting for transfers between devices  8.86 us (4%)
  starting transfers between devices  4.95 us (2%)
    all_to_all x8, blocking collectives, exchange(): lax.all_to_all(values, ('row', 'col'), split_axis=0, concat_axis=0, tiled...  196 us
    pallas_call x14, Pallas kernels, call(): pl.pallas_call(kernel, name=name, out_shape=shapes, in_specs=specs or [VE...  20.5 us
    all_to_all x1, blocking collectives, exchange_chips(): lax.all_to_all(values, ('row', 'col'), split_axis=0, concat_axis=0, axis_...  12.5 us
    all_to_all x1, waiting for transfers between devices, exchange_chips(): lax.all_to_all(values, ('row', 'col'), split_axis=0, concat_axis=0, axis_...  7.69 us
  transfers between devices with their start and end apart: 4, of which 4 were waited for; matrix products, arithmetic and copies ran while one was open for 0% of the time, Pallas kernels for 1%

profile of v14, /device:TPU:0, one launch (start us, length us, event | category | flops | bytes accessed | tf_op | source)
XLA Modules:
  0.0 244.4 jit_solution(1082719434372853552)
XLA Ops:
  1.3 3.7 %start.1 = (bf16[32,2,4,16,128]{4,3,2,1,0:T(8,128)(2,1)S(1)}, bf16[16,128,128]{2,1,0:T(8,128)(2,1)S(1)}, f32[16,256,128]{2,1,0:T(8,128)S(1)}, f32[16,256,128]{2,...) custom-call(s32[1]{0:T(128)S(6)} %copy.21.lengths, ...), custom_call_target="tpu_custom_call" | custom-call | flops 268435456 | bytes 7620612 | tf_op jit(solution)/shard_map/start/pallas_call | solution.py:570
  5.0 0.0 copy-start
  5.1 0.0 copy-start.1
  5.1 0.0 copy-start.2
  5.1 0.0 copy-start.3
  5.1 0.0 copy-start.5
  5.1 0.0 copy-start.6
  5.1 0.0 copy-start.7
  5.1 0.0 copy-start.8
  5.1 0.0 copy-start.9
  5.2 33.3 %all_to_all.50 = bf16[32,2,4,16,128]{4,3,2,1,0:T(8,128)(2,1)S(1)} all-to-all(bf16[32,2,4,16,128]{4,3,2,1,0:T(8,128)(2,1)S(1)} %get-tuple-element.57), channel_id=1, replica_groups=mesh['grp'=1,'row'=16,'col'=2,'ch'=1] {'row','col'}, dimensions={0} | all-to-all | bytes 2097152 | tf_op jit(solution)/shard_map/all_to_all | solution.py:585
  38.5 0.3 outgoing.1
  38.8 18.4 %all_to_all.51.tri = bf16[32,4,16,128]{3,2,1,0:T(8,128)(2,1)S(1)} all-to-all(bf16[32,4,16,128]{3,2,1,0:T(8,128)(2,1)S(1)} %bitcast.16), channel_id=1, replica_groups=mesh['grp'=1,'row'=16,'col'=2,'ch'=1] {'row','col'}, dimensions={0} | all-to-all | bytes 1048576 | tf_op jit(solution)/shard_map/all_to_all | solution.py:585
  57.3 0.0 copy-done
  57.3 0.0 copy-done.1
  57.3 0.0 copy-done.2
  57.3 0.0 copy-done.3
  57.3 0.0 copy-done.5
  57.3 0.0 copy-done.6
  57.3 0.0 copy-done.7
  57.3 0.0 copy-done.8
  57.3 0.0 copy-done.9
  57.3 2.9 %between.1 = (bf16[32,2,4,16,128]{4,3,2,1,0:T(8,128)(2,1)S(1)}, bf16[16,128,128]{2,1,0:T(8,128)(2,1)S(1)}, bf16[16,128,128]{2,1,0:T(8,128)(2,1)S(1)}, f32[16,256...) custom-call(f32[16,128]{1,0:T(8,128)S(1)} %get-tuple-element.58.mask, ...), custom_call_target="tpu_custom_call" | custom-call | flops 402653184 | bytes 11431936 | tf_op jit(solution)/shard_map/between/pallas_call | solution.py:570
  60.3 0.0 copy-start.4
  60.3 29.7 %all_to_all.52 = bf16[32,2,4,16,128]{4,3,2,1,0:T(8,128)(2,1)S(1)} all-to-all(bf16[32,2,4,16,128]{4,3,2,1,0:T(8,128)(2,1)S(1)} %get-tuple-element.60), channel_id=1, replica_groups=mesh['grp'=1,'row'=16,'col'=2,'ch'=1] {'row','col'}, dimensions={0} | all-to-all | bytes 2097152 | tf_op jit(solution)/shard_map/all_to_all | solution.py:585
  90.0 0.3 incoming.1
  90.3 18.4 %all_to_all.53.tri = bf16[32,4,16,128]{3,2,1,0:T(8,128)(2,1)S(1)} all-to-all(bf16[32,4,16,128]{3,2,1,0:T(8,128)(2,1)S(1)} %bitcast.17), channel_id=1, replica_groups=mesh['grp'=1,'row'=16,'col'=2,'ch'=1] {'row','col'}, dimensions={0} | all-to-all | bytes 1048576 | tf_op jit(solution)/shard_map/all_to_all | solution.py:585
  108.7 0.0 copy-done.4
  108.7 2.5 %turn.1 = (bf16[32,4,16,128]{3,2,1,0:T(8,128)(2,1)S(1)}, bf16[16,128,128]{2,1,0:T(8,128)(2,1)S(1)}, f32[16,128,128]{2,1,0:T(8,128)S(1)}, f32[16,128,128]{2,1,0:T...) custom-call(bf16[32,4,16,128]{3,2,1,0:T(8,128)(2,1)S(1)} %all_to_all.53.tri, ...), custom_call_target="tpu_custom_call" | custom-call | flops 402653184 | bytes 5442560 | tf_op jit(solution)/shard_map/turn/pallas_call | solution.py:570
  111.2 18.4 %all_to_all.54 = bf16[32,4,16,128]{3,2,1,0:T(8,128)(2,1)S(1)} all-to-all(bf16[32,4,16,128]{3,2,1,0:T(8,128)(2,1)S(1)} %get-tuple-element.63), channel_id=1, replica_groups=mesh['grp'=1,'row'=16,'col'=2,'ch'=1] {'row','col'}, dimensions={0} | all-to-all | bytes 1048576 | tf_op jit(solution)/shard_map/all_to_all | solution.py:585
  129.6 0.4 incoming_grad.1
  130.1 29.7 %all_to_all.55.d_edge = bf16[32,2,4,16,128]{4,3,2,1,0:T(8,128)(2,1)S(1)} all-to-all(bf16[32,2,4,16,128]{4,3,2,1,0:T(8,128)(2,1)S(1)} %bitcast.12), channel_id=1, replica_groups=mesh['grp'=1,'row'=16,'col'=2,'ch'=1] {'row','col'}, dimensions={0} | all-to-all | bytes 2097152 | tf_op jit(solution)/shard_map/all_to_all | solution.py:585
  159.8 4.0 %middle.1 = (bf16[32,4,16,128]{3,2,1,0:T(8,128)(2,1)S(1)}, f32[16,128,128]{2,1,0:T(8,128)S(1)}, f32[16,128,128]{2,1,0:T(8,128)S(1)}, bf16[256,128]{1,0:T(8,128)(...) custom-call(bf16[32,2,4,16,128]{4,3,2,1,0:T(8,128)(2,1)S(1)} %all_to_all.55.d_edge, ...), custom_call_target="tpu_custom_call" | custom-call | flops 872415232 | bytes 14767104 | tf_op jit(solution)/shard_map/middle/pallas_call | solution.py:570
  163.7 18.4 %all_to_all.56 = bf16[32,4,16,128]{3,2,1,0:T(8,128)(2,1)S(1)} all-to-all(bf16[32,4,16,128]{3,2,1,0:T(8,128)(2,1)S(1)} %get-tuple-element.73), channel_id=1, replica_groups=mesh['grp'=1,'row'=16,'col'=2,'ch'=1] {'row','col'}, dimensions={0} | all-to-all | bytes 1048576 | tf_op jit(solution)/shard_map/all_to_all | solution.py:585
  182.2 0.5 outgoing_grad.1
  182.6 29.7 %all_to_all.57.d_edge = bf16[32,2,4,16,128]{4,3,2,1,0:T(8,128)(2,1)S(1)} all-to-all(bf16[32,2,4,16,128]{4,3,2,1,0:T(8,128)(2,1)S(1)} %bitcast.13), channel_id=1, replica_groups=mesh['grp'=1,'row'=16,'col'=2,'ch'=1] {'row','col'}, dimensions={0} | all-to-all | bytes 2097152 | tf_op jit(solution)/shard_map/all_to_all | solution.py:585
  212.3 1.3 finish.1
  213.6 0.1 collective-permute-start
  213.7 1.4 norm_sums.1
  215.1 0.1 collective-permute-done.second
  215.1 0.7 add_cores.1
  215.9 4.6 %all-to-all-start.8 = ((bf16[16,48,128]{2,1,0:T(8,128)(2,1)}), bf16[16,48,128]{2,1,0:T(8,128)(2,1)S(1)}, u32[]{:S(2)}, u32[]{:S(2)}) async-start(bf16[16,48,128]{2,1,0:T(8,128)(2,1)} %get-tuple-element.89), calls=%async_computation.8 | async-start | bytes 393216 | tf_op jit(solution)/shard_map/all_to_all | solution.py:597
  220.5 0.2 collective-permute-start.1
  220.7 1.0 collective-permute-done.1.small_other
  221.7 7.7 %all-to-all-done.8.parts = bf16[16,48,128]{2,1,0:T(8,128)(2,1)S(1)} async-done(((bf16[16,48,128]{2,1,0:T(8,128)(2,1)}), bf16[16,48,128]{2,1,0:T(8,128)(2,1)S(1)}, u32[]{:S(2)}, u32[]{:S(2)}) %all-to-all-start.8) | async-done | bytes 196640 | tf_op jit(solution)/shard_map/all_to_all | solution.py:597
  229.5 12.5 %all_to_all.58.shared.own = bf16[16,56,128]{2,1,0:T(8,128)(2,1)S(1)} all-to-all(bf16[16,56,128]{2,1,0:T(8,128)(2,1)S(1)} %sum_weights.1), channel_id=1, replica_groups={{0,1,4,5,8,9,12,13,16,17,20,21,24,25,28,29},{2,3,6,7,10,11,14,15,18,19,..., dimensions={0} | all-to-all | bytes 458752 | tf_op jit(solution)/shard_map/all_to_all | solution.py:597
  241.9 0.0 collective-permute-start.2
  241.9 1.4 grad_pair.1
  243.3 0.1 collective-permute-done.2.other
  243.4 1.0 unpack.1
  (1 shorter events, 0.0 us)
Async XLA Ops:
  5.0 52.2 %copy-start = (bf16[2,2,128,128]{3,2,1,0:T(8,128)(2,1)S(1)}, bf16[2,2,128,128]{3,2,1,0:T(8,128)(2,1)}, u32[]{:S(2)}) copy-start(bf16[2,2,128,128]{3,2,1,0:T(8,128)(2,1)} %proj_w.5) | copy-start | bytes 393220
  5.1 52.2 %copy-start.1 = (bf16[2,2,128,128]{3,2,1,0:T(8,128)(2,1)S(1)}, bf16[2,2,128,128]{3,2,1,0:T(8,128)(2,1)}, u32[]{:S(2)}) copy-start(bf16[2,2,128,128]{3,2,1,0:T(8,128)(2,1)} %gate_w.5) | copy-start | bytes 393220
  5.1 52.2 %copy-start.2 = (bf16[2,128,128]{2,1,0:T(8,128)(2,1)S(1)}, bf16[2,128,128]{2,1,0:T(8,128)(2,1)}, u32[]{:S(2)}) copy-start(bf16[2,128,128]{2,1,0:T(8,128)(2,1)} %out_w.5) | copy-start | bytes 196612
  5.1 52.2 %copy-start.3 = (bf16[2,128,128]{2,1,0:T(8,128)(2,1)S(1)}, bf16[2,128,128]{2,1,0:T(8,128)(2,1)}, u32[]{:S(2)}) copy-start(bf16[2,128,128]{2,1,0:T(8,128)(2,1)} %outgate_w.5) | copy-start | bytes 196612
  5.1 52.2 %copy-start.5 = (bf16[16,128,128]{2,1,0:T(8,128)(2,1)S(1)}, bf16[16,128,128]{2,1,0:T(8,128)(2,1)}, u32[]{:S(2)}) copy-start(bf16[16,128,128]{2,1,0:T(8,128)(2,1)} %pair.1) | copy-start | bytes 1572868
  5.1 52.2 %copy-start.6 = (f32[2,128]{1,0:T(2,128)S(1)}, f32[2,128]{1,0:T(2,128)}, u32[]{:S(2)}) copy-start(f32[2,128]{1,0:T(2,128)} %mgain.5) | copy-start | bytes 3076
  5.1 52.2 %copy-start.7 = (f32[2,128]{1,0:T(2,128)S(1)}, f32[2,128]{1,0:T(2,128)}, u32[]{:S(2)}) copy-start(f32[2,128]{1,0:T(2,128)} %mbias.5) | copy-start | bytes 3076
  5.1 52.2 %copy-start.8 = (f32[2,128]{1,0:T(2,128)S(1)}, f32[2,128]{1,0:T(2,128)}, u32[]{:S(2)}) copy-start(f32[2,128]{1,0:T(2,128)} %ngain.5) | copy-start | bytes 3076
  5.1 52.2 %copy-start.9 = (f32[2,128]{1,0:T(2,128)S(1)}, f32[2,128]{1,0:T(2,128)}, u32[]{:S(2)}) copy-start(f32[2,128]{1,0:T(2,128)} %nbias.1) | copy-start | bytes 3076
  60.3 48.5 %copy-start.4 = (bf16[16,128,128]{2,1,0:T(8,128)(2,1)S(1)}, bf16[16,128,128]{2,1,0:T(8,128)(2,1)}, u32[]{:S(2)}) copy-start(bf16[16,128,128]{2,1,0:T(8,128)(2,1)} %cot.1) | copy-start | bytes 1572868
  213.6 1.5 collective-permute-start
  215.9 13.6 %all-to-all-start.8 = ((bf16[16,48,128]{2,1,0:T(8,128)(2,1)}), bf16[16,48,128]{2,1,0:T(8,128)(2,1)S(1)}, u32[]{:S(2)}, u32[]{:S(2)}) async-start(bf16[16,48,128]{2,1,0:T(8,128)(2,1)} %get-tuple-element.89), calls=%async_computation.8 | async-start | bytes 393216 | tf_op jit(solution)/shard_map/all_to_all | solution.py:597
  220.5 1.2 collective-permute-start.1
  241.9 1.5 collective-permute-start.2

commit v15 on v12

--- a/solution.py
+++ b/solution.py
@@ -328,7 +328,7 @@
         put_pair(scr, step, d_tri.astype(BF16))
         unit = (scaled_mid * gain_mid + bias_mid).astype(BF16)
         outer = dot(out_t, unit)
-        put_turned_pair(new_out, step, pair_of(mid, step).astype(F32) + outer * outgate)
+        put_pair(new_out, step, (pair_of(mid, step).astype(F32) + outer * outgate).astype(BF16))
         d_gatepre = (gated * outer * (1.0 - outgate)).astype(BF16)
         put_pair(d_normed_out, step, dot(outgate_w[1], d_gatepre))
         unit_all[:, here] = unit
@@ -437,8 +437,8 @@
 
 
 def norm_sums_kernel(
-    d_in, d_normed_gate, scaled_in, proj_w, gate_w, small_middle, small1,
-    d_normed_out, extra_out, back, sums,
+    d_in, d_normed_gate, scaled_in, proj_w, gate_w, small_middle, small1, new_t,
+    d_normed_out, extra_out, new_out, back, sums,
 ):
     rows, channels, lanes = scaled_in.shape
     sums[...] = jnp.zeros_like(sums)
@@ -448,6 +448,7 @@
         here = d_in[:, lane_block(step, lanes)]
         d_normed = pair_of(d_normed_gate, step) + dot(back[...], here)
         put_pair(d_normed_out, step, d_normed)
+        put_turned_pair(new_out, step, pair_of(new_t, step).astype(F32))
         return d_normed * pair_of(scaled_in, step), d_normed
 
     each_pair(rows, body, sums)
@@ -652,8 +653,8 @@
         functools.partial(triangle_kernel, True), "incoming", [tri_grid], [edge1], (), triangle,
     )
     tri1 = exchange(here.reshape(tri[0]))
-    sent, new_pair, cot_t, d_normed_gate1, out_grads1, small1 = call(
-        turn_kernel, "turn", [tri, (pair.shape, BF16), wide, wide, out_rows, small(2)],
+    sent, new_t, cot_t, d_normed_gate1, out_grads1, small1 = call(
+        turn_kernel, "turn", [tri, tile, wide, wide, out_rows, small(2)],
         [tri1, mid_t, normed1, cotangent, mgain, mbias, out_w, outgate_w],
         [mid, mid, flat, flat, flat, flat, sums(2)], 6 * dense,
     )
@@ -687,9 +688,10 @@
         [big, flat, ((12 * H, H), BF16)], 4 * dense,
     )
     other = swap_cores(other, many, few)
-    d_normed0, extra = call(
-        norm_sums_kernel, "norm_sums", [wide, ((16, H), BF16)],
-        [d_in0, d_normed_gate0, scaled0, proj_w, gate_w, small_middle, small1], [back, sums(2)],
+    d_normed0, extra, new_pair = call(
+        norm_sums_kernel, "norm_sums", [wide, ((16, H), BF16), (pair.shape, BF16)],
+        [d_in0, d_normed_gate0, scaled0, proj_w, gate_w, small_middle, small1, new_t],
+        [back, sums(2)],
         4 * dense,
     )
     own, extra = call(add_kernel, "add_cores", [held, ((16, H), BF16)], [own, other, extra])

time: 244 us -> 244 us (level)
  no operation moved by 1% of the time
where the time goes in v15:
time: 244 us; the launch traced here: 243 us
  blocking collectives  222 us (91%)
  Pallas kernels  19.1 us (8%)
    all_to_all x8, blocking collectives, exchange(): lax.all_to_all(values, ('row', 'col'), split_axis=0, concat_axis=0, tiled...  196 us
    all_to_all x2, blocking collectives, exchange_chips(): lax.all_to_all(values, ('row', 'col'), split_axis=0, concat_axis=0, axis_...  26.4 us
    pallas_call x14, Pallas kernels, call(): pl.pallas_call(kernel, name=name, out_shape=shapes, in_specs=specs or [VE...  19.1 us
  transfers between devices with their start and end apart: 2, of which 2 were waited for; matrix products, arithmetic and copies ran while one was open for 0% of the time, Pallas kernels for 1%

profile of v15, /device:TPU:0, one launch (start us, length us, event | category | flops | bytes accessed | tf_op | source)
XLA Modules:
  0.0 243.3 jit_solution(14596825412290349621)
XLA Ops:
  1.3 2.9 %start.1 = (bf16[32,2,4,16,128]{4,3,2,1,0:T(8,128)(2,1)S(1)}, bf16[16,128,128]{2,1,0:T(8,128)(2,1)S(1)}, f32[16,256,128]{2,1,0:T(8,128)S(1)}, f32[16,256,128]{2,...) custom-call(s32[1]{0:T(128)S(6)} %copy.21.lengths, ...), custom_call_target="tpu_custom_call" | custom-call | flops 268435456 | bytes 7620612 | tf_op jit(solution)/shard_map/start/pallas_call | solution.py:564
  4.2 0.0 copy-start
  4.3 0.0 copy-start.1
  4.3 0.0 copy-start.2
  4.3 0.0 copy-start.3
  4.3 0.0 copy-start.5
  4.3 0.0 copy-start.6
  4.3 0.0 copy-start.7
  4.3 0.0 copy-start.8
  4.3 0.0 copy-start.9
  4.3 33.3 %all_to_all.50 = bf16[32,2,4,16,128]{4,3,2,1,0:T(8,128)(2,1)S(1)} all-to-all(bf16[32,2,4,16,128]{4,3,2,1,0:T(8,128)(2,1)S(1)} %get-tuple-element.57), channel_id=1, replica_groups=mesh['grp'=1,'row'=16,'col'=2,'ch'=1] {'row','col'}, dimensions={0} | all-to-all | bytes 2097152 | tf_op jit(solution)/shard_map/all_to_all | solution.py:579
  37.7 0.3 outgoing.1
  38.0 18.4 %all_to_all.51.tri = bf16[32,4,16,128]{3,2,1,0:T(8,128)(2,1)S(1)} all-to-all(bf16[32,4,16,128]{3,2,1,0:T(8,128)(2,1)S(1)} %bitcast.16), channel_id=1, replica_groups=mesh['grp'=1,'row'=16,'col'=2,'ch'=1] {'row','col'}, dimensions={0} | all-to-all | bytes 1048576 | tf_op jit(solution)/shard_map/all_to_all | solution.py:579
  56.5 0.0 copy-done
  56.5 0.0 copy-done.1
  56.5 0.0 copy-done.2
  56.5 0.0 copy-done.3
  56.5 0.0 copy-done.5
  56.5 0.0 copy-done.6
  56.5 0.0 copy-done.7
  56.5 0.0 copy-done.8
  56.5 0.0 copy-done.9
  56.5 3.0 %between.1 = (bf16[32,2,4,16,128]{4,3,2,1,0:T(8,128)(2,1)S(1)}, bf16[16,128,128]{2,1,0:T(8,128)(2,1)S(1)}, bf16[16,128,128]{2,1,0:T(8,128)(2,1)S(1)}, f32[16,256...) custom-call(f32[16,128]{1,0:T(8,128)S(1)} %get-tuple-element.58.mask, ...), custom_call_target="tpu_custom_call" | custom-call | flops 402653184 | bytes 11431936 | tf_op jit(solution)/shard_map/between/pallas_call | solution.py:564
  59.5 0.0 copy-start.4
  59.5 29.7 %all_to_all.52 = bf16[32,2,4,16,128]{4,3,2,1,0:T(8,128)(2,1)S(1)} all-to-all(bf16[32,2,4,16,128]{4,3,2,1,0:T(8,128)(2,1)S(1)} %get-tuple-element.60), channel_id=1, replica_groups=mesh['grp'=1,'row'=16,'col'=2,'ch'=1] {'row','col'}, dimensions={0} | all-to-all | bytes 2097152 | tf_op jit(solution)/shard_map/all_to_all | solution.py:579
  89.2 0.3 incoming.1
  89.5 18.4 %all_to_all.53.tri = bf16[32,4,16,128]{3,2,1,0:T(8,128)(2,1)S(1)} all-to-all(bf16[32,4,16,128]{3,2,1,0:T(8,128)(2,1)S(1)} %bitcast.17), channel_id=1, replica_groups=mesh['grp'=1,'row'=16,'col'=2,'ch'=1] {'row','col'}, dimensions={0} | all-to-all | bytes 1048576 | tf_op jit(solution)/shard_map/all_to_all | solution.py:579
  107.9 0.0 copy-done.4
  107.9 2.5 %turn.1 = (bf16[32,4,16,128]{3,2,1,0:T(8,128)(2,1)S(1)}, bf16[16,128,128]{2,1,0:T(8,128)(2,1)S(1)}, f32[16,128,128]{2,1,0:T(8,128)S(1)}, f32[16,128,128]{2,1,0:T...) custom-call(bf16[32,4,16,128]{3,2,1,0:T(8,128)(2,1)S(1)} %all_to_all.53.tri, ...), custom_call_target="tpu_custom_call" | custom-call | flops 402653184 | bytes 5442560 | tf_op jit(solution)/shard_map/turn/pallas_call | solution.py:564
  110.4 18.4 %all_to_all.54 = bf16[32,4,16,128]{3,2,1,0:T(8,128)(2,1)S(1)} all-to-all(bf16[32,4,16,128]{3,2,1,0:T(8,128)(2,1)S(1)} %get-tuple-element.63), channel_id=1, replica_groups=mesh['grp'=1,'row'=16,'col'=2,'ch'=1] {'row','col'}, dimensions={0} | all-to-all | bytes 1048576 | tf_op jit(solution)/shard_map/all_to_all | solution.py:579
  128.8 0.4 incoming_grad.1
  129.3 29.7 %all_to_all.55.d_edge = bf16[32,2,4,16,128]{4,3,2,1,0:T(8,128)(2,1)S(1)} all-to-all(bf16[32,2,4,16,128]{4,3,2,1,0:T(8,128)(2,1)S(1)} %bitcast.12), channel_id=1, replica_groups=mesh['grp'=1,'row'=16,'col'=2,'ch'=1] {'row','col'}, dimensions={0} | all-to-all | bytes 2097152 | tf_op jit(solution)/shard_map/all_to_all | solution.py:579
  159.0 3.9 %middle.1 = (bf16[32,4,16,128]{3,2,1,0:T(8,128)(2,1)S(1)}, f32[16,128,128]{2,1,0:T(8,128)S(1)}, f32[16,128,128]{2,1,0:T(8,128)S(1)}, bf16[256,128]{1,0:T(8,128)(...) custom-call(bf16[32,2,4,16,128]{4,3,2,1,0:T(8,128)(2,1)S(1)} %all_to_all.55.d_edge, ...), custom_call_target="tpu_custom_call" | custom-call | flops 872415232 | bytes 14767104 | tf_op jit(solution)/shard_map/middle/pallas_call | solution.py:564
  162.9 18.4 %all_to_all.56 = bf16[32,4,16,128]{3,2,1,0:T(8,128)(2,1)S(1)} all-to-all(bf16[32,4,16,128]{3,2,1,0:T(8,128)(2,1)S(1)} %get-tuple-element.73), channel_id=1, replica_groups=mesh['grp'=1,'row'=16,'col'=2,'ch'=1] {'row','col'}, dimensions={0} | all-to-all | bytes 1048576 | tf_op jit(solution)/shard_map/all_to_all | solution.py:579
  181.3 0.5 outgoing_grad.1
  181.8 29.7 %all_to_all.57.d_edge = bf16[32,2,4,16,128]{4,3,2,1,0:T(8,128)(2,1)S(1)} all-to-all(bf16[32,2,4,16,128]{4,3,2,1,0:T(8,128)(2,1)S(1)} %bitcast.13), channel_id=1, replica_groups=mesh['grp'=1,'row'=16,'col'=2,'ch'=1] {'row','col'}, dimensions={0} | all-to-all | bytes 2097152 | tf_op jit(solution)/shard_map/all_to_all | solution.py:579
  211.5 1.3 finish.1
  212.8 0.1 collective-permute-start
  212.9 1.4 norm_sums.1
  214.2 0.1 collective-permute-done.second
  214.3 13.4 %all_to_all.58.parts = bf16[16,48,128]{2,1,0:T(8,128)(2,1)S(1)} all-to-all(bf16[16,48,128]{2,1,0:T(8,128)(2,1)S(1)} %get-tuple-element.89), channel_id=1, replica_groups={{0,1,4,5,8,9,12,13,16,17,20,21,24,25,28,29},{2,3,6,7,10,11,14,15,18,19,..., dimensions={0} | all-to-all | bytes 393216 | tf_op jit(solution)/shard_map/all_to_all | solution.py:591
  227.8 13.1 %all_to_all.59.shared.own = bf16[16,64,128]{2,1,0:T(8,128)(2,1)S(1)} all-to-all(bf16[16,64,128]{2,1,0:T(8,128)(2,1)S(1)} %sum_weights.1), channel_id=1, replica_groups={{0,1,4,5,8,9,12,13,16,17,20,21,24,25,28,29},{2,3,6,7,10,11,14,15,18,19,..., dimensions={0} | all-to-all | bytes 524288 | tf_op jit(solution)/shard_map/all_to_all | solution.py:591
  240.8 0.0 collective-permute-start.1
  240.8 1.4 grad_pair.1
  242.2 0.1 collective-permute-done.1.other
  242.4 1.0 unpack.1
  (2 shorter events, 0.1 us)
Async XLA Ops:
  4.2 52.2 %copy-start = (bf16[2,2,128,128]{3,2,1,0:T(8,128)(2,1)S(1)}, bf16[2,2,128,128]{3,2,1,0:T(8,128)(2,1)}, u32[]{:S(2)}) copy-start(bf16[2,2,128,128]{3,2,1,0:T(8,128)(2,1)} %proj_w.5) | copy-start | bytes 393220
  4.3 52.2 %copy-start.1 = (bf16[2,2,128,128]{3,2,1,0:T(8,128)(2,1)S(1)}, bf16[2,2,128,128]{3,2,1,0:T(8,128)(2,1)}, u32[]{:S(2)}) copy-start(bf16[2,2,128,128]{3,2,1,0:T(8,128)(2,1)} %gate_w.5) | copy-start | bytes 393220
  4.3 52.2 %copy-start.2 = (bf16[2,128,128]{2,1,0:T(8,128)(2,1)S(1)}, bf16[2,128,128]{2,1,0:T(8,128)(2,1)}, u32[]{:S(2)}) copy-start(bf16[2,128,128]{2,1,0:T(8,128)(2,1)} %out_w.5) | copy-start | bytes 196612
  4.3 52.2 %copy-start.3 = (bf16[2,128,128]{2,1,0:T(8,128)(2,1)S(1)}, bf16[2,128,128]{2,1,0:T(8,128)(2,1)}, u32[]{:S(2)}) copy-start(bf16[2,128,128]{2,1,0:T(8,128)(2,1)} %outgate_w.5) | copy-start | bytes 196612
  4.3 52.2 %copy-start.5 = (bf16[16,128,128]{2,1,0:T(8,128)(2,1)S(1)}, bf16[16,128,128]{2,1,0:T(8,128)(2,1)}, u32[]{:S(2)}) copy-start(bf16[16,128,128]{2,1,0:T(8,128)(2,1)} %pair.1) | copy-start | bytes 1572868
  4.3 52.2 %copy-start.6 = (f32[2,128]{1,0:T(2,128)S(1)}, f32[2,128]{1,0:T(2,128)}, u32[]{:S(2)}) copy-start(f32[2,128]{1,0:T(2,128)} %mgain.5) | copy-start | bytes 3076
  4.3 52.2 %copy-start.7 = (f32[2,128]{1,0:T(2,128)S(1)}, f32[2,128]{1,0:T(2,128)}, u32[]{:S(2)}) copy-start(f32[2,128]{1,0:T(2,128)} %mbias.5) | copy-start | bytes 3076
  4.3 52.2 %copy-start.8 = (f32[2,128]{1,0:T(2,128)S(1)}, f32[2,128]{1,0:T(2,128)}, u32[]{:S(2)}) copy-start(f32[2,128]{1,0:T(2,128)} %ngain.5) | copy-start | bytes 3076
  4.3 52.2 %copy-start.9 = (f32[2,128]{1,0:T(2,128)S(1)}, f32[2,128]{1,0:T(2,128)}, u32[]{:S(2)}) copy-start(f32[2,128]{1,0:T(2,128)} %nbias.1) | copy-start | bytes 3076
  59.5 48.5 %copy-start.4 = (bf16[16,128,128]{2,1,0:T(8,128)(2,1)S(1)}, bf16[16,128,128]{2,1,0:T(8,128)(2,1)}, u32[]{:S(2)}) copy-start(bf16[16,128,128]{2,1,0:T(8,128)(2,1)} %cot.1) | copy-start | bytes 1572868
  212.8 1.5 collective-permute-start
  240.8 1.5 collective-permute-start.1

commit v16 on v15

--- a/solution.py
+++ b/solution.py
@@ -47,7 +47,7 @@
 
 
 def turned(weight):
-    return jnp.transpose(weight.astype(F32)).astype(BF16)
+    return jnp.transpose(weight)
 
 
 def column(ref, module, lanes):
@@ -80,15 +80,14 @@
 
 
 def turned_pair(ref, step):
-    return beside(
-        jnp.transpose(ref[2 * step].astype(F32)), jnp.transpose(ref[2 * step + 1].astype(F32))
-    )
+    return beside(jnp.transpose(ref[2 * step]), jnp.transpose(ref[2 * step + 1])).astype(F32)
 
 
 def put_turned_pair(ref, step, values):
     lanes = ref.shape[1]
-    ref[2 * step] = jnp.transpose(values[:, :lanes]).astype(BF16)
-    ref[2 * step + 1] = jnp.transpose(values[:, lanes:]).astype(BF16)
+    values = values.astype(BF16)
+    ref[2 * step] = jnp.transpose(values[:, :lanes])
+    ref[2 * step + 1] = jnp.transpose(values[:, lanes:])
 
 
 def as_row(total):
@@ -448,7 +447,7 @@
         here = d_in[:, lane_block(step, lanes)]
         d_normed = pair_of(d_normed_gate, step) + dot(back[...], here)
         put_pair(d_normed_out, step, d_normed)
-        put_turned_pair(new_out, step, pair_of(new_t, step).astype(F32))
+        put_turned_pair(new_out, step, pair_of(new_t, step))
         return d_normed * pair_of(scaled_in, step), d_normed
 
     each_pair(rows, body, sums)

time: 244 us -> 244 us (level)
  transfers between devices with their start and end apart: 2 -> 2, of which waited for: 2 -> 1; matrix products, arithmetic and copies ran while one was open for 0% -> 0% of each run, Pallas kernels for 1% -> 1%
where the time goes in v16:
time: 244 us; the launch traced here: 243 us
  blocking collectives  223 us (91%)
  Pallas kernels  18.9 us (8%)
    all_to_all x8, blocking collectives, exchange(): lax.all_to_all(values, ('row', 'col'), split_axis=0, concat_axis=0, tiled...  196 us
    all_to_all x2, blocking collectives, exchange_chips(): lax.all_to_all(values, ('row', 'col'), split_axis=0, concat_axis=0, axis_...  26.5 us
    pallas_call x14, Pallas kernels, call(): pl.pallas_call(kernel, name=name, out_shape=shapes, in_specs=specs or [VE...  18.9 us
  transfers between devices with their start and end apart: 2, of which 1 were waited for; matrix products, arithmetic and copies ran while one was open for 0% of the time, Pallas kernels for 1%

profile of v16, /device:TPU:0, one launch (start us, length us, event | category | flops | bytes accessed | tf_op | source)
XLA Modules:
  0.0 243.2 jit_solution(4774372656029093997)
XLA Ops:
  1.3 2.8 %start.1 = (bf16[32,2,4,16,128]{4,3,2,1,0:T(8,128)(2,1)S(1)}, bf16[16,128,128]{2,1,0:T(8,128)(2,1)S(1)}, f32[16,256,128]{2,1,0:T(8,128)S(1)}, f32[16,256,128]{2,...) custom-call(s32[1]{0:T(128)S(6)} %copy.21.lengths, ...), custom_call_target="tpu_custom_call" | custom-call | flops 268435456 | bytes 7620612 | tf_op jit(solution)/shard_map/start/pallas_call | solution.py:563
  4.1 0.0 copy-start
  4.1 0.0 copy-start.1
  4.1 0.0 copy-start.2
  4.1 0.0 copy-start.3
  4.2 0.0 copy-start.5
  4.2 0.0 copy-start.6
  4.2 0.0 copy-start.7
  4.2 0.0 copy-start.8
  4.2 0.0 copy-start.9
  4.2 33.3 %all_to_all.50 = bf16[32,2,4,16,128]{4,3,2,1,0:T(8,128)(2,1)S(1)} all-to-all(bf16[32,2,4,16,128]{4,3,2,1,0:T(8,128)(2,1)S(1)} %get-tuple-element.57), channel_id=1, replica_groups=mesh['grp'=1,'row'=16,'col'=2,'ch'=1] {'row','col'}, dimensions={0} | all-to-all | bytes 2097152 | tf_op jit(solution)/shard_map/all_to_all | solution.py:578
  37.6 0.3 outgoing.1
  37.9 18.4 %all_to_all.51.tri = bf16[32,4,16,128]{3,2,1,0:T(8,128)(2,1)S(1)} all-to-all(bf16[32,4,16,128]{3,2,1,0:T(8,128)(2,1)S(1)} %bitcast.16), channel_id=1, replica_groups=mesh['grp'=1,'row'=16,'col'=2,'ch'=1] {'row','col'}, dimensions={0} | all-to-all | bytes 1048576 | tf_op jit(solution)/shard_map/all_to_all | solution.py:578
  56.3 0.0 copy-done
  56.3 0.0 copy-done.1
  56.3 0.0 copy-done.2
  56.3 0.0 copy-done.3
  56.3 0.0 copy-done.5
  56.4 0.0 copy-done.6
  56.4 0.0 copy-done.7
  56.4 0.0 copy-done.8
  56.4 0.0 copy-done.9
  56.4 3.0 %between.1 = (bf16[32,2,4,16,128]{4,3,2,1,0:T(8,128)(2,1)S(1)}, bf16[16,128,128]{2,1,0:T(8,128)(2,1)S(1)}, bf16[16,128,128]{2,1,0:T(8,128)(2,1)S(1)}, f32[16,256...) custom-call(f32[16,128]{1,0:T(8,128)S(1)} %get-tuple-element.58.mask, ...), custom_call_target="tpu_custom_call" | custom-call | flops 402653184 | bytes 11431936 | tf_op jit(solution)/shard_map/between/pallas_call | solution.py:563
  59.4 0.0 copy-start.4
  59.4 29.7 %all_to_all.52 = bf16[32,2,4,16,128]{4,3,2,1,0:T(8,128)(2,1)S(1)} all-to-all(bf16[32,2,4,16,128]{4,3,2,1,0:T(8,128)(2,1)S(1)} %get-tuple-element.60), channel_id=1, replica_groups=mesh['grp'=1,'row'=16,'col'=2,'ch'=1] {'row','col'}, dimensions={0} | all-to-all | bytes 2097152 | tf_op jit(solution)/shard_map/all_to_all | solution.py:578
  89.1 0.3 incoming.1
  89.4 18.4 %all_to_all.53.tri = bf16[32,4,16,128]{3,2,1,0:T(8,128)(2,1)S(1)} all-to-all(bf16[32,4,16,128]{3,2,1,0:T(8,128)(2,1)S(1)} %bitcast.17), channel_id=1, replica_groups=mesh['grp'=1,'row'=16,'col'=2,'ch'=1] {'row','col'}, dimensions={0} | all-to-all | bytes 1048576 | tf_op jit(solution)/shard_map/all_to_all | solution.py:578
  107.8 0.0 copy-done.4
  107.8 2.4 turn.1
  110.2 18.4 %all_to_all.54 = bf16[32,4,16,128]{3,2,1,0:T(8,128)(2,1)S(1)} all-to-all(bf16[32,4,16,128]{3,2,1,0:T(8,128)(2,1)S(1)} %get-tuple-element.63), channel_id=1, replica_groups=mesh['grp'=1,'row'=16,'col'=2,'ch'=1] {'row','col'}, dimensions={0} | all-to-all | bytes 1048576 | tf_op jit(solution)/shard_map/all_to_all | solution.py:578
  128.6 0.4 incoming_grad.1
  129.1 29.7 %all_to_all.55.d_edge = bf16[32,2,4,16,128]{4,3,2,1,0:T(8,128)(2,1)S(1)} all-to-all(bf16[32,2,4,16,128]{4,3,2,1,0:T(8,128)(2,1)S(1)} %bitcast.12), channel_id=1, replica_groups=mesh['grp'=1,'row'=16,'col'=2,'ch'=1] {'row','col'}, dimensions={0} | all-to-all | bytes 2097152 | tf_op jit(solution)/shard_map/all_to_all | solution.py:578
  158.8 3.9 %middle.1 = (bf16[32,4,16,128]{3,2,1,0:T(8,128)(2,1)S(1)}, f32[16,128,128]{2,1,0:T(8,128)S(1)}, f32[16,128,128]{2,1,0:T(8,128)S(1)}, bf16[256,128]{1,0:T(8,128)(...) custom-call(bf16[32,2,4,16,128]{4,3,2,1,0:T(8,128)(2,1)S(1)} %all_to_all.55.d_edge, ...), custom_call_target="tpu_custom_call" | custom-call | flops 872415232 | bytes 14767104 | tf_op jit(solution)/shard_map/middle/pallas_call | solution.py:563
  162.7 18.4 %all_to_all.56 = bf16[32,4,16,128]{3,2,1,0:T(8,128)(2,1)S(1)} all-to-all(bf16[32,4,16,128]{3,2,1,0:T(8,128)(2,1)S(1)} %get-tuple-element.73), channel_id=1, replica_groups=mesh['grp'=1,'row'=16,'col'=2,'ch'=1] {'row','col'}, dimensions={0} | all-to-all | bytes 1048576 | tf_op jit(solution)/shard_map/all_to_all | solution.py:578
  181.1 0.5 outgoing_grad.1
  181.6 29.7 %all_to_all.57.d_edge = bf16[32,2,4,16,128]{4,3,2,1,0:T(8,128)(2,1)S(1)} all-to-all(bf16[32,2,4,16,128]{4,3,2,1,0:T(8,128)(2,1)S(1)} %bitcast.13), channel_id=1, replica_groups=mesh['grp'=1,'row'=16,'col'=2,'ch'=1] {'row','col'}, dimensions={0} | all-to-all | bytes 2097152 | tf_op jit(solution)/shard_map/all_to_all | solution.py:578
  211.3 1.3 finish.1
  212.6 0.1 collective-permute-start
  212.7 1.4 norm_sums.1
  214.1 0.0 collective-permute-done.second
  214.2 13.4 %all_to_all.58.parts = bf16[16,48,128]{2,1,0:T(8,128)(2,1)S(1)} all-to-all(bf16[16,48,128]{2,1,0:T(8,128)(2,1)S(1)} %get-tuple-element.89), channel_id=1, replica_groups={{0,1,4,5,8,9,12,13,16,17,20,21,24,25,28,29},{2,3,6,7,10,11,14,15,18,19,..., dimensions={0} | all-to-all | bytes 393216 | tf_op jit(solution)/shard_map/all_to_all | solution.py:590
  227.6 13.1 %all_to_all.59.shared.own = bf16[16,64,128]{2,1,0:T(8,128)(2,1)S(1)} all-to-all(bf16[16,64,128]{2,1,0:T(8,128)(2,1)S(1)} %sum_weights.1), channel_id=1, replica_groups={{0,1,4,5,8,9,12,13,16,17,20,21,24,25,28,29},{2,3,6,7,10,11,14,15,18,19,..., dimensions={0} | all-to-all | bytes 524288 | tf_op jit(solution)/shard_map/all_to_all | solution.py:590
  240.7 0.0 collective-permute-start.1
  240.7 1.4 grad_pair.1
  242.1 0.1 collective-permute-done.1.other
  242.2 1.0 unpack.1
  (2 shorter events, 0.1 us)
Async XLA Ops:
  4.1 52.2 %copy-start = (bf16[2,2,128,128]{3,2,1,0:T(8,128)(2,1)S(1)}, bf16[2,2,128,128]{3,2,1,0:T(8,128)(2,1)}, u32[]{:S(2)}) copy-start(bf16[2,2,128,128]{3,2,1,0:T(8,128)(2,1)} %proj_w.5) | copy-start | bytes 393220
  4.1 52.2 %copy-start.1 = (bf16[2,2,128,128]{3,2,1,0:T(8,128)(2,1)S(1)}, bf16[2,2,128,128]{3,2,1,0:T(8,128)(2,1)}, u32[]{:S(2)}) copy-start(bf16[2,2,128,128]{3,2,1,0:T(8,128)(2,1)} %gate_w.5) | copy-start | bytes 393220
  4.1 52.2 %copy-start.2 = (bf16[2,128,128]{2,1,0:T(8,128)(2,1)S(1)}, bf16[2,128,128]{2,1,0:T(8,128)(2,1)}, u32[]{:S(2)}) copy-start(bf16[2,128,128]{2,1,0:T(8,128)(2,1)} %out_w.5) | copy-start | bytes 196612
  4.1 52.2 %copy-start.3 = (bf16[2,128,128]{2,1,0:T(8,128)(2,1)S(1)}, bf16[2,128,128]{2,1,0:T(8,128)(2,1)}, u32[]{:S(2)}) copy-start(bf16[2,128,128]{2,1,0:T(8,128)(2,1)} %outgate_w.5) | copy-start | bytes 196612
  4.2 52.2 %copy-start.5 = (bf16[16,128,128]{2,1,0:T(8,128)(2,1)S(1)}, bf16[16,128,128]{2,1,0:T(8,128)(2,1)}, u32[]{:S(2)}) copy-start(bf16[16,128,128]{2,1,0:T(8,128)(2,1)} %pair.1) | copy-start | bytes 1572868
  4.2 52.2 %copy-start.6 = (f32[2,128]{1,0:T(2,128)S(1)}, f32[2,128]{1,0:T(2,128)}, u32[]{:S(2)}) copy-start(f32[2,128]{1,0:T(2,128)} %mgain.5) | copy-start | bytes 3076
  4.2 52.2 %copy-start.7 = (f32[2,128]{1,0:T(2,128)S(1)}, f32[2,128]{1,0:T(2,128)}, u32[]{:S(2)}) copy-start(f32[2,128]{1,0:T(2,128)} %mbias.5) | copy-start | bytes 3076
  4.2 52.2 %copy-start.8 = (f32[2,128]{1,0:T(2,128)S(1)}, f32[2,128]{1,0:T(2,128)}, u32[]{:S(2)}) copy-start(f32[2,128]{1,0:T(2,128)} %ngain.5) | copy-start | bytes 3076
  4.2 52.2 %copy-start.9 = (f32[2,128]{1,0:T(2,128)S(1)}, f32[2,128]{1,0:T(2,128)}, u32[]{:S(2)}) copy-start(f32[2,128]{1,0:T(2,128)} %nbias.1) | copy-start | bytes 3076
  59.4 48.5 %copy-start.4 = (bf16[16,128,128]{2,1,0:T(8,128)(2,1)S(1)}, bf16[16,128,128]{2,1,0:T(8,128)(2,1)}, u32[]{:S(2)}) copy-start(bf16[16,128,128]{2,1,0:T(8,128)(2,1)} %cot.1) | copy-start | bytes 1572868
  212.6 1.5 collective-permute-start
  240.7 1.5 collective-permute-start.1

commit v17 on v16

--- a/solution.py
+++ b/solution.py
@@ -33,8 +33,8 @@
     return lax.dot_general(left, right, (((0,), (0,)), ((), ())), preferred_element_type=F32)
 
 
-def sigmoid(values):
-    return 0.5 * jnp.tanh(0.5 * values) + 0.5
+def sigmoid_of_minus(values):
+    return 1.0 / (1.0 + jnp.exp(values))
 
 
 def norm_rows(values):
@@ -105,7 +105,7 @@
     width = proj_ref.shape[-1]
     for side in range(2):
         scratch[side * width : (side + 1) * width, :] = turned(proj_ref[module, side])
-        scratch[(2 + side) * width : (3 + side) * width, :] = turned(gate_ref[module, side])
+        scratch[(2 + side) * width : (3 + side) * width, :] = -turned(gate_ref[module, side])
 
 
 def load_back_weights(proj_ref, gate_ref, module, scratch):
@@ -213,7 +213,7 @@
 def save_edges(step, normed, in_weights, mask, proj_out, gate_out):
     pre = dot(in_weights, normed)
     half = pre.shape[0] // 2
-    gating = sigmoid(pre[half:])
+    gating = sigmoid_of_minus(pre[half:])
     factor = gating * mask
     value = pre[:half] * factor
     put_pair(proj_out, step, factor)
@@ -260,7 +260,7 @@
 ):
     rows, lanes, channels = pair.shape
     load_in_weights(proj_w, gate_w, 1, wts)
-    out_t, outgate_t = turned(out_w[0]), turned(outgate_w[0])
+    out_t, outgate_t = turned(out_w[0]), -turned(outgate_w[0])
     gain, bias = column(ngain, 1, lanes), column(nbias, 1, lanes)
     gain_mid, bias_mid = column(mgain, 0, lanes), column(mbias, 0, lanes)
     collect_triangle(tri, tri_in)
@@ -271,7 +271,7 @@
         put_pair_of_rows(inverse_mid_out, step, inverse_mid)
         unit = (scaled_mid * gain_mid + bias_mid).astype(BF16)
         outer = dot(out_t, unit)
-        outgate = sigmoid(dot(outgate_t, pair_of(normed0, step)))
+        outgate = sigmoid_of_minus(dot(outgate_t, pair_of(normed0, step)))
         put_pair(outgate_out, step, outgate)
         mid = (turned_pair(pair, step) + outer * outgate).astype(BF16)
         put_pair(mid_out, step, mid)
@@ -308,7 +308,7 @@
     tri_in, scr, unit_all, outer_all, normed_all, gate_all, sums,
 ):
     rows, channels, lanes = mid.shape
-    out_t, outgate_t = turned(out_w[1]), turned(outgate_w[1])
+    out_t, outgate_t = turned(out_w[1]), -turned(outgate_w[1])
     gain_mid, bias_mid = column(mgain, 1, lanes), column(mbias, 1, lanes)
     collect_triangle(tri, tri_in)
     sums[...] = jnp.zeros_like(sums)
@@ -318,7 +318,7 @@
         grad = turned_pair(cot, step)
         put_pair(grad_out, step, grad)
         here_normed = pair_of(normed, step)
-        outgate = sigmoid(dot(outgate_t, here_normed))
+        outgate = sigmoid_of_minus(dot(outgate_t, here_normed))
         gated = grad * outgate
         d_outer = gated.astype(BF16)
         d_unit = dot(out_w[1], d_outer)

time: 244 us -> 244 us (level)
  no operation moved by 1% of the time
where the time goes in v17:
time: 244 us; the launch traced here: 243 us
  blocking collectives  223 us (91%)
  Pallas kernels  19 us (8%)
    all_to_all x8, blocking collectives, exchange(): lax.all_to_all(values, ('row', 'col'), split_axis=0, concat_axis=0, tiled...  196 us
    all_to_all x2, blocking collectives, exchange_chips(): lax.all_to_all(values, ('row', 'col'), split_axis=0, concat_axis=0, axis_...  26.5 us
    pallas_call x14, Pallas kernels, call(): pl.pallas_call(kernel, name=name, out_shape=shapes, in_specs=specs or [VE...  19 us
  transfers between devices with their start and end apart: 2, of which 1 were waited for; matrix products, arithmetic and copies ran while one was open for 0% of the time, Pallas kernels for 1%

profile of v17, /device:TPU:0, one launch (start us, length us, event | category | flops | bytes accessed | tf_op | source)
XLA Modules:
  0.0 243.3 jit_solution(3788654046929637141)
XLA Ops:
  1.3 2.9 %start.1 = (bf16[32,2,4,16,128]{4,3,2,1,0:T(8,128)(2,1)S(1)}, bf16[16,128,128]{2,1,0:T(8,128)(2,1)S(1)}, f32[16,256,128]{2,1,0:T(8,128)S(1)}, f32[16,256,128]{2,...) custom-call(s32[1]{0:T(128)S(6)} %copy.21.lengths, ...), custom_call_target="tpu_custom_call" | custom-call | flops 268435456 | bytes 7620612 | tf_op jit(solution)/shard_map/start/pallas_call | solution.py:563
  4.2 0.0 copy-start
  4.2 0.0 copy-start.1
  4.2 0.0 copy-start.2
  4.2 0.0 copy-start.3
  4.2 0.0 copy-start.5
  4.2 0.0 copy-start.6
  4.2 0.0 copy-start.7
  4.3 0.0 copy-start.8
  4.3 0.0 copy-start.9
  4.3 33.3 %all_to_all.50 = bf16[32,2,4,16,128]{4,3,2,1,0:T(8,128)(2,1)S(1)} all-to-all(bf16[32,2,4,16,128]{4,3,2,1,0:T(8,128)(2,1)S(1)} %get-tuple-element.57), channel_id=1, replica_groups=mesh['grp'=1,'row'=16,'col'=2,'ch'=1] {'row','col'}, dimensions={0} | all-to-all | bytes 2097152 | tf_op jit(solution)/shard_map/all_to_all | solution.py:578
  37.6 0.3 outgoing.1
  37.9 18.4 %all_to_all.51.tri = bf16[32,4,16,128]{3,2,1,0:T(8,128)(2,1)S(1)} all-to-all(bf16[32,4,16,128]{3,2,1,0:T(8,128)(2,1)S(1)} %bitcast.16), channel_id=1, replica_groups=mesh['grp'=1,'row'=16,'col'=2,'ch'=1] {'row','col'}, dimensions={0} | all-to-all | bytes 1048576 | tf_op jit(solution)/shard_map/all_to_all | solution.py:578
  56.4 0.0 copy-done
  56.4 0.0 copy-done.1
  56.4 0.0 copy-done.2
  56.4 0.0 copy-done.3
  56.4 0.0 copy-done.5
  56.4 0.0 copy-done.6
  56.4 0.0 copy-done.7
  56.4 0.0 copy-done.8
  56.4 0.0 copy-done.9
  56.5 3.0 %between.1 = (bf16[32,2,4,16,128]{4,3,2,1,0:T(8,128)(2,1)S(1)}, bf16[16,128,128]{2,1,0:T(8,128)(2,1)S(1)}, bf16[16,128,128]{2,1,0:T(8,128)(2,1)S(1)}, f32[16,256...) custom-call(f32[16,128]{1,0:T(8,128)S(1)} %get-tuple-element.58.mask, ...), custom_call_target="tpu_custom_call" | custom-call | flops 402653184 | bytes 11431936 | tf_op jit(solution)/shard_map/between/pallas_call | solution.py:563
  59.5 0.0 copy-start.4
  59.5 29.7 %all_to_all.52 = bf16[32,2,4,16,128]{4,3,2,1,0:T(8,128)(2,1)S(1)} all-to-all(bf16[32,2,4,16,128]{4,3,2,1,0:T(8,128)(2,1)S(1)} %get-tuple-element.60), channel_id=1, replica_groups=mesh['grp'=1,'row'=16,'col'=2,'ch'=1] {'row','col'}, dimensions={0} | all-to-all | bytes 2097152 | tf_op jit(solution)/shard_map/all_to_all | solution.py:578
  89.2 0.3 incoming.1
  89.5 18.4 %all_to_all.53.tri = bf16[32,4,16,128]{3,2,1,0:T(8,128)(2,1)S(1)} all-to-all(bf16[32,4,16,128]{3,2,1,0:T(8,128)(2,1)S(1)} %bitcast.17), channel_id=1, replica_groups=mesh['grp'=1,'row'=16,'col'=2,'ch'=1] {'row','col'}, dimensions={0} | all-to-all | bytes 1048576 | tf_op jit(solution)/shard_map/all_to_all | solution.py:578
  108.0 0.0 copy-done.4
  108.0 2.4 turn.1
  110.3 18.4 %all_to_all.54 = bf16[32,4,16,128]{3,2,1,0:T(8,128)(2,1)S(1)} all-to-all(bf16[32,4,16,128]{3,2,1,0:T(8,128)(2,1)S(1)} %get-tuple-element.63), channel_id=1, replica_groups=mesh['grp'=1,'row'=16,'col'=2,'ch'=1] {'row','col'}, dimensions={0} | all-to-all | bytes 1048576 | tf_op jit(solution)/shard_map/all_to_all | solution.py:578
  128.7 0.4 incoming_grad.1
  129.2 29.7 %all_to_all.55.d_edge = bf16[32,2,4,16,128]{4,3,2,1,0:T(8,128)(2,1)S(1)} all-to-all(bf16[32,2,4,16,128]{4,3,2,1,0:T(8,128)(2,1)S(1)} %bitcast.12), channel_id=1, replica_groups=mesh['grp'=1,'row'=16,'col'=2,'ch'=1] {'row','col'}, dimensions={0} | all-to-all | bytes 2097152 | tf_op jit(solution)/shard_map/all_to_all | solution.py:578
  158.9 3.9 %middle.1 = (bf16[32,4,16,128]{3,2,1,0:T(8,128)(2,1)S(1)}, f32[16,128,128]{2,1,0:T(8,128)S(1)}, f32[16,128,128]{2,1,0:T(8,128)S(1)}, bf16[256,128]{1,0:T(8,128)(...) custom-call(bf16[32,2,4,16,128]{4,3,2,1,0:T(8,128)(2,1)S(1)} %all_to_all.55.d_edge, ...), custom_call_target="tpu_custom_call" | custom-call | flops 872415232 | bytes 14767104 | tf_op jit(solution)/shard_map/middle/pallas_call | solution.py:563
  162.8 18.4 %all_to_all.56 = bf16[32,4,16,128]{3,2,1,0:T(8,128)(2,1)S(1)} all-to-all(bf16[32,4,16,128]{3,2,1,0:T(8,128)(2,1)S(1)} %get-tuple-element.73), channel_id=1, replica_groups=mesh['grp'=1,'row'=16,'col'=2,'ch'=1] {'row','col'}, dimensions={0} | all-to-all | bytes 1048576 | tf_op jit(solution)/shard_map/all_to_all | solution.py:578
  181.2 0.5 outgoing_grad.1
  181.7 29.7 %all_to_all.57.d_edge = bf16[32,2,4,16,128]{4,3,2,1,0:T(8,128)(2,1)S(1)} all-to-all(bf16[32,2,4,16,128]{4,3,2,1,0:T(8,128)(2,1)S(1)} %bitcast.13), channel_id=1, replica_groups=mesh['grp'=1,'row'=16,'col'=2,'ch'=1] {'row','col'}, dimensions={0} | all-to-all | bytes 2097152 | tf_op jit(solution)/shard_map/all_to_all | solution.py:578
  211.4 1.3 finish.1
  212.7 0.1 collective-permute-start
  212.8 1.4 norm_sums.1
  214.2 0.0 collective-permute-done.second
  214.3 13.4 %all_to_all.58.parts = bf16[16,48,128]{2,1,0:T(8,128)(2,1)S(1)} all-to-all(bf16[16,48,128]{2,1,0:T(8,128)(2,1)S(1)} %get-tuple-element.89), channel_id=1, replica_groups={{0,1,4,5,8,9,12,13,16,17,20,21,24,25,28,29},{2,3,6,7,10,11,14,15,18,19,..., dimensions={0} | all-to-all | bytes 393216 | tf_op jit(solution)/shard_map/all_to_all | solution.py:590
  227.7 13.1 %all_to_all.59.shared.own = bf16[16,64,128]{2,1,0:T(8,128)(2,1)S(1)} all-to-all(bf16[16,64,128]{2,1,0:T(8,128)(2,1)S(1)} %sum_weights.1), channel_id=1, replica_groups={{0,1,4,5,8,9,12,13,16,17,20,21,24,25,28,29},{2,3,6,7,10,11,14,15,18,19,..., dimensions={0} | all-to-all | bytes 524288 | tf_op jit(solution)/shard_map/all_to_all | solution.py:590
  240.8 0.0 collective-permute-start.1
  240.8 1.4 grad_pair.1
  242.2 0.1 collective-permute-done.1.other
  242.3 1.0 unpack.1
  (2 shorter events, 0.1 us)
Async XLA Ops:
  4.2 52.2 %copy-start = (bf16[2,2,128,128]{3,2,1,0:T(8,128)(2,1)S(1)}, bf16[2,2,128,128]{3,2,1,0:T(8,128)(2,1)}, u32[]{:S(2)}) copy-start(bf16[2,2,128,128]{3,2,1,0:T(8,128)(2,1)} %proj_w.5) | copy-start | bytes 393220
  4.2 52.2 %copy-start.1 = (bf16[2,2,128,128]{3,2,1,0:T(8,128)(2,1)S(1)}, bf16[2,2,128,128]{3,2,1,0:T(8,128)(2,1)}, u32[]{:S(2)}) copy-start(bf16[2,2,128,128]{3,2,1,0:T(8,128)(2,1)} %gate_w.5) | copy-start | bytes 393220
  4.2 52.2 %copy-start.2 = (bf16[2,128,128]{2,1,0:T(8,128)(2,1)S(1)}, bf16[2,128,128]{2,1,0:T(8,128)(2,1)}, u32[]{:S(2)}) copy-start(bf16[2,128,128]{2,1,0:T(8,128)(2,1)} %out_w.5) | copy-start | bytes 196612
  4.2 52.2 %copy-start.3 = (bf16[2,128,128]{2,1,0:T(8,128)(2,1)S(1)}, bf16[2,128,128]{2,1,0:T(8,128)(2,1)}, u32[]{:S(2)}) copy-start(bf16[2,128,128]{2,1,0:T(8,128)(2,1)} %outgate_w.5) | copy-start | bytes 196612
  4.2 52.2 %copy-start.5 = (bf16[16,128,128]{2,1,0:T(8,128)(2,1)S(1)}, bf16[16,128,128]{2,1,0:T(8,128)(2,1)}, u32[]{:S(2)}) copy-start(bf16[16,128,128]{2,1,0:T(8,128)(2,1)} %pair.1) | copy-start | bytes 1572868
  4.2 52.2 %copy-start.6 = (f32[2,128]{1,0:T(2,128)S(1)}, f32[2,128]{1,0:T(2,128)}, u32[]{:S(2)}) copy-start(f32[2,128]{1,0:T(2,128)} %mgain.5) | copy-start | bytes 3076
  4.2 52.2 %copy-start.7 = (f32[2,128]{1,0:T(2,128)S(1)}, f32[2,128]{1,0:T(2,128)}, u32[]{:S(2)}) copy-start(f32[2,128]{1,0:T(2,128)} %mbias.5) | copy-start | bytes 3076
  4.3 52.2 %copy-start.8 = (f32[2,128]{1,0:T(2,128)S(1)}, f32[2,128]{1,0:T(2,128)}, u32[]{:S(2)}) copy-start(f32[2,128]{1,0:T(2,128)} %ngain.5) | copy-start | bytes 3076
  4.3 52.2 %copy-start.9 = (f32[2,128]{1,0:T(2,128)S(1)}, f32[2,128]{1,0:T(2,128)}, u32[]{:S(2)}) copy-start(f32[2,128]{1,0:T(2,128)} %nbias.1) | copy-start | bytes 3076
  59.5 48.5 %copy-start.4 = (bf16[16,128,128]{2,1,0:T(8,128)(2,1)S(1)}, bf16[16,128,128]{2,1,0:T(8,128)(2,1)}, u32[]{:S(2)}) copy-start(bf16[16,128,128]{2,1,0:T(8,128)(2,1)} %cot.1) | copy-start | bytes 1572868
  212.7 1.5 collective-permute-start
  240.8 1.5 collective-permute-start.1

commit v18 on v17

--- a/solution.py
+++ b/solution.py
@@ -293,9 +293,10 @@
 
 def in_weight_grads(normed_all, d_in_all, out_ref):
     width = normed_all.shape[0]
+    grads = dot_rt(normed_all[...], d_in_all[...]).astype(out_ref.dtype)
     for part in range(d_in_all.shape[0] // width):
         block = slice(part * width, (part + 1) * width)
-        out_ref[block, :] = dot_rt(normed_all[...], d_in_all[block, :]).astype(out_ref.dtype)
+        out_ref[block, :] = grads[:, block]
 
 
 def lane_block(step, lanes):
@@ -397,8 +398,25 @@
         gate_all[:, place] = d_gatepre
         return d_unit * scaled, d_unit
 
-    each_pair(rows, upper, sums.at[2:4])
-    each_pair(rows, lower, sums.at[0:2])
+    def both(step):
+        last = rows // 2 - 1
+        above = upper(step) if step <= last else None
+        below = lower(step - 1) if step > 0 else None
+        return above, below
+
+    totals = [None, None, None, None]
+    for step in range(rows // 2 + 1):
+        above, below = both(step)
+        for first, parts in ((2, above), (0, below)):
+            for index in range(0 if parts is None else 2):
+                at = first + index
+                part = parts[index][:, :lanes] + parts[index][:, lanes:]
+                totals[at] = part if totals[at] is None else totals[at] + part
+        if step % 2 == 1 or step == rows // 2:
+            for at in range(4):
+                if totals[at] is not None:
+                    sums[at] += totals[at]
+            totals = [None, None, None, None]
     spread_triangle(scr_tri, d_tri_out)
     out_weight_grads(unit_all, outer_all, normed_all, gate_all, out_weights)
     in_weight_grads(upper_all, d_in_all, in_weights)

time: 244 us -> 244 us (level)
  no operation moved by 1% of the time
where the time goes in v18:
time: 244 us; the launch traced here: 243 us
  blocking collectives  223 us (91%)
  Pallas kernels  19.1 us (8%)
    all_to_all x8, blocking collectives, exchange(): lax.all_to_all(values, ('row', 'col'), split_axis=0, concat_axis=0, tiled...  196 us
    all_to_all x2, blocking collectives, exchange_chips(): lax.all_to_all(values, ('row', 'col'), split_axis=0, concat_axis=0, axis_...  26.5 us
    pallas_call x14, Pallas kernels, call(): pl.pallas_call(kernel, name=name, out_shape=shapes, in_specs=specs or [VE...  19.1 us
  transfers between devices with their start and end apart: 2, of which 1 were waited for; matrix products, arithmetic and copies ran while one was open for 0% of the time, Pallas kernels for 1%

profile of v18, /device:TPU:0, one launch (start us, length us, event | category | flops | bytes accessed | tf_op | source)
XLA Modules:
  0.0 243.4 jit_solution(346808098885523040)
XLA Ops:
  1.3 2.9 %start.1 = (bf16[32,2,4,16,128]{4,3,2,1,0:T(8,128)(2,1)S(1)}, bf16[16,128,128]{2,1,0:T(8,128)(2,1)S(1)}, f32[16,256,128]{2,1,0:T(8,128)S(1)}, f32[16,256,128]{2,...) custom-call(s32[1]{0:T(128)S(6)} %copy.21.lengths, ...), custom_call_target="tpu_custom_call" | custom-call | flops 268435456 | bytes 7620612 | tf_op jit(solution)/shard_map/start/pallas_call | solution.py:581
  4.2 0.0 copy-start
  4.2 0.0 copy-start.1
  4.2 0.0 copy-start.2
  4.2 0.0 copy-start.3
  4.2 0.0 copy-start.5
  4.2 0.0 copy-start.6
  4.2 0.0 copy-start.7
  4.3 0.0 copy-start.8
  4.3 0.0 copy-start.9
  4.3 33.3 %all_to_all.50 = bf16[32,2,4,16,128]{4,3,2,1,0:T(8,128)(2,1)S(1)} all-to-all(bf16[32,2,4,16,128]{4,3,2,1,0:T(8,128)(2,1)S(1)} %get-tuple-element.57), channel_id=1, replica_groups=mesh['grp'=1,'row'=16,'col'=2,'ch'=1] {'row','col'}, dimensions={0} | all-to-all | bytes 2097152 | tf_op jit(solution)/shard_map/all_to_all | solution.py:596
  37.6 0.3 outgoing.1
  37.9 18.4 %all_to_all.51.tri = bf16[32,4,16,128]{3,2,1,0:T(8,128)(2,1)S(1)} all-to-all(bf16[32,4,16,128]{3,2,1,0:T(8,128)(2,1)S(1)} %bitcast.16), channel_id=1, replica_groups=mesh['grp'=1,'row'=16,'col'=2,'ch'=1] {'row','col'}, dimensions={0} | all-to-all | bytes 1048576 | tf_op jit(solution)/shard_map/all_to_all | solution.py:596
  56.4 0.0 copy-done
  56.4 0.0 copy-done.1
  56.4 0.0 copy-done.2
  56.4 0.0 copy-done.3
  56.4 0.0 copy-done.5
  56.4 0.0 copy-done.6
  56.4 0.0 copy-done.7
  56.4 0.0 copy-done.8
  56.4 0.0 copy-done.9
  56.5 3.0 %between.1 = (bf16[32,2,4,16,128]{4,3,2,1,0:T(8,128)(2,1)S(1)}, bf16[16,128,128]{2,1,0:T(8,128)(2,1)S(1)}, bf16[16,128,128]{2,1,0:T(8,128)(2,1)S(1)}, f32[16,256...) custom-call(f32[16,128]{1,0:T(8,128)S(1)} %get-tuple-element.58.mask, ...), custom_call_target="tpu_custom_call" | custom-call | flops 402653184 | bytes 11431936 | tf_op jit(solution)/shard_map/between/pallas_call | solution.py:581
  59.5 0.0 copy-start.4
  59.5 29.7 %all_to_all.52 = bf16[32,2,4,16,128]{4,3,2,1,0:T(8,128)(2,1)S(1)} all-to-all(bf16[32,2,4,16,128]{4,3,2,1,0:T(8,128)(2,1)S(1)} %get-tuple-element.60), channel_id=1, replica_groups=mesh['grp'=1,'row'=16,'col'=2,'ch'=1] {'row','col'}, dimensions={0} | all-to-all | bytes 2097152 | tf_op jit(solution)/shard_map/all_to_all | solution.py:596
  89.2 0.3 incoming.1
  89.5 18.4 %all_to_all.53.tri = bf16[32,4,16,128]{3,2,1,0:T(8,128)(2,1)S(1)} all-to-all(bf16[32,4,16,128]{3,2,1,0:T(8,128)(2,1)S(1)} %bitcast.17), channel_id=1, replica_groups=mesh['grp'=1,'row'=16,'col'=2,'ch'=1] {'row','col'}, dimensions={0} | all-to-all | bytes 1048576 | tf_op jit(solution)/shard_map/all_to_all | solution.py:596
  108.0 0.0 copy-done.4
  108.0 2.4 turn.1
  110.3 18.4 %all_to_all.54 = bf16[32,4,16,128]{3,2,1,0:T(8,128)(2,1)S(1)} all-to-all(bf16[32,4,16,128]{3,2,1,0:T(8,128)(2,1)S(1)} %get-tuple-element.63), channel_id=1, replica_groups=mesh['grp'=1,'row'=16,'col'=2,'ch'=1] {'row','col'}, dimensions={0} | all-to-all | bytes 1048576 | tf_op jit(solution)/shard_map/all_to_all | solution.py:596
  128.7 0.4 incoming_grad.1
  129.2 29.7 %all_to_all.55.d_edge = bf16[32,2,4,16,128]{4,3,2,1,0:T(8,128)(2,1)S(1)} all-to-all(bf16[32,2,4,16,128]{4,3,2,1,0:T(8,128)(2,1)S(1)} %bitcast.12), channel_id=1, replica_groups=mesh['grp'=1,'row'=16,'col'=2,'ch'=1] {'row','col'}, dimensions={0} | all-to-all | bytes 2097152 | tf_op jit(solution)/shard_map/all_to_all | solution.py:596
  158.9 3.9 %middle.1 = (bf16[32,4,16,128]{3,2,1,0:T(8,128)(2,1)S(1)}, f32[16,128,128]{2,1,0:T(8,128)S(1)}, f32[16,128,128]{2,1,0:T(8,128)S(1)}, bf16[256,128]{1,0:T(8,128)(...) custom-call(bf16[32,2,4,16,128]{4,3,2,1,0:T(8,128)(2,1)S(1)} %all_to_all.55.d_edge, ...), custom_call_target="tpu_custom_call" | custom-call | flops 872415232 | bytes 14767104 | tf_op jit(solution)/shard_map/middle/pallas_call | solution.py:581
  162.8 18.4 %all_to_all.56 = bf16[32,4,16,128]{3,2,1,0:T(8,128)(2,1)S(1)} all-to-all(bf16[32,4,16,128]{3,2,1,0:T(8,128)(2,1)S(1)} %get-tuple-element.73), channel_id=1, replica_groups=mesh['grp'=1,'row'=16,'col'=2,'ch'=1] {'row','col'}, dimensions={0} | all-to-all | bytes 1048576 | tf_op jit(solution)/shard_map/all_to_all | solution.py:596
  181.3 0.5 outgoing_grad.1
  181.7 29.7 %all_to_all.57.d_edge = bf16[32,2,4,16,128]{4,3,2,1,0:T(8,128)(2,1)S(1)} all-to-all(bf16[32,2,4,16,128]{4,3,2,1,0:T(8,128)(2,1)S(1)} %bitcast.13), channel_id=1, replica_groups=mesh['grp'=1,'row'=16,'col'=2,'ch'=1] {'row','col'}, dimensions={0} | all-to-all | bytes 2097152 | tf_op jit(solution)/shard_map/all_to_all | solution.py:596
  211.4 1.4 finish.1
  212.8 0.1 collective-permute-start
  212.9 1.4 norm_sums.1
  214.3 0.0 collective-permute-done.second
  214.3 13.4 %all_to_all.58.parts = bf16[16,48,128]{2,1,0:T(8,128)(2,1)S(1)} all-to-all(bf16[16,48,128]{2,1,0:T(8,128)(2,1)S(1)} %get-tuple-element.89), channel_id=1, replica_groups={{0,1,4,5,8,9,12,13,16,17,20,21,24,25,28,29},{2,3,6,7,10,11,14,15,18,19,..., dimensions={0} | all-to-all | bytes 393216 | tf_op jit(solution)/shard_map/all_to_all | solution.py:608
  227.8 13.1 %all_to_all.59.shared.own = bf16[16,64,128]{2,1,0:T(8,128)(2,1)S(1)} all-to-all(bf16[16,64,128]{2,1,0:T(8,128)(2,1)S(1)} %sum_weights.1), channel_id=1, replica_groups={{0,1,4,5,8,9,12,13,16,17,20,21,24,25,28,29},{2,3,6,7,10,11,14,15,18,19,..., dimensions={0} | all-to-all | bytes 524288 | tf_op jit(solution)/shard_map/all_to_all | solution.py:608
  240.9 0.0 collective-permute-start.1
  240.9 1.4 grad_pair.1
  242.3 0.1 collective-permute-done.1.other
  242.4 1.0 unpack.1
  (2 shorter events, 0.1 us)
Async XLA Ops:
  4.2 52.2 %copy-start = (bf16[2,2,128,128]{3,2,1,0:T(8,128)(2,1)S(1)}, bf16[2,2,128,128]{3,2,1,0:T(8,128)(2,1)}, u32[]{:S(2)}) copy-start(bf16[2,2,128,128]{3,2,1,0:T(8,128)(2,1)} %proj_w.5) | copy-start | bytes 393220
  4.2 52.2 %copy-start.1 = (bf16[2,2,128,128]{3,2,1,0:T(8,128)(2,1)S(1)}, bf16[2,2,128,128]{3,2,1,0:T(8,128)(2,1)}, u32[]{:S(2)}) copy-start(bf16[2,2,128,128]{3,2,1,0:T(8,128)(2,1)} %gate_w.5) | copy-start | bytes 393220
  4.2 52.2 %copy-start.2 = (bf16[2,128,128]{2,1,0:T(8,128)(2,1)S(1)}, bf16[2,128,128]{2,1,0:T(8,128)(2,1)}, u32[]{:S(2)}) copy-start(bf16[2,128,128]{2,1,0:T(8,128)(2,1)} %out_w.5) | copy-start | bytes 196612
  4.2 52.2 %copy-start.3 = (bf16[2,128,128]{2,1,0:T(8,128)(2,1)S(1)}, bf16[2,128,128]{2,1,0:T(8,128)(2,1)}, u32[]{:S(2)}) copy-start(bf16[2,128,128]{2,1,0:T(8,128)(2,1)} %outgate_w.5) | copy-start | bytes 196612
  4.2 52.2 %copy-start.5 = (bf16[16,128,128]{2,1,0:T(8,128)(2,1)S(1)}, bf16[16,128,128]{2,1,0:T(8,128)(2,1)}, u32[]{:S(2)}) copy-start(bf16[16,128,128]{2,1,0:T(8,128)(2,1)} %pair.1) | copy-start | bytes 1572868
  4.2 52.2 %copy-start.6 = (f32[2,128]{1,0:T(2,128)S(1)}, f32[2,128]{1,0:T(2,128)}, u32[]{:S(2)}) copy-start(f32[2,128]{1,0:T(2,128)} %mgain.5) | copy-start | bytes 3076
  4.2 52.2 %copy-start.7 = (f32[2,128]{1,0:T(2,128)S(1)}, f32[2,128]{1,0:T(2,128)}, u32[]{:S(2)}) copy-start(f32[2,128]{1,0:T(2,128)} %mbias.5) | copy-start | bytes 3076
  4.3 52.2 %copy-start.8 = (f32[2,128]{1,0:T(2,128)S(1)}, f32[2,128]{1,0:T(2,128)}, u32[]{:S(2)}) copy-start(f32[2,128]{1,0:T(2,128)} %ngain.5) | copy-start | bytes 3076
  4.3 52.2 %copy-start.9 = (f32[2,128]{1,0:T(2,128)S(1)}, f32[2,128]{1,0:T(2,128)}, u32[]{:S(2)}) copy-start(f32[2,128]{1,0:T(2,128)} %nbias.1) | copy-start | bytes 3076
  59.5 48.5 %copy-start.4 = (bf16[16,128,128]{2,1,0:T(8,128)(2,1)S(1)}, bf16[16,128,128]{2,1,0:T(8,128)(2,1)}, u32[]{:S(2)}) copy-start(bf16[16,128,128]{2,1,0:T(8,128)(2,1)} %cot.1) | copy-start | bytes 1572868
  212.8 1.5 collective-permute-start
  240.9 1.5 collective-permute-start.1

commit v19 on v17

--- a/solution.py
+++ b/solution.py
@@ -216,8 +216,8 @@
     gating = sigmoid_of_minus(pre[half:])
     factor = gating * mask
     value = pre[:half] * factor
-    put_pair(proj_out, step, factor)
-    put_pair(gate_out, step, value * (1.0 - gating))
+    put_pair(proj_out, step, factor.astype(BF16))
+    put_pair(gate_out, step, (value * (1.0 - gating)).astype(BF16))
     return value.astype(BF16)
 
 
@@ -345,8 +345,8 @@
 
 def edge_backward(step, scratch, proj_factor, gate_factor):
     here = pair_of(scratch, step).astype(F32)
-    d_proj = (here * pair_of(proj_factor, step)).astype(BF16)
-    d_gate = (here * pair_of(gate_factor, step)).astype(BF16)
+    d_proj = (here * pair_of(proj_factor, step).astype(F32)).astype(BF16)
+    d_gate = (here * pair_of(gate_factor, step).astype(F32)).astype(BF16)
     return jnp.concatenate([d_proj, d_gate], axis=0)
 
 
@@ -606,7 +606,7 @@
     tile = ((rows, channels, lanes), BF16)
     wide = ((rows, channels, lanes), F32)
     row = ((rows, lanes), F32)
-    factor = ((rows, 2 * H, lanes), F32)
+    factor = ((rows, 2 * H, lanes), BF16)
     back = ((channels, 4 * H), BF16)
     wts = ((4 * H, channels), BF16)
     big = ((rows, 2 * H, lanes), BF16)

time: 244 us -> 244 us (level)
  no operation moved by 1% of the time
where the time goes in v19:
time: 244 us; the launch traced here: 243 us
  blocking collectives  223 us (91%)
  Pallas kernels  19.1 us (8%)
    all_to_all x8, blocking collectives, exchange(): lax.all_to_all(values, ('row', 'col'), split_axis=0, concat_axis=0, tiled...  196 us
    all_to_all x2, blocking collectives, exchange_chips(): lax.all_to_all(values, ('row', 'col'), split_axis=0, concat_axis=0, axis_...  26.5 us
    pallas_call x14, Pallas kernels, call(): pl.pallas_call(kernel, name=name, out_shape=shapes, in_specs=specs or [VE...  19.1 us
  transfers between devices with their start and end apart: 2, of which 1 were waited for; matrix products, arithmetic and copies ran while one was open for 0% of the time, Pallas kernels for 1%

profile of v19, /device:TPU:0, one launch (start us, length us, event | category | flops | bytes accessed | tf_op | source)
XLA Modules:
  0.0 243.4 jit_solution(5278574146161557753)
XLA Ops:
  1.3 2.9 %start.1 = (bf16[32,2,4,16,128]{4,3,2,1,0:T(8,128)(2,1)S(1)}, bf16[16,128,128]{2,1,0:T(8,128)(2,1)S(1)}, bf16[16,256,128]{2,1,0:T(8,128)(2,1)S(1)}, bf16[16,256,...) custom-call(s32[1]{0:T(128)S(6)} %copy.21.lengths, ...), custom_call_target="tpu_custom_call" | custom-call | flops 268435456 | bytes 5523460 | tf_op jit(solution)/shard_map/start/pallas_call | solution.py:563
  4.2 0.0 copy-start
  4.2 0.0 copy-start.1
  4.3 0.0 copy-start.2
  4.3 0.0 copy-start.3
  4.3 0.0 copy-start.5
  4.3 0.0 copy-start.6
  4.3 0.0 copy-start.7
  4.3 0.0 copy-start.8
  4.3 0.0 copy-start.9
  4.3 33.3 %all_to_all.50 = bf16[32,2,4,16,128]{4,3,2,1,0:T(8,128)(2,1)S(1)} all-to-all(bf16[32,2,4,16,128]{4,3,2,1,0:T(8,128)(2,1)S(1)} %get-tuple-element.57), channel_id=1, replica_groups=mesh['grp'=1,'row'=16,'col'=2,'ch'=1] {'row','col'}, dimensions={0} | all-to-all | bytes 2097152 | tf_op jit(solution)/shard_map/all_to_all | solution.py:578
  37.7 0.3 outgoing.1
  38.0 18.4 %all_to_all.51.tri = bf16[32,4,16,128]{3,2,1,0:T(8,128)(2,1)S(1)} all-to-all(bf16[32,4,16,128]{3,2,1,0:T(8,128)(2,1)S(1)} %bitcast.16), channel_id=1, replica_groups=mesh['grp'=1,'row'=16,'col'=2,'ch'=1] {'row','col'}, dimensions={0} | all-to-all | bytes 1048576 | tf_op jit(solution)/shard_map/all_to_all | solution.py:578
  56.5 0.0 copy-done
  56.5 0.0 copy-done.1
  56.5 0.0 copy-done.2
  56.5 0.0 copy-done.3
  56.5 0.0 copy-done.5
  56.5 0.0 copy-done.6
  56.5 0.0 copy-done.7
  56.5 0.0 copy-done.8
  56.5 0.0 copy-done.9
  56.5 3.1 %between.1 = (bf16[32,2,4,16,128]{4,3,2,1,0:T(8,128)(2,1)S(1)}, bf16[16,128,128]{2,1,0:T(8,128)(2,1)S(1)}, bf16[16,128,128]{2,1,0:T(8,128)(2,1)S(1)}, bf16[16,25...) custom-call(f32[16,128]{1,0:T(8,128)S(1)} %get-tuple-element.58.mask, ...), custom_call_target="tpu_custom_call" | custom-call | flops 402653184 | bytes 9334784 | tf_op jit(solution)/shard_map/between/pallas_call | solution.py:563
  59.6 0.0 copy-start.4
  59.6 29.7 %all_to_all.52 = bf16[32,2,4,16,128]{4,3,2,1,0:T(8,128)(2,1)S(1)} all-to-all(bf16[32,2,4,16,128]{4,3,2,1,0:T(8,128)(2,1)S(1)} %get-tuple-element.60), channel_id=1, replica_groups=mesh['grp'=1,'row'=16,'col'=2,'ch'=1] {'row','col'}, dimensions={0} | all-to-all | bytes 2097152 | tf_op jit(solution)/shard_map/all_to_all | solution.py:578
  89.3 0.3 incoming.1
  89.6 18.4 %all_to_all.53.tri = bf16[32,4,16,128]{3,2,1,0:T(8,128)(2,1)S(1)} all-to-all(bf16[32,4,16,128]{3,2,1,0:T(8,128)(2,1)S(1)} %bitcast.17), channel_id=1, replica_groups=mesh['grp'=1,'row'=16,'col'=2,'ch'=1] {'row','col'}, dimensions={0} | all-to-all | bytes 1048576 | tf_op jit(solution)/shard_map/all_to_all | solution.py:578
  108.1 0.0 copy-done.4
  108.1 2.3 turn.1
  110.4 18.4 %all_to_all.54 = bf16[32,4,16,128]{3,2,1,0:T(8,128)(2,1)S(1)} all-to-all(bf16[32,4,16,128]{3,2,1,0:T(8,128)(2,1)S(1)} %get-tuple-element.63), channel_id=1, replica_groups=mesh['grp'=1,'row'=16,'col'=2,'ch'=1] {'row','col'}, dimensions={0} | all-to-all | bytes 1048576 | tf_op jit(solution)/shard_map/all_to_all | solution.py:578
  128.8 0.4 incoming_grad.1
  129.3 29.7 %all_to_all.55.d_edge = bf16[32,2,4,16,128]{4,3,2,1,0:T(8,128)(2,1)S(1)} all-to-all(bf16[32,2,4,16,128]{4,3,2,1,0:T(8,128)(2,1)S(1)} %bitcast.12), channel_id=1, replica_groups=mesh['grp'=1,'row'=16,'col'=2,'ch'=1] {'row','col'}, dimensions={0} | all-to-all | bytes 2097152 | tf_op jit(solution)/shard_map/all_to_all | solution.py:578
  159.0 3.9 %middle.1 = (bf16[32,4,16,128]{3,2,1,0:T(8,128)(2,1)S(1)}, f32[16,128,128]{2,1,0:T(8,128)S(1)}, f32[16,128,128]{2,1,0:T(8,128)S(1)}, bf16[256,128]{1,0:T(8,128)(...) custom-call(bf16[32,2,4,16,128]{4,3,2,1,0:T(8,128)(2,1)S(1)} %all_to_all.55.d_edge, ...), custom_call_target="tpu_custom_call" | custom-call | flops 872415232 | bytes 12669952 | tf_op jit(solution)/shard_map/middle/pallas_call | solution.py:563
  162.8 18.4 %all_to_all.56 = bf16[32,4,16,128]{3,2,1,0:T(8,128)(2,1)S(1)} all-to-all(bf16[32,4,16,128]{3,2,1,0:T(8,128)(2,1)S(1)} %get-tuple-element.73), channel_id=1, replica_groups=mesh['grp'=1,'row'=16,'col'=2,'ch'=1] {'row','col'}, dimensions={0} | all-to-all | bytes 1048576 | tf_op jit(solution)/shard_map/all_to_all | solution.py:578
  181.3 0.5 outgoing_grad.1
  181.7 29.7 %all_to_all.57.d_edge = bf16[32,2,4,16,128]{4,3,2,1,0:T(8,128)(2,1)S(1)} all-to-all(bf16[32,2,4,16,128]{4,3,2,1,0:T(8,128)(2,1)S(1)} %bitcast.13), channel_id=1, replica_groups=mesh['grp'=1,'row'=16,'col'=2,'ch'=1] {'row','col'}, dimensions={0} | all-to-all | bytes 2097152 | tf_op jit(solution)/shard_map/all_to_all | solution.py:578
  211.4 1.3 finish.1
  212.8 0.1 collective-permute-start
  212.8 1.5 norm_sums.1
  214.3 0.0 collective-permute-done.second
  214.4 13.4 %all_to_all.58.parts = bf16[16,48,128]{2,1,0:T(8,128)(2,1)S(1)} all-to-all(bf16[16,48,128]{2,1,0:T(8,128)(2,1)S(1)} %get-tuple-element.89), channel_id=1, replica_groups={{0,1,4,5,8,9,12,13,16,17,20,21,24,25,28,29},{2,3,6,7,10,11,14,15,18,19,..., dimensions={0} | all-to-all | bytes 393216 | tf_op jit(solution)/shard_map/all_to_all | solution.py:590
  227.8 13.1 %all_to_all.59.shared.own = bf16[16,64,128]{2,1,0:T(8,128)(2,1)S(1)} all-to-all(bf16[16,64,128]{2,1,0:T(8,128)(2,1)S(1)} %sum_weights.1), channel_id=1, replica_groups={{0,1,4,5,8,9,12,13,16,17,20,21,24,25,28,29},{2,3,6,7,10,11,14,15,18,19,..., dimensions={0} | all-to-all | bytes 524288 | tf_op jit(solution)/shard_map/all_to_all | solution.py:590
  240.9 0.0 collective-permute-start.1
  240.9 1.4 grad_pair.1
  242.3 0.1 collective-permute-done.1.other
  242.4 1.0 unpack.1
  (2 shorter events, 0.1 us)
Async XLA Ops:
  4.2 52.2 %copy-start = (bf16[2,2,128,128]{3,2,1,0:T(8,128)(2,1)S(1)}, bf16[2,2,128,128]{3,2,1,0:T(8,128)(2,1)}, u32[]{:S(2)}) copy-start(bf16[2,2,128,128]{3,2,1,0:T(8,128)(2,1)} %proj_w.5) | copy-start | bytes 393220
  4.2 52.2 %copy-start.1 = (bf16[2,2,128,128]{3,2,1,0:T(8,128)(2,1)S(1)}, bf16[2,2,128,128]{3,2,1,0:T(8,128)(2,1)}, u32[]{:S(2)}) copy-start(bf16[2,2,128,128]{3,2,1,0:T(8,128)(2,1)} %gate_w.5) | copy-start | bytes 393220
  4.3 52.2 %copy-start.2 = (bf16[2,128,128]{2,1,0:T(8,128)(2,1)S(1)}, bf16[2,128,128]{2,1,0:T(8,128)(2,1)}, u32[]{:S(2)}) copy-start(bf16[2,128,128]{2,1,0:T(8,128)(2,1)} %out_w.5) | copy-start | bytes 196612
  4.3 52.2 %copy-start.3 = (bf16[2,128,128]{2,1,0:T(8,128)(2,1)S(1)}, bf16[2,128,128]{2,1,0:T(8,128)(2,1)}, u32[]{:S(2)}) copy-start(bf16[2,128,128]{2,1,0:T(8,128)(2,1)} %outgate_w.5) | copy-start | bytes 196612
  4.3 52.2 %copy-start.5 = (bf16[16,128,128]{2,1,0:T(8,128)(2,1)S(1)}, bf16[16,128,128]{2,1,0:T(8,128)(2,1)}, u32[]{:S(2)}) copy-start(bf16[16,128,128]{2,1,0:T(8,128)(2,1)} %pair.1) | copy-start | bytes 1572868
  4.3 52.2 %copy-start.6 = (f32[2,128]{1,0:T(2,128)S(1)}, f32[2,128]{1,0:T(2,128)}, u32[]{:S(2)}) copy-start(f32[2,128]{1,0:T(2,128)} %mgain.5) | copy-start | bytes 3076
  4.3 52.2 %copy-start.7 = (f32[2,128]{1,0:T(2,128)S(1)}, f32[2,128]{1,0:T(2,128)}, u32[]{:S(2)}) copy-start(f32[2,128]{1,0:T(2,128)} %mbias.5) | copy-start | bytes 3076
  4.3 52.2 %copy-start.8 = (f32[2,128]{1,0:T(2,128)S(1)}, f32[2,128]{1,0:T(2,128)}, u32[]{:S(2)}) copy-start(f32[2,128]{1,0:T(2,128)} %ngain.5) | copy-start | bytes 3076
  4.3 52.2 %copy-start.9 = (f32[2,128]{1,0:T(2,128)S(1)}, f32[2,128]{1,0:T(2,128)}, u32[]{:S(2)}) copy-start(f32[2,128]{1,0:T(2,128)} %nbias.1) | copy-start | bytes 3076
  59.6 48.5 %copy-start.4 = (bf16[16,128,128]{2,1,0:T(8,128)(2,1)S(1)}, bf16[16,128,128]{2,1,0:T(8,128)(2,1)}, u32[]{:S(2)}) copy-start(bf16[16,128,128]{2,1,0:T(8,128)(2,1)} %cot.1) | copy-start | bytes 1572868
  212.8 1.6 collective-permute-start
  240.9 1.5 collective-permute-start.1

commit v20 on v17

--- a/solution.py
+++ b/solution.py
@@ -180,10 +180,10 @@
 
 
 def each_pair(rows, body, sums=None):
-    for block in range(0, rows // 2, 2):
-        parts = [body(block + step) for step in range(2)]
+    for block in range(0, rows // 2, 4):
+        parts = [body(block + step) for step in range(4)]
         for index in range(0 if sums is None else sums.shape[0]):
-            total = parts[0][index] + parts[1][index]
+            total = (parts[0][index] + parts[1][index]) + (parts[2][index] + parts[3][index])
             lanes = sums.shape[-1]
             sums[index] += total[:, :lanes] + total[:, lanes:]
 

time: 244 us -> 244 us (level)
  no operation moved by 1% of the time
where the time goes in v20:
time: 244 us; the launch traced here: 243 us
  blocking collectives  223 us (91%)
  Pallas kernels  19.1 us (8%)
    all_to_all x8, blocking collectives, exchange(): lax.all_to_all(values, ('row', 'col'), split_axis=0, concat_axis=0, tiled...  196 us
    all_to_all x2, blocking collectives, exchange_chips(): lax.all_to_all(values, ('row', 'col'), split_axis=0, concat_axis=0, axis_...  26.5 us
    pallas_call x14, Pallas kernels, call(): pl.pallas_call(kernel, name=name, out_shape=shapes, in_specs=specs or [VE...  19.1 us
  transfers between devices with their start and end apart: 2, of which 1 were waited for; matrix products, arithmetic and copies ran while one was open for 0% of the time, Pallas kernels for 1%

profile of v20, /device:TPU:0, one launch (start us, length us, event | category | flops | bytes accessed | tf_op | source)
XLA Modules:
  0.0 243.4 jit_solution(10735936639877215818)
XLA Ops:
  1.3 2.9 %start.1 = (bf16[32,2,4,16,128]{4,3,2,1,0:T(8,128)(2,1)S(1)}, bf16[16,128,128]{2,1,0:T(8,128)(2,1)S(1)}, f32[16,256,128]{2,1,0:T(8,128)S(1)}, f32[16,256,128]{2,...) custom-call(s32[1]{0:T(128)S(6)} %copy.21.lengths, ...), custom_call_target="tpu_custom_call" | custom-call | flops 268435456 | bytes 7620612 | tf_op jit(solution)/shard_map/start/pallas_call | solution.py:563
  4.2 0.0 copy-start
  4.2 0.0 copy-start.1
  4.2 0.0 copy-start.2
  4.2 0.0 copy-start.3
  4.2 0.0 copy-start.5
  4.2 0.0 copy-start.6
  4.2 0.0 copy-start.7
  4.3 0.0 copy-start.8
  4.3 0.0 copy-start.9
  4.3 33.3 %all_to_all.50 = bf16[32,2,4,16,128]{4,3,2,1,0:T(8,128)(2,1)S(1)} all-to-all(bf16[32,2,4,16,128]{4,3,2,1,0:T(8,128)(2,1)S(1)} %get-tuple-element.57), channel_id=1, replica_groups=mesh['grp'=1,'row'=16,'col'=2,'ch'=1] {'row','col'}, dimensions={0} | all-to-all | bytes 2097152 | tf_op jit(solution)/shard_map/all_to_all | solution.py:578
  37.6 0.3 outgoing.1
  37.9 18.4 %all_to_all.51.tri = bf16[32,4,16,128]{3,2,1,0:T(8,128)(2,1)S(1)} all-to-all(bf16[32,4,16,128]{3,2,1,0:T(8,128)(2,1)S(1)} %bitcast.16), channel_id=1, replica_groups=mesh['grp'=1,'row'=16,'col'=2,'ch'=1] {'row','col'}, dimensions={0} | all-to-all | bytes 1048576 | tf_op jit(solution)/shard_map/all_to_all | solution.py:578
  56.4 0.0 copy-done
  56.4 0.0 copy-done.1
  56.4 0.0 copy-done.2
  56.4 0.0 copy-done.3
  56.4 0.0 copy-done.5
  56.4 0.0 copy-done.6
  56.4 0.0 copy-done.7
  56.4 0.0 copy-done.8
  56.4 0.0 copy-done.9
  56.5 3.0 %between.1 = (bf16[32,2,4,16,128]{4,3,2,1,0:T(8,128)(2,1)S(1)}, bf16[16,128,128]{2,1,0:T(8,128)(2,1)S(1)}, bf16[16,128,128]{2,1,0:T(8,128)(2,1)S(1)}, f32[16,256...) custom-call(f32[16,128]{1,0:T(8,128)S(1)} %get-tuple-element.58.mask, ...), custom_call_target="tpu_custom_call" | custom-call | flops 402653184 | bytes 11431936 | tf_op jit(solution)/shard_map/between/pallas_call | solution.py:563
  59.5 0.0 copy-start.4
  59.5 29.7 %all_to_all.52 = bf16[32,2,4,16,128]{4,3,2,1,0:T(8,128)(2,1)S(1)} all-to-all(bf16[32,2,4,16,128]{4,3,2,1,0:T(8,128)(2,1)S(1)} %get-tuple-element.60), channel_id=1, replica_groups=mesh['grp'=1,'row'=16,'col'=2,'ch'=1] {'row','col'}, dimensions={0} | all-to-all | bytes 2097152 | tf_op jit(solution)/shard_map/all_to_all | solution.py:578
  89.2 0.3 incoming.1
  89.5 18.4 %all_to_all.53.tri = bf16[32,4,16,128]{3,2,1,0:T(8,128)(2,1)S(1)} all-to-all(bf16[32,4,16,128]{3,2,1,0:T(8,128)(2,1)S(1)} %bitcast.17), channel_id=1, replica_groups=mesh['grp'=1,'row'=16,'col'=2,'ch'=1] {'row','col'}, dimensions={0} | all-to-all | bytes 1048576 | tf_op jit(solution)/shard_map/all_to_all | solution.py:578
  108.0 0.0 copy-done.4
  108.0 2.4 turn.1
  110.3 18.4 %all_to_all.54 = bf16[32,4,16,128]{3,2,1,0:T(8,128)(2,1)S(1)} all-to-all(bf16[32,4,16,128]{3,2,1,0:T(8,128)(2,1)S(1)} %get-tuple-element.63), channel_id=1, replica_groups=mesh['grp'=1,'row'=16,'col'=2,'ch'=1] {'row','col'}, dimensions={0} | all-to-all | bytes 1048576 | tf_op jit(solution)/shard_map/all_to_all | solution.py:578
  128.8 0.4 incoming_grad.1
  129.2 29.7 %all_to_all.55.d_edge = bf16[32,2,4,16,128]{4,3,2,1,0:T(8,128)(2,1)S(1)} all-to-all(bf16[32,2,4,16,128]{4,3,2,1,0:T(8,128)(2,1)S(1)} %bitcast.12), channel_id=1, replica_groups=mesh['grp'=1,'row'=16,'col'=2,'ch'=1] {'row','col'}, dimensions={0} | all-to-all | bytes 2097152 | tf_op jit(solution)/shard_map/all_to_all | solution.py:578
  158.9 4.0 %middle.1 = (bf16[32,4,16,128]{3,2,1,0:T(8,128)(2,1)S(1)}, f32[16,128,128]{2,1,0:T(8,128)S(1)}, f32[16,128,128]{2,1,0:T(8,128)S(1)}, bf16[256,128]{1,0:T(8,128)(...) custom-call(bf16[32,2,4,16,128]{4,3,2,1,0:T(8,128)(2,1)S(1)} %all_to_all.55.d_edge, ...), custom_call_target="tpu_custom_call" | custom-call | flops 872415232 | bytes 14767104 | tf_op jit(solution)/shard_map/middle/pallas_call | solution.py:563
  162.9 18.4 %all_to_all.56 = bf16[32,4,16,128]{3,2,1,0:T(8,128)(2,1)S(1)} all-to-all(bf16[32,4,16,128]{3,2,1,0:T(8,128)(2,1)S(1)} %get-tuple-element.73), channel_id=1, replica_groups=mesh['grp'=1,'row'=16,'col'=2,'ch'=1] {'row','col'}, dimensions={0} | all-to-all | bytes 1048576 | tf_op jit(solution)/shard_map/all_to_all | solution.py:578
  181.3 0.5 outgoing_grad.1
  181.8 29.7 %all_to_all.57.d_edge = bf16[32,2,4,16,128]{4,3,2,1,0:T(8,128)(2,1)S(1)} all-to-all(bf16[32,2,4,16,128]{4,3,2,1,0:T(8,128)(2,1)S(1)} %bitcast.13), channel_id=1, replica_groups=mesh['grp'=1,'row'=16,'col'=2,'ch'=1] {'row','col'}, dimensions={0} | all-to-all | bytes 2097152 | tf_op jit(solution)/shard_map/all_to_all | solution.py:578
  211.5 1.3 finish.1
  212.8 0.1 collective-permute-start
  212.9 1.4 norm_sums.1
  214.3 0.0 collective-permute-done.second
  214.4 13.4 %all_to_all.58.parts = bf16[16,48,128]{2,1,0:T(8,128)(2,1)S(1)} all-to-all(bf16[16,48,128]{2,1,0:T(8,128)(2,1)S(1)} %get-tuple-element.89), channel_id=1, replica_groups={{0,1,4,5,8,9,12,13,16,17,20,21,24,25,28,29},{2,3,6,7,10,11,14,15,18,19,..., dimensions={0} | all-to-all | bytes 393216 | tf_op jit(solution)/shard_map/all_to_all | solution.py:590
  227.8 13.1 %all_to_all.59.shared.own = bf16[16,64,128]{2,1,0:T(8,128)(2,1)S(1)} all-to-all(bf16[16,64,128]{2,1,0:T(8,128)(2,1)S(1)} %sum_weights.1), channel_id=1, replica_groups={{0,1,4,5,8,9,12,13,16,17,20,21,24,25,28,29},{2,3,6,7,10,11,14,15,18,19,..., dimensions={0} | all-to-all | bytes 524288 | tf_op jit(solution)/shard_map/all_to_all | solution.py:590
  240.9 0.0 collective-permute-start.1
  240.9 1.4 grad_pair.1
  242.3 0.1 collective-permute-done.1.other
  242.4 1.0 unpack.1
  (2 shorter events, 0.1 us)
Async XLA Ops:
  4.2 52.2 %copy-start = (bf16[2,2,128,128]{3,2,1,0:T(8,128)(2,1)S(1)}, bf16[2,2,128,128]{3,2,1,0:T(8,128)(2,1)}, u32[]{:S(2)}) copy-start(bf16[2,2,128,128]{3,2,1,0:T(8,128)(2,1)} %proj_w.5) | copy-start | bytes 393220
  4.2 52.2 %copy-start.1 = (bf16[2,2,128,128]{3,2,1,0:T(8,128)(2,1)S(1)}, bf16[2,2,128,128]{3,2,1,0:T(8,128)(2,1)}, u32[]{:S(2)}) copy-start(bf16[2,2,128,128]{3,2,1,0:T(8,128)(2,1)} %gate_w.5) | copy-start | bytes 393220
  4.2 52.2 %copy-start.2 = (bf16[2,128,128]{2,1,0:T(8,128)(2,1)S(1)}, bf16[2,128,128]{2,1,0:T(8,128)(2,1)}, u32[]{:S(2)}) copy-start(bf16[2,128,128]{2,1,0:T(8,128)(2,1)} %out_w.5) | copy-start | bytes 196612
  4.2 52.2 %copy-start.3 = (bf16[2,128,128]{2,1,0:T(8,128)(2,1)S(1)}, bf16[2,128,128]{2,1,0:T(8,128)(2,1)}, u32[]{:S(2)}) copy-start(bf16[2,128,128]{2,1,0:T(8,128)(2,1)} %outgate_w.5) | copy-start | bytes 196612
  4.2 52.2 %copy-start.5 = (bf16[16,128,128]{2,1,0:T(8,128)(2,1)S(1)}, bf16[16,128,128]{2,1,0:T(8,128)(2,1)}, u32[]{:S(2)}) copy-start(bf16[16,128,128]{2,1,0:T(8,128)(2,1)} %pair.1) | copy-start | bytes 1572868
  4.2 52.2 %copy-start.6 = (f32[2,128]{1,0:T(2,128)S(1)}, f32[2,128]{1,0:T(2,128)}, u32[]{:S(2)}) copy-start(f32[2,128]{1,0:T(2,128)} %mgain.5) | copy-start | bytes 3076
  4.2 52.2 %copy-start.7 = (f32[2,128]{1,0:T(2,128)S(1)}, f32[2,128]{1,0:T(2,128)}, u32[]{:S(2)}) copy-start(f32[2,128]{1,0:T(2,128)} %mbias.5) | copy-start | bytes 3076
  4.3 52.2 %copy-start.8 = (f32[2,128]{1,0:T(2,128)S(1)}, f32[2,128]{1,0:T(2,128)}, u32[]{:S(2)}) copy-start(f32[2,128]{1,0:T(2,128)} %ngain.5) | copy-start | bytes 3076
  4.3 52.2 %copy-start.9 = (f32[2,128]{1,0:T(2,128)S(1)}, f32[2,128]{1,0:T(2,128)}, u32[]{:S(2)}) copy-start(f32[2,128]{1,0:T(2,128)} %nbias.1) | copy-start | bytes 3076
  59.5 48.5 %copy-start.4 = (bf16[16,128,128]{2,1,0:T(8,128)(2,1)S(1)}, bf16[16,128,128]{2,1,0:T(8,128)(2,1)}, u32[]{:S(2)}) copy-start(bf16[16,128,128]{2,1,0:T(8,128)(2,1)} %cot.1) | copy-start | bytes 1572868
  212.8 1.5 collective-permute-start
  240.9 1.5 collective-permute-start.1
